TPU v7x, 32 devices: a whole 2x2x4 slice. The times are simulated.
32 devices in a mesh: expert: 8 (over z, x), tensor: 4 (over y, core).
Axes of the slice: x: 2, y: 2, z: 4, core: 2. Of those that a mesh axis runs over, the one named last changes fastest.
Arguments:
- tokens: bfloat16 [4096, 2048], P('expert'), may hold values from -6 to 6
- documents: int32 [4096], P('expert'), may hold values from 0 to 4095, as said below
- routes: int32 [4096, 8], P('expert'), may hold values from 0 to 15, all different within a row; in each aligned block of 512 rows (0 to 511, 512 to 1023, ...) at most 512 rows name the same one
- norm1_gain: float32 [2048], replicated, may hold values from 0.1 to 1.9
- q_gain: float32 [16, 128], P('tensor'), may hold values from 0.1 to 1.9
- k_gain: float32 [16, 128], P('tensor'), may hold values from 0.1 to 1.9
- w_query: bfloat16 [2048, 2048], P(None, 'tensor'), may hold values from -0.125 to 0.125
- w_key: bfloat16 [2048, 2048], P(None, 'tensor'), may hold values from -0.125 to 0.125
- w_value: bfloat16 [2048, 2048], P(None, 'tensor'), may hold values from -0.125 to 0.125
- w_out: bfloat16 [2048, 2048], P('tensor'), may hold values from -2 to 2
- norm2_gain: float32 [2048], replicated, may hold values from 0.1 to 1.9
- router_w: bfloat16 [2048, 16], replicated, may hold values from -0.0625 to 0.0625
- w_gate: bfloat16 [16, 2048, 1024], P('expert', None, 'tensor'), may hold values from -0.125 to 0.125
- w_up: bfloat16 [16, 2048, 1024], P('expert', None, 'tensor'), may hold values from -0.125 to 0.125
- w_down: bfloat16 [16, 1024, 2048], P('expert', 'tensor'), may hold values from -1.5 to 1.5
- out_grad: bfloat16 [4096, 2048], P('expert'), may hold values from -6 to 6
Outputs:
- output: bfloat16 [4096, 2048], P('expert')
- input_grad: float32 [4096, 2048], P('expert')
- norm1_gain_grad: float32 [2048], P('expert')
- q_gain_grad: float32 [16, 128], P('tensor', 'expert')
- k_gain_grad: float32 [16, 128], P('tensor', 'expert')
- w_query_grad: float32 [2048, 2048], P('expert', 'tensor')
- w_key_grad: float32 [2048, 2048], P('expert', 'tensor')
- w_value_grad: float32 [2048, 2048], P('expert', 'tensor')
- w_out_grad: float32 [2048, 2048], P('tensor', 'expert')
- norm2_gain_grad: float32 [2048], P('expert')
- router_grad: float32 [2048, 16], P('expert')
- w_gate_grad: float32 [16, 2048, 1024], P('expert', None, 'tensor')
- w_up_grad: float32 [16, 2048, 1024], P('expert', None, 'tensor')
- w_down_grad: float32 [16, 1024, 2048], P('expert', 'tensor')
Inputs may be any that keep to these rules, and one draw needn't show every extreme that they name: `documents`: document numbers never fall; those of the tokens s * 2048 to s * 2048 + 2047 lie in s * 2048 to s * 2048 + 2047, so that no document crosses the end of a sequence; in one sequence a single document fills it. `routes`: A token's 8 experts differ. Among the picks of the 512 tokens of one index of the expert axis (aligned blocks of 512 tokens) no expert is named more than 512 times, and in every draw some expert is named exactly 512 times.
All inputs are finite; a program needn't handle non-finite values.
Results may differ from a plain program's by a relative error of at most 0.023.
Values may be sent and summed in bfloat16 or wider, within the bound.
A program may use at most 448 MiB of HBM per device.

v0:
```python
import jax
import jax.numpy as jnp
from jax import lax
from jax.sharding import PartitionSpec as P

HD = 128
TOP = 8
WINDOW = 1024
LENGTH = 2048


NORM_EPSILON = 1e-05
HIGHEST_PRECISION = lax.Precision.HIGHEST


def for_sending(value):
    return jax.tree.map(lambda a: a.astype(jnp.bfloat16) if a.dtype == jnp.float32 else a, value)


def shifted(value, axis, steps):
    count = lax.axis_size(axis)
    initial, last = (max(0, -steps), min(count, count - steps))
    return lax.ppermute(value, axis, [(source, source + steps) for source in range(initial, last)])


def rope_tables(positions):
    half_width = HD // 2
    frequency = 10000.0 ** (-jnp.arange(half_width, dtype=jnp.float32) * 2.0 / HD)
    angles = positions.astype(jnp.float32)[:, None] * frequency[None, :]
    angles = jnp.concatenate([angles, angles], axis=-1)
    return (jnp.cos(angles)[:, None, :], jnp.sin(angles)[:, None, :])


def rotate(values, cosine, sine):
    half_width = values.shape[-1] // 2
    turned = jnp.concatenate([-values[..., half_width:], values[..., :half_width]], axis=-1)
    return values * cosine + turned * sine


def rotate_back(grads, cosine, sine):
    half_width = grads.shape[-1] // 2
    scaled = grads * sine
    turned = jnp.concatenate([scaled[..., half_width:], -scaled[..., :half_width]], axis=-1)
    return grads * cosine + turned


def previous_block(pieces):
    return jax.tree.map(
        lambda part, own: part.astype(own.dtype), shifted(for_sending(pieces), "expert", 1), pieces
    )


def following_block(pieces):
    return shifted((for_sending(pieces[0]), for_sending(pieces[1])), "expert", -1)


def body(
    tokens,
    documents,
    routes,
    norm1_gain,
    q_gain,
    k_gain,
    w_query,
    w_key,
    w_value,
    w_out,
    norm2_gain,
    router_w,
    w_gate,
    w_up,
    w_down,
    out_grad,
):
    row_count, model_width = tokens.shape
    groups = lax.axis_size("expert")
    local_experts = w_gate.shape[0]
    experts = local_experts * groups
    capacity = 2 * row_count * TOP // experts
    slots_group = local_experts * capacity
    heads = w_query.shape[1] // HD
    score_scale = HD ** (-0.5)
    first_row = lax.axis_index("expert") * row_count
    positions = first_row + jnp.arange(row_count, dtype=jnp.int32)
    cosine, sine = rope_tables(positions % LENGTH)
    inputs = tokens.astype(jnp.float32)
    scale_one = lax.rsqrt(jnp.mean(inputs * inputs, axis=-1, keepdims=True) + NORM_EPSILON)
    normed_one = (inputs * scale_one * norm1_gain).astype(jnp.bfloat16)
    query_raw = jnp.dot(normed_one, w_query, preferred_element_type=jnp.float32)
    key_raw = jnp.dot(normed_one, w_key, preferred_element_type=jnp.float32)
    values = jnp.dot(normed_one, w_value, preferred_element_type=jnp.float32).astype(jnp.bfloat16)
    query_square, key_square = lax.psum(
        (jnp.sum(query_raw * query_raw, axis=-1), jnp.sum(key_raw * key_raw, axis=-1)), "tensor"
    )
    query_scale = lax.rsqrt(query_square / model_width + NORM_EPSILON)[:, None]
    key_scale = lax.rsqrt(key_square / model_width + NORM_EPSILON)[:, None]
    query_gain = q_gain.reshape(-1)
    key_gain = k_gain.reshape(-1)
    queries = rotate(
        (query_raw * query_scale * query_gain).reshape(row_count, heads, HD), cosine, sine
    ).astype(jnp.bfloat16)
    key_heads = rotate(
        (key_raw * key_scale * key_gain).reshape(row_count, heads, HD), cosine, sine
    ).astype(jnp.bfloat16)
    value_heads = values.reshape(row_count, heads, HD)
    labels = jnp.stack([documents // 256, documents % 256]).astype(jnp.bfloat16)
    previous_one = previous_block((key_heads, value_heads, labels))
    previous_two = previous_block(previous_one)
    all_keys = jnp.concatenate([previous_two[0], previous_one[0], key_heads], axis=0)
    all_values = jnp.concatenate([previous_two[1], previous_one[1], value_heads], axis=0)
    all_labels = jnp.concatenate([previous_two[2], previous_one[2], labels], axis=1)
    key_pos = first_row - 2 * row_count + jnp.arange(3 * row_count, dtype=jnp.int32)
    same_doc = (all_labels[0][None, :] == labels[0][:, None]) & (
        all_labels[1][None, :] == labels[1][:, None]
    )
    allowed = (
        same_doc
        & (key_pos[None, :] <= positions[:, None])
        & (positions[:, None] - key_pos[None, :] < WINDOW)
        & (key_pos[None, :] >= 0)
    )

    def masked_scores():
        raw_scores = (
            jnp.einsum("qhd,khd->hqk", queries, all_keys, preferred_element_type=jnp.float32)
            * score_scale
        )
        return jnp.where(allowed[None], raw_scores, -1e30)

    scores = masked_scores()
    highest = jnp.max(scores, axis=-1, keepdims=True)
    weights = jnp.where(allowed[None], jnp.exp(scores - highest), 0.0)
    denominator = jnp.sum(weights, axis=-1, keepdims=True)
    log_total = highest + jnp.log(denominator)
    attn_probs = weights / denominator
    attended = jnp.einsum(
        "hqk,khd->qhd",
        attn_probs.astype(jnp.bfloat16),
        all_values,
        preferred_element_type=jnp.float32,
    )
    attended = attended.reshape(row_count, -1).astype(jnp.bfloat16)
    attention = lax.psum(jnp.dot(attended, w_out, preferred_element_type=jnp.float32), "tensor")
    state = inputs + attention
    scale_two = lax.rsqrt(jnp.mean(state * state, axis=-1, keepdims=True) + NORM_EPSILON)
    normed_two = (state * scale_two * norm2_gain).astype(jnp.bfloat16)
    router_probs = jax.nn.softmax(
        jnp.dot(normed_two, router_w, preferred_element_type=jnp.float32), axis=-1
    )
    chosen = (routes[:, :, None] == jnp.arange(experts, dtype=jnp.int32)[None, None, :]).astype(
        jnp.float32
    )
    gates = jnp.sum(chosen * router_probs[:, None, :], axis=-1)
    flat_routes = routes.reshape(-1)
    onehot = (flat_routes[:, None] == jnp.arange(experts, dtype=jnp.int32)[None, :]).astype(
        jnp.int32
    )
    slot_index = jnp.sum(jnp.cumsum(onehot, axis=0) * onehot, axis=1) - 1
    target = flat_routes * capacity + slot_index
    source = (
        jnp.full((experts * capacity,), -1, jnp.int32)
        .at[target]
        .set(jnp.arange(row_count * TOP, dtype=jnp.int32))
    )
    live_slot = source >= 0
    pick_index = jnp.maximum(source, 0)
    send_rows = jnp.where(
        live_slot[:, None], normed_two[pick_index // TOP], jnp.zeros((), jnp.bfloat16)
    ).reshape(groups, slots_group, model_width)
    grad_float = out_grad.astype(jnp.float32)
    pick_grads = (
        (gates[:, :, None] * grad_float[:, None, :])
        .astype(jnp.bfloat16)
        .reshape(row_count * TOP, model_width)
    )
    send_grads = jnp.where(
        live_slot[:, None], pick_grads[pick_index], jnp.zeros((), jnp.bfloat16)
    ).reshape(groups, slots_group, model_width)
    arrived = lax.all_to_all(send_rows, "expert", split_axis=0, concat_axis=0, tiled=True)
    stacked = arrived.reshape(groups, local_experts, capacity, model_width)
    gate_pre = jnp.einsum("secd,edf->secf", stacked, w_gate, preferred_element_type=jnp.float32)
    up_pre = jnp.einsum("secd,edf->secf", stacked, w_up, preferred_element_type=jnp.float32)
    activated = jax.nn.silu(gate_pre)
    inner_act = (activated * up_pre).astype(jnp.bfloat16)
    produced = jnp.einsum(
        "secf,efd->secd", inner_act, w_down, preferred_element_type=jnp.float32
    ).astype(jnp.bfloat16)
    returned = lax.all_to_all(
        produced.reshape(groups, slots_group, model_width),
        "expert",
        split_axis=0,
        concat_axis=0,
        tiled=True,
    )
    back_rows = (
        returned.reshape(experts * capacity, model_width)[target]
        .reshape(row_count, TOP, model_width)
        .astype(jnp.float32)
    )
    expert_part = jnp.sum(gates[:, :, None] * back_rows, axis=1)
    expert_mix = lax.psum(expert_part.astype(jnp.bfloat16), "tensor").astype(jnp.float32)
    output = (state + expert_mix).astype(jnp.bfloat16)
    gate_part = jnp.sum(grad_float[:, None, :] * back_rows, axis=-1)
    arrived_grad = lax.all_to_all(send_grads, "expert", split_axis=0, concat_axis=0, tiled=True)
    slot_grad = arrived_grad.reshape(groups, local_experts, capacity, model_width)
    w_down_grad = jnp.einsum(
        "secf,secd->efd", inner_act, slot_grad, preferred_element_type=jnp.float32
    )
    inner_grad = jnp.einsum("secd,efd->secf", slot_grad, w_down, preferred_element_type=jnp.float32)
    logistic = jax.nn.sigmoid(gate_pre)
    gate_pre_grad = (inner_grad * up_pre * logistic * (1.0 + gate_pre * (1.0 - logistic))).astype(
        jnp.bfloat16
    )
    up_pre_grad = (inner_grad * activated).astype(jnp.bfloat16)
    w_gate_grad = jnp.einsum(
        "secd,secf->edf", stacked, gate_pre_grad, preferred_element_type=jnp.float32
    )
    w_up_grad = jnp.einsum(
        "secd,secf->edf", stacked, up_pre_grad, preferred_element_type=jnp.float32
    )
    row_grad = jnp.einsum(
        "secf,edf->secd", gate_pre_grad, w_gate, preferred_element_type=jnp.float32
    )
    row_grad = (
        row_grad
        + jnp.einsum("secf,edf->secd", up_pre_grad, w_up, preferred_element_type=jnp.float32)
    ).astype(jnp.bfloat16)
    grad_back = lax.all_to_all(
        row_grad.reshape(groups, slots_group, model_width),
        "expert",
        split_axis=0,
        concat_axis=0,
        tiled=True,
    )
    grad_picks = (
        grad_back.reshape(experts * capacity, model_width)[target]
        .reshape(row_count, TOP, model_width)
        .astype(jnp.float32)
    )
    normed_part = jnp.sum(grad_picks, axis=1)
    normed_two_grad, gate_cot = lax.psum((normed_part, gate_part), "tensor")
    prob_cot = jnp.sum(gate_cot[:, :, None] * chosen, axis=1)
    logit_cot = router_probs * (prob_cot - jnp.sum(router_probs * prob_cot, axis=-1, keepdims=True))
    router_float = router_w.astype(jnp.float32)
    normed_two_grad = normed_two_grad + jnp.einsum(
        "te,de->td", logit_cot, router_float, precision=HIGHEST_PRECISION
    )
    router_grad = jnp.einsum(
        "td,te->de", normed_two.astype(jnp.float32), logit_cot, precision=HIGHEST_PRECISION
    )
    norm2_grad = jnp.sum(normed_two_grad * state * scale_two, axis=0)
    inner_two = jnp.sum(normed_two_grad * norm2_gain * state, axis=-1, keepdims=True)
    state_cot = (
        grad_float
        + scale_two * norm2_gain * normed_two_grad
        - state * scale_two**3 * inner_two / model_width
    )
    state_low = state_cot.astype(jnp.bfloat16)
    w_out_grad = jnp.einsum("tf,td->fd", attended, state_low, preferred_element_type=jnp.float32)
    attended_cot = (
        jnp.einsum("td,fd->tf", state_low, w_out, preferred_element_type=jnp.float32)
        .astype(jnp.bfloat16)
        .reshape(row_count, heads, HD)
    )
    scores = masked_scores()
    attn_probs = jnp.where(allowed[None], jnp.exp(scores - log_total), 0.0)
    value_cot_all = jnp.einsum(
        "hqk,qhd->khd",
        attn_probs.astype(jnp.bfloat16),
        attended_cot,
        preferred_element_type=jnp.float32,
    )
    prob_grad = jnp.einsum(
        "qhd,khd->hqk", attended_cot, all_values, preferred_element_type=jnp.float32
    )
    delta = jnp.sum(attn_probs * prob_grad, axis=-1, keepdims=True)
    score_cot = (attn_probs * (prob_grad - delta)).astype(jnp.bfloat16)
    query_cot = (
        jnp.einsum("hqk,khd->qhd", score_cot, all_keys, preferred_element_type=jnp.float32)
        * score_scale
    )
    key_cot_all = (
        jnp.einsum("hqk,qhd->khd", score_cot, queries, preferred_element_type=jnp.float32)
        * score_scale
    )
    carried = following_block((key_cot_all[:row_count], value_cot_all[:row_count]))
    carried = following_block(
        (
            key_cot_all[row_count : 2 * row_count] + carried[0],
            value_cot_all[row_count : 2 * row_count] + carried[1],
        )
    )
    key_cot = key_cot_all[2 * row_count :] + carried[0]
    value_cot = value_cot_all[2 * row_count :] + carried[1]
    query_norm_cot = rotate_back(query_cot, cosine, sine).reshape(row_count, -1)
    key_norm_cot = rotate_back(key_cot, cosine, sine).reshape(row_count, -1)
    q_gain_local = jnp.sum(query_norm_cot * query_raw * query_scale, axis=0).reshape(heads, HD)
    k_gain_local = jnp.sum(key_norm_cot * key_raw * key_scale, axis=0).reshape(heads, HD)
    query_inner, key_inner = lax.psum(
        (
            jnp.sum(query_norm_cot * query_gain * query_raw, axis=-1),
            jnp.sum(key_norm_cot * key_gain * key_raw, axis=-1),
        ),
        "tensor",
    )
    query_raw_cot = (
        query_scale * query_gain * query_norm_cot
        - query_raw * query_scale**3 * query_inner[:, None] / model_width
    ).astype(jnp.bfloat16)
    key_raw_cot = (
        key_scale * key_gain * key_norm_cot
        - key_raw * key_scale**3 * key_inner[:, None] / model_width
    ).astype(jnp.bfloat16)
    value_low = value_cot.reshape(row_count, -1).astype(jnp.bfloat16)
    w_query_local = jnp.einsum(
        "td,tf->df", normed_one, query_raw_cot, preferred_element_type=jnp.float32
    )
    w_key_local = jnp.einsum(
        "td,tf->df", normed_one, key_raw_cot, preferred_element_type=jnp.float32
    )
    w_value_local = jnp.einsum(
        "td,tf->df", normed_one, value_low, preferred_element_type=jnp.float32
    )
    normed_part_one = jnp.einsum(
        "tf,df->td", query_raw_cot, w_query, preferred_element_type=jnp.float32
    )
    normed_part_one = normed_part_one + jnp.einsum(
        "tf,df->td", key_raw_cot, w_key, preferred_element_type=jnp.float32
    )
    normed_part_one = normed_part_one + jnp.einsum(
        "tf,df->td", value_low, w_value, preferred_element_type=jnp.float32
    )
    normed_one_grad = lax.psum(normed_part_one.astype(jnp.bfloat16), "tensor").astype(jnp.float32)
    norm1_grad = jnp.sum(normed_one_grad * inputs * scale_one, axis=0)
    inner_one = jnp.sum(normed_one_grad * norm1_gain * inputs, axis=-1, keepdims=True)
    input_grad = (
        state_cot
        + scale_one * norm1_gain * normed_one_grad
        - inputs * scale_one**3 * inner_one / model_width
    )
    summed = (
        lax.psum_scatter(
            w_query_local.astype(jnp.bfloat16), "expert", scatter_dimension=0, tiled=True
        ).astype(jnp.float32),
        lax.psum_scatter(
            w_key_local.astype(jnp.bfloat16), "expert", scatter_dimension=0, tiled=True
        ).astype(jnp.float32),
        lax.psum_scatter(
            w_value_local.astype(jnp.bfloat16), "expert", scatter_dimension=0, tiled=True
        ).astype(jnp.float32),
        lax.psum_scatter(
            w_out_grad.astype(jnp.bfloat16), "expert", scatter_dimension=1, tiled=True
        ).astype(jnp.float32),
        lax.psum_scatter(
            router_grad.astype(jnp.bfloat16), "expert", scatter_dimension=0, tiled=True
        ).astype(jnp.float32),
        lax.psum_scatter(
            norm1_grad.astype(jnp.bfloat16), "expert", scatter_dimension=0, tiled=True
        ).astype(jnp.float32),
        lax.psum_scatter(
            norm2_grad.astype(jnp.bfloat16), "expert", scatter_dimension=0, tiled=True
        ).astype(jnp.float32),
        lax.psum_scatter(
            q_gain_local.astype(jnp.bfloat16), "expert", scatter_dimension=1, tiled=True
        ).astype(jnp.float32),
        lax.psum_scatter(
            k_gain_local.astype(jnp.bfloat16), "expert", scatter_dimension=1, tiled=True
        ).astype(jnp.float32),
    )
    return (
        output,
        input_grad,
        summed[5],
        summed[7],
        summed[8],
        summed[0],
        summed[1],
        summed[2],
        summed[3],
        summed[6],
        summed[4],
        w_gate_grad,
        w_up_grad,
        w_down_grad,
    )


def solution(mesh):
    placed = (
        P("expert", None),
        P("expert"),
        P("expert", None),
        P(),
        P("tensor", None),
        P("tensor", None),
        P(None, "tensor"),
        P(None, "tensor"),
        P(None, "tensor"),
        P("tensor", None),
        P(),
        P(),
        P("expert", None, "tensor"),
        P("expert", None, "tensor"),
        P("expert", "tensor", None),
        P("expert", None),
    )
    return jax.shard_map(
        body,
        mesh=mesh,
        in_specs=placed,
        out_specs=(
            P("expert", None),
            P("expert", None),
            P("expert"),
            P("tensor", "expert"),
            P("tensor", "expert"),
            P("expert", "tensor"),
            P("expert", "tensor"),
            P("expert", "tensor"),
            P("tensor", "expert"),
            P("expert"),
            P("expert", None),
            P("expert", None, "tensor"),
            P("expert", None, "tensor"),
            P("expert", "tensor", None),
        ),
        check_vma=False,
    )
```

profile of v0, /device:TPU:10, one launch (start us, length us, event | category | flops | bytes accessed | tf_op | source)
XLA Modules:
  0.0 4118.6 jit_solution(1108156213575433211)
XLA Ops:
  108.5 16.0 scatter_custom_fusion
  129.2 59.7 %all-reduce.10.cloned.1.call-done = f32[512,2048]{1,0:T(8,128)} async-done(((f32[512,2048]{1,0:T(8,128)}), f32[512,2048]{1,0:T(8,128)}) %all-reduce.10.cloned.1.call-update) | async-done | bytes 4194320 | tf_op jit(solution)/shard_map/psum | solution.py:143
  198.2 63.2 %gather_fusion = bf16[8192,2048]{1,0:T(8,128)(2,1)} fusion(bf16[512,2048]{1,0:T(8,128)(2,1)} %copy-done.2, s32[8192]{0:T(1024)S(1)} %get-tuple-element.54), kind=kCustom, calls=%fused_computation | custom fusion | bytes 67141632 | tf_op jit(solution)/shard_map/gather | solution.py:168
  271.3 69.3 %gather_fusion.2 = bf16[8192,2048]{1,0:T(8,128)(2,1)} fusion(bf16[4096,2048]{1,0:T(8,128)(2,1)} %fusion.2, s32[8192]{0:T(1024)S(1)} %get-tuple-element.53), kind=kCustom, calls=%fused_computation.2 | custom fusion | bytes 67141632 | tf_op jit(solution)/shard_map/gather | solution.py:177
  340.6 43.8 %broadcast_select_fusion = (bf16[8,1024,2048]{2,1,0:T(8,128)(2,1)}, bf16[8,1024,2048]{2,1,0:T(8,128)(2,1)}) fusion(bf16[8,1024,2048]{2,1,0:T(8,128)(2,1)} %bitcast.202, pred[8,1024]{1,0:T(8,128)(4,1)S(1)} %copy-done.59, bf16[8,1024,2048]{2,1,0:T(8,128)(2,1)} %bitcast.201), kind=kLoop, calls=%fused_computation.14 | loop fusion | flops 33554432 | bytes 134225920 | tf_op jit(solution)/shard_map/jit(_where)/select_n | solution.py:176
  384.4 731.9 %all_to_all.20 = bf16[8,1024,2048]{2,1,0:T(8,128)(2,1)} all-to-all(bf16[8,1024,2048]{2,1,0:T(8,128)(2,1)} %get-tuple-element.56), channel_id=1, replica_groups=mesh['expert'=8,'tensor'=4] {'expert'}, dimensions={0} | all-to-all | bytes 67108864 | tf_op jit(solution)/shard_map/all_to_all | solution.py:179
  1125.7 17.6 fusion.7
  1143.3 17.7 fusion.9
  1161.0 682.8 %all-to-all-done.2 = bf16[8,1024,2048]{2,1,0:T(8,128)(2,1)} async-done(((bf16[8,1024,2048]{2,1,0:T(8,128)(2,1)}), bf16[8,1024,2048]{2,1,0:T(8,128)(2,1)}, u32[]{:S(2)}, u32[]{:S(2)}) %all-to-all-start.2) | async-done | bytes 33554464 | tf_op jit(solution)/shard_map/all_to_all | solution.py:204
  1843.8 23.4 fusion.16
  1867.2 16.3 convert_bitcast_fusion
  1883.4 22.9 copy.149
  1916.7 26.7 fusion.57
  1943.5 34.1 fusion.11
  1977.6 22.9 copy.152
  2000.5 633.5 %all-to-all-done.1 = bf16[8,1024,2048]{2,1,0:T(8,128)(2,1)} async-done(((bf16[8,1024,2048]{2,1,0:T(8,128)(2,1)}), bf16[8,1024,2048]{2,1,0:T(8,128)(2,1)}, u32[]{:S(2)}, u32[]{:S(2)}) %all-to-all-start.1) | async-done | bytes 33554464 | tf_op jit(solution)/shard_map/all_to_all | solution.py:188
  2645.7 96.2 %gather_fusion.1 = bf16[4096,2048]{1,0:T(8,128)(2,1)} fusion(bf16[8192,2048]{1,0:T(8,128)(2,1)} %bitcast.22, s32[4096]{0:T(1024)S(1)} %broadcast_clamp_fusion), kind=kCustom, calls=%fused_computation.1 | custom fusion | bytes 33570816 | tf_op jit(solution)/shard_map/gather | solution.py:196
  2741.9 619.5 %all-to-all-done.3 = bf16[8,1024,2048]{2,1,0:T(8,128)(2,1)} async-done(((bf16[8,1024,2048]{2,1,0:T(8,128)(2,1)}), bf16[8,1024,2048]{2,1,0:T(8,128)(2,1)}, u32[]{:S(2)}, u32[]{:S(2)}) %all-to-all-start.3) | async-done | bytes 33554464 | tf_op jit(solution)/shard_map/all_to_all | solution.py:228
  3361.4 95.7 %gather_fusion.3 = bf16[4096,2048]{1,0:T(8,128)(2,1)} fusion(bf16[8192,2048]{1,0:T(8,128)(2,1)} %bitcast.33, s32[4096]{0:T(1024)S(1)} %broadcast_clamp_fusion), kind=kCustom, calls=%fused_computation.3 | custom fusion | bytes 33570816 | tf_op jit(solution)/shard_map/gather | solution.py:236
  3457.2 15.4 convert_reduce_fusion
  3473.5 17.1 fusion.1
  3490.5 20.0 psum.68
  3512.6 54.0 %all-reduce.12.cloned.1.call-done = f32[512,2048]{1,0:T(8,128)} async-done(((f32[512,2048]{1,0:T(8,128)}), f32[512,2048]{1,0:T(8,128)}) %all-reduce.12.cloned.1.call-update) | async-done | bytes 4194320 | tf_op jit(solution)/shard_map/psum | solution.py:241
  3685.9 21.0 fusion.43
  3706.8 21.0 fusion.40
  3730.8 17.9 fusion.46
  3752.7 73.7 %all-reduce.14.cloned.1.call-done = (bf16[512,2048]{1,0:T(8,128)(2,1)}, bf16[512,2048]{1,0:T(8,128)(2,1)}) async-done(((bf16[512,2048]{1,0:T(8,128)(2,1)}, bf16[512,2048]{1,0:T(8,128)(2,1)}), (bf16[512,2048]{1,0:T(8,128)(2,1)}, bf16[512,2048]{1,0:T(8,128)(2,1)})) %all-reduce.14.cloned.1.call-update) | async-done | bytes 4194320 | tf_op jit(solution)/shard_map/psum | solution.py:201
  3829.5 15.4 all-reduce.4
  3855.9 42.3 %reduce-scatter.18.cloned.1.call-done = bf16[512,256]{1,0:T(8,128)(2,1)} async-done(((bf16[512,2048]{1,0:T(8,128)(2,1)}), bf16[512,256]{1,0:T(8,128)(2,1)}) %reduce-scatter.18.cloned.1.call-update) | async-done | bytes 262160 | tf_op jit(solution)/shard_map/reduce_scatter | solution.py:351
  3899.9 68.8 %reduce-scatter.16.cloned.1.call-done = bf16[256,512]{1,0:T(8,128)(2,1)} async-done(((bf16[2048,512]{1,0:T(8,128)(2,1)}), bf16[256,512]{1,0:T(8,128)(2,1)}) %reduce-scatter.16.cloned.1.call-update) | async-done | bytes 262160 | tf_op jit(solution)/shard_map/reduce_scatter | solution.py:348
  3970.5 68.8 %reduce-scatter.12.cloned.1.call-done = bf16[256,512]{1,0:T(8,128)(2,1)} async-done(((bf16[2048,512]{1,0:T(8,128)(2,1)}), bf16[256,512]{1,0:T(8,128)(2,1)}) %reduce-scatter.12.cloned.1.call-update) | async-done | bytes 262160 | tf_op jit(solution)/shard_map/reduce_scatter | solution.py:342
  4041.1 68.6 %reduce-scatter.14.cloned.1.call-done = bf16[256,512]{1,0:T(8,128)(2,1)} async-done(((bf16[2048,512]{1,0:T(8,128)(2,1)}), bf16[256,512]{1,0:T(8,128)(2,1)}) %reduce-scatter.14.cloned.1.call-update) | async-done | bytes 262160 | tf_op jit(solution)/shard_map/reduce_scatter | solution.py:345
  (348 shorter events, 305.0 us)
Async XLA Ops:
  7.2 1836.6 %copy-start = (bf16[2,256,2048]{2,1,0:T(8,128)(2,1)S(1)}, bf16[2,256,2048]{2,1,0:T(8,128)(2,1)}, u32[]{:S(2)}) copy-start(bf16[2,256,2048]{2,1,0:T(8,128)(2,1)} %param.30) | copy-start | bytes 6291460
  7.2 181.8 %all-reduce.10.cloned.1.call-start = ((), (), s32[]{:S(2)}) async-start(), calls=%async_computation.11 | async-start | bytes 8388608 | tf_op jit(solution)/shard_map/psum | solution.py:143
  8.1 45.0 %collective-permute-start.2 = (bf16[2,512]{1,0:T(2,128)(2,1)S(1)}, bf16[2,512]{1,0:T(2,128)(2,1)S(1)}, u32[]{:S(2)}, u32[]{:S(2)}) collective-permute-start(bf16[2,512]{1,0:T(2,128)(2,1)S(1)} %pad_maximum_fusion.7), channel_id=1, source_target_pairs={{0,4},{4,8},{8,12},{12,16},{16,20},{20,24},{24,28},{1,5},{5,9},{9,... | collective-permute-start | bytes 6152 | tf_op jit(solution)/shard_map/ppermute | solution.py:23
  18.7 51.7 %collective-permute-start = (bf16[512,4,128]{0,2,1:T(8,128)(2,1)}, bf16[512,4,128]{0,2,1:T(8,128)(2,1)}, u32[]{:S(2)}, u32[]{:S(2)}) collective-permute-start(bf16[512,4,128]{0,2,1:T(8,128)(2,1)} %bitcast), channel_id=1, source_target_pairs={{0,4},{4,8},{8,12},{12,16},{16,20},{20,24},{24,28},{1,5},{5,9},{9,... | collective-permute-start | bytes 1572872 | tf_op jit(solution)/shard_map/ppermute | solution.py:23
  49.2 15.2 collective-permute-start.4
  53.1 11.2 collective-permute-start.3
  64.4 16.8 collective-permute-start.5
  70.4 21.6 collective-permute-start.1
  108.5 84.0 %copy-start.53 = (s32[4096,1]{0,1:T(1,128)}, s32[4096,1]{0,1:T(1,128)S(1)}, u32[]{:S(2)}) copy-start(s32[4096,1]{0,1:T(1,128)S(1)} %compare_select_fusion) | copy-start | bytes 49156
  129.2 64.5 %copy-start.51 = (f32[2048]{0:T(1024)S(1)}, f32[2048]{0:T(1024)}, u32[]{:S(2)}) copy-start(f32[2048]{0:T(1024)} %param.26) | copy-start | bytes 24580
  198.1 63.4 %copy-start.26 = (f32[512,8]{1,0:T(8,128)}, f32[512,8]{1,0:T(8,128)S(1)}, u32[]{:S(2)}) copy-start(f32[512,8]{1,0:T(8,128)S(1)} %copy.143) | copy-start | bytes 49156
  271.3 69.3 %copy-start.59 = (pred[8,1024]{1,0:T(8,128)(4,1)S(1)}, pred[8,1024]{1,0:T(8,128)(4,1)}, u32[]{:S(2)}) copy-start(pred[8,1024]{1,0:T(8,128)(4,1)} %broadcast_in_dim.54) | copy-start | bytes 24580
  1116.3 727.5 %all-to-all-start.2 = ((bf16[8,1024,2048]{2,1,0:T(8,128)(2,1)}), bf16[8,1024,2048]{2,1,0:T(8,128)(2,1)}, u32[]{:S(2)}, u32[]{:S(2)}) async-start(bf16[8,1024,2048]{2,1,0:T(8,128)(2,1)} %get-tuple-element.55), calls=%async_computation.2 | async-start | bytes 67108864 | tf_op jit(solution)/shard_map/all_to_all | solution.py:204
  1906.4 727.7 %all-to-all-start.1 = ((bf16[8,1024,2048]{2,1,0:T(8,128)(2,1)}), bf16[8,1024,2048]{2,1,0:T(8,128)(2,1)}, u32[]{:S(2)}, u32[]{:S(2)}) async-start(bf16[8,1024,2048]{2,1,0:T(8,128)(2,1)} %bitcast.200), calls=%async_computation.1 | async-start | bytes 67108864 | tf_op jit(solution)/shard_map/all_to_all | solution.py:188
  2634.0 727.4 %all-to-all-start.3 = ((bf16[8,1024,2048]{2,1,0:T(8,128)(2,1)}), bf16[8,1024,2048]{2,1,0:T(8,128)(2,1)}, u32[]{:S(2)}, u32[]{:S(2)}) async-start(bf16[8,1024,2048]{2,1,0:T(8,128)(2,1)} %bitcast.199), calls=%async_computation.3 | async-start | bytes 67108864 | tf_op jit(solution)/shard_map/all_to_all | solution.py:228
  2644.7 921.9 %all-reduce.12.cloned.1.call-start = ((), (), s32[]{:S(2)}) async-start(), calls=%async_computation.12 | async-start | bytes 8388608 | tf_op jit(solution)/shard_map/psum | solution.py:241
  3472.6 93.9 %copy-start.47 = (bf16[2048,16]{0,1:T(8,128)(2,1)S(1)}, bf16[2048,16]{0,1:T(8,128)(2,1)}, u32[]{:S(2)}) copy-start(bf16[2048,16]{0,1:T(8,128)(2,1)} %param.27) | copy-start | bytes 196612
  3472.6 93.9 %copy-start.52 = (f32[2048]{0:T(1024)S(1)}, f32[2048]{0:T(1024)}, u32[]{:S(2)}) copy-start(f32[2048]{0:T(1024)} %param.26) | copy-start | bytes 24580
  3472.6 93.9 %copy-start.69 = (f32[512]{0:T(512)S(1)}, f32[512]{0:T(512)}, u32[]{:S(2)}) copy-start(f32[512]{0:T(512)} %copy-done.68) | copy-start | bytes 6148
  3472.6 276.1 %reduce-scatter.20.cloned.1.call-start = ((), (), s32[]{:S(2)}) async-start(), calls=%async_computation.17 | async-start | bytes 73728 | tf_op jit(solution)/shard_map/reduce_scatter | solution.py:354
  3512.3 237.7 %reduce-scatter.22.cloned.1.call-start = ((), (), s32[]{:S(2)}) async-start(), calls=%async_computation.18 | async-start | bytes 36864
  3586.2 42.1 %collective-permute-start.8 = (bf16[512,4,128]{0,2,1:T(8,128)(2,1)}, bf16[512,4,128]{0,2,1:T(8,128)(2,1)}, u32[]{:S(2)}, u32[]{:S(2)}) collective-permute-start(bf16[512,4,128]{0,2,1:T(8,128)(2,1)} %slice.131), channel_id=1, source_target_pairs={{4,0},{8,4},{12,8},{16,12},{20,16},{24,20},{28,24},{5,1},{9,5},{13... | collective-permute-start | bytes 1572872 | tf_op jit(solution)/shard_map/ppermute | solution.py:23
  3607.4 16.3 collective-permute-start.6
  3624.6 18.0 collective-permute-start.7
  3628.3 123.1 %reduce-scatter.24.cloned.1.call-start = ((), (), s32[]{:S(2)}) async-start(), calls=%async_computation.19 | async-start | bytes 36864
  3630.7 37.7 collective-permute-start.9
  3665.2 161.2 %all-reduce.14.cloned.1.call-start = ((), (), s32[]{:S(2)}) async-start(), calls=%async_computation.20 | async-start | bytes 8388608 | tf_op jit(solution)/shard_map/psum | solution.py:201
  3672.7 225.4 %reduce-scatter.18.cloned.1.call-start = ((), (), s32[]{:S(2)}) async-start(), calls=%async_computation.16 | async-start | bytes 2359296 | tf_op jit(solution)/shard_map/reduce_scatter | solution.py:351
  3678.5 290.2 %reduce-scatter.16.cloned.1.call-start = ((), (), s32[]{:S(2)}) async-start(), calls=%async_computation.15 | async-start | bytes 2359296 | tf_op jit(solution)/shard_map/reduce_scatter | solution.py:348
  3681.5 357.8 %reduce-scatter.12.cloned.1.call-start = ((), (), s32[]{:S(2)}) async-start(), calls=%async_computation.13 | async-start | bytes 2359296 | tf_op jit(solution)/shard_map/reduce_scatter | solution.py:342
  3685.6 424.1 %reduce-scatter.14.cloned.1.call-start = ((), (), s32[]{:S(2)}) async-start(), calls=%async_computation.14 | async-start | bytes 2359296 | tf_op jit(solution)/shard_map/reduce_scatter | solution.py:345
  3852.4 259.1 %copy-start.1 = (bf16[2,256,2048]{2,1,0:T(8,128)(2,1)S(1)}, bf16[2,256,2048]{2,1,0:T(8,128)(2,1)}, u32[]{:S(2)}) copy-start(bf16[2,256,2048]{2,1,0:T(8,128)(2,1)} %param.30) | copy-start | bytes 6291460
  (83 other events, 912.7 us)
Sparse Core Ops, SparseCore 0:
  102.4 86.4 all-reduce.9
  3472.7 93.8 all-reduce.11
  3569.7 56.2 reduce-scatter.19
  3629.5 53.5 reduce-scatter.21
  3686.1 52.5 reduce-scatter.23
  3741.6 84.7 all-reduce.13
  3830.3 67.7 reduce-scatter.17
  3902.1 66.5 reduce-scatter.15
  3972.7 66.5 reduce-scatter.11
  4043.1 66.5 reduce-scatter.13
where the time goes:
time: 4130 us; the launch traced here: 4120 us
  waiting for transfers between devices  2410 us (58%)
  blocking collectives  780 us (19%)
  local copies, waits for them, and re-layouts  410 us (10%)
  matrix products  276 us (7%)
  other arithmetic  167 us (4%)
  starting transfers between devices  63.7 us (2%)
    all_to_all x1, blocking collectives, body(): lax.all_to_all(send_rows, 'expert', split_axis=0, concat_axis=0, tiled=True)  732 us
    all_to_all x1, waiting for transfers between devices, body(): lax.all_to_all(send_grads, 'expert', split_axis=0, concat_axis=0, tiled=T...  683 us
    all_to_all x1, waiting for transfers between devices, body(): lax.all_to_all(produced.reshape(groups, slots_group, model_width), 'exper...  634 us
    all_to_all x1, waiting for transfers between devices, body(): lax.all_to_all(row_grad.reshape(groups, slots_group, model_width), 'exper...  620 us
    gather x1, local copies, waits for them, and re-layouts, body(): returned.reshape(experts * capacity, model_width)[target]  96.2 us
    gather x1, local copies, waits for them, and re-layouts, body(): grad_back.reshape(experts * capacity, model_width)[target]  95.7 us
  transfers between devices with their start and end apart: 23, of which 14 were waited for; matrix products, arithmetic and copies ran while one was open for 11% of the time, Pallas kernels for 0%

commit v1 on v0

--- a/solution.py
+++ b/solution.py
@@ -1,6 +1,10 @@
+import functools
+
 import jax
 import jax.numpy as jnp
 from jax import lax
+from jax.experimental import pallas as pl
+from jax.experimental.pallas import tpu as pltpu
 from jax.sharding import PartitionSpec as P
 
 HD = 128
@@ -54,7 +58,7 @@
     return shifted((for_sending(pieces[0]), for_sending(pieces[1])), "expert", -1)
 
 
-def body(
+def body_routed(
     tokens,
     documents,
     routes,
@@ -385,6 +389,715 @@
     )
 
 
+MESH = pl.DeviceIdType.MESH
+ANY = pl.BlockSpec(memory_space=pl.ANY)
+VMEM = pl.BlockSpec(memory_space=pltpu.VMEM)
+VMEM_BYTES = 60 * 1024 * 1024
+LOW = jnp.bfloat16
+FULL = jnp.float32
+
+
+def place():
+    group, part = lax.axis_index("expert"), lax.axis_index("tensor")
+    return group // 2, group % 2, part // 2, part % 2
+
+
+def device(z, x, y, core):
+    return (2 * z + x, 2 * y + core)
+
+
+def swapped(index, step):
+    result, bit = index, 1
+    while bit <= step:
+        if step & bit:
+            result = result + bit - 2 * bit * ((index // bit) % 2)
+        bit *= 2
+    return result
+
+
+def greet(partners):
+    barrier = pltpu.get_barrier_semaphore()
+    for partner in partners:
+        pl.semaphore_signal(barrier, inc=1, device_id=partner, device_id_type=MESH)
+    pl.semaphore_wait(barrier, len(partners))
+
+
+def remote(source, target, send, arrive, to):
+    return pltpu.make_async_remote_copy(
+        src_ref=source, dst_ref=target, send_sem=send, recv_sem=arrive, device_id=to, device_id_type=MESH
+    )
+
+
+def dma(*shape):
+    return pltpu.SemaphoreType.DMA(shape)
+
+
+def comm_params(number):
+    return pltpu.CompilerParams(collective_id=number, has_side_effects=True, vmem_limit_bytes=VMEM_BYTES)
+
+
+def add_rows(target, sources, rows, step=16):
+    @pl.loop(0, rows // step)
+    def _(index):
+        part = pl.ds(index * step, step)
+        total = sources[0][part].astype(FULL)
+        for source in sources[1:]:
+            total = total + source[part].astype(FULL)
+        target[part] = total.astype(target.dtype)
+
+
+def gather_rows_kernel(depth, rows, x_ref, small_ref, o_ref, smalls_ref, z_send, z_recv, p_send, p_recv, s_send, s_recv, local):
+    z, x, y, core = place()
+    here = 2 * x + y
+    over_x, over_y = (z, 1 - x, y, core), (z, x, 1 - y, core)
+    half = rows // 2
+    upper, lower = pl.ds(0, half), pl.ds(half, half)
+    others = []
+    for step in range(depth):
+        for turn in range(4):
+            if step or turn:
+                other = (swapped(z, step), swapped(x, turn // 2), swapped(y, turn % 2), core)
+                others.append((step * 4 + turn, other))
+    greet([device(*other) for _, other in others])
+    own = pltpu.make_async_copy(x_ref, o_ref.at[z, here], local.at[0])
+    own.start()
+    own_small = pltpu.make_async_copy(small_ref, smalls_ref.at[z, here], local.at[1])
+    own_small.start()
+    pending = []
+
+    def start(copy):
+        copy.start()
+        pending.append(copy)
+        return copy
+
+    along_z = []
+    for step in range(1, depth):
+        along_z.append(
+            start(remote(x_ref, o_ref.at[z, here], z_send.at[step], z_recv.at[step], device(swapped(z, step), x, y, core)))
+        )
+    for number, other in others:
+        start(remote(small_ref, smalls_ref.at[z, here], s_send.at[number], s_recv.at[number], device(*other)))
+    own.wait()
+    own_small.wait()
+    forwards = []
+    for step in range(depth):
+        if step:
+            along_z[step - 1].wait_recv()
+        at = swapped(z, step)
+        mine = o_ref.at[at, here]
+        x_up = start(remote(mine.at[upper], mine.at[upper], p_send.at[step, 0], p_recv.at[step, 0], device(*over_x)))
+        y_low = start(remote(mine.at[lower], mine.at[lower], p_send.at[step, 1], p_recv.at[step, 1], device(*over_y)))
+        start(remote(mine.at[lower], mine.at[lower], p_send.at[step, 2], p_recv.at[step, 2], device(*over_x)))
+        start(remote(mine.at[upper], mine.at[upper], p_send.at[step, 3], p_recv.at[step, 3], device(*over_y)))
+        forwards.append((step, at, x_up, y_low))
+    for step, at, x_up, y_low in forwards:
+        x_up.wait_recv()
+        from_x = o_ref.at[at, 2 * (1 - x) + y, upper]
+        start(remote(from_x, from_x, p_send.at[step, 4], p_recv.at[step, 4], device(*over_y)))
+        y_low.wait_recv()
+        from_y = o_ref.at[at, 2 * x + 1 - y, lower]
+        start(remote(from_y, from_y, p_send.at[step, 5], p_recv.at[step, 5], device(*over_x)))
+    received = set(id(c) for c in along_z) | set(id(c) for f in forwards for c in f[2:])
+    for copy in pending:
+        copy.wait_send()
+        if id(copy) not in received:
+            copy.wait_recv()
+
+
+def gather_rows(block, small, depth, number):
+    rows = block.shape[0]
+    return pl.pallas_call(
+        functools.partial(gather_rows_kernel, depth, rows),
+        out_shape=(
+            jax.ShapeDtypeStruct((depth, 4) + block.shape, block.dtype),
+            jax.ShapeDtypeStruct((depth, 4) + small.shape, small.dtype),
+        ),
+        in_specs=[ANY, ANY],
+        out_specs=(ANY, ANY),
+        scratch_shapes=[dma(depth), dma(depth), dma(depth, 6), dma(depth, 6), dma(4 * depth), dma(4 * depth), dma(2)],
+        compiler_params=comm_params(number),
+    )(block, small)
+
+
+def scatter_rows_kernel(
+    depth, rows, p_ref, small_ref, o_ref, smalls_ref,
+    work, diagonal, from_x, from_y, passing, from_z,
+    load, d_send, d_recv, x_send, x_recv, y_send, y_recv, z_send, z_recv, s_send, s_recv, local,
+):
+    z, x, y, core = place()
+    here, x_place, y_place, far = 2 * x + y, 2 * (1 - x) + y, 2 * x + 1 - y, 2 * (1 - x) + 1 - y
+    over_x, over_y = device(z, 1 - x, y, core), device(z, x, 1 - y, core)
+    half = rows // 2
+    upper, lower = pl.ds(0, half), pl.ds(half, half)
+    others = []
+    for step in range(depth):
+        for turn in range(4):
+            if step or turn:
+                other = (swapped(z, step), swapped(x, turn // 2), swapped(y, turn % 2), core)
+                others.append((step * 4 + turn, other))
+    greet([device(*other) for _, other in others])
+    pending = []
+
+    def start(copy):
+        copy.start()
+        pending.append(copy)
+        return copy
+
+    for number, (oz, ox, oy, oc) in others:
+        start(
+            remote(
+                small_ref.at[oz, 2 * ox + oy], smalls_ref.at[z, here], s_send.at[number], s_recv.at[number], device(oz, ox, oy, oc)
+            )
+        )
+    own_small = pltpu.make_async_copy(small_ref.at[z, here], smalls_ref.at[z, here], local.at[0])
+    own_small.start()
+    loads = []
+    order = [step for step in range(1, depth)] + [0]
+    for step in order:
+        at = swapped(z, step)
+        copy = pltpu.make_async_copy(p_ref.at[at], work.at[step], load.at[step])
+        copy.start()
+        loads.append(copy)
+    diagonals, sides = {}, {}
+    for step, copy in zip(order, loads):
+        copy.wait()
+        diagonals[step] = (
+            start(remote(work.at[step, far, upper], diagonal.at[step, 0], d_send.at[step, 0], d_recv.at[step, 0], over_y)),
+            start(remote(work.at[step, far, lower], diagonal.at[step, 1], d_send.at[step, 1], d_recv.at[step, 1], over_x)),
+        )
+    for step in order:
+        via_y, via_x = diagonals[step]
+        via_y.wait_recv()
+        add_rows(work.at[step, x_place, upper], [work.at[step, x_place, upper], diagonal.at[step, 0]], half)
+        to_x = start(remote(work.at[step, x_place], from_x.at[step], x_send.at[step], x_recv.at[step], over_x))
+        via_x.wait_recv()
+        add_rows(work.at[step, y_place, lower], [work.at[step, y_place, lower], diagonal.at[step, 1]], half)
+        to_y = start(remote(work.at[step, y_place], from_y.at[step], y_send.at[step], y_recv.at[step], over_y))
+        sides[step] = (to_x, to_y)
+    along_z = []
+    for step in order:
+        for side in sides[step]:
+            side.wait_recv()
+        terms = [work.at[step, here], from_x.at[step], from_y.at[step]]
+        if step:
+            add_rows(passing.at[step], terms, rows)
+            along_z.append(
+                start(
+                    remote(
+                        passing.at[step], from_z.at[step], z_send.at[step], z_recv.at[step], device(swapped(z, step), x, y, core)
+                    )
+                )
+            )
+    for copy in along_z:
+        copy.wait_recv()
+    add_rows(o_ref, [work.at[0, here], from_x.at[0], from_y.at[0]] + [from_z.at[step] for step in range(1, depth)], rows)
+    own_small.wait()
+    received = set(id(c) for c in along_z) | set(id(c) for v in list(diagonals.values()) + list(sides.values()) for c in v)
+    for copy in pending:
+        copy.wait_send()
+        if id(copy) not in received:
+            copy.wait_recv()
+
+
+def scatter_rows(parts, small, number):
+    depth, _, rows, width = parts.shape
+    return pl.pallas_call(
+        functools.partial(scatter_rows_kernel, depth, rows),
+        out_shape=(jax.ShapeDtypeStruct((rows, width), FULL), jax.ShapeDtypeStruct(small.shape, small.dtype)),
+        in_specs=[ANY, ANY],
+        out_specs=(VMEM, ANY),
+        scratch_shapes=[
+            pltpu.VMEM(parts.shape, parts.dtype),
+            pltpu.VMEM((depth, 2, rows // 2, width), parts.dtype),
+            pltpu.VMEM((depth, rows, width), parts.dtype),
+            pltpu.VMEM((depth, rows, width), parts.dtype),
+            pltpu.VMEM((depth, rows, width), parts.dtype),
+            pltpu.VMEM((depth, rows, width), parts.dtype),
+            dma(depth), dma(depth, 2), dma(depth, 2), dma(depth), dma(depth), dma(depth), dma(depth), dma(depth), dma(depth),
+            dma(4 * depth), dma(4 * depth), dma(1),
+        ],
+        compiler_params=comm_params(number),
+    )(parts, small)
+
+
+def pair_weights_kernel(count, *refs):
+    ins, outs, (send, recv, local) = refs[:count], refs[count : 2 * count], refs[2 * count :]
+    z, x, y, core = place()
+    sibling = device(z, x, y, 1 - core)
+    greet([sibling])
+    waits = []
+    for index in range(count):
+        copy = remote(ins[index], outs[index].at[core], send.at[index], recv.at[index], sibling)
+        copy.start()
+        mine = pltpu.make_async_copy(ins[index], outs[index].at[core], local.at[index])
+        mine.start()
+        waits += [copy, mine]
+    for copy in waits:
+        copy.wait()
+
+
+def pair_weights(arrays, number):
+    count = len(arrays)
+    return pl.pallas_call(
+        functools.partial(pair_weights_kernel, count),
+        out_shape=tuple(jax.ShapeDtypeStruct((2,) + a.shape, a.dtype) for a in arrays),
+        in_specs=[ANY] * count,
+        out_specs=(ANY,) * count,
+        scratch_shapes=[dma(count), dma(count), dma(count)],
+        compiler_params=comm_params(number),
+    )(*arrays)
+
+
+def pair_swap_kernel(count, *refs):
+    ins, outs, (send, recv) = refs[:count], refs[count : 2 * count], refs[2 * count :]
+    z, x, y, core = place()
+    sibling = device(z, x, y, 1 - core)
+    greet([sibling])
+    waits = []
+    for index in range(count):
+        copy = remote(ins[index].at[1 - core], outs[index], send.at[index], recv.at[index], sibling)
+        copy.start()
+        waits.append(copy)
+    for copy in waits:
+        copy.wait()
+
+
+def pair_swap(arrays, number):
+    count = len(arrays)
+    return pl.pallas_call(
+        functools.partial(pair_swap_kernel, count),
+        out_shape=tuple(jax.ShapeDtypeStruct(a.shape[1:], a.dtype) for a in arrays),
+        in_specs=[ANY] * count,
+        out_specs=(ANY,) * count,
+        scratch_shapes=[dma(count), dma(count)],
+        compiler_params=comm_params(number),
+    )(*arrays)
+
+
+def tensor_scatter_kernel(rows, p_ref, o_ref, work, from_pair, from_y, load, send, recv):
+    z, x, y, core = place()
+    sibling, over_y = device(z, x, y, 1 - core), device(z, x, 1 - y, core)
+    greet([sibling, over_y])
+    fetch = pltpu.make_async_copy(p_ref, work, load.at[0])
+    fetch.start()
+    pairs = []
+    for turn in (1, 0):
+        row = swapped(y, turn)
+        copy = remote(p_ref.at[row, 1 - core], from_pair.at[turn], send.at[turn], recv.at[turn], sibling)
+        copy.start()
+        pairs.append(copy)
+    fetch.wait()
+    pairs[0].wait_recv()
+    add_rows(work.at[1 - y, core], [work.at[1 - y, core], from_pair.at[1]], rows)
+    across = remote(work.at[1 - y, core], from_y, send.at[2], recv.at[2], over_y)
+    across.start()
+    pairs[1].wait_recv()
+    across.wait_recv()
+    add_rows(o_ref, [work.at[y, core], from_pair.at[0], from_y], rows)
+    for copy in pairs + [across]:
+        copy.wait_send()
+
+
+def tensor_scatter(parts, number):
+    rows, width = parts.shape[0] // 4, parts.shape[1]
+    shaped = parts.reshape(2, 2, rows, width)
+    return pl.pallas_call(
+        functools.partial(tensor_scatter_kernel, rows),
+        out_shape=jax.ShapeDtypeStruct((rows, width), FULL),
+        in_specs=[ANY],
+        out_specs=VMEM,
+        scratch_shapes=[
+            pltpu.VMEM(shaped.shape, parts.dtype),
+            pltpu.VMEM((2, rows, width), parts.dtype),
+            pltpu.VMEM((rows, width), parts.dtype),
+            dma(1), dma(3), dma(3),
+        ],
+        compiler_params=comm_params(number),
+    )(shaped)
+
+
+def tensor_gather_kernel(x_ref, o_ref, send, recv, local):
+    z, x, y, core = place()
+    sibling, over_y = device(z, x, y, 1 - core), device(z, x, 1 - y, core)
+    greet([sibling, over_y])
+    own = pltpu.make_async_copy(x_ref, o_ref.at[y, core], local.at[0])
+    own.start()
+    across = remote(x_ref, o_ref.at[y, core], send.at[0], recv.at[0], over_y)
+    across.start()
+    near = remote(x_ref, o_ref.at[y, core], send.at[1], recv.at[1], sibling)
+    near.start()
+    across.wait_recv()
+    block = o_ref.at[1 - y, core]
+    passed = remote(block, block, send.at[2], recv.at[2], sibling)
+    passed.start()
+    own.wait()
+    across.wait_send()
+    near.wait()
+    passed.wait()
+
+
+def tensor_gather(block, number):
+    rows, width = block.shape
+    gathered = pl.pallas_call(
+        tensor_gather_kernel,
+        out_shape=jax.ShapeDtypeStruct((2, 2, rows, width), block.dtype),
+        in_specs=[ANY],
+        out_specs=ANY,
+        scratch_shapes=[dma(3), dma(3), dma(1)],
+        compiler_params=comm_params(number),
+    )(block)
+    return gathered.reshape(4 * rows, width)
+
+
+def expert_scatter_kernel(depth, rows, p_ref, o_ref, work, from_x, from_z, load, send, recv):
+    z, x, y, core = place()
+    over_x = device(z, 1 - x, y, core)
+    greet([over_x] + [device(swapped(z, step), x, y, core) for step in range(1, depth)])
+    order = [step for step in range(1, depth)] + [0]
+    sides, along, loads = {}, [], {}
+    for step in order:
+        at = swapped(z, step)
+        sides[step] = remote(p_ref.at[at, 1 - x], from_x.at[step], send.at[0, step], recv.at[0, step], over_x)
+        sides[step].start()
+        loads[step] = pltpu.make_async_copy(p_ref.at[at, x], work.at[step], load.at[step])
+        loads[step].start()
+    for step in order:
+        loads[step].wait()
+        sides[step].wait_recv()
+        if step:
+            add_rows(work.at[step], [work.at[step], from_x.at[step]], rows)
+            copy = remote(work.at[step], from_z.at[step], send.at[1, step], recv.at[1, step], device(swapped(z, step), x, y, core))
+            copy.start()
+            along.append(copy)
+    for copy in along:
+        copy.wait_recv()
+    add_rows(o_ref, [work.at[0], from_x.at[0]] + [from_z.at[step] for step in range(1, depth)], rows)
+    for copy in list(sides.values()) + along:
+        copy.wait_send()
+
+
+def expert_scatter(parts, depth, number):
+    rows, width = parts.shape[0] // (2 * depth), parts.shape[1]
+    shaped = parts.reshape(depth, 2, rows, width)
+    return pl.pallas_call(
+        functools.partial(expert_scatter_kernel, depth, rows),
+        out_shape=jax.ShapeDtypeStruct((rows, width), FULL),
+        in_specs=[ANY],
+        out_specs=VMEM,
+        scratch_shapes=[
+            pltpu.VMEM((depth, rows, width), parts.dtype),
+            pltpu.VMEM((depth, rows, width), parts.dtype),
+            pltpu.VMEM((depth, rows, width), parts.dtype),
+            dma(depth), dma(2, depth), dma(2, depth),
+        ],
+        compiler_params=comm_params(number),
+    )(shaped)
+
+
+def halo_kernel(chain, forward, count, *refs):
+    ins, outs, (send, recv) = refs[:count], refs[count : 2 * count], refs[2 * count :]
+    group, part = lax.axis_index("expert"), lax.axis_index("tensor")
+    spot = group % chain
+    barrier = pltpu.get_barrier_semaphore()
+    distances = (1, 2)
+
+    def each(before, after):
+        for distance in distances:
+            if after is not None:
+                pl.when(spot < chain - distance)(functools.partial(after, distance))
+            if before is not None:
+                pl.when(spot >= distance)(functools.partial(before, distance))
+
+    def signal(to):
+        pl.semaphore_signal(barrier, inc=1, device_id=(to, part), device_id_type=MESH)
+
+    each(lambda d: signal(group - d), lambda d: signal(group + d))
+    pl.semaphore_wait(barrier, jnp.minimum(spot, 2) + jnp.minimum(chain - 1 - spot, 2))
+
+    def copies(distance, to):
+        return [
+            remote(
+                ins[i] if forward else ins[i].at[2 - distance],
+                outs[i].at[2 - distance],
+                send.at[i, distance],
+                recv.at[i, distance],
+                (to, part),
+            )
+            for i in range(count)
+        ]
+
+    def start(sign, distance):
+        for copy in copies(distance, group + sign * distance):
+            copy.start()
+
+    def finish(sign, distance):
+        for copy in copies(distance, group + sign * distance):
+            copy.wait_send()
+
+    def take(sign, distance):
+        for copy in copies(distance, group - sign * distance):
+            copy.wait_recv()
+
+    if forward:
+        each(None, functools.partial(start, 1))
+        each(functools.partial(take, 1), None)
+        each(None, functools.partial(finish, 1))
+    else:
+        each(functools.partial(start, -1), None)
+        each(None, functools.partial(take, -1))
+        each(functools.partial(finish, -1), None)
+
+
+def halo(arrays, chain, forward, number):
+    count = len(arrays)
+    return pl.pallas_call(
+        functools.partial(halo_kernel, chain, forward, count),
+        out_shape=tuple(jax.ShapeDtypeStruct(((2,) + a.shape) if forward else a.shape, a.dtype) for a in arrays),
+        in_specs=[ANY] * count,
+        out_specs=(ANY,) * count,
+        scratch_shapes=[dma(count, 3), dma(count, 3)],
+        compiler_params=comm_params(number),
+    )(*arrays)
+
+
+def dot(left, right):
+    return jnp.dot(left, right, preferred_element_type=FULL)
+
+
+def dot_t(left, right):
+    return lax.dot_general(left, right, (((1,), (1,)), ((), ())), preferred_element_type=FULL)
+
+
+def t_dot(left, right):
+    return lax.dot_general(left, right, (((0,), (0,)), ((), ())), preferred_element_type=FULL)
+
+
+def body(
+    groups, parts,
+    tokens, documents, routes, norm1_gain, q_gain, k_gain, w_query, w_key, w_value, w_out, norm2_gain, router_w,
+    w_gate, w_up, w_down, out_grad,
+):
+    row_count, width = tokens.shape
+    local_experts, _, hidden = w_gate.shape
+    experts = local_experts * groups
+    chain = LENGTH // row_count
+    if not (parts == 4 and groups % 2 == 0 and experts <= 2 * TOP and row_count * chain == LENGTH and WINDOW == 2 * row_count):
+        return body_routed(
+            tokens, documents, routes, norm1_gain, q_gain, k_gain, w_query, w_key, w_value, w_out, norm2_gain, router_w,
+            w_gate, w_up, w_down, out_grad,
+        )
+    depth = groups // 2
+    rows = row_count // parts
+    seen = groups * row_count // 2
+    heads = w_query.shape[1] // HD
+    score_scale = HD ** (-0.5)
+    group, part = lax.axis_index("expert"), lax.axis_index("tensor")
+    core = part % 2
+
+    def quarter(array):
+        return lax.dynamic_slice_in_dim(array, part * rows, rows, 0)
+
+    gate_pair, up_pair, down_pair = pair_weights([w_gate, w_up, w_down], 1)
+    units = 2 * local_experts * hidden
+    gate_all = gate_pair.reshape(2 * local_experts, width, hidden).transpose(1, 0, 2).reshape(width, units)
+    up_all = up_pair.reshape(2 * local_experts, width, hidden).transpose(1, 0, 2).reshape(width, units)
+    down_all = down_pair.reshape(units, width)
+
+    first_row = group * row_count
+    positions = first_row + jnp.arange(row_count, dtype=jnp.int32)
+    cosine, sine = rope_tables(positions % LENGTH)
+    inputs = tokens.astype(FULL)
+    scale_one = lax.rsqrt(jnp.mean(inputs * inputs, axis=-1, keepdims=True) + NORM_EPSILON)
+    normed_one = (inputs * scale_one * norm1_gain).astype(LOW)
+    query_raw = dot(normed_one, w_query)
+    key_raw = dot(normed_one, w_key)
+    values = dot(normed_one, w_value).astype(LOW)
+    squares = lax.psum(
+        jnp.stack([jnp.sum(query_raw * query_raw, axis=-1), jnp.sum(key_raw * key_raw, axis=-1)]), "tensor"
+    )
+    query_scale = lax.rsqrt(squares[0] / width + NORM_EPSILON)[:, None]
+    key_scale = lax.rsqrt(squares[1] / width + NORM_EPSILON)[:, None]
+    query_gain, key_gain = q_gain.reshape(-1), k_gain.reshape(-1)
+    queries = rotate((query_raw * query_scale * query_gain).reshape(row_count, heads, HD), cosine, sine).astype(LOW)
+    key_heads = rotate((key_raw * key_scale * key_gain).reshape(row_count, heads, HD), cosine, sine).astype(LOW)
+    own_kv = jnp.concatenate([key_heads.reshape(row_count, -1), values], axis=1)
+    own_docs = documents.reshape(row_count // 128, 128)
+    before_kv, before_docs = halo([own_kv, own_docs], chain, True, 2)
+    spot = group % chain
+    exists = jnp.stack([spot >= 2, spot >= 1])
+    before_kv = jnp.where(exists[:, None, None], before_kv, jnp.zeros((), LOW))
+    before_docs = jnp.where(exists[:, None, None], before_docs, -1)
+    all_kv = jnp.concatenate([before_kv[0], before_kv[1], own_kv], axis=0)
+    all_keys = all_kv[:, : heads * HD].reshape(3 * row_count, heads, HD)
+    all_values = all_kv[:, heads * HD :].reshape(3 * row_count, heads, HD)
+    all_docs = jnp.concatenate([before_docs[0], before_docs[1], own_docs], axis=0).reshape(-1)
+    key_pos = first_row - 2 * row_count + jnp.arange(3 * row_count, dtype=jnp.int32)
+    allowed = (
+        (all_docs[None, :] == documents[:, None])
+        & (key_pos[None, :] <= positions[:, None])
+        & (positions[:, None] - key_pos[None, :] < WINDOW)
+    )
+
+    def masked_scores():
+        raw_scores = jnp.einsum("qhd,khd->hqk", queries, all_keys, preferred_element_type=FULL) * score_scale
+        return jnp.where(allowed[None], raw_scores, -1e30)
+
+    scores = masked_scores()
+    highest = jnp.max(scores, axis=-1, keepdims=True)
+    weights = jnp.where(allowed[None], jnp.exp(scores - highest), 0.0)
+    denominator = jnp.sum(weights, axis=-1, keepdims=True)
+    log_total = highest + jnp.log(denominator)
+    attn_probs = weights / denominator
+    attended = jnp.einsum("hqk,khd->qhd", attn_probs.astype(LOW), all_values, preferred_element_type=FULL)
+    attended = attended.reshape(row_count, -1).astype(LOW)
+    attention = tensor_scatter(dot(attended, w_out).astype(LOW), 3)
+
+    own_inputs = quarter(tokens).astype(FULL)
+    own_grad = quarter(out_grad)
+    own_grad_float = own_grad.astype(FULL)
+    state = own_inputs + attention
+    scale_two = lax.rsqrt(jnp.mean(state * state, axis=-1, keepdims=True) + NORM_EPSILON)
+    normed_two = (state * scale_two * norm2_gain).astype(LOW)
+    router_probs = jax.nn.softmax(dot(normed_two, router_w), axis=-1)
+    picked = jnp.any(
+        quarter(routes)[:, :, None] == jnp.arange(experts, dtype=jnp.int32)[None, None, :], axis=1
+    ).astype(FULL)
+
+    no_small = jnp.zeros((8, 128), FULL)
+    all_grad, _ = gather_rows(own_grad, no_small, depth, 4)
+    all_normed, all_gates = gather_rows(normed_two, (router_probs * picked).T, depth, 5)
+    all_normed = all_normed.reshape(seen, width)
+    all_grad = all_grad.reshape(seen, width)
+    own_gates = lax.dynamic_slice_in_dim(all_gates, group * local_experts, local_experts, 2)
+    own_gates = own_gates.transpose(0, 1, 3, 2).reshape(seen, 1, local_experts, 1)
+    split = (seen, 2, local_experts, hidden)
+    gate_pre = dot(all_normed, gate_all)
+    up_pre = dot(all_normed, up_all)
+    logistic = jax.nn.sigmoid(gate_pre)
+    activated = gate_pre * logistic
+    inner_act = activated * up_pre
+    inner_back = dot_t(all_grad, down_all)
+    gate_cot = jnp.sum((inner_act * inner_back).reshape(split), axis=(1, 3))
+    gate_wide = jnp.broadcast_to(own_gates, split).reshape(seen, units)
+    gated = (gate_wide * inner_act).astype(LOW)
+    inner_grad = gate_wide * inner_back
+    gate_pre_grad = (inner_grad * up_pre * logistic * (1.0 + gate_pre * (1.0 - logistic))).astype(LOW)
+    up_pre_grad = (inner_grad * activated).astype(LOW)
+    produced = dot(gated, down_all).astype(LOW).reshape(depth, 4, rows, width)
+    row_grad = (dot_t(gate_pre_grad, gate_all) + dot_t(up_pre_grad, up_all)).astype(LOW).reshape(depth, 4, rows, width)
+    gate_cot = gate_cot.reshape(depth, 4, rows, local_experts).transpose(0, 1, 3, 2)
+    gate_cot = jnp.concatenate([gate_cot, jnp.zeros((depth, 4, 8 - local_experts, rows), FULL)], axis=2)
+    normed_two_grad, gate_cots = scatter_rows(row_grad, gate_cot, 6)
+    expert_mix, _ = scatter_rows(produced, jnp.zeros((depth, 4, 8, 128), FULL), 7)
+
+    def expert_grads(left, right):
+        return t_dot(left, right)
+
+    gate_wgrad = expert_grads(all_normed, gate_pre_grad).reshape(width, 2, local_experts, hidden).transpose(1, 2, 0, 3)
+    up_wgrad = expert_grads(all_normed, up_pre_grad).reshape(width, 2, local_experts, hidden).transpose(1, 2, 0, 3)
+    down_wgrad = expert_grads(gated, all_grad).reshape(2, local_experts, hidden, width)
+    swaps = pair_swap([gate_wgrad, up_wgrad, down_wgrad], 8)
+    w_gate_grad, w_up_grad, w_down_grad = (
+        lax.dynamic_index_in_dim(mine, core, 0, keepdims=False) + other
+        for mine, other in zip((gate_wgrad, up_wgrad, down_wgrad), swaps)
+    )
+
+    output = tensor_gather((state + expert_mix).astype(LOW), 9)
+
+    prob_cot = gate_cots[:, :, :local_experts].reshape(depth, 2, 2, local_experts, rows).sum(axis=2)
+    prob_cot = prob_cot.reshape(experts, rows).T * picked
+    logit_cot = router_probs * (prob_cot - jnp.sum(router_probs * prob_cot, axis=-1, keepdims=True))
+    normed_two_grad = normed_two_grad + jnp.einsum(
+        "te,de->td", logit_cot, router_w.astype(FULL), precision=HIGHEST_PRECISION
+    )
+    router_grad = jnp.einsum("td,te->ed", normed_two.astype(FULL), logit_cot, precision=HIGHEST_PRECISION)
+    norm2_grad = jnp.sum(normed_two_grad * state * scale_two, axis=0)
+    inner_two = jnp.sum(normed_two_grad * norm2_gain * state, axis=-1, keepdims=True)
+    state_cot = own_grad_float + scale_two * norm2_gain * normed_two_grad - state * scale_two**3 * inner_two / width
+    state_low = tensor_gather(state_cot.astype(LOW), 10)
+
+    w_out_grad = t_dot(state_low, attended)
+    attended_cot = dot_t(state_low, w_out).astype(LOW).reshape(row_count, heads, HD)
+    scores = masked_scores()
+    attn_probs = jnp.where(allowed[None], jnp.exp(scores - log_total), 0.0)
+    value_cot_all = jnp.einsum("hqk,qhd->khd", attn_probs.astype(LOW), attended_cot, preferred_element_type=FULL)
+    prob_grad = jnp.einsum("qhd,khd->hqk", attended_cot, all_values, preferred_element_type=FULL)
+    delta = jnp.sum(attn_probs * prob_grad, axis=-1, keepdims=True)
+    score_cot = (attn_probs * (prob_grad - delta)).astype(LOW)
+    query_cot = jnp.einsum("hqk,khd->qhd", score_cot, all_keys, preferred_element_type=FULL) * score_scale
+    key_cot_all = jnp.einsum("hqk,qhd->khd", score_cot, queries, preferred_element_type=FULL) * score_scale
+    kv_cot = jnp.concatenate(
+        [key_cot_all.reshape(3, row_count, -1), value_cot_all.reshape(3, row_count, -1)], axis=2
+    )
+    (after_kv,) = halo([kv_cot[:2].astype(LOW)], chain, False, 11)
+    follows = jnp.stack([spot < chain - 2, spot < chain - 1])
+    after_kv = jnp.where(follows[:, None, None], after_kv, jnp.zeros((), LOW)).astype(FULL)
+    kv_cot = kv_cot[2] + after_kv[0] + after_kv[1]
+    key_cot = kv_cot[:, : heads * HD].reshape(row_count, heads, HD)
+    value_low = kv_cot[:, heads * HD :].astype(LOW)
+    query_norm_cot = rotate_back(query_cot, cosine, sine).reshape(row_count, -1)
+    key_norm_cot = rotate_back(key_cot, cosine, sine).reshape(row_count, -1)
+    q_gain_local = jnp.sum(query_norm_cot * query_raw * query_scale, axis=0).reshape(heads, HD)
+    k_gain_local = jnp.sum(key_norm_cot * key_raw * key_scale, axis=0).reshape(heads, HD)
+    inners = lax.psum(
+        jnp.stack(
+            [
+                jnp.sum(query_norm_cot * query_gain * query_raw, axis=-1),
+                jnp.sum(key_norm_cot * key_gain * key_raw, axis=-1),
+            ]
+        ),
+        "tensor",
+    )
+    query_raw_cot = (
+        query_scale * query_gain * query_norm_cot - query_raw * query_scale**3 * inners[0][:, None] / width
+    ).astype(LOW)
+    key_raw_cot = (
+        key_scale * key_gain * key_norm_cot - key_raw * key_scale**3 * inners[1][:, None] / width
+    ).astype(LOW)
+    normed_part = dot_t(query_raw_cot, w_query) + dot_t(key_raw_cot, w_key) + dot_t(value_low, w_value)
+    normed_one_grad = tensor_scatter(normed_part.astype(LOW), 12)
+    own_scale = quarter(scale_one)
+    norm1_grad = jnp.sum(normed_one_grad * own_inputs * own_scale, axis=0)
+    inner_one = jnp.sum(normed_one_grad * norm1_gain * own_inputs, axis=-1, keepdims=True)
+    input_grad = (
+        state_cot + own_scale * norm1_gain * normed_one_grad - own_inputs * own_scale**3 * inner_one / width
+    )
+    input_grad = tensor_gather(input_grad.astype(LOW), 13).astype(FULL)
+
+    local = jnp.concatenate(
+        [
+            t_dot(normed_one, query_raw_cot),
+            t_dot(normed_one, key_raw_cot),
+            t_dot(normed_one, value_low),
+            w_out_grad,
+        ],
+        axis=1,
+    ).astype(LOW)
+    summed = expert_scatter(local, depth, 14)
+    w_query_grad, w_key_grad, w_value_grad, w_out_grad = jnp.split(summed, 4, axis=1)
+    vectors = jnp.concatenate([router_grad, norm1_grad[None], norm2_grad[None]], axis=0)
+    vectors = lax.psum(lax.psum_scatter(vectors, "expert", scatter_dimension=1, tiled=True), "tensor")
+    gains = lax.psum_scatter(
+        jnp.concatenate([q_gain_local, k_gain_local], axis=0), "expert", scatter_dimension=1, tiled=True
+    )
+    return (
+        output,
+        input_grad,
+        vectors[experts],
+        gains[:heads],
+        gains[heads:],
+        w_query_grad,
+        w_key_grad,
+        w_value_grad,
+        w_out_grad.T,
+        vectors[experts + 1],
+        vectors[:experts].T,
+        w_gate_grad,
+        w_up_grad,
+        w_down_grad,
+    )
+
+
 def solution(mesh):
     placed = (
         P("expert", None),
@@ -405,7 +1118,7 @@
         P("expert", None),
     )
     return jax.shard_map(
-        body,
+        functools.partial(body, mesh.shape["expert"], mesh.shape["tensor"]),
         mesh=mesh,
         in_specs=placed,
         out_specs=(

time: 4130 us -> 1350 us (0.33)
  waiting for transfers between devices: 2410 us -> 0.04 us
  Pallas kernels: 0 us -> 913 us
  blocking collectives: 780 us -> 24.5 us
  local copies, waits for them, and re-layouts: 410 us -> 90.3 us
  matrix products: 276 us -> 199 us
  other arithmetic: 167 us -> 98.8 us
  starting transfers between devices: 63.7 us -> 0.08 us
    all_to_all x3 -> x0, waiting for transfers between devices: 1940 us -> none  [the longest x1 683 us: body(): lax.all_to_all(send_grads, 'expert', split_axis=0, concat_axis=0, tiled=T...]
    pallas_call x0 -> x14, Pallas kernels: none -> 913 us  [the longest x2 194 us: scatter_rows(): pl.pallas_call(functools.partial(scatter_rows_kernel, depth, rows), out_s...]
    all_to_all x1 -> x0, blocking collectives: 732 us -> none  [body(): lax.all_to_all(send_rows, 'expert', split_axis=0, concat_axis=0, tiled=True)]
    gather x4 -> x0, local copies, waits for them, and re-layouts: 324 us -> none  [the longest x1 96.2 us: body(): returned.reshape(experts * capacity, model_width)[target]]
    reduce_scatter x5 -> x1, waiting for transfers between devices: 248 us -> 0.01 us  [body(): lax.psum_scatter(vectors, 'expert', scatter_dimension=1, tiled=True)]
    psum x3 -> x0, waiting for transfers between devices: 187 us -> none  [the longest x1 73.7 us: body(): lax.psum(expert_part.astype(jnp.bfloat16), 'tensor').astype(jnp.float32)]
    dot_general x29, matrix products: 267 us -> 190 us  [the longest x7 59.1 us: dot_t(): lax.dot_general(left, right, (((1,), (1,)), ((), ())), preferred_element_...]
    convert_element_type x2 -> x0, local copies, waits for them, and re-layouts: 45.8 us -> none  [the longest x1 22.9 us: body(): produced = jnp.einsum('secf,efd->secd', inner_act, w_down, preferred_elem...]
  transfers between devices with their start and end apart: 23 -> 2, of which waited for: 14 -> 0; matrix products, arithmetic and copies ran while one was open for 11% -> 7% of each run, Pallas kernels for 0% -> 18%
where the time goes in v1:
time: 1350 us; the launch traced here: 1340 us
  Pallas kernels  913 us (68%)
  matrix products  199 us (15%)
  other arithmetic  98.8 us (7%)
  local copies, waits for them, and re-layouts  90.3 us (7%)
  blocking collectives  24.5 us (2%)
  between operations  15.5 us (1%)
    pallas_call x2, Pallas kernels, scatter_rows(): pl.pallas_call(functools.partial(scatter_rows_kernel, depth, rows), out_s...  194 us
    pallas_call x1, Pallas kernels, pair_weights(): pl.pallas_call(functools.partial(pair_weights_kernel, count), out_shape=t...  192 us
    pallas_call x2, Pallas kernels, gather_rows(): pl.pallas_call(functools.partial(gather_rows_kernel, depth, rows), out_sh...  181 us
    pallas_call x1, Pallas kernels, expert_scatter(): pl.pallas_call(functools.partial(expert_scatter_kernel, depth, rows), out...  166 us
    pallas_call x2, Pallas kernels, halo(): pl.pallas_call(functools.partial(halo_kernel, chain, forward, count), out...  70.1 us
    dot_general x7, matrix products, dot_t(): lax.dot_general(left, right, (((1,), (1,)), ((), ())), preferred_element_...  59.1 us
    pallas_call x3, Pallas kernels, tensor_gather(): pl.pallas_call(tensor_gather_kernel, out_shape=jax.ShapeDtypeStruct((2, 2...  54.5 us
    dot_general x8, matrix products, dot(): return jnp.dot(left, right, preferred_element_type=FULL)  53 us
  transfers between devices with their start and end apart: 2, of which 0 were waited for; matrix products, arithmetic and copies ran while one was open for 7% of the time, Pallas kernels for 18%

profile of v1, /device:TPU:10, one launch (start us, length us, event | category | flops | bytes accessed | tf_op | source)
XLA Modules:
  0.0 1340.4 jit_solution(10052905117826349543)
XLA Ops:
  27.3 6.9 psum.21
  54.6 46.6 %shard_map.263 = (bf16[2,512,1024]{2,1,0:T(8,128)(2,1)}, s32[2,4,128]{2,1,0:T(4,128)}) custom-call(bf16[512,1024]{1,0:T(8,128)(2,1)} %pad_maximum_fusion.1.refs_0_, s32[4,128]{1,0:T(4,128)} %bitcast.260), custom_call_target="tpu_custom_call" | custom-call | tf_op jit(solution)/shard_map/pallas_call | solution.py:853
  103.4 8.0 maximum_maximum_fusion
  116.1 191.8 %shard_map.266 = (bf16[2,2,2048,256]{3,2,1,0:T(8,128)(2,1)}, bf16[2,2,2048,256]{3,2,1,0:T(8,128)(2,1)}, bf16[2,2,256,2048]{3,2,1,0:T(8,128)(2,1)}) custom-call(bf16[2,2048,256]{2,1,0:T(8,128)(2,1)} %refs_0_.1, bf16[2,2048,256]{2,1,0:T(8,128)(2,1)} %refs_1_.1, bf16[2,256,2048]{2,1,0:T(8,128)(2,1)} %refs_2_.1), custom_call_target="tpu_custom_call" | custom-call | tf_op jit(solution)/shard_map/pallas_call | solution.py:641
  314.1 6.3 copy.149
  338.7 17.7 %shard_map.264 = f32[128,2048]{1,0:T(8,128)} custom-call(bf16[2,2,128,2048]{3,2,1,0:T(8,128)(2,1)} %bitcast.232), custom_call_target="tpu_custom_call" | custom-call | tf_op jit(solution)/shard_map/pallas_call | solution.py:704
  360.1 92.2 %shard_map.265 = (bf16[4,4,128,2048]{3,2,1,0:T(8,128)(2,1)}, f32[4,4,16,128]{3,2,1,0:T(8,128)}) custom-call(bf16[128,2048]{1,0:T(8,128)(2,1)} %copy-done.17, f32[16,128]{1,0:T(8,128)} %select_bitcast_fusion.small_ref), custom_call_target="tpu_custom_call" | custom-call | tf_op jit(solution)/shard_map/pallas_call | solution.py:509
  452.3 14.6 %fusion.72 = f32[2048,1024]{0,1:T(8,128)} fusion(bf16[2048,2048]{1,0:T(8,128)(2,1)} %bitcast.275, bf16[2048,1024]{0,1:T(8,128)(2,1)} %bitcast.222), kind=kOutput, calls=%fused_computation.178 | convolution fusion | flops 8589934592 | bytes 20971520 | tf_op jit(solution)/shard_map/dot_general | solution.py:864
  466.9 11.3 fusion.71
  478.8 88.6 %shard_map.269 = (bf16[4,4,128,2048]{3,2,1,0:T(8,128)(2,1)}, f32[4,4,8,128]{3,2,1,0:T(8,128)}) custom-call(bf16[128,2048]{1,0:T(8,128)(2,1)} %constant_dynamic-slice_fusion.x_ref, f32[8,128]{1,0:T(8,128)} %broadcast_in_dim.122.small_ref), custom_call_target="tpu_custom_call" | custom-call | tf_op jit(solution)/shard_map/pallas_call | solution.py:509
  568.3 23.9 %multiply_multiply_fusion = (f32[2048,1024]{0,1:T(8,128)}, bf16[2048,1024]{0,1:T(8,128)(2,1)}, bf16[2048,1024]{0,1:T(8,128)(2,1)}, bf16[2048,1024]{0,1:T(8,128)(2,1)}) fusion(f32[2048,1024]{0,1:T(8,128)} %fusion.72, f32[2048,1024]{0,1:T(8,128)} %fusion.71, f32[2048,2]{0,1:T(2,128)S(1)} %bitcast.247, bf16[2048,2048]{1,0:T(8,128)(2,1)} %bitcast.213, ...), kind=kOutput, calls=%fused_computation.31 | convolution fusion | flops 8627683328 | bytes 50348032 | tf_op jit(solution)/shard_map/dot_general | solution.py:868
  596.6 14.4 %convolution_convert_fusion = bf16[2048,2048]{1,0:T(8,128)(2,1)} fusion(bf16[2048,1024]{0,1:T(8,128)(2,1)} %get-tuple-element.115, bf16[1024,2048]{1,0:T(8,128)(2,1)} %bitcast.219), kind=kOutput, calls=%fused_computation.17 | convolution fusion | flops 8594128896 | bytes 16777216 | tf_op jit(solution)/shard_map/dot_general | solution.py:864
  611.0 11.7 fusion.73
  622.7 14.7 %add_convert_fusion = bf16[2048,2048]{1,0:T(8,128)(2,1)} fusion(f32[2048,2048]{1,0:T(8,128)} %fusion.73, bf16[2048,1024]{0,1:T(8,128)(2,1)S(1)} %copy-done.24, bf16[2048,1024]{0,1:T(8,128)(2,1)S(1)} %bitcast.223), kind=kOutput, calls=%fused_computation | convolution fusion | flops 8598323200 | bytes 33554432 | tf_op jit(solution)/shard_map/dot_general | solution.py:868
  637.4 96.9 %shard_map.270 = (f32[128,2048]{1,0:T(8,128)}, f32[4,4,8,128]{3,2,1,0:T(8,128)}) custom-call(bf16[4,4,128,2048]{3,2,1,0:T(8,128)(2,1)} %bitcast.211, f32[4,4,8,128]{3,2,1,0:T(8,128)} %concatenate.63.small_ref), custom_call_target="tpu_custom_call" | custom-call | tf_op jit(solution)/shard_map/pallas_call | solution.py:604
  735.8 97.6 %shard_map.267 = (f32[128,2048]{1,0:T(8,128)}, f32[4,4,8,128]{3,2,1,0:T(8,128)}) custom-call(bf16[4,4,128,2048]{3,2,1,0:T(8,128)(2,1)} %bitcast.210, f32[4,4,8,128]{3,2,1,0:T(8,128)} %broadcast_in_dim.121.small_ref), custom_call_target="tpu_custom_call" | custom-call | tf_op jit(solution)/shard_map/pallas_call | solution.py:604
  839.3 18.4 %shard_map.271 = bf16[2,2,128,2048]{3,2,1,0:T(8,128)(2,1)} custom-call(bf16[128,2048]{1,0:T(8,128)(2,1)} %get-tuple-element.109.x_ref), custom_call_target="tpu_custom_call" | custom-call | tf_op jit(solution)/shard_map/pallas_call | solution.py:741
  861.4 8.9 fusion.11
  870.4 8.5 multiply_reduce_fusion
  888.8 9.8 multiply_convert_fusion
  930.0 23.5 %shard_map.272 = bf16[2,512,1024]{2,1,0:T(8,128)(2,1)} custom-call(bf16[2,512,1024]{2,1,0:T(8,128)(2,1)} %slice.183.refs_0_), custom_call_target="tpu_custom_call" | custom-call | tf_op jit(solution)/shard_map/pallas_call | solution.py:853
  985.6 17.9 %shard_map.273 = f32[128,2048]{1,0:T(8,128)} custom-call(bf16[2,2,128,2048]{3,2,1,0:T(8,128)(2,1)} %bitcast.212), custom_call_target="tpu_custom_call" | custom-call | tf_op jit(solution)/shard_map/pallas_call | solution.py:704
  1017.5 11.2 fusion.77
  1028.7 11.3 fusion.76
  1047.1 7.1 pad_maximum_fusion.p_ref
  1054.2 165.8 %shard_map.275 = f32[256,2048]{1,0:T(8,128)} custom-call(bf16[4,2,256,2048]{3,2,1,0:T(8,128)(2,1)} %pad_maximum_fusion.p_ref), custom_call_target="tpu_custom_call" | custom-call | tf_op jit(solution)/shard_map/pallas_call | solution.py:782
  1222.6 18.4 %shard_map.274 = bf16[2,2,128,2048]{3,2,1,0:T(8,128)(2,1)} custom-call(bf16[128,2048]{1,0:T(8,128)(2,1)} %fusion.27.x_ref), custom_call_target="tpu_custom_call" | custom-call | tf_op jit(solution)/shard_map/pallas_call | solution.py:741
  1245.1 14.7 %fusion.78.refs_2_ = f32[2,2,256,2048]{3,2,1,0:T(8,128)} fusion(bf16[2,2,256,2048]{3,2,1,0:T(8,128)(2,1)} %bitcast.215, bf16[2048,2048,1,1]{1,0,3,2:T(8,128)(2,1)} %bitcast.214), kind=kOutput, calls=%fused_computation.184 | convolution fusion | flops 8589934592 | bytes 20971520 | tf_op jit(solution)/shard_map/dot_general | solution.py:872
  1259.9 19.6 %shard_map.276 = (f32[2,2048,256]{2,1,0:T(8,128)}, f32[2,2048,256]{2,1,0:T(8,128)}, f32[2,256,2048]{2,1,0:T(8,128)}) custom-call(f32[2,2,2048,256]{3,2,1,0:T(8,128)} %bitcast.204, f32[2,2,2048,256]{3,2,1,0:T(8,128)} %bitcast.201, f32[2,2,256,2048]{3,2,1,0:T(8,128)} %fusion.78.refs_2_), custom_call_target="tpu_custom_call" | custom-call | tf_op jit(solution)/shard_map/pallas_call | solution.py:667
  1279.5 6.7 bitcast_add_fusion.2
  1296.0 17.7 %shard_map.268 = bf16[2,2,128,2048]{3,2,1,0:T(8,128)(2,1)} custom-call(bf16[128,2048]{1,0:T(8,128)(2,1)} %get-tuple-element.129.x_ref), custom_call_target="tpu_custom_call" | custom-call | tf_op jit(solution)/shard_map/pallas_call | solution.py:741
  1316.9 11.9 psum.23
  (273 shorter events, 210.5 us)
Async XLA Ops:
  7.2 16.2 %copy-start = (bf16[2048,512]{1,0:T(8,128)(2,1)S(1)}, bf16[2048,512]{1,0:T(8,128)(2,1)}, u32[]{:S(2)}) copy-start(bf16[2048,512]{1,0:T(8,128)(2,1)} %param.23) | copy-start | bytes 6291460
  7.2 8.9 copy-start.55
  7.2 1307.5 %reduce-scatter.7.cloned.1.call-start = ((), (), s32[]{:S(2)}) async-start(), calls=%async_computation.3 | async-start | bytes 73728
  9.5 13.8 %copy-start.61 = (f32[512]{0:T(512)}, f32[512]{0:T(512)S(1)}, u32[]{:S(2)}) copy-start(f32[512]{0:T(512)S(1)} %add_rsqrt_fusion) | copy-start | bytes 6148
  13.9 32.6 %copy-start.33 = (f32[512,128]{0,1:T(8,128)}, f32[512,128]{0,1:T(8,128)S(1)}, u32[]{:S(2)}) copy-start(f32[512,128]{0,1:T(8,128)S(1)} %get-tuple-element.138) | copy-start | bytes 786436
  23.3 12.5 copy-start.53
  27.3 12.4 copy-start.58
  34.3 7.8 copy-start.51
  34.3 16.4 %copy-start.48 = (f32[1,512]{1,0:T(1,128)}, f32[1,512]{1,0:T(1,128)S(1)}, u32[]{:S(2)}) copy-start(f32[1,512]{1,0:T(1,128)S(1)} %get-tuple-element.148) | copy-start | bytes 6148
  35.9 14.9 %copy-start.2 = (f32[512,512]{1,0:T(8,128)}, f32[512,512]{1,0:T(8,128)S(1)}, u32[]{:S(2)}) copy-start(f32[512,512]{1,0:T(8,128)S(1)} %copy.135) | copy-start | bytes 3145732
  314.1 7.3 copy-start.18
  338.7 20.3 %copy-start.50 = (f32[2048]{0:T(1024)S(1)}, f32[2048]{0:T(1024)}, u32[]{:S(2)}) copy-start(f32[2048]{0:T(1024)} %param.26) | copy-start | bytes 24580
  338.7 20.4 %copy-start.47 = (bf16[2048,16]{0,1:T(8,128)(2,1)S(1)}, bf16[2048,16]{0,1:T(8,128)(2,1)}, u32[]{:S(2)}) copy-start(bf16[2048,16]{0,1:T(8,128)(2,1)} %param.27) | copy-start | bytes 196612
  452.3 14.6 %copy-start.27 = (bf16[4,2048,256]{1,2,0:T(8,128)(2,1)S(1)}, bf16[4,2048,256]{1,2,0:T(8,128)(2,1)}, u32[]{:S(2)}) copy-start(bf16[4,2048,256]{1,2,0:T(8,128)(2,1)} %copy.148) | copy-start | bytes 12582916
  452.3 14.6 %copy-start.63 = (bf16[4,4,128,2048]{3,2,1,0:T(8,128)(2,1)S(1)}, bf16[4,4,128,2048]{3,2,1,0:T(8,128)(2,1)}, u32[]{:S(2)}) copy-start(bf16[4,4,128,2048]{3,2,1,0:T(8,128)(2,1)} %get-tuple-element.31) | copy-start | bytes 25165828
  596.6 14.4 %copy-start.22 = (bf16[2048,1024]{0,1:T(8,128)(2,1)S(1)}, bf16[2048,1024]{0,1:T(8,128)(2,1)}, u32[]{:S(2)}) copy-start(bf16[2048,1024]{0,1:T(8,128)(2,1)} %get-tuple-element.114) | copy-start | bytes 12582916
  596.6 14.4 %copy-start.28 = (bf16[4,2048,256]{1,2,0:T(8,128)(2,1)S(1)}, bf16[4,2048,256]{1,2,0:T(8,128)(2,1)}, u32[]{:S(2)}) copy-start(bf16[4,2048,256]{1,2,0:T(8,128)(2,1)} %copy.148) | copy-start | bytes 12582916
  611.0 11.7 copy-start.24
  611.0 11.7 copy-start.26
  857.7 12.6 slice-start
  861.4 9.0 slice-start.1
  861.4 9.0 slice-start.2
  861.4 8.9 copy-start.44
  888.8 9.8 copy-start.19
  909.8 6.5 copy-start.46
  963.1 6.5 copy-start.62
  969.6 347.3 %reduce-scatter.5.cloned.1.call-start = ((), (), s32[]{:S(2)}) async-start(), calls=%async_computation.2 | async-start | bytes 221184 | tf_op jit(solution)/shard_map/reduce_scatter | solution.py:1079
  982.9 20.5 %copy-start.56 = (f32[2048]{0:T(1024)S(1)}, f32[2048]{0:T(1024)}, u32[]{:S(2)}) copy-start(f32[2048]{0:T(1024)} %param.19) | copy-start | bytes 24580
  1017.5 11.2 copy-start.23
  1054.2 165.8 %copy-start.13 = (f32[128,2048]{1,0:T(8,128)S(1)}, f32[128,2048]{1,0:T(8,128)}, u32[]{:S(2)}) copy-start(f32[128,2048]{1,0:T(8,128)} %shard_map.273) | copy-start | bytes 3145732
  1279.5 6.7 copy-start.30
  1279.5 11.9 slice-start.3
  (44 other events, 151.1 us)
Sparse Core Ops, SparseCore 0:
  969.7 83.1 reduce-scatter.6
  1056.1 60.7 reduce-scatter.4

commit v2 on v1

--- a/solution.py
+++ b/solution.py
@@ -446,206 +446,385 @@
         target[part] = total.astype(target.dtype)
 
 
-def gather_rows_kernel(depth, rows, x_ref, small_ref, o_ref, smalls_ref, z_send, z_recv, p_send, p_recv, s_send, s_recv, local):
+class Copies:
+    def __init__(self):
+        self.open = []
+
+    def start(self, copy):
+        copy.start()
+        self.open.append([copy, True])
+        return copy
+
+    def arrived(self, copy):
+        copy.wait_recv()
+        for entry in self.open:
+            if entry[0] is copy:
+                entry[1] = False
+
+    def finish(self):
+        for copy, receiving in self.open:
+            copy.wait_send()
+            if receiving:
+                copy.wait_recv()
+
+
+class Gather:
+    def __init__(self, copies, block, target, rows, z_send, z_recv, p_send, p_recv):
+        self.copies, self.block, self.target, self.rows = copies, block, target, rows
+        self.z_send, self.z_recv, self.p_send, self.p_recv = z_send, z_recv, p_send, p_recv
+        z, x, y, core = place()
+        self.over_x, self.over_y = device(z, 1 - x, y, core), device(z, x, 1 - y, core)
+        self.here, self.x_place, self.y_place = 2 * x + y, 2 * (1 - x) + y, 2 * x + 1 - y
+        self.column = [device(swapped(z, step), x, y, core) for step in range(target.shape[0])]
+        self.along, self.planes, self.diagonals = {}, {}, {}
+
+    def at(self, step, spot, part):
+        half = self.rows // 2
+        if part is None:
+            return self.target.at[step, pl.ds(pl.multiple_of(spot * self.rows, self.rows), self.rows)]
+        return self.target.at[step, pl.ds(pl.multiple_of(spot * self.rows + part * half, half), half)]
+
+    def begin(self):
+        self.spread(0)
+        for step in range(1, len(self.column)):
+            self.along[step] = self.copies.start(
+                remote(self.block, self.at(step, self.here, None), self.z_send.at[step], self.z_recv.at[step], self.column[step])
+            )
+
+    def spread(self, step):
+        if step:
+            self.copies.arrived(self.along[step])
+        half = self.rows // 2
+        planes = []
+        for number, (to, part) in enumerate([(self.over_x, 0), (self.over_y, 1), (self.over_x, 1), (self.over_y, 0)]):
+            here = self.at(step, self.here, part)
+            source = here if step else self.block.at[pl.ds(part * half, half)]
+            planes.append(self.copies.start(remote(source, here, self.p_send.at[step, number], self.p_recv.at[step, number], to)))
+        self.planes[step] = planes
+
+    def turn(self, step):
+        self.copies.arrived(self.planes[step][0])
+        passed = self.at(step, self.x_place, 0)
+        first = self.copies.start(remote(passed, passed, self.p_send.at[step, 4], self.p_recv.at[step, 4], self.over_y))
+        self.copies.arrived(self.planes[step][1])
+        passed = self.at(step, self.y_place, 1)
+        second = self.copies.start(remote(passed, passed, self.p_send.at[step, 5], self.p_recv.at[step, 5], self.over_x))
+        self.diagonals[step] = (first, second)
+
+    def complete(self, step):
+        for copy in self.planes[step][2:] + list(self.diagonals[step]):
+            self.copies.arrived(copy)
+
+
+class Scatter:
+    def __init__(self, copies, work, diagonal, from_x, from_y, from_z, rows, send, recv):
+        self.copies, self.work, self.rows, self.send, self.recv = copies, work, rows, send, recv
+        self.diagonal, self.from_x, self.from_y, self.from_z = diagonal, from_x, from_y, from_z
+        z, x, y, core = place()
+        self.over_x, self.over_y = device(z, 1 - x, y, core), device(z, x, 1 - y, core)
+        self.here, self.x_place, self.y_place = 2 * x + y, 2 * (1 - x) + y, 2 * x + 1 - y
+        self.far = 2 * (1 - x) + 1 - y
+        self.column = [device(swapped(z, step), x, y, core) for step in range(work.shape[0])]
+        self.corners, self.sides, self.along = {}, {}, {}
+
+    def at(self, step, spot, part=None):
+        half = self.rows // 2
+        if part is None:
+            return self.work.at[step, pl.ds(pl.multiple_of(spot * self.rows, self.rows), self.rows)]
+        return self.work.at[step, pl.ds(pl.multiple_of(spot * self.rows + part * half, half), half)]
+
+    def copy(self, step, number, source, target, to):
+        return self.copies.start(remote(source, target, self.send.at[step, number], self.recv.at[step, number], to))
+
+    def corner(self, step):
+        self.corners[step] = (
+            self.copy(step, 0, self.at(step, self.far, 0), self.diagonal.at[step, 0], self.over_y),
+            self.copy(step, 1, self.at(step, self.far, 1), self.diagonal.at[step, 1], self.over_x),
+        )
+
+    def side(self, step):
+        via_y, via_x = self.corners[step]
+        self.copies.arrived(via_y)
+        add_rows(self.at(step, self.x_place, 0), [self.at(step, self.x_place, 0), self.diagonal.at[step, 0]], self.rows // 2)
+        to_x = self.copy(step, 2, self.at(step, self.x_place), self.from_x.at[step], self.over_x)
+        self.copies.arrived(via_x)
+        add_rows(self.at(step, self.y_place, 1), [self.at(step, self.y_place, 1), self.diagonal.at[step, 1]], self.rows // 2)
+        to_y = self.copy(step, 3, self.at(step, self.y_place), self.from_y.at[step], self.over_y)
+        self.sides[step] = (to_x, to_y)
+
+    def climb(self, step):
+        for copy in self.sides[step]:
+            self.copies.arrived(copy)
+        if step:
+            here = self.at(step, self.here)
+            add_rows(here, [here, self.from_x.at[step], self.from_y.at[step]], self.rows)
+            self.along[step] = self.copy(step, 4, here, self.from_z.at[step], self.column[step])
+
+    def result(self, target):
+        for copy in self.along.values():
+            self.copies.arrived(copy)
+        terms = [self.at(0, self.here), self.from_x.at[0], self.from_y.at[0]]
+        add_rows(target, terms + [self.from_z.at[step] for step in self.along], self.rows)
+
+    @staticmethod
+    def scratch(depth, rows, width):
+        return [
+            pltpu.VMEM((depth, 2, rows // 2, width), LOW),
+            pltpu.VMEM((depth, rows, width), LOW),
+            pltpu.VMEM((depth, rows, width), LOW),
+            pltpu.VMEM((depth, rows, width), LOW),
+            dma(depth, 5),
+            dma(depth, 5),
+        ]
+
+
+def greet_column_and_plane(depth):
     z, x, y, core = place()
-    here = 2 * x + y
-    over_x, over_y = (z, 1 - x, y, core), (z, x, 1 - y, core)
-    half = rows // 2
-    upper, lower = pl.ds(0, half), pl.ds(half, half)
-    others = []
-    for step in range(depth):
-        for turn in range(4):
-            if step or turn:
-                other = (swapped(z, step), swapped(x, turn // 2), swapped(y, turn % 2), core)
-                others.append((step * 4 + turn, other))
-    greet([device(*other) for _, other in others])
-    own = pltpu.make_async_copy(x_ref, o_ref.at[z, here], local.at[0])
+    greet(
+        [device(swapped(z, step), x, y, core) for step in range(1, depth)]
+        + [device(z, 1 - x, y, core), device(z, x, 1 - y, core)]
+    )
+
+
+def gather_rows_kernel(depth, rows, x_ref, o_ref, z_send, z_recv, p_send, p_recv, local):
+    z, x, y, core = place()
+    greet_column_and_plane(depth)
+    copies = Copies()
+    gather = Gather(copies, x_ref, o_ref, rows, z_send, z_recv, p_send, p_recv)
+    gather.begin()
+    own = pltpu.make_async_copy(x_ref, gather.at(0, gather.here, None), local.at[0])
     own.start()
-    own_small = pltpu.make_async_copy(small_ref, smalls_ref.at[z, here], local.at[1])
-    own_small.start()
-    pending = []
-
-    def start(copy):
-        copy.start()
-        pending.append(copy)
-        return copy
-
-    along_z = []
-    for step in range(1, depth):
-        along_z.append(
-            start(remote(x_ref, o_ref.at[z, here], z_send.at[step], z_recv.at[step], device(swapped(z, step), x, y, core)))
-        )
-    for number, other in others:
-        start(remote(small_ref, smalls_ref.at[z, here], s_send.at[number], s_recv.at[number], device(*other)))
-    own.wait()
-    own_small.wait()
-    forwards = []
     for step in range(depth):
         if step:
-            along_z[step - 1].wait_recv()
-        at = swapped(z, step)
-        mine = o_ref.at[at, here]
-        x_up = start(remote(mine.at[upper], mine.at[upper], p_send.at[step, 0], p_recv.at[step, 0], device(*over_x)))
-        y_low = start(remote(mine.at[lower], mine.at[lower], p_send.at[step, 1], p_recv.at[step, 1], device(*over_y)))
-        start(remote(mine.at[lower], mine.at[lower], p_send.at[step, 2], p_recv.at[step, 2], device(*over_x)))
-        start(remote(mine.at[upper], mine.at[upper], p_send.at[step, 3], p_recv.at[step, 3], device(*over_y)))
-        forwards.append((step, at, x_up, y_low))
-    for step, at, x_up, y_low in forwards:
-        x_up.wait_recv()
-        from_x = o_ref.at[at, 2 * (1 - x) + y, upper]
-        start(remote(from_x, from_x, p_send.at[step, 4], p_recv.at[step, 4], device(*over_y)))
-        y_low.wait_recv()
-        from_y = o_ref.at[at, 2 * x + 1 - y, lower]
-        start(remote(from_y, from_y, p_send.at[step, 5], p_recv.at[step, 5], device(*over_x)))
-    received = set(id(c) for c in along_z) | set(id(c) for f in forwards for c in f[2:])
-    for copy in pending:
-        copy.wait_send()
-        if id(copy) not in received:
-            copy.wait_recv()
-
-
-def gather_rows(block, small, depth, number):
-    rows = block.shape[0]
+            gather.spread(step)
+        gather.turn(step)
+    own.wait()
+    copies.finish()
+
+
+def gather_rows(block, depth, number):
+    rows, width = block.shape
     return pl.pallas_call(
         functools.partial(gather_rows_kernel, depth, rows),
-        out_shape=(
-            jax.ShapeDtypeStruct((depth, 4) + block.shape, block.dtype),
-            jax.ShapeDtypeStruct((depth, 4) + small.shape, small.dtype),
-        ),
-        in_specs=[ANY, ANY],
-        out_specs=(ANY, ANY),
-        scratch_shapes=[dma(depth), dma(depth), dma(depth, 6), dma(depth, 6), dma(4 * depth), dma(4 * depth), dma(2)],
+        out_shape=jax.ShapeDtypeStruct((depth, 4 * rows, width), block.dtype),
+        in_specs=[ANY],
+        out_specs=ANY,
+        scratch_shapes=[dma(depth), dma(depth), dma(depth, 6), dma(depth, 6), dma(1)],
         compiler_params=comm_params(number),
-    )(block, small)
-
-
-def scatter_rows_kernel(
-    depth, rows, p_ref, small_ref, o_ref, smalls_ref,
-    work, diagonal, from_x, from_y, passing, from_z,
-    load, d_send, d_recv, x_send, x_recv, y_send, y_recv, z_send, z_recv, s_send, s_recv, local,
+    )(block)
+
+
+def experts_kernel(
+    depth, rows, local, hidden,
+    x_ref, gates_ref, grad_ref, gate_ref, up_ref, down_ref,
+    sum_ref, cots_ref, normed_ref, gated_ref, gate_grad_ref, up_grad_ref, produced_ref,
+    wg, wu, wd, x_all, grads, work, y_out, gated, gate_grad, up_grad, gates, gate_wide, cots, cot_rows,
+    diagonal, from_x, from_y, from_z, r_send, r_recv,
+    z_send, z_recv, p_send, p_recv, s_send, s_recv, w_send, w_recv, w_load, g_load, saves, local_sem,
 ):
     z, x, y, core = place()
-    here, x_place, y_place, far = 2 * x + y, 2 * (1 - x) + y, 2 * x + 1 - y, 2 * (1 - x) + 1 - y
-    over_x, over_y = device(z, 1 - x, y, core), device(z, x, 1 - y, core)
-    half = rows // 2
-    upper, lower = pl.ds(0, half), pl.ds(half, half)
-    others = []
-    for step in range(depth):
-        for turn in range(4):
-            if step or turn:
-                other = (swapped(z, step), swapped(x, turn // 2), swapped(y, turn % 2), core)
-                others.append((step * 4 + turn, other))
-    greet([device(*other) for _, other in others])
-    pending = []
-
-    def start(copy):
+    here, sibling = 2 * x + y, device(z, x, y, 1 - core)
+    others = [
+        (step, turn, (swapped(z, step), swapped(x, turn // 2), swapped(y, turn % 2)))
+        for step in range(depth)
+        for turn in range(4)
+        if step or turn
+    ]
+    greet([device(*other, core) for _, _, other in others] + [sibling])
+    copies = Copies()
+    gather = Gather(copies, x_ref, x_all, rows, z_send, z_recv, p_send, p_recv)
+    gather.begin()
+    plain = []
+
+    def fetch(source, target, sem):
+        copy = pltpu.make_async_copy(source, target, sem)
         copy.start()
-        pending.append(copy)
         return copy
 
-    for number, (oz, ox, oy, oc) in others:
-        start(
-            remote(
-                small_ref.at[oz, 2 * ox + oy], smalls_ref.at[z, here], s_send.at[number], s_recv.at[number], device(oz, ox, oy, oc)
+    plain.append(fetch(x_ref, gather.at(0, here, None), local_sem.at[0]))
+    weights = []
+    for index in range(local):
+        first = pl.multiple_of((core * local + index) * hidden, hidden)
+        columns = pl.ds(first, hidden)
+        for number, (source, target) in enumerate(
+            [(gate_ref, wg.at[:, columns]), (up_ref, wu.at[:, columns]), (down_ref, wd.at[columns])]
+        ):
+            weights.append(copies.start(remote(source.at[index], target, w_send.at[number, index], w_recv.at[number, index], sibling)))
+            plain.append(fetch(source.at[index], target, w_load.at[number, index]))
+    smalls = []
+    for step, turn, other in others:
+        oz, ox, oy = other
+        smalls.append(
+            copies.start(
+                remote(
+                    gates_ref.at[2 * oz + ox], gates.at[step, here], s_send.at[0, step, turn], s_recv.at[0, step, turn],
+                    device(oz, ox, oy, core),
+                )
             )
         )
-    own_small = pltpu.make_async_copy(small_ref.at[z, here], smalls_ref.at[z, here], local.at[0])
-    own_small.start()
-    loads = []
+    plain.append(fetch(gates_ref.at[2 * z + x], gates.at[0, here], local_sem.at[1]))
+    grad_copies = [fetch(grad_ref.at[0], grads.at[0], g_load.at[0])]
+    scatter = Scatter(copies, work, diagonal, from_x, from_y, from_z, rows, r_send, r_recv)
+    saving, producing, keeping = [], [], []
+    wave_rows = 4 * rows
+    lanes = lax.broadcasted_iota(jnp.int32, (wave_rows, 128), 1)
+
+    def first_half(step):
+        for copy in saving:
+            copy.wait()
+        saving.clear()
+        for spot in range(4):
+            padded = jnp.concatenate([gates[step, spot], jnp.zeros((120, 128), FULL)], axis=0)
+            gate_wide[pl.ds(spot * rows, rows), :] = padded.T
+        cots[...] = jnp.zeros_like(cots)
+        grad_copies[step].wait()
+        if step + 1 < depth:
+            grad_copies.append(fetch(grad_ref.at[step + 1], grads.at[(step + 1) % 2], g_load.at[(step + 1) % 2]))
+        grad = grads.at[step % 2]
+
+        @pl.loop(0, 2 * local)
+        def _(unit):
+            columns = pl.ds(pl.multiple_of(unit * hidden, hidden), hidden)
+            expert = lax.rem(unit, local)
+            gate_pre = dot(x_all[step], wg[:, columns])
+            up_pre = dot(x_all[step], wu[:, columns])
+            back = dot_t(grad[...], wd[columns, :])
+            logistic = 1.0 / (1.0 + jnp.exp(-gate_pre))
+            activated = gate_pre * logistic
+            inner = activated * up_pre
+            cot = jnp.sum(inner * back, axis=-1, keepdims=True)
+            cots[...] += jnp.where(lanes == expert, cot, 0.0)
+            gate = jnp.sum(jnp.where(lanes == expert, gate_wide[...], 0.0), axis=-1, keepdims=True)
+            gated[:, columns] = (gate * inner).astype(LOW)
+            inner_grad = gate * back
+            gate_grad[:, columns] = (inner_grad * up_pre * logistic * (1.0 + gate_pre * (1.0 - logistic))).astype(LOW)
+            up_grad[:, columns] = (inner_grad * activated).astype(LOW)
+
+        for spot in range(4):
+            cot_rows[step, spot] = cots[pl.ds(spot * rows, rows), :].T[:8]
+        for number, (source, target) in enumerate([(gated, gated_ref), (gate_grad, gate_grad_ref), (up_grad, up_grad_ref)]):
+            saving.append(fetch(source, target.at[step], saves.at[number]))
+        keeping.append(fetch(x_all.at[step], normed_ref.at[step], saves.at[4 + step]))
+
+    def second_half(step):
+        for copy in producing:
+            copy.wait()
+        producing.clear()
+        tile = 512
+
+        @pl.loop(0, x_all.shape[2] // tile)
+        def _(index):
+            columns = pl.ds(pl.multiple_of(index * tile, tile), tile)
+            y_out[:, columns] = dot(gated[...], wd[:, columns]).astype(LOW)
+            work[step, :, columns] = (dot_t(gate_grad[...], wg[columns, :]) + dot_t(up_grad[...], wu[columns, :])).astype(LOW)
+
+        producing.append(fetch(y_out, produced_ref.at[step], saves.at[3]))
+
+    gather.turn(0)
+    if depth > 1:
+        gather.spread(1)
+    gather.complete(0)
+    for copy in plain:
+        copy.wait()
+    for copy in weights + smalls:
+        copies.arrived(copy)
+    for step in range(depth):
+        if step:
+            gather.complete(step)
+        first_half(step)
+        if step + 1 < depth:
+            gather.turn(step + 1)
+        if step + 2 < depth:
+            gather.spread(step + 2)
+        if step >= 1:
+            scatter.side(step - 1)
+        if step >= 2:
+            scatter.climb(step - 2)
+        second_half(step)
+        scatter.corner(step)
+    for step, turn, (oz, ox, oy) in others:
+        copies.start(
+            remote(
+                cot_rows.at[step, 2 * ox + oy], cots_ref.at[step, here], s_send.at[1, step, turn], s_recv.at[1, step, turn],
+                device(oz, ox, oy, core),
+            )
+        )
+    own_cots = fetch(cot_rows.at[0, here], cots_ref.at[0, here], local_sem.at[2])
+    if depth > 1:
+        scatter.climb(depth - 2)
+    scatter.side(depth - 1)
+    scatter.climb(depth - 1)
+    scatter.result(sum_ref)
+    own_cots.wait()
+    for copy in saving + producing + keeping:
+        copy.wait()
+    copies.finish()
+
+
+def run_experts(block, gates, grads, w_gate, w_up, w_down, number):
+    depth, wave, width = grads.shape
+    rows = wave // 4
+    local, _, hidden = w_gate.shape
+    units = 2 * local * hidden
+    kept = jax.ShapeDtypeStruct((depth, wave, units), LOW)
+    wide = jax.ShapeDtypeStruct((depth, wave, width), LOW)
+    return pl.pallas_call(
+        functools.partial(experts_kernel, depth, rows, local, hidden),
+        out_shape=(
+            jax.ShapeDtypeStruct((rows, width), FULL),
+            jax.ShapeDtypeStruct((depth, 4, 8, 128), FULL),
+            wide, kept, kept, kept, wide,
+        ),
+        in_specs=[ANY] * 6,
+        out_specs=(VMEM, VMEM, ANY, ANY, ANY, ANY, ANY),
+        scratch_shapes=[
+            pltpu.VMEM((width, units), LOW), pltpu.VMEM((width, units), LOW), pltpu.VMEM((units, width), LOW),
+            pltpu.VMEM((depth, wave, width), LOW), pltpu.VMEM((2, wave, width), LOW),
+            pltpu.VMEM((depth, wave, width), LOW), pltpu.VMEM((wave, width), LOW),
+            pltpu.VMEM((wave, units), LOW), pltpu.VMEM((wave, units), LOW), pltpu.VMEM((wave, units), LOW),
+            pltpu.VMEM((depth, 4, 8, 128), FULL), pltpu.VMEM((wave, 128), FULL), pltpu.VMEM((wave, 128), FULL),
+            pltpu.VMEM((depth, 4, 8, 128), FULL),
+        ]
+        + Scatter.scratch(depth, rows, width)
+        + [
+            dma(depth), dma(depth), dma(depth, 6), dma(depth, 6), dma(2, depth, 4), dma(2, depth, 4),
+            dma(3, local), dma(3, local), dma(3, local), dma(2), dma(4 + depth), dma(3),
+        ],
+        compiler_params=comm_params(number),
+    )(block, gates, grads, w_gate, w_up, w_down)
+
+
+def scatter_rows_kernel(depth, rows, p_ref, o_ref, work, diagonal, from_x, from_y, from_z, send, recv, load):
+    greet_column_and_plane(depth)
+    copies = Copies()
     order = [step for step in range(1, depth)] + [0]
+    loads = {}
     for step in order:
-        at = swapped(z, step)
-        copy = pltpu.make_async_copy(p_ref.at[at], work.at[step], load.at[step])
-        copy.start()
-        loads.append(copy)
-    diagonals, sides = {}, {}
-    for step, copy in zip(order, loads):
-        copy.wait()
-        diagonals[step] = (
-            start(remote(work.at[step, far, upper], diagonal.at[step, 0], d_send.at[step, 0], d_recv.at[step, 0], over_y)),
-            start(remote(work.at[step, far, lower], diagonal.at[step, 1], d_send.at[step, 1], d_recv.at[step, 1], over_x)),
-        )
+        loads[step] = pltpu.make_async_copy(p_ref.at[step], work.at[step], load.at[step])
+        loads[step].start()
+    scatter = Scatter(copies, work, diagonal, from_x, from_y, from_z, rows, send, recv)
     for step in order:
-        via_y, via_x = diagonals[step]
-        via_y.wait_recv()
-        add_rows(work.at[step, x_place, upper], [work.at[step, x_place, upper], diagonal.at[step, 0]], half)
-        to_x = start(remote(work.at[step, x_place], from_x.at[step], x_send.at[step], x_recv.at[step], over_x))
-        via_x.wait_recv()
-        add_rows(work.at[step, y_place, lower], [work.at[step, y_place, lower], diagonal.at[step, 1]], half)
-        to_y = start(remote(work.at[step, y_place], from_y.at[step], y_send.at[step], y_recv.at[step], over_y))
-        sides[step] = (to_x, to_y)
-    along_z = []
+        loads[step].wait()
+        scatter.corner(step)
     for step in order:
-        for side in sides[step]:
-            side.wait_recv()
-        terms = [work.at[step, here], from_x.at[step], from_y.at[step]]
-        if step:
-            add_rows(passing.at[step], terms, rows)
-            along_z.append(
-                start(
-                    remote(
-                        passing.at[step], from_z.at[step], z_send.at[step], z_recv.at[step], device(swapped(z, step), x, y, core)
-                    )
-                )
-            )
-    for copy in along_z:
-        copy.wait_recv()
-    add_rows(o_ref, [work.at[0, here], from_x.at[0], from_y.at[0]] + [from_z.at[step] for step in range(1, depth)], rows)
-    own_small.wait()
-    received = set(id(c) for c in along_z) | set(id(c) for v in list(diagonals.values()) + list(sides.values()) for c in v)
-    for copy in pending:
-        copy.wait_send()
-        if id(copy) not in received:
-            copy.wait_recv()
-
-
-def scatter_rows(parts, small, number):
-    depth, _, rows, width = parts.shape
+        scatter.side(step)
+    for step in order:
+        scatter.climb(step)
+    scatter.result(o_ref)
+    copies.finish()
+
+
+def scatter_rows(parts, number):
+    depth, wave, width = parts.shape
+    rows = wave // 4
     return pl.pallas_call(
         functools.partial(scatter_rows_kernel, depth, rows),
-        out_shape=(jax.ShapeDtypeStruct((rows, width), FULL), jax.ShapeDtypeStruct(small.shape, small.dtype)),
-        in_specs=[ANY, ANY],
-        out_specs=(VMEM, ANY),
-        scratch_shapes=[
-            pltpu.VMEM(parts.shape, parts.dtype),
-            pltpu.VMEM((depth, 2, rows // 2, width), parts.dtype),
-            pltpu.VMEM((depth, rows, width), parts.dtype),
-            pltpu.VMEM((depth, rows, width), parts.dtype),
-            pltpu.VMEM((depth, rows, width), parts.dtype),
-            pltpu.VMEM((depth, rows, width), parts.dtype),
-            dma(depth), dma(depth, 2), dma(depth, 2), dma(depth), dma(depth), dma(depth), dma(depth), dma(depth), dma(depth),
-            dma(4 * depth), dma(4 * depth), dma(1),
-        ],
+        out_shape=jax.ShapeDtypeStruct((rows, width), FULL),
+        in_specs=[ANY],
+        out_specs=VMEM,
+        scratch_shapes=[pltpu.VMEM(parts.shape, parts.dtype)] + Scatter.scratch(depth, rows, width) + [dma(depth)],
         compiler_params=comm_params(number),
-    )(parts, small)
-
-
-def pair_weights_kernel(count, *refs):
-    ins, outs, (send, recv, local) = refs[:count], refs[count : 2 * count], refs[2 * count :]
-    z, x, y, core = place()
-    sibling = device(z, x, y, 1 - core)
-    greet([sibling])
-    waits = []
-    for index in range(count):
-        copy = remote(ins[index], outs[index].at[core], send.at[index], recv.at[index], sibling)
-        copy.start()
-        mine = pltpu.make_async_copy(ins[index], outs[index].at[core], local.at[index])
-        mine.start()
-        waits += [copy, mine]
-    for copy in waits:
-        copy.wait()
-
-
-def pair_weights(arrays, number):
-    count = len(arrays)
-    return pl.pallas_call(
-        functools.partial(pair_weights_kernel, count),
-        out_shape=tuple(jax.ShapeDtypeStruct((2,) + a.shape, a.dtype) for a in arrays),
-        in_specs=[ANY] * count,
-        out_specs=(ANY,) * count,
-        scratch_shapes=[dma(count), dma(count), dma(count)],
-        compiler_params=comm_params(number),
-    )(*arrays)
+    )(parts)
 
 
 def pair_swap_kernel(count, *refs):
@@ -741,8 +920,8 @@
     gathered = pl.pallas_call(
         tensor_gather_kernel,
         out_shape=jax.ShapeDtypeStruct((2, 2, rows, width), block.dtype),
-        in_specs=[ANY],
-        out_specs=ANY,
+        in_specs=[VMEM],
+        out_specs=VMEM,
         scratch_shapes=[dma(3), dma(3), dma(1)],
         compiler_params=comm_params(number),
     )(block)
@@ -897,12 +1076,6 @@
     def quarter(array):
         return lax.dynamic_slice_in_dim(array, part * rows, rows, 0)
 
-    gate_pair, up_pair, down_pair = pair_weights([w_gate, w_up, w_down], 1)
-    units = 2 * local_experts * hidden
-    gate_all = gate_pair.reshape(2 * local_experts, width, hidden).transpose(1, 0, 2).reshape(width, units)
-    up_all = up_pair.reshape(2 * local_experts, width, hidden).transpose(1, 0, 2).reshape(width, units)
-    down_all = down_pair.reshape(units, width)
-
     first_row = group * row_count
     positions = first_row + jnp.arange(row_count, dtype=jnp.int32)
     cosine, sine = rope_tables(positions % LENGTH)
@@ -963,32 +1136,16 @@
         quarter(routes)[:, :, None] == jnp.arange(experts, dtype=jnp.int32)[None, None, :], axis=1
     ).astype(FULL)
 
-    no_small = jnp.zeros((8, 128), FULL)
-    all_grad, _ = gather_rows(own_grad, no_small, depth, 4)
-    all_normed, all_gates = gather_rows(normed_two, (router_probs * picked).T, depth, 5)
-    all_normed = all_normed.reshape(seen, width)
-    all_grad = all_grad.reshape(seen, width)
-    own_gates = lax.dynamic_slice_in_dim(all_gates, group * local_experts, local_experts, 2)
-    own_gates = own_gates.transpose(0, 1, 3, 2).reshape(seen, 1, local_experts, 1)
-    split = (seen, 2, local_experts, hidden)
-    gate_pre = dot(all_normed, gate_all)
-    up_pre = dot(all_normed, up_all)
-    logistic = jax.nn.sigmoid(gate_pre)
-    activated = gate_pre * logistic
-    inner_act = activated * up_pre
-    inner_back = dot_t(all_grad, down_all)
-    gate_cot = jnp.sum((inner_act * inner_back).reshape(split), axis=(1, 3))
-    gate_wide = jnp.broadcast_to(own_gates, split).reshape(seen, units)
-    gated = (gate_wide * inner_act).astype(LOW)
-    inner_grad = gate_wide * inner_back
-    gate_pre_grad = (inner_grad * up_pre * logistic * (1.0 + gate_pre * (1.0 - logistic))).astype(LOW)
-    up_pre_grad = (inner_grad * activated).astype(LOW)
-    produced = dot(gated, down_all).astype(LOW).reshape(depth, 4, rows, width)
-    row_grad = (dot_t(gate_pre_grad, gate_all) + dot_t(up_pre_grad, up_all)).astype(LOW).reshape(depth, 4, rows, width)
-    gate_cot = gate_cot.reshape(depth, 4, rows, local_experts).transpose(0, 1, 3, 2)
-    gate_cot = jnp.concatenate([gate_cot, jnp.zeros((depth, 4, 8 - local_experts, rows), FULL)], axis=2)
-    normed_two_grad, gate_cots = scatter_rows(row_grad, gate_cot, 6)
-    expert_mix, _ = scatter_rows(produced, jnp.zeros((depth, 4, 8, 128), FULL), 7)
+    all_grad = gather_rows(own_grad, depth, 4)
+    gates = (router_probs * picked).T.reshape(groups, local_experts, rows)
+    gates = jnp.concatenate([gates, jnp.zeros((groups, 8 - local_experts, rows), FULL)], axis=1)
+    normed_two_grad, gate_cots, all_normed, gated, gate_pre_grad, up_pre_grad, produced = run_experts(
+        normed_two, gates, all_grad, w_gate, w_up, w_down, 5
+    )
+    units = 2 * local_experts * hidden
+    all_normed, all_grad = all_normed.reshape(seen, width), all_grad.reshape(seen, width)
+    gated, gate_pre_grad, up_pre_grad = (a.reshape(seen, units) for a in (gated, gate_pre_grad, up_pre_grad))
+    expert_mix = scatter_rows(produced, 7)
 
     def expert_grads(left, right):
         return t_dot(left, right)
@@ -1005,7 +1162,8 @@
     output = tensor_gather((state + expert_mix).astype(LOW), 9)
 
     prob_cot = gate_cots[:, :, :local_experts].reshape(depth, 2, 2, local_experts, rows).sum(axis=2)
-    prob_cot = prob_cot.reshape(experts, rows).T * picked
+    plane = jnp.arange(depth, dtype=jnp.int32) ^ (group // 2)
+    prob_cot = prob_cot[plane].reshape(experts, rows).T * picked
     logit_cot = router_probs * (prob_cot - jnp.sum(router_probs * prob_cot, axis=-1, keepdims=True))
     normed_two_grad = normed_two_grad + jnp.einsum(
         "te,de->td", logit_cot, router_w.astype(FULL), precision=HIGHEST_PRECISION

time: 1350 us -> 1070 us (0.79)
  Pallas kernels: 913 us -> 718 us
  matrix products: 199 us -> 113 us
    pallas_call x2 -> x1, Pallas kernels: 181 us -> 71.7 us  [gather_rows(): pl.pallas_call(functools.partial(gather_rows_kernel, depth, rows), out_sh...]
    pallas_call x2 -> x1, Pallas kernels: 194 us -> 95 us  [scatter_rows(): pl.pallas_call(functools.partial(scatter_rows_kernel, depth, rows), out_s...]
    dot_general x7 -> x4, matrix products: 59.1 us -> 8.86 us  [dot_t(): lax.dot_general(left, right, (((1,), (1,)), ((), ())), preferred_element_...]
    dot_general x8 -> x5, matrix products: 53 us -> 12.7 us  [dot(): return jnp.dot(left, right, preferred_element_type=FULL)]
    dot_general x1 -> x4, local copies, waits for them, and re-layouts: 3.98 us -> 22.2 us  [t_dot(): lax.dot_general(left, right, (((0,), (0,)), ((), ())), preferred_element_...]
    pallas_call x1, Pallas kernels: 192 us -> 206 us  [run_experts(): pl.pallas_call(functools.partial(experts_kernel, depth, rows, local, hidd...]
  transfers between devices with their start and end apart: 2 -> 2, of which waited for: 0 -> 0; matrix products, arithmetic and copies ran while one was open for 7% -> 11% of each run, Pallas kernels for 18% -> 22%
where the time goes in v2:
time: 1070 us; the launch traced here: 1060 us
  Pallas kernels  718 us (67%)
  matrix products  113 us (11%)
  other arithmetic  95.9 us (9%)
  local copies, waits for them, and re-layouts  95.1 us (9%)
  blocking collectives  24.5 us (2%)
  between operations  15.5 us (1%)
    pallas_call x1, Pallas kernels, run_experts(): pl.pallas_call(functools.partial(experts_kernel, depth, rows, local, hidd...  206 us
    pallas_call x1, Pallas kernels, expert_scatter(): pl.pallas_call(functools.partial(expert_scatter_kernel, depth, rows), out...  166 us
    pallas_call x1, Pallas kernels, scatter_rows(): pl.pallas_call(functools.partial(scatter_rows_kernel, depth, rows), out_s...  95 us
    pallas_call x1, Pallas kernels, gather_rows(): pl.pallas_call(functools.partial(gather_rows_kernel, depth, rows), out_sh...  71.7 us
    pallas_call x2, Pallas kernels, halo(): pl.pallas_call(functools.partial(halo_kernel, chain, forward, count), out...  70.9 us
    dot_general x7, matrix products, t_dot(): lax.dot_general(left, right, (((0,), (0,)), ((), ())), preferred_element_...  54.5 us
    pallas_call x3, Pallas kernels, tensor_gather(): pl.pallas_call(tensor_gather_kernel, out_shape=jax.ShapeDtypeStruct((2, 2...  53.5 us
    pallas_call x2, Pallas kernels, tensor_scatter(): pl.pallas_call(functools.partial(tensor_scatter_kernel, rows), out_shape=...  35.5 us
  transfers between devices with their start and end apart: 2, of which 0 were waited for; matrix products, arithmetic and copies ran while one was open for 11% of the time, Pallas kernels for 22%

profile of v2, /device:TPU:10, one launch (start us, length us, event | category | flops | bytes accessed | tf_op | source)
XLA Modules:
  0.0 1062.2 jit_solution(4278723114097708593)
XLA Ops:
  28.0 6.9 psum.21
  55.1 46.6 %shard_map.263 = (bf16[2,512,1024]{2,1,0:T(8,128)(2,1)}, s32[2,4,128]{2,1,0:T(4,128)}) custom-call(bf16[512,1024]{1,0:T(8,128)(2,1)} %pad_maximum_fusion.1.refs_0_, s32[4,128]{1,0:T(4,128)} %bitcast.217), custom_call_target="tpu_custom_call" | custom-call | tf_op jit(solution)/shard_map/pallas_call | solution.py:1032
  103.9 8.0 maximum_maximum_fusion
  116.6 71.7 %shard_map.265.grad_ref = bf16[4,512,2048]{2,1,0:T(8,128)(2,1)} custom-call(bf16[128,2048]{1,0:T(8,128)(2,1)} %constant_dynamic-slice_fusion.x_ref), custom_call_target="tpu_custom_call" | custom-call | tf_op jit(solution)/shard_map/pallas_call | solution.py:607
  193.9 4.9 fusion
  206.0 17.7 %shard_map.264 = f32[128,2048]{1,0:T(8,128)} custom-call(bf16[2,2,128,2048]{3,2,1,0:T(8,128)(2,1)} %bitcast.190), custom_call_target="tpu_custom_call" | custom-call | tf_op jit(solution)/shard_map/pallas_call | solution.py:883
  227.5 206.0 %shard_map.266 = (f32[128,2048]{1,0:T(8,128)}, f32[4,4,8,128]{3,2,1,0:T(8,128)}, bf16[4,512,2048]{2,1,0:T(8,128)(2,1)}, bf16[4,512,1024]{2,1,0:T(8,128)(2,1)}, b...) custom-call(bf16[128,2048]{1,0:T(8,128)(2,1)} %copy-done.16, ...), custom_call_target="tpu_custom_call" | custom-call | tf_op jit(solution)/shard_map/pallas_call | solution.py:771
  433.5 95.0 %shard_map.267 = f32[128,2048]{1,0:T(8,128)} custom-call(bf16[4,512,2048]{2,1,0:T(8,128)(2,1)} %get-tuple-element.28.p_ref), custom_call_target="tpu_custom_call" | custom-call | tf_op jit(solution)/shard_map/pallas_call | solution.py:820
  536.9 17.6 %shard_map.269 = bf16[2,2,128,2048]{3,2,1,0:T(8,128)(2,1)} custom-call(bf16[128,2048]{1,0:T(8,128)(2,1)} %get-tuple-element.91.x_ref), custom_call_target="tpu_custom_call" | custom-call | tf_op jit(solution)/shard_map/pallas_call | solution.py:920
  558.3 9.4 fusion.9
  567.7 8.5 multiply_reduce_fusion
  576.2 4.8 copy.122
  581.1 5.0 reshape.426
  586.1 9.8 multiply_convert_fusion
  607.0 5.0 reshape.425
  627.4 24.2 %shard_map.270 = bf16[2,512,1024]{2,1,0:T(8,128)(2,1)} custom-call(bf16[2,512,1024]{2,1,0:T(8,128)(2,1)} %slice.185.refs_0_), custom_call_target="tpu_custom_call" | custom-call | tf_op jit(solution)/shard_map/pallas_call | solution.py:1032
  671.4 5.9 psum.22
  686.5 17.8 %shard_map.271 = f32[128,2048]{1,0:T(8,128)} custom-call(bf16[2,2,128,2048]{3,2,1,0:T(8,128)(2,1)} %bitcast.177), custom_call_target="tpu_custom_call" | custom-call | tf_op jit(solution)/shard_map/pallas_call | solution.py:883
  719.7 6.4 copy.131
  726.1 6.4 copy.133
  732.6 14.8 %fusion.72 = f32[2048,2,2,256]{3,0,2,1:T(8,128)} fusion(bf16[2048,2048,1,1]{1,0,3,2:T(8,128)(2,1)} %bitcast.232, bf16[2,2,256,2048]{3,2,1,0:T(8,128)(2,1)} %bitcast.185), kind=kOutput, calls=%fused_computation.172 | convolution fusion | flops 8589934592 | bytes 20971520 | tf_op jit(solution)/shard_map/dot_general | solution.py:1051
  747.4 13.6 %fusion.73 = f32[2048,2,2,256]{3,0,2,1:T(8,128)} fusion(bf16[2048,2048,1,1]{1,0,3,2:T(8,128)(2,1)} %bitcast.233, bf16[2,2,256,2048]{3,2,1,0:T(8,128)(2,1)S(1)} %bitcast.184), kind=kOutput, calls=%fused_computation.173 | convolution fusion | flops 8589934592 | bytes 20971520 | tf_op jit(solution)/shard_map/dot_general | solution.py:1051
  761.0 6.5 copy.135
  769.7 7.1 pad_maximum_fusion.p_ref
  776.8 165.6 %shard_map.273 = f32[256,2048]{1,0:T(8,128)} custom-call(bf16[4,2,256,2048]{3,2,1,0:T(8,128)(2,1)} %pad_maximum_fusion.p_ref), custom_call_target="tpu_custom_call" | custom-call | tf_op jit(solution)/shard_map/pallas_call | solution.py:961
  944.7 17.6 %shard_map.272 = bf16[2,2,128,2048]{3,2,1,0:T(8,128)(2,1)} custom-call(bf16[128,2048]{1,0:T(8,128)(2,1)} %fusion.25.x_ref), custom_call_target="tpu_custom_call" | custom-call | tf_op jit(solution)/shard_map/pallas_call | solution.py:920
  966.4 14.8 %fusion.74.refs_2_ = f32[2,2,256,2048]{3,2,1,0:T(8,128)} fusion(bf16[2,2,256,2048]{3,2,1,0:T(8,128)(2,1)} %bitcast.183, bf16[2048,2048,1,1]{1,0,3,2:T(8,128)(2,1)} %bitcast.165), kind=kOutput, calls=%fused_computation.174 | convolution fusion | flops 8589934592 | bytes 20971520 | tf_op jit(solution)/shard_map/dot_general | solution.py:1051
  981.3 19.6 %shard_map.274 = (f32[2,2048,256]{2,1,0:T(8,128)}, f32[2,2048,256]{2,1,0:T(8,128)}, f32[2,256,2048]{2,1,0:T(8,128)}) custom-call(f32[2,2,2048,256]{3,2,1,0:T(8,128)} %bitcast.171, f32[2,2,2048,256]{3,2,1,0:T(8,128)} %bitcast.168, f32[2,2,256,2048]{3,2,1,0:T(8,128)} %fusion.74.refs_2_), custom_call_target="tpu_custom_call" | custom-call | tf_op jit(solution)/shard_map/pallas_call | solution.py:846
  1000.9 6.7 bitcast_add_fusion.2
  1007.6 5.2 bitcast_add_fusion.1
  1017.4 18.3 %shard_map.268 = bf16[2,2,128,2048]{3,2,1,0:T(8,128)(2,1)} custom-call(bf16[128,2048]{1,0:T(8,128)(2,1)} %get-tuple-element.107.x_ref), custom_call_target="tpu_custom_call" | custom-call | tf_op jit(solution)/shard_map/pallas_call | solution.py:920
  1038.8 11.7 %psum.23 = f32[18,256]{1,0:T(8,128)S(1)} all-reduce(f32[18,256]{1,0:T(8,128)} %reduce-scatter.5.cloned.1.call-done), channel_id=1, replica_groups=mesh['expert'=8,'tensor'=4] {'tensor'}, use_global_device_ids=true, to_apply=%region_21.22 | all-reduce | flops 4608 | bytes 36864 | tf_op jit(solution)/shard_map/psum | solution.py:1237
  (242 shorter events, 167.1 us)
Async XLA Ops:
  7.2 16.9 %copy-start = (bf16[2048,512]{1,0:T(8,128)(2,1)S(1)}, bf16[2048,512]{1,0:T(8,128)(2,1)}, u32[]{:S(2)}) copy-start(bf16[2048,512]{1,0:T(8,128)(2,1)} %param.23) | copy-start | bytes 6291460
  7.2 9.6 copy-start.43
  7.2 1029.5 %reduce-scatter.7.cloned.1.call-start = ((), (), s32[]{:S(2)}) async-start(), calls=%async_computation.3 | async-start | bytes 73728
  9.5 14.5 %copy-start.53 = (f32[512]{0:T(512)}, f32[512]{0:T(512)S(1)}, u32[]{:S(2)}) copy-start(f32[512]{0:T(512)S(1)} %add_rsqrt_fusion) | copy-start | bytes 6148
  24.0 12.5 %copy-start.42 = (f32[4,128]{1,0:T(4,128)S(1)}, f32[4,128]{1,0:T(4,128)}, u32[]{:S(2)}) copy-start(f32[4,128]{1,0:T(4,128)} %param.21) | copy-start | bytes 6148
  28.0 12.2 %copy-start.45 = (f32[4,128]{1,0:T(4,128)S(1)}, f32[4,128]{1,0:T(4,128)}, u32[]{:S(2)}) copy-start(f32[4,128]{1,0:T(4,128)} %param.20) | copy-start | bytes 6148
  116.6 71.8 %copy-start.44 = (s32[512]{0:T(512)S(1)}, s32[512]{0:T(512)}, u32[]{:S(2)}) copy-start(s32[512]{0:T(512)} %param.17) | copy-start | bytes 6148
  116.6 72.8 %copy-start.17 = (bf16[512,4,128]{0,2,1:T(8,128)(2,1)S(1)}, bf16[512,4,128]{0,2,1:T(8,128)(2,1)}, u32[]{:S(2)}) copy-start(bf16[512,4,128]{0,2,1:T(8,128)(2,1)} %get-tuple-element.113) | copy-start | bytes 1572868
  189.3 9.5 copy-start.3
  206.0 20.4 %copy-start.41 = (f32[2048]{0:T(1024)S(1)}, f32[2048]{0:T(1024)}, u32[]{:S(2)}) copy-start(f32[2048]{0:T(1024)} %param.26) | copy-start | bytes 24580
  206.0 20.5 %copy-start.40 = (bf16[2048,16]{0,1:T(8,128)(2,1)S(1)}, bf16[2048,16]{0,1:T(8,128)(2,1)}, u32[]{:S(2)}) copy-start(bf16[2048,16]{0,1:T(8,128)(2,1)} %param.27) | copy-start | bytes 196612
  226.8 206.7 %copy-start.47 = (f32[128]{0:T(128)}, f32[128]{0:T(128)S(1)}, u32[]{:S(2)}) copy-start(f32[128]{0:T(128)S(1)} %get-tuple-element.136) | copy-start | bytes 1540
  226.9 206.7 %copy-start.49 = (f32[128]{0:T(128)}, f32[128]{0:T(128)S(1)}, u32[]{:S(2)}) copy-start(f32[128]{0:T(128)S(1)} %fusion.35) | copy-start | bytes 1540
  554.5 13.1 %slice-start = ((s8[12582912]{0:T(1024)(128)(4,1)}), s8[4194304]{0:T(1024)(128)(4,1)S(1)}, s32[]{:S(2)}) async-start(s8[12582912]{0:T(1024)(128)(4,1)} %bitcast.163), calls=%async_computation.4 | async-start | bytes 8388608
  558.2 9.5 slice-start.1
  558.2 9.4 slice-start.2
  558.2 9.4 copy-start.38
  586.1 9.9 copy-start.18
  612.0 6.4 copy-start.46
  663.3 6.5 copy-start.54
  663.4 6.6 copy-start.48
  663.4 6.6 copy-start.50
  669.8 369.0 %reduce-scatter.5.cloned.1.call-start = ((), (), s32[]{:S(2)}) async-start(), calls=%async_computation.2 | async-start | bytes 221184 | tf_op jit(solution)/shard_map/reduce_scatter | solution.py:1237
  686.5 20.3 %copy-start.28 = (bf16[512,512]{1,0:T(8,128)(2,1)S(1)}, bf16[512,512]{1,0:T(8,128)(2,1)}, u32[]{:S(2)}) copy-start(bf16[512,512]{1,0:T(8,128)(2,1)} %copy-done.27) | copy-start | bytes 1572868
  732.6 14.8 %copy-start.23 = (bf16[1024,2048]{1,0:T(8,128)(2,1)S(1)}, bf16[1024,2048]{1,0:T(8,128)(2,1)}, u32[]{:S(2)}) copy-start(bf16[1024,2048]{1,0:T(8,128)(2,1)} %copy.133) | copy-start | bytes 12582916
  761.0 6.5 copy-start.57
  776.8 165.6 %copy-start.12 = (f32[128,2048]{1,0:T(8,128)S(1)}, f32[128,2048]{1,0:T(8,128)}, u32[]{:S(2)}) copy-start(f32[128,2048]{1,0:T(8,128)} %shard_map.271) | copy-start | bytes 3145732
  776.8 165.6 %copy-start.24 = (f32[128,2048]{1,0:T(8,128)S(1)}, f32[128,2048]{1,0:T(8,128)}, u32[]{:S(2)}) copy-start(f32[128,2048]{1,0:T(8,128)} %get-tuple-element.92) | copy-start | bytes 3145732
  1000.9 6.7 copy-start.22
  1000.9 11.9 %slice-start.3 = ((s8[8388608]{0:T(1024)(128)(4,1)}), s8[4194304]{0:T(1024)(128)(4,1)S(1)}, s32[]{:S(2)}) async-start(s8[8388608]{0:T(1024)(128)(4,1)} %bitcast.169), calls=%async_computation.7 | async-start | bytes 8388608
  1007.6 6.1 copy-start.21
  1016.2 38.6 %copy-start.1 = (bf16[2048,512]{1,0:T(8,128)(2,1)S(1)}, bf16[2048,512]{1,0:T(8,128)(2,1)}, u32[]{:S(2)}) copy-start(bf16[2048,512]{1,0:T(8,128)(2,1)} %param.23) | copy-start | bytes 6291460
  (33 other events, 87.0 us)
Sparse Core Ops, SparseCore 0:
  669.9 84.1 reduce-scatter.6
  757.4 60.1 reduce-scatter.4

commit v3 on v2

--- a/solution.py
+++ b/solution.py
@@ -576,42 +576,6 @@
             dma(depth, 5),
             dma(depth, 5),
         ]
-
-
-def greet_column_and_plane(depth):
-    z, x, y, core = place()
-    greet(
-        [device(swapped(z, step), x, y, core) for step in range(1, depth)]
-        + [device(z, 1 - x, y, core), device(z, x, 1 - y, core)]
-    )
-
-
-def gather_rows_kernel(depth, rows, x_ref, o_ref, z_send, z_recv, p_send, p_recv, local):
-    z, x, y, core = place()
-    greet_column_and_plane(depth)
-    copies = Copies()
-    gather = Gather(copies, x_ref, o_ref, rows, z_send, z_recv, p_send, p_recv)
-    gather.begin()
-    own = pltpu.make_async_copy(x_ref, gather.at(0, gather.here, None), local.at[0])
-    own.start()
-    for step in range(depth):
-        if step:
-            gather.spread(step)
-        gather.turn(step)
-    own.wait()
-    copies.finish()
-
-
-def gather_rows(block, depth, number):
-    rows, width = block.shape
-    return pl.pallas_call(
-        functools.partial(gather_rows_kernel, depth, rows),
-        out_shape=jax.ShapeDtypeStruct((depth, 4 * rows, width), block.dtype),
-        in_specs=[ANY],
-        out_specs=ANY,
-        scratch_shapes=[dma(depth), dma(depth), dma(depth, 6), dma(depth, 6), dma(1)],
-        compiler_params=comm_params(number),
-    )(block)
 
 
 def experts_kernel(
@@ -794,37 +758,326 @@
     )(block, gates, grads, w_gate, w_up, w_down)
 
 
-def scatter_rows_kernel(depth, rows, p_ref, o_ref, work, diagonal, from_x, from_y, from_z, send, recv, load):
-    greet_column_and_plane(depth)
+class TensorScatter:
+    def __init__(self, copies, work, from_pair, from_y, send, recv):
+        self.copies, self.work, self.from_pair, self.from_y, self.send, self.recv = copies, work, from_pair, from_y, send, recv
+        z, x, self.y, self.core = place()
+        self.sibling, self.over_y = device(z, x, self.y, 1 - self.core), device(z, x, 1 - self.y, self.core)
+        self.rows = work.shape[2]
+
+    def begin(self):
+        self.pairs = []
+        for turn in (1, 0):
+            source = self.work.at[swapped(self.y, turn), 1 - self.core]
+            self.pairs.append(
+                self.copies.start(remote(source, self.from_pair.at[turn], self.send.at[turn], self.recv.at[turn], self.sibling))
+            )
+
+    def cross(self):
+        self.copies.arrived(self.pairs[0])
+        block = self.work.at[1 - self.y, self.core]
+        add_rows(block, [block, self.from_pair.at[1]], self.rows)
+        self.across = self.copies.start(remote(block, self.from_y, self.send.at[2], self.recv.at[2], self.over_y))
+
+    def result(self, target):
+        self.copies.arrived(self.pairs[1])
+        self.copies.arrived(self.across)
+        add_rows(target, [self.work.at[self.y, self.core], self.from_pair.at[0], self.from_y], self.rows)
+
+    @staticmethod
+    def scratch(rows, width):
+        return [
+            pltpu.VMEM((2, 2, rows, width), LOW),
+            pltpu.VMEM((2, rows, width), LOW),
+            pltpu.VMEM((rows, width), LOW),
+            dma(3),
+            dma(3),
+        ]
+
+
+class TensorGather:
+    def __init__(self, copies, block, target, send, recv):
+        self.copies, self.target, self.send, self.recv = copies, target, send, recv
+        z, x, self.y, self.core = place()
+        self.sibling, over_y = device(z, x, self.y, 1 - self.core), device(z, x, 1 - self.y, self.core)
+        mine = target.at[self.y, self.core]
+        self.across = copies.start(remote(block, mine, send.at[0], recv.at[0], over_y))
+        self.near = copies.start(remote(block, mine, send.at[1], recv.at[1], self.sibling))
+        self.own = pltpu.make_async_copy(block, mine, send.at[3])
+        self.own.start()
+
+    def cross(self):
+        self.copies.arrived(self.across)
+        block = self.target.at[1 - self.y, self.core]
+        self.passed = self.copies.start(remote(block, block, self.send.at[2], self.recv.at[2], self.sibling))
+
+    def finish(self):
+        self.own.wait()
+        self.copies.arrived(self.near)
+        self.copies.arrived(self.passed)
+
+
+def partners_of(depth):
+    z, x, y, core = place()
+    return [device(swapped(z, step), x, y, core) for step in range(1, depth)] + [
+        device(z, 1 - x, y, core),
+        device(z, x, 1 - y, core),
+        device(z, x, y, 1 - core),
+        device(swapped(z, 1), 1 - x, y, core),
+    ]
+
+
+def mask_bias(bias, key_docs, query_docs, length):
+    blocks = bias.shape[0] // length
+
+    @pl.loop(0, bias.shape[0] // 128)
+    def _(index):
+        part = pl.ds(pl.multiple_of(index * 128, 128), 128)
+        key = index * 128 + lax.broadcasted_iota(jnp.int32, (128, length), 0) - (blocks - 1) * length
+        query = lax.broadcasted_iota(jnp.int32, (128, length), 1)
+        seen = (key_docs[part, :] == query_docs[0:1, :]) & (key <= query) & (query - key < WINDOW)
+        bias[part, :] = jnp.where(seen, 0.0, -1e30)
+
+
+def attention_kernel(
+    depth, rows, heads, chain,
+    query_ref, kv_ref, key_docs, query_docs, w_out, grad_ref,
+    kv_all, attended, logs, sum_ref, all_grad,
+    scores, bias, partial, from_pair, from_y, t_send, t_recv,
+    z_send, z_recv, p_send, p_recv, h_send, h_recv, local,
+):
+    z, x, y, core = place()
+    group, part = lax.axis_index("expert"), lax.axis_index("tensor")
+    spot = group % chain
+    greet(partners_of(depth))
     copies = Copies()
+    length = kv_ref.shape[0]
+    scale = HD ** (-0.5)
+
+    def halo_copy(distance, to):
+        return remote(kv_ref, kv_all.at[2 - distance], h_send.at[distance], h_recv.at[distance], (to, part))
+
+    for distance in (1, 2):
+
+        @pl.when(spot < chain - distance)
+        def _():
+            halo_copy(distance, group + distance).start()
+
+    gather = Gather(copies, grad_ref, all_grad, rows, z_send, z_recv, p_send, p_recv)
+    gather.begin()
+    own = pltpu.make_async_copy(grad_ref, gather.at(0, gather.here, None), local.at[0])
+    own.start()
+    kv_all[2] = kv_ref[...]
+    mask_bias(bias, key_docs, query_docs, length)
+
+    def score(block):
+        @pl.loop(0, heads)
+        def _(head):
+            columns = pl.ds(pl.multiple_of(head * HD, HD), HD)
+            keys = pl.ds(block * length, length)
+            scores[head, keys, :] = dot_t(kv_all[block, :, columns], query_ref[:, columns]) * scale + bias[keys, :]
+
+    score(2)
+    gather.turn(0)
+    for distance in (1, 2):
+
+        @pl.when(spot >= distance)
+        def _():
+            halo_copy(distance, group - distance).wait_recv()
+
+        @pl.when(spot < distance)
+        def _():
+            kv_all[2 - distance] = jnp.zeros_like(kv_ref)
+
+        score(2 - distance)
+    if depth > 1:
+        gather.spread(1)
+
+    @pl.loop(0, heads)
+    def _(head):
+        columns = pl.ds(pl.multiple_of(head * HD, HD), HD)
+        mine = scores.at[head]
+        highest = jnp.max(mine[...], axis=0, keepdims=True)
+        total = jnp.zeros_like(highest)
+        mixed = jnp.zeros((HD, length), FULL)
+        for block in range(3):
+            weights = jnp.exp(mine[pl.ds(block * length, length), :] - highest)
+            total = total + jnp.sum(weights, axis=0, keepdims=True)
+            mine[pl.ds(block * length, length), :] = weights
+        for block in range(3):
+            probs = (mine[pl.ds(block * length, length), :] * (1.0 / total)).astype(LOW)
+            values = pl.ds(pl.multiple_of((heads + head) * HD, HD), HD)
+            mixed = mixed + t_dot(kv_all[block, :, values], probs)
+        attended[:, columns] = mixed.T.astype(LOW)
+        logs[head] = jnp.broadcast_to(highest + jnp.log(total), (8, length))
+
+    if depth > 1:
+        gather.turn(1)
+    if depth > 2:
+        gather.spread(2)
+    for index in range(4):
+        partial[index // 2, index % 2] = dot(attended[pl.ds(index * rows, rows), :], w_out[...]).astype(LOW)
+    scatter = TensorScatter(copies, partial, from_pair, from_y, t_send, t_recv)
+    scatter.begin()
+    scatter.cross()
+    if depth > 2:
+        gather.turn(2)
+    for step in range(3, depth):
+        gather.spread(step)
+    scatter.result(sum_ref)
+    for step in range(3, depth):
+        gather.turn(step)
+    own.wait()
+    for distance in (1, 2):
+
+        @pl.when(spot < chain - distance)
+        def _():
+            halo_copy(distance, group + distance).wait_send()
+
+    copies.finish()
+
+
+def run_attention(queries, kv, key_docs, query_docs, w_out, grads, depth, chain, number):
+    length, wide = kv.shape
+    heads = wide // (2 * HD)
+    rows, width = grads.shape
+    return pl.pallas_call(
+        functools.partial(attention_kernel, depth, rows, heads, chain),
+        out_shape=(
+            jax.ShapeDtypeStruct((3, length, wide), LOW),
+            jax.ShapeDtypeStruct(queries.shape, LOW),
+            jax.ShapeDtypeStruct((heads, 8, length), FULL),
+            jax.ShapeDtypeStruct((rows, width), FULL),
+            jax.ShapeDtypeStruct((depth, 4 * rows, width), LOW),
+        ),
+        in_specs=[VMEM] * 5 + [ANY],
+        out_specs=(VMEM, VMEM, VMEM, VMEM, ANY),
+        scratch_shapes=[pltpu.VMEM((heads, 3 * length, length), FULL), pltpu.VMEM((3 * length, length), FULL)]
+        + TensorScatter.scratch(rows, width)
+        + [dma(depth), dma(depth), dma(depth, 6), dma(depth, 6), dma(3), dma(3), dma(1)],
+        compiler_params=comm_params(number),
+    )(queries, kv, key_docs, query_docs, w_out, grads)
+
+
+def attention_back_kernel(
+    depth, rows, heads, chain,
+    low_ref, query_ref, kv_all, attended, logs, key_docs, query_docs, w_out, produced_ref,
+    lows, query_cot, kv_cot, mix_ref,
+    bias, cots, deltas, turned, sending, landed, work,
+    diagonal, from_x, from_y, from_z, r_send, r_recv, t_send, t_recv, h_send, h_recv, load,
+):
+    group, part = lax.axis_index("expert"), lax.axis_index("tensor")
+    spot = group % chain
+    greet(partners_of(depth))
+    copies = Copies()
+    length = query_ref.shape[0]
+    scale = HD ** (-0.5)
+    wide = heads * HD
+    gather = TensorGather(copies, low_ref, lows, t_send, t_recv)
     order = [step for step in range(1, depth)] + [0]
     loads = {}
     for step in order:
-        loads[step] = pltpu.make_async_copy(p_ref.at[step], work.at[step], load.at[step])
+        loads[step] = pltpu.make_async_copy(produced_ref.at[step], work.at[step], load.at[step])
         loads[step].start()
-    scatter = Scatter(copies, work, diagonal, from_x, from_y, from_z, rows, send, recv)
+    scatter = Scatter(copies, work, diagonal, from_x, from_y, from_z, rows, r_send, r_recv)
     for step in order:
         loads[step].wait()
         scatter.corner(step)
-    for step in order:
+    mask_bias(bias, key_docs, query_docs, length)
+    gather.cross()
+    gather.finish()
+    for index in range(4):
+        cots[pl.ds(index * rows, rows), :] = dot_t(lows[index // 2, index % 2], w_out[...]).astype(LOW)
+    for head in range(heads):
+        columns = pl.ds(head * HD, HD)
+        product = cots[:, columns].astype(FULL) * attended[:, columns].astype(FULL)
+        deltas[head] = jnp.broadcast_to(jnp.sum(product.T, axis=0, keepdims=True), (8, length))
+    turned[...] = jnp.zeros_like(turned)
+
+    def back(block, target):
+        @pl.loop(0, heads)
+        def _(head):
+            columns = pl.ds(pl.multiple_of(head * HD, HD), HD)
+            others = pl.ds(pl.multiple_of((heads + head) * HD, HD), HD)
+            query, cot = query_ref[:, columns], cots[:, columns]
+            log, delta = logs[head, 0:1, :], deltas[head, 0:1, :]
+            tile = 256
+
+            @pl.loop(0, length // tile)
+            def _(index):
+                keys = pl.ds(pl.multiple_of(index * tile, tile), tile)
+                key, value = kv_all[block, keys, columns], kv_all[block, keys, others]
+                hidden = bias[pl.ds(pl.multiple_of(block * length + index * tile, tile), tile), :]
+                probs = jnp.exp(dot_t(key, query) * scale + hidden - log)
+                score_cot = (probs * (dot_t(value, cot) - delta)).astype(LOW)
+                turned[head] += t_dot(key, score_cot)
+                target[keys, columns] = (dot(score_cot, query) * scale).astype(target.dtype)
+                target[keys, others] = dot(probs.astype(LOW), cot).astype(target.dtype)
+
+    def halo_copy(distance, to):
+        return remote(sending.at[2 - distance], landed.at[2 - distance], h_send.at[distance], h_recv.at[distance], (to, part))
+
+    def send(distance):
+        @pl.when(spot >= distance)
+        def _():
+            halo_copy(distance, group - distance).start()
+
+    back(1, sending.at[1])
+    send(1)
+    scatter.side(order[0])
+    back(0, sending.at[0])
+    send(2)
+    for step in order[1:-1]:
         scatter.side(step)
-    for step in order:
+    back(2, kv_cot)
+    for head in range(heads):
+        query_cot[:, pl.ds(head * HD, HD)] = turned[head].T * scale
+    scatter.side(order[-1])
+    for step in order[:-1]:
         scatter.climb(step)
-    scatter.result(o_ref)
+    for distance in (1, 2):
+
+        @pl.when(spot < chain - distance)
+        def _():
+            halo_copy(distance, group + distance).wait_recv()
+            add_rows(kv_cot, [kv_cot, landed.at[2 - distance]], length)
+
+    scatter.climb(order[-1])
+    scatter.result(mix_ref)
+    for distance in (1, 2):
+
+        @pl.when(spot >= distance)
+        def _():
+            halo_copy(distance, group - distance).wait_send()
+
     copies.finish()
 
 
-def scatter_rows(parts, number):
-    depth, wave, width = parts.shape
-    rows = wave // 4
+def run_attention_back(low, queries, kv_all, attended, logs, key_docs, query_docs, w_out, produced, chain, number):
+    depth = produced.shape[0]
+    rows, width = low.shape
+    length, wide = kv_all.shape[1:]
+    heads = wide // (2 * HD)
     return pl.pallas_call(
-        functools.partial(scatter_rows_kernel, depth, rows),
-        out_shape=jax.ShapeDtypeStruct((rows, width), FULL),
-        in_specs=[ANY],
-        out_specs=VMEM,
-        scratch_shapes=[pltpu.VMEM(parts.shape, parts.dtype)] + Scatter.scratch(depth, rows, width) + [dma(depth)],
+        functools.partial(attention_back_kernel, depth, rows, heads, chain),
+        out_shape=(
+            jax.ShapeDtypeStruct((2, 2, rows, width), LOW),
+            jax.ShapeDtypeStruct(queries.shape, FULL),
+            jax.ShapeDtypeStruct((length, wide), FULL),
+            jax.ShapeDtypeStruct((rows, width), FULL),
+        ),
+        in_specs=[VMEM] * 8 + [ANY],
+        out_specs=(VMEM,) * 4,
+        scratch_shapes=[
+            pltpu.VMEM((3 * length, length), FULL), pltpu.VMEM((length, wide // 2), LOW),
+            pltpu.VMEM((heads, 8, length), FULL), pltpu.VMEM((heads, HD, length), FULL),
+            pltpu.VMEM((2, length, wide), LOW), pltpu.VMEM((2, length, wide), LOW),
+            pltpu.VMEM(produced.shape, LOW),
+        ]
+        + Scatter.scratch(depth, rows, width)
+        + [dma(4), dma(3), dma(3), dma(3), dma(depth)],
         compiler_params=comm_params(number),
-    )(parts)
+    )(low, queries, kv_all, attended, logs, key_docs, query_docs, w_out, produced)
 
 
 def pair_swap_kernel(count, *refs):
@@ -973,72 +1226,6 @@
     )(shaped)
 
 
-def halo_kernel(chain, forward, count, *refs):
-    ins, outs, (send, recv) = refs[:count], refs[count : 2 * count], refs[2 * count :]
-    group, part = lax.axis_index("expert"), lax.axis_index("tensor")
-    spot = group % chain
-    barrier = pltpu.get_barrier_semaphore()
-    distances = (1, 2)
-
-    def each(before, after):
-        for distance in distances:
-            if after is not None:
-                pl.when(spot < chain - distance)(functools.partial(after, distance))
-            if before is not None:
-                pl.when(spot >= distance)(functools.partial(before, distance))
-
-    def signal(to):
-        pl.semaphore_signal(barrier, inc=1, device_id=(to, part), device_id_type=MESH)
-
-    each(lambda d: signal(group - d), lambda d: signal(group + d))
-    pl.semaphore_wait(barrier, jnp.minimum(spot, 2) + jnp.minimum(chain - 1 - spot, 2))
-
-    def copies(distance, to):
-        return [
-            remote(
-                ins[i] if forward else ins[i].at[2 - distance],
-                outs[i].at[2 - distance],
-                send.at[i, distance],
-                recv.at[i, distance],
-                (to, part),
-            )
-            for i in range(count)
-        ]
-
-    def start(sign, distance):
-        for copy in copies(distance, group + sign * distance):
-            copy.start()
-
-    def finish(sign, distance):
-        for copy in copies(distance, group + sign * distance):
-            copy.wait_send()
-
-    def take(sign, distance):
-        for copy in copies(distance, group - sign * distance):
-            copy.wait_recv()
-
-    if forward:
-        each(None, functools.partial(start, 1))
-        each(functools.partial(take, 1), None)
-        each(None, functools.partial(finish, 1))
-    else:
-        each(functools.partial(start, -1), None)
-        each(None, functools.partial(take, -1))
-        each(functools.partial(finish, -1), None)
-
-
-def halo(arrays, chain, forward, number):
-    count = len(arrays)
-    return pl.pallas_call(
-        functools.partial(halo_kernel, chain, forward, count),
-        out_shape=tuple(jax.ShapeDtypeStruct(((2,) + a.shape) if forward else a.shape, a.dtype) for a in arrays),
-        in_specs=[ANY] * count,
-        out_specs=(ANY,) * count,
-        scratch_shapes=[dma(count, 3), dma(count, 3)],
-        compiler_params=comm_params(number),
-    )(*arrays)
-
-
 def dot(left, right):
     return jnp.dot(left, right, preferred_element_type=FULL)
 
@@ -1060,7 +1247,7 @@
     local_experts, _, hidden = w_gate.shape
     experts = local_experts * groups
     chain = LENGTH // row_count
-    if not (parts == 4 and groups % 2 == 0 and experts <= 2 * TOP and row_count * chain == LENGTH and WINDOW == 2 * row_count):
+    if not (parts == 4 and groups % 2 == 0 and experts <= 2 * TOP and chain == 4 and 4 * row_count == LENGTH and WINDOW == 2 * row_count):
         return body_routed(
             tokens, documents, routes, norm1_gain, q_gain, k_gain, w_query, w_key, w_value, w_out, norm2_gain, router_w,
             w_gate, w_up, w_down, out_grad,
@@ -1069,7 +1256,6 @@
     rows = row_count // parts
     seen = groups * row_count // 2
     heads = w_query.shape[1] // HD
-    score_scale = HD ** (-0.5)
     group, part = lax.axis_index("expert"), lax.axis_index("tensor")
     core = part % 2
 
@@ -1093,37 +1279,17 @@
     query_gain, key_gain = q_gain.reshape(-1), k_gain.reshape(-1)
     queries = rotate((query_raw * query_scale * query_gain).reshape(row_count, heads, HD), cosine, sine).astype(LOW)
     key_heads = rotate((key_raw * key_scale * key_gain).reshape(row_count, heads, HD), cosine, sine).astype(LOW)
+    queries = queries.reshape(row_count, -1)
     own_kv = jnp.concatenate([key_heads.reshape(row_count, -1), values], axis=1)
-    own_docs = documents.reshape(row_count // 128, 128)
-    before_kv, before_docs = halo([own_kv, own_docs], chain, True, 2)
+    every_doc = jnp.concatenate([jnp.full((2 * row_count,), -1, jnp.int32), lax.all_gather(documents, "expert", tiled=True)])
+    key_docs = lax.dynamic_slice_in_dim(every_doc, first_row, 3 * row_count, 0)
     spot = group % chain
-    exists = jnp.stack([spot >= 2, spot >= 1])
-    before_kv = jnp.where(exists[:, None, None], before_kv, jnp.zeros((), LOW))
-    before_docs = jnp.where(exists[:, None, None], before_docs, -1)
-    all_kv = jnp.concatenate([before_kv[0], before_kv[1], own_kv], axis=0)
-    all_keys = all_kv[:, : heads * HD].reshape(3 * row_count, heads, HD)
-    all_values = all_kv[:, heads * HD :].reshape(3 * row_count, heads, HD)
-    all_docs = jnp.concatenate([before_docs[0], before_docs[1], own_docs], axis=0).reshape(-1)
-    key_pos = first_row - 2 * row_count + jnp.arange(3 * row_count, dtype=jnp.int32)
-    allowed = (
-        (all_docs[None, :] == documents[:, None])
-        & (key_pos[None, :] <= positions[:, None])
-        & (positions[:, None] - key_pos[None, :] < WINDOW)
-    )
-
-    def masked_scores():
-        raw_scores = jnp.einsum("qhd,khd->hqk", queries, all_keys, preferred_element_type=FULL) * score_scale
-        return jnp.where(allowed[None], raw_scores, -1e30)
-
-    scores = masked_scores()
-    highest = jnp.max(scores, axis=-1, keepdims=True)
-    weights = jnp.where(allowed[None], jnp.exp(scores - highest), 0.0)
-    denominator = jnp.sum(weights, axis=-1, keepdims=True)
-    log_total = highest + jnp.log(denominator)
-    attn_probs = weights / denominator
-    attended = jnp.einsum("hqk,khd->qhd", attn_probs.astype(LOW), all_values, preferred_element_type=FULL)
-    attended = attended.reshape(row_count, -1).astype(LOW)
-    attention = tensor_scatter(dot(attended, w_out).astype(LOW), 3)
+    block_of = jnp.arange(3 * row_count, dtype=jnp.int32) // row_count
+    key_docs = jnp.where(spot + block_of >= 2, key_docs, -1)[:, None]
+    query_docs = jnp.broadcast_to(documents[None, :], (8, row_count))
+    kv_all, attended, logs, attention, all_grad = run_attention(
+        queries, own_kv, key_docs, query_docs, w_out, quarter(out_grad), depth, chain, 3
+    )
 
     own_inputs = quarter(tokens).astype(FULL)
     own_grad = quarter(out_grad)
@@ -1136,7 +1302,6 @@
         quarter(routes)[:, :, None] == jnp.arange(experts, dtype=jnp.int32)[None, None, :], axis=1
     ).astype(FULL)
 
-    all_grad = gather_rows(own_grad, depth, 4)
     gates = (router_probs * picked).T.reshape(groups, local_experts, rows)
     gates = jnp.concatenate([gates, jnp.zeros((groups, 8 - local_experts, rows), FULL)], axis=1)
     normed_two_grad, gate_cots, all_normed, gated, gate_pre_grad, up_pre_grad, produced = run_experts(
@@ -1145,7 +1310,6 @@
     units = 2 * local_experts * hidden
     all_normed, all_grad = all_normed.reshape(seen, width), all_grad.reshape(seen, width)
     gated, gate_pre_grad, up_pre_grad = (a.reshape(seen, units) for a in (gated, gate_pre_grad, up_pre_grad))
-    expert_mix = scatter_rows(produced, 7)
 
     def expert_grads(left, right):
         return t_dot(left, right)
@@ -1159,8 +1323,6 @@
         for mine, other in zip((gate_wgrad, up_wgrad, down_wgrad), swaps)
     )
 
-    output = tensor_gather((state + expert_mix).astype(LOW), 9)
-
     prob_cot = gate_cots[:, :, :local_experts].reshape(depth, 2, 2, local_experts, rows).sum(axis=2)
     plane = jnp.arange(depth, dtype=jnp.int32) ^ (group // 2)
     prob_cot = prob_cot[plane].reshape(experts, rows).T * picked
@@ -1172,25 +1334,13 @@
     norm2_grad = jnp.sum(normed_two_grad * state * scale_two, axis=0)
     inner_two = jnp.sum(normed_two_grad * norm2_gain * state, axis=-1, keepdims=True)
     state_cot = own_grad_float + scale_two * norm2_gain * normed_two_grad - state * scale_two**3 * inner_two / width
-    state_low = tensor_gather(state_cot.astype(LOW), 10)
-
+    state_low, query_cot, kv_cot, expert_mix = run_attention_back(
+        state_cot.astype(LOW), queries, kv_all, attended, logs, key_docs, query_docs, w_out, produced, chain, 10
+    )
+    state_low = state_low.reshape(row_count, width)
+    output = tensor_gather((state + expert_mix).astype(LOW), 9)
     w_out_grad = t_dot(state_low, attended)
-    attended_cot = dot_t(state_low, w_out).astype(LOW).reshape(row_count, heads, HD)
-    scores = masked_scores()
-    attn_probs = jnp.where(allowed[None], jnp.exp(scores - log_total), 0.0)
-    value_cot_all = jnp.einsum("hqk,qhd->khd", attn_probs.astype(LOW), attended_cot, preferred_element_type=FULL)
-    prob_grad = jnp.einsum("qhd,khd->hqk", attended_cot, all_values, preferred_element_type=FULL)
-    delta = jnp.sum(attn_probs * prob_grad, axis=-1, keepdims=True)
-    score_cot = (attn_probs * (prob_grad - delta)).astype(LOW)
-    query_cot = jnp.einsum("hqk,khd->qhd", score_cot, all_keys, preferred_element_type=FULL) * score_scale
-    key_cot_all = jnp.einsum("hqk,qhd->khd", score_cot, queries, preferred_element_type=FULL) * score_scale
-    kv_cot = jnp.concatenate(
-        [key_cot_all.reshape(3, row_count, -1), value_cot_all.reshape(3, row_count, -1)], axis=2
-    )
-    (after_kv,) = halo([kv_cot[:2].astype(LOW)], chain, False, 11)
-    follows = jnp.stack([spot < chain - 2, spot < chain - 1])
-    after_kv = jnp.where(follows[:, None, None], after_kv, jnp.zeros((), LOW)).astype(FULL)
-    kv_cot = kv_cot[2] + after_kv[0] + after_kv[1]
+    query_cot = query_cot.reshape(row_count, heads, HD)
     key_cot = kv_cot[:, : heads * HD].reshape(row_count, heads, HD)
     value_low = kv_cot[:, heads * HD :].astype(LOW)
     query_norm_cot = rotate_back(query_cot, cosine, sine).reshape(row_count, -1)

time: 1070 us -> 945 us (0.88)
  Pallas kernels: 718 us -> 678 us
  matrix products: 113 us -> 74.2 us
  other arithmetic: 95.9 us -> 59.4 us
  local copies, waits for them, and re-layouts: 95.1 us -> 60 us
  blocking collectives: 24.5 us -> 48.1 us
    dot_general x6 -> x0, matrix products: 33.2 us -> none  [the longest x1 9.42 us: body(): jnp.einsum('hqk,qhd->khd', attn_probs.astype(LOW), attended_cot, preferre...]
    all_gather x0 -> x1, blocking collectives: none -> 25 us  [body(): lax.all_gather(documents, 'expert', tiled=True)]
    pallas_call x2 -> x1, Pallas kernels: 35.5 us -> 17.9 us  [tensor_scatter(): pl.pallas_call(functools.partial(tensor_scatter_kernel, rows), out_shape=...]
    pallas_call x3 -> x2, Pallas kernels: 53.5 us -> 37.1 us  [tensor_gather(): pl.pallas_call(tensor_gather_kernel, out_shape=jax.ShapeDtypeStruct((2, 2...]
    pallas_call x1, Pallas kernels: 166 us -> 151 us  [expert_scatter(): pl.pallas_call(functools.partial(expert_scatter_kernel, depth, rows), out...]
    reshape x4 -> x1, local copies, waits for them, and re-layouts: 15.1 us -> 2.55 us  [body(): query_cot = query_cot.reshape(row_count, heads, HD)]
    convert_element_type x3 -> x2, other arithmetic: 15.3 us -> 3.89 us  [the longest x1 2.97 us: body(): state_cot.astype(LOW)]
    pallas_call x4 -> x2, Pallas kernels: 238 us -> 246 us  [the longest x1 129 us: run_attention(): pl.pallas_call(functools.partial(attention_kernel, depth, rows, heads, ch...]
  transfers between devices with their start and end apart: 2 -> 2, of which waited for: 0 -> 0; matrix products, arithmetic and copies ran while one was open for 11% -> 13% of each run, Pallas kernels for 22% -> 24%
where the time goes in v3:
time: 945 us; the launch traced here: 935 us
  Pallas kernels  678 us (72%)
  matrix products  74.2 us (8%)
  local copies, waits for them, and re-layouts  60 us (6%)
  other arithmetic  59.4 us (6%)
  blocking collectives  48.1 us (5%)
  between operations  15.1 us (2%)
    pallas_call x1, Pallas kernels, run_experts(): pl.pallas_call(functools.partial(experts_kernel, depth, rows, local, hidd...  207 us
    pallas_call x1, Pallas kernels, expert_scatter(): pl.pallas_call(functools.partial(expert_scatter_kernel, depth, rows), out...  151 us
    pallas_call x1, Pallas kernels, run_attention(): pl.pallas_call(functools.partial(attention_kernel, depth, rows, heads, ch...  129 us
    pallas_call x1, Pallas kernels, run_attention_back(): pl.pallas_call(functools.partial(attention_back_kernel, depth, rows, head...  117 us
    dot_general x7, matrix products, t_dot(): lax.dot_general(left, right, (((0,), (0,)), ((), ())), preferred_element_...  53.4 us
    pallas_call x2, Pallas kernels, tensor_gather(): pl.pallas_call(tensor_gather_kernel, out_shape=jax.ShapeDtypeStruct((2, 2...  37.1 us
    all_gather x1, blocking collectives, body(): lax.all_gather(documents, 'expert', tiled=True)  25 us
    dot_general x4, local copies, waits for them, and re-layouts, t_dot(): lax.dot_general(left, right, (((0,), (0,)), ((), ())), preferred_element_...  22.1 us
  transfers between devices with their start and end apart: 2, of which 0 were waited for; matrix products, arithmetic and copies ran while one was open for 13% of the time, Pallas kernels for 24%

profile of v3, /device:TPU:10, one launch (start us, length us, event | category | flops | bytes accessed | tf_op | source)
XLA Modules:
  0.0 934.8 jit_solution(16572957206087754291)
XLA Ops:
  10.8 25.0 %all-gather = s32[8,1,512]{2,1,0:T(1,128)S(1)} all-gather(s32[1,1,512]{2,1,0:T(1,128)} %bitcast.200), channel_id=1, replica_groups=mesh['expert'=8,'tensor'=4] {'expert'}, dimensions={0}, use_global_device_ids=true | all-gather | bytes 18432 | tf_op jit(solution)/shard_map/all_gather | solution.py:1284
  40.9 4.5 convolution_convert_fusion.4
  49.4 4.6 multiply_reduce_fusion.8
  54.0 5.7 psum.21
  70.7 3.4 slice_negate_fusion.2
  78.4 128.7 %shard_map.263 = (bf16[3,512,1024]{2,1,0:T(8,128)(2,1)}, bf16[512,512]{1,0:T(8,128)(2,1)}, f32[4,8,512]{2,1,0:T(8,128)}, f32[128,2048]{1,0:T(8,128)}, bf16[4,512,2048]{2,1,0:T(8,128)(2,1)}) custom-call(bf16[512,512]{1,0:T(8,128)(2,1)} %get-tuple-element.136.query_ref, bf16[512,1024]{1,0:T(8,128)(2,1)} %pad_maximum_fusion.1.kv_ref, ...), custom_call_target="tpu_custom_call" | custom-call | tf_op jit(solution)/shard_map/pallas_call | solution.py:944
  211.0 206.9 %shard_map.264 = (f32[128,2048]{1,0:T(8,128)}, f32[4,4,8,128]{3,2,1,0:T(8,128)}, bf16[4,512,2048]{2,1,0:T(8,128)(2,1)}, bf16[4,512,1024]{2,1,0:T(8,128)(2,1)}, b...) custom-call(bf16[128,2048]{1,0:T(8,128)(2,1)} %copy-done.11, ...), custom_call_target="tpu_custom_call" | custom-call | tf_op jit(solution)/shard_map/pallas_call | solution.py:735
  422.6 3.0 fusion.45
  425.6 117.2 %shard_map.265 = (bf16[2,2,128,2048]{3,2,1,0:T(8,128)(2,1)}, f32[512,512]{1,0:T(8,128)}, f32[512,1024]{1,0:T(8,128)}, f32[128,2048]{1,0:T(8,128)}) custom-call(bf16[128,2048]{1,0:T(8,128)(2,1)} %get-tuple-element.120.low_ref, bf16[512,512]{1,0:T(8,128)(2,1)} %get-tuple-element.136.query_ref, bf16[3,512,1024]{2,1,0:T(8,128)(2,1)} %get-tuple-element.37.kv_all, ...), custom_call_target="tpu_custom_call" | custom-call | tf_op jit(solution)/shard_map/pallas_call | solution.py:1061
  560.4 6.3 psum.22
  572.9 2.6 add_convert_fusion
  575.5 17.9 %shard_map.267 = f32[128,2048]{1,0:T(8,128)} custom-call(bf16[2,2,128,2048]{3,2,1,0:T(8,128)(2,1)} %bitcast.150), custom_call_target="tpu_custom_call" | custom-call | tf_op jit(solution)/shard_map/pallas_call | solution.py:1136
  595.6 4.0 convolution_convert_fusion
  599.6 2.7 convolution_convert_fusion.2
  602.4 2.7 convolution_convert_fusion.1
  606.0 2.9 copy.96
  611.1 5.7 pad_maximum_fusion.p_ref
  616.8 150.5 %shard_map.269 = f32[256,2048]{1,0:T(8,128)} custom-call(bf16[4,2,256,2048]{3,2,1,0:T(8,128)(2,1)} %pad_maximum_fusion.p_ref), custom_call_target="tpu_custom_call" | custom-call | tf_op jit(solution)/shard_map/pallas_call | solution.py:1214
  769.6 18.8 %shard_map.268 = bf16[2,2,128,2048]{3,2,1,0:T(8,128)(2,1)} custom-call(bf16[128,2048]{1,0:T(8,128)(2,1)} %fusion.6.x_ref), custom_call_target="tpu_custom_call" | custom-call | tf_op jit(solution)/shard_map/pallas_call | solution.py:1173
  788.4 4.1 bitcast_convert_fusion
  792.6 6.4 copy.97
  799.0 6.4 copy.99
  805.4 14.7 %fusion.54 = f32[2048,2,2,256]{3,0,2,1:T(8,128)} fusion(bf16[2048,2048,1,1]{1,0,3,2:T(8,128)(2,1)} %bitcast.205, bf16[2,2,256,2048]{3,2,1,0:T(8,128)(2,1)} %bitcast.158), kind=kOutput, calls=%fused_computation.136 | convolution fusion | flops 8589934592 | bytes 20971520 | tf_op jit(solution)/shard_map/dot_general | solution.py:1238
  820.2 13.5 %fusion.55 = f32[2048,2,2,256]{3,0,2,1:T(8,128)} fusion(bf16[2048,2048,1,1]{1,0,3,2:T(8,128)(2,1)} %bitcast.206, bf16[2,2,256,2048]{3,2,1,0:T(8,128)(2,1)S(1)} %bitcast.157), kind=kOutput, calls=%fused_computation.137 | convolution fusion | flops 8589934592 | bytes 20971520 | tf_op jit(solution)/shard_map/dot_general | solution.py:1238
  833.6 6.4 copy.101
  840.0 14.5 %fusion.56.refs_2_ = f32[2,2,256,2048]{3,2,1,0:T(8,128)} fusion(bf16[2,2,256,2048]{3,2,1,0:T(8,128)(2,1)} %bitcast.156, bf16[2048,2048,1,1]{1,0,3,2:T(8,128)(2,1)} %bitcast.149), kind=kOutput, calls=%fused_computation.138 | convolution fusion | flops 8589934592 | bytes 20971520 | tf_op jit(solution)/shard_map/dot_general | solution.py:1238
  854.6 19.6 %shard_map.270 = (f32[2,2048,256]{2,1,0:T(8,128)}, f32[2,2048,256]{2,1,0:T(8,128)}, f32[2,256,2048]{2,1,0:T(8,128)}) custom-call(f32[2,2,2048,256]{3,2,1,0:T(8,128)} %bitcast.145, f32[2,2,2048,256]{3,2,1,0:T(8,128)} %bitcast.142, f32[2,2,256,2048]{3,2,1,0:T(8,128)} %fusion.56.refs_2_), custom_call_target="tpu_custom_call" | custom-call | tf_op jit(solution)/shard_map/pallas_call | solution.py:1099
  874.2 6.7 bitcast_add_fusion.2
  880.9 5.2 bitcast_add_fusion.1
  890.7 18.2 %shard_map.266 = bf16[2,2,128,2048]{3,2,1,0:T(8,128)(2,1)} custom-call(bf16[128,2048]{1,0:T(8,128)(2,1)} %add_convert_fusion.1.x_ref), custom_call_target="tpu_custom_call" | custom-call | tf_op jit(solution)/shard_map/pallas_call | solution.py:1173
  912.1 11.1 %psum.23 = f32[18,256]{1,0:T(8,128)S(1)} all-reduce(f32[18,256]{1,0:T(8,128)} %reduce-scatter.5.cloned.1.call-done), channel_id=1, replica_groups=mesh['expert'=8,'tensor'=4] {'tensor'}, use_global_device_ids=true, to_apply=%region_18.19 | all-reduce | flops 4608 | bytes 36864 | tf_op jit(solution)/shard_map/psum | solution.py:1387
  924.4 3.2 copy.132
  (176 shorter events, 76.5 us)
Async XLA Ops:
  7.2 38.2 %copy-start = (bf16[2048,512]{1,0:T(8,128)(2,1)S(1)}, bf16[2048,512]{1,0:T(8,128)(2,1)}, u32[]{:S(2)}) copy-start(bf16[2048,512]{1,0:T(8,128)(2,1)} %param.23) | copy-start | bytes 6291460
  7.2 33.7 %copy-start.35 = (f32[2048]{0:T(1024)S(1)}, f32[2048]{0:T(1024)}, u32[]{:S(2)}) copy-start(f32[2048]{0:T(1024)} %param.19) | copy-start | bytes 24580
  7.2 902.7 %reduce-scatter.7.cloned.1.call-start = ((), (), s32[]{:S(2)}) async-start(), calls=%async_computation.3 | async-start | bytes 73728
  9.5 39.8 %copy-start.44 = (f32[512]{0:T(512)}, f32[512]{0:T(512)S(1)}, u32[]{:S(2)}) copy-start(f32[512]{0:T(512)S(1)} %add_rsqrt_fusion) | copy-start | bytes 6148
  40.9 4.5 copy-start.12
  49.4 12.8 %copy-start.37 = (f32[4,128]{1,0:T(4,128)S(1)}, f32[4,128]{1,0:T(4,128)}, u32[]{:S(2)}) copy-start(f32[4,128]{1,0:T(4,128)} %param.20) | copy-start | bytes 6148
  54.0 13.1 %copy-start.36 = (f32[4,128]{1,0:T(4,128)S(1)}, f32[4,128]{1,0:T(4,128)}, u32[]{:S(2)}) copy-start(f32[4,128]{1,0:T(4,128)} %param.21) | copy-start | bytes 6148
  77.8 132.0 %copy-start.34 = (f32[2048]{0:T(1024)S(1)}, f32[2048]{0:T(1024)}, u32[]{:S(2)}) copy-start(f32[2048]{0:T(1024)} %param.26) | copy-start | bytes 24580
  78.4 131.6 %copy-start.33 = (bf16[2048,16]{0,1:T(8,128)(2,1)S(1)}, bf16[2048,16]{0,1:T(8,128)(2,1)}, u32[]{:S(2)}) copy-start(bf16[2048,16]{0,1:T(8,128)(2,1)} %param.27) | copy-start | bytes 196612
  210.3 207.6 %copy-start.38 = (f32[128]{0:T(128)}, f32[128]{0:T(128)S(1)}, u32[]{:S(2)}) copy-start(f32[128]{0:T(128)S(1)} %fusion.23) | copy-start | bytes 1540
  420.1 122.7 %copy-start.41 = (f32[128]{0:T(128)}, f32[128]{0:T(128)S(1)}, u32[]{:S(2)}) copy-start(f32[128]{0:T(128)S(1)} %multiply_reduce_fusion.9) | copy-start | bytes 1540
  553.8 2.5 copy-start.18
  556.2 2.7 copy-start.45
  556.2 2.8 copy-start.39
  556.2 2.8 copy-start.42
  558.9 353.2 %reduce-scatter.5.cloned.1.call-start = ((), (), s32[]{:S(2)}) async-start(), calls=%async_computation.2 | async-start | bytes 221184 | tf_op jit(solution)/shard_map/reduce_scatter | solution.py:1387
  568.2 2.4 copy-start.25
  572.9 20.5 %copy-start.13 = (bf16[512,2048]{1,0:T(8,128)(2,1)S(1)}, bf16[512,2048]{1,0:T(8,128)(2,1)}, u32[]{:S(2)}) copy-start(bf16[512,2048]{1,0:T(8,128)(2,1)} %param.16) | copy-start | bytes 6291460
  599.6 2.7 copy-start.14
  599.6 2.7 copy-start.24
  602.3 2.8 copy-start.6
  602.3 2.8 copy-start.30
  605.1 3.8 copy-start.31
  616.8 150.5 %copy-start.9 = (f32[128,2048]{1,0:T(8,128)S(1)}, f32[128,2048]{1,0:T(8,128)}, u32[]{:S(2)}) copy-start(f32[128,2048]{1,0:T(8,128)} %shard_map.267) | copy-start | bytes 3145732
  616.8 150.5 %copy-start.22 = (f32[128,2048]{1,0:T(8,128)S(1)}, f32[128,2048]{1,0:T(8,128)}, u32[]{:S(2)}) copy-start(f32[128,2048]{1,0:T(8,128)} %get-tuple-element.121) | copy-start | bytes 3145732
  805.4 14.7 %copy-start.21 = (bf16[1024,2048]{1,0:T(8,128)(2,1)S(1)}, bf16[1024,2048]{1,0:T(8,128)(2,1)}, u32[]{:S(2)}) copy-start(bf16[1024,2048]{1,0:T(8,128)(2,1)} %copy.99) | copy-start | bytes 12582916
  874.1 6.7 copy-start.20
  874.1 11.9 %slice-start = ((s8[8388608]{0:T(1024)(128)(4,1)}), s8[4194304]{0:T(1024)(128)(4,1)S(1)}, s32[]{:S(2)}) async-start(s8[8388608]{0:T(1024)(128)(4,1)} %bitcast.143), calls=%async_computation.4 | async-start | bytes 8388608
  880.9 5.2 slice-start.1
  880.9 6.1 copy-start.19
  886.9 2.6 copy-start.10
  889.5 38.1 %copy-start.1 = (bf16[2048,512]{1,0:T(8,128)(2,1)S(1)}, bf16[2048,512]{1,0:T(8,128)(2,1)}, u32[]{:S(2)}) copy-start(bf16[2048,512]{1,0:T(8,128)(2,1)} %param.23) | copy-start | bytes 6291460
  (18 other events, 28.2 us)
Sparse Core Ops, SparseCore 0:
  559.0 67.9 reduce-scatter.6
  630.2 97.5 reduce-scatter.4

commit v4 on v3

--- a/solution.py
+++ b/solution.py
@@ -452,19 +452,27 @@
 
     def start(self, copy):
         copy.start()
-        self.open.append([copy, True])
+        self.open.append((copy, set()))
         return copy
+
+    def mark(self, copy, what):
+        for entry, done in self.open:
+            if entry is copy:
+                done.add(what)
 
     def arrived(self, copy):
         copy.wait_recv()
-        for entry in self.open:
-            if entry[0] is copy:
-                entry[1] = False
+        self.mark(copy, "arrived")
+
+    def sent(self, copy):
+        copy.wait_send()
+        self.mark(copy, "sent")
 
     def finish(self):
-        for copy, receiving in self.open:
-            copy.wait_send()
-            if receiving:
+        for copy, done in self.open:
+            if "sent" not in done:
+                copy.wait_send()
+            if "arrived" not in done:
                 copy.wait_recv()
 
 
@@ -1080,162 +1088,290 @@
     )(low, queries, kv_all, attended, logs, key_docs, query_docs, w_out, produced)
 
 
-def pair_swap_kernel(count, *refs):
-    ins, outs, (send, recv) = refs[:count], refs[count : 2 * count], refs[2 * count :]
+def dot(left, right):
+    return jnp.dot(left, right, preferred_element_type=FULL)
+
+
+def dot_t(left, right):
+    return lax.dot_general(left, right, (((1,), (1,)), ((), ())), preferred_element_type=FULL)
+
+
+def t_dot(left, right):
+    return lax.dot_general(left, right, (((0,), (0,)), ((), ())), preferred_element_type=FULL)
+
+
+class ExpertScatter:
+    def __init__(self, copies, parts, work, from_x, from_z, load, send, recv):
+        self.copies, self.parts, self.work, self.from_x, self.from_z = copies, parts, work, from_x, from_z
+        self.load, self.send, self.recv = load, send, recv
+        self.z, self.x, y, core = place()
+        self.depth, self.rows = work.shape[1], work.shape[2]
+        self.over_x = device(self.z, 1 - self.x, y, core)
+        self.column = [device(swapped(self.z, step), self.x, y, core) for step in range(self.depth)]
+        self.order = list(range(self.depth - 1, -1, -1))
+        self.loads, self.sides, self.along = {}, {}, {}
+
+    def begin(self, index):
+        for step in self.order:
+            at = swapped(self.z, step)
+            self.sides[index, step] = self.copies.start(
+                remote(
+                    self.parts[index].at[at, 1 - self.x], self.from_x.at[index, step],
+                    self.send.at[0, index, step], self.recv.at[0, index, step], self.over_x,
+                )
+            )
+            load = pltpu.make_async_copy(self.parts[index].at[at, self.x], self.work.at[index, step], self.load.at[index, step])
+            load.start()
+            self.loads[index, step] = load
+
+    def climb(self, index, step):
+        self.loads[index, step].wait()
+        self.copies.arrived(self.sides[index, step])
+        mine = self.work.at[index, step]
+        if step:
+            add_rows(mine, [mine, self.from_x.at[index, step]], self.rows)
+            self.along[index, step] = self.copies.start(
+                remote(
+                    mine, self.from_z.at[index, step],
+                    self.send.at[1, index, step], self.recv.at[1, index, step], self.column[step],
+                )
+            )
+
+    def result(self, index, target):
+        terms = [self.work.at[index, 0], self.from_x.at[index, 0]]
+        for step in range(1, self.depth):
+            self.copies.arrived(self.along[index, step])
+            terms.append(self.from_z.at[index, step])
+        add_rows(target, terms, self.rows)
+
+
+def gradients_kernel(
+    depth, rows, local, hidden, matrices, *refs,
+):
+    parts, refs = refs[:matrices], refs[matrices:]
+    (
+        normed_part, tokens_ref, state_cot, scale_ref, gain_ref, out_ref, vector_ref,
+        normed_ref, grad_ref, gated_ref, gate_grad_ref, up_grad_ref,
+    ) = refs[:12]
+    sums, refs = refs[12 : 12 + matrices], refs[12 + matrices :]
+    (
+        input_grads, outputs, vector_sum,
+        gate_own, up_own, down_own, gate_other, up_other, down_other,
+        work, from_x, from_z, partial, from_pair, from_y, normed_grad, low, vectors, vector_in, vector_mid, vector_turn,
+        tiles, turned, acts, gated_turned, near, far, near_down, far_down,
+        e_load, e_send, e_recv, t_send, t_recv, g_send, g_recv, o_send, o_recv, v_send, v_recv, u_send, u_recv,
+        tile_load, act_load, save, pair_send, pair_recv, local_sem,
+    ) = refs
     z, x, y, core = place()
+    group = 2 * z + x
     sibling = device(z, x, y, 1 - core)
-    greet([sibling])
-    waits = []
-    for index in range(count):
-        copy = remote(ins[index].at[1 - core], outs[index], send.at[index], recv.at[index], sibling)
+    groups = [(step, turn) for step in range(depth) for turn in range(2) if step or turn]
+    peers = [device(swapped(z, step), swapped(x, turn), y, core) for step, turn in groups]
+    mates = [(z, x, swapped(y, turn // 2), swapped(core, turn % 2)) for turn in range(1, 4)]
+    greet(peers + [device(*mate) for mate in mates])
+    copies = Copies()
+    width = normed_ref.shape[1]
+    tile = 512
+    count = width // tile
+
+    def fetch(source, target, sem):
+        copy = pltpu.make_async_copy(source, target, sem)
         copy.start()
-        waits.append(copy)
-    for copy in waits:
+        return copy
+
+    experts = ExpertScatter(copies, parts, work, from_x, from_z, e_load, e_send, e_recv)
+    loaded = fetch(normed_part, partial, local_sem.at[0])
+    experts.begin(0)
+    loaded.wait()
+    scatter = TensorScatter(copies, partial, from_pair, from_y, t_send, t_recv)
+    scatter.begin()
+    out_gather = TensorGather(copies, out_ref, outputs, o_send, o_recv)
+    for index in range(1, matrices):
+        experts.begin(index)
+    act_copies = [fetch(gate_grad_ref, acts.at[0], act_load.at[0]), fetch(up_grad_ref, acts.at[1], act_load.at[1])]
+
+    def fetch_tile(number):
+        source = normed_ref if number < count else grad_ref
+        columns = pl.ds((number % count) * tile, tile)
+        return fetch(source.at[:, columns], tiles.at[number % 2], tile_load.at[number % 2])
+
+    tile_copies = [fetch_tile(0)]
+    saving = {}
+
+    def first_unit(owner):
+        return owner * local * hidden
+
+    def gate_and_up(number):
+        slot = number % 2
+        tile_copies[number].wait()
+        tile_copies.append(fetch_tile(number + 1))
+        turned[...] = tiles[slot].T
+        for copy, remote_one in saving.pop(slot, []):
+            copies.sent(copy) if remote_one else copy.wait()
+        for which in range(2):
+            for owner, target in ((1 - core, far), (core, near)):
+
+                @pl.loop(0, local)
+                def _(expert):
+                    columns = pl.ds(pl.multiple_of(first_unit(owner) + expert * hidden, hidden), hidden)
+                    target[which, slot, expert] = dot(turned[...], acts[which, :, columns]).astype(target.dtype)
+
+        saves = []
+        place_of = pl.ds(number * tile, tile)
+        for which, (own, other) in enumerate(((gate_own, gate_other), (up_own, up_other))):
+            away = remote(
+                far.at[which, slot], other.at[:, place_of], pair_send.at[which, number], pair_recv.at[which, number], sibling
+            )
+            copies.start(away)
+            saves.append((away, True))
+            saves.append((fetch(near.at[which, slot], own.at[:, place_of], save.at[which, slot]), False))
+        saving[slot] = saves
+
+    def down(number):
+        slot = number % 2
+        tile_copies[count + number].wait()
+        if number + 1 < count:
+            tile_copies.append(fetch_tile(count + number + 1))
+        for copy, remote_one in saving.pop(("down", slot), []):
+            copies.sent(copy) if remote_one else copy.wait()
+        for owner, target in ((1 - core, far_down), (core, near_down)):
+
+            @pl.loop(0, local)
+            def _(expert):
+                units = pl.ds(pl.multiple_of(first_unit(owner) + expert * hidden, hidden), hidden)
+                target[slot, expert] = dot(gated_turned[units, :], tiles[slot]).astype(target.dtype)
+
+        columns = pl.ds(number * tile, tile)
+        away = remote(
+            far_down.at[slot], down_other.at[:, :, columns], pair_send.at[2, number], pair_recv.at[2, number], sibling
+        )
+        copies.start(away)
+        saving["down", slot] = [
+            (away, True), (fetch(near_down.at[slot], down_own.at[:, :, columns], save.at[2, slot]), False)
+        ]
+
+    for copy in act_copies:
         copy.wait()
-
-
-def pair_swap(arrays, number):
-    count = len(arrays)
-    return pl.pallas_call(
-        functools.partial(pair_swap_kernel, count),
-        out_shape=tuple(jax.ShapeDtypeStruct(a.shape[1:], a.dtype) for a in arrays),
-        in_specs=[ANY] * count,
-        out_specs=(ANY,) * count,
-        scratch_shapes=[dma(count), dma(count)],
-        compiler_params=comm_params(number),
-    )(*arrays)
-
-
-def tensor_scatter_kernel(rows, p_ref, o_ref, work, from_pair, from_y, load, send, recv):
-    z, x, y, core = place()
-    sibling, over_y = device(z, x, y, 1 - core), device(z, x, 1 - y, core)
-    greet([sibling, over_y])
-    fetch = pltpu.make_async_copy(p_ref, work, load.at[0])
-    fetch.start()
-    pairs = []
-    for turn in (1, 0):
-        row = swapped(y, turn)
-        copy = remote(p_ref.at[row, 1 - core], from_pair.at[turn], send.at[turn], recv.at[turn], sibling)
-        copy.start()
-        pairs.append(copy)
-    fetch.wait()
-    pairs[0].wait_recv()
-    add_rows(work.at[1 - y, core], [work.at[1 - y, core], from_pair.at[1]], rows)
-    across = remote(work.at[1 - y, core], from_y, send.at[2], recv.at[2], over_y)
-    across.start()
-    pairs[1].wait_recv()
-    across.wait_recv()
-    add_rows(o_ref, [work.at[y, core], from_pair.at[0], from_y], rows)
-    for copy in pairs + [across]:
-        copy.wait_send()
-
-
-def tensor_scatter(parts, number):
-    rows, width = parts.shape[0] // 4, parts.shape[1]
-    shaped = parts.reshape(2, 2, rows, width)
-    return pl.pallas_call(
-        functools.partial(tensor_scatter_kernel, rows),
-        out_shape=jax.ShapeDtypeStruct((rows, width), FULL),
-        in_specs=[ANY],
-        out_specs=VMEM,
-        scratch_shapes=[
-            pltpu.VMEM(shaped.shape, parts.dtype),
-            pltpu.VMEM((2, rows, width), parts.dtype),
-            pltpu.VMEM((rows, width), parts.dtype),
-            dma(1), dma(3), dma(3),
+    gate_and_up(0)
+    scatter.cross()
+    experts.climb(0, experts.order[0])
+    gate_and_up(1)
+    out_gather.cross()
+    experts.climb(0, experts.order[1])
+    scatter.result(normed_grad)
+
+    inputs = tokens_ref[...].astype(FULL)
+    factor, gain = scale_ref[:, 0:1], gain_ref[0:1, :]
+    normed = normed_grad[...]
+    inner = jnp.sum(normed * gain * inputs, axis=-1, keepdims=True)
+    low[...] = (
+        state_cot[...] + factor * gain * normed - inputs * (factor * factor * factor) * inner * (1.0 / width)
+    ).astype(LOW)
+    gain_grad = jnp.sum(normed * inputs * factor, axis=0, keepdims=True)
+    grad_gather = TensorGather(copies, low, input_grads, g_send, g_recv)
+    vectors[...] = vector_ref[...]
+    slice_width = vectors.shape[2]
+    for index in range(vectors.shape[0]):
+        vectors[index, 16:17, :] = gain_grad[:, index * slice_width : (index + 1) * slice_width]
+    vector_copies = []
+    for number, ((step, turn), peer) in enumerate(zip(groups, peers)):
+        to = 2 * swapped(z, step) + swapped(x, turn)
+        vector_copies.append(
+            copies.start(remote(vectors.at[to], vector_in.at[number], v_send.at[number], v_recv.at[number], peer))
+        )
+
+    for step in experts.order[2:]:
+        experts.climb(0, step)
+    gate_and_up(2)
+    for step in experts.order[:2]:
+        experts.climb(1, step)
+    grad_gather.cross()
+    gate_and_up(3)
+    for copy in vector_copies:
+        copies.arrived(copy)
+    total = vectors[group]
+    for number in range(len(peers)):
+        total = total + vector_in[number]
+    vector_mid[...] = total
+    turn_copies = [
+        copies.start(remote(vector_mid, vector_turn.at[number], u_send.at[number], u_recv.at[number], device(*mate)))
+        for number, mate in enumerate(mates)
+    ]
+    for step in experts.order[2:]:
+        experts.climb(1, step)
+    gated_copy = fetch(gated_ref, acts.at[0], act_load.at[0])
+    gated_copy.wait()
+    for index in range(2):
+        half = pl.ds(index * local * hidden, local * hidden)
+        gated_turned[half, :] = acts[0, :, half].T
+    experts.result(0, sums[0])
+    down(0)
+    experts.climb(2, experts.order[0])
+    down(1)
+    for step in experts.order[1:]:
+        experts.climb(2, step)
+    down(2)
+    experts.result(1, sums[1])
+    down(3)
+    for copy in turn_copies:
+        copies.arrived(copy)
+    total = vector_mid[...]
+    for number in range(len(mates)):
+        total = total + vector_turn[number]
+    keep = lax.broadcasted_iota(jnp.int32, total.shape, 0) < 18
+    vector_sum[...] = jnp.where(keep, total, vector_mid[...])
+    for index in range(3, matrices):
+        for step in experts.order:
+            experts.climb(index, step)
+    for index in range(2, matrices):
+        experts.result(index, sums[index])
+    out_gather.finish()
+    grad_gather.finish()
+    for entries in saving.values():
+        for copy, remote_one in entries:
+            if not remote_one:
+                copy.wait()
+    copies.finish()
+
+
+def run_gradients(parts, normed_part, tokens, state_cot, scale, gain, out, vectors, normed, grads, gated, gate_grad, up_grad, local, number):
+    matrices = len(parts)
+    depth, _, piece, columns = parts[0].shape
+    rows, width = tokens.shape
+    seen, units = gated.shape
+    hidden = units // (2 * local)
+    tile = 512
+    sum_of = jax.ShapeDtypeStruct((piece, columns), FULL)
+    spread = jax.ShapeDtypeStruct((2, 2, rows, width), LOW)
+    wide, tall = (local, width, hidden), (local, hidden, width)
+    results = pl.pallas_call(
+        functools.partial(gradients_kernel, depth, rows, local, hidden, matrices),
+        out_shape=(sum_of,) * matrices
+        + (
+            spread, spread, jax.ShapeDtypeStruct(vectors.shape[1:], FULL),
+            jax.ShapeDtypeStruct(wide, FULL), jax.ShapeDtypeStruct(wide, FULL), jax.ShapeDtypeStruct(tall, FULL),
+            jax.ShapeDtypeStruct(wide, LOW), jax.ShapeDtypeStruct(wide, LOW), jax.ShapeDtypeStruct(tall, LOW),
+        ),
+        in_specs=[ANY] * (matrices + 1) + [VMEM] * 6 + [ANY] * 5,
+        out_specs=(VMEM,) * (matrices + 3) + (ANY,) * 6,
+        scratch_shapes=[pltpu.VMEM((matrices, depth, piece, columns), LOW)] * 3
+        + TensorScatter.scratch(rows, width)[:3]
+        + [
+            pltpu.VMEM((rows, width), FULL), pltpu.VMEM((rows, width), LOW),
+            pltpu.VMEM(vectors.shape, FULL), pltpu.VMEM((2 * depth - 1,) + vectors.shape[1:], FULL),
+            pltpu.VMEM(vectors.shape[1:], FULL), pltpu.VMEM((3,) + vectors.shape[1:], FULL),
+            pltpu.VMEM((2, seen, tile), LOW), pltpu.VMEM((tile, seen), LOW),
+            pltpu.VMEM((2, seen, units), LOW), pltpu.VMEM((units, seen), LOW),
+            pltpu.VMEM((2, 2, local, tile, hidden), FULL), pltpu.VMEM((2, 2, local, tile, hidden), LOW),
+            pltpu.VMEM((2, local, hidden, tile), FULL), pltpu.VMEM((2, local, hidden, tile), LOW),
+            dma(matrices, depth), dma(2, matrices, depth), dma(2, matrices, depth),
+            dma(3), dma(3), dma(4), dma(3), dma(4), dma(3),
+            dma(2 * depth - 1), dma(2 * depth - 1), dma(3), dma(3),
+            dma(2), dma(2), dma(3, 2), dma(3, width // tile), dma(3, width // tile), dma(1),
         ],
         compiler_params=comm_params(number),
-    )(shaped)
-
-
-def tensor_gather_kernel(x_ref, o_ref, send, recv, local):
-    z, x, y, core = place()
-    sibling, over_y = device(z, x, y, 1 - core), device(z, x, 1 - y, core)
-    greet([sibling, over_y])
-    own = pltpu.make_async_copy(x_ref, o_ref.at[y, core], local.at[0])
-    own.start()
-    across = remote(x_ref, o_ref.at[y, core], send.at[0], recv.at[0], over_y)
-    across.start()
-    near = remote(x_ref, o_ref.at[y, core], send.at[1], recv.at[1], sibling)
-    near.start()
-    across.wait_recv()
-    block = o_ref.at[1 - y, core]
-    passed = remote(block, block, send.at[2], recv.at[2], sibling)
-    passed.start()
-    own.wait()
-    across.wait_send()
-    near.wait()
-    passed.wait()
-
-
-def tensor_gather(block, number):
-    rows, width = block.shape
-    gathered = pl.pallas_call(
-        tensor_gather_kernel,
-        out_shape=jax.ShapeDtypeStruct((2, 2, rows, width), block.dtype),
-        in_specs=[VMEM],
-        out_specs=VMEM,
-        scratch_shapes=[dma(3), dma(3), dma(1)],
-        compiler_params=comm_params(number),
-    )(block)
-    return gathered.reshape(4 * rows, width)
-
-
-def expert_scatter_kernel(depth, rows, p_ref, o_ref, work, from_x, from_z, load, send, recv):
-    z, x, y, core = place()
-    over_x = device(z, 1 - x, y, core)
-    greet([over_x] + [device(swapped(z, step), x, y, core) for step in range(1, depth)])
-    order = [step for step in range(1, depth)] + [0]
-    sides, along, loads = {}, [], {}
-    for step in order:
-        at = swapped(z, step)
-        sides[step] = remote(p_ref.at[at, 1 - x], from_x.at[step], send.at[0, step], recv.at[0, step], over_x)
-        sides[step].start()
-        loads[step] = pltpu.make_async_copy(p_ref.at[at, x], work.at[step], load.at[step])
-        loads[step].start()
-    for step in order:
-        loads[step].wait()
-        sides[step].wait_recv()
-        if step:
-            add_rows(work.at[step], [work.at[step], from_x.at[step]], rows)
-            copy = remote(work.at[step], from_z.at[step], send.at[1, step], recv.at[1, step], device(swapped(z, step), x, y, core))
-            copy.start()
-            along.append(copy)
-    for copy in along:
-        copy.wait_recv()
-    add_rows(o_ref, [work.at[0], from_x.at[0]] + [from_z.at[step] for step in range(1, depth)], rows)
-    for copy in list(sides.values()) + along:
-        copy.wait_send()
-
-
-def expert_scatter(parts, depth, number):
-    rows, width = parts.shape[0] // (2 * depth), parts.shape[1]
-    shaped = parts.reshape(depth, 2, rows, width)
-    return pl.pallas_call(
-        functools.partial(expert_scatter_kernel, depth, rows),
-        out_shape=jax.ShapeDtypeStruct((rows, width), FULL),
-        in_specs=[ANY],
-        out_specs=VMEM,
-        scratch_shapes=[
-            pltpu.VMEM((depth, rows, width), parts.dtype),
-            pltpu.VMEM((depth, rows, width), parts.dtype),
-            pltpu.VMEM((depth, rows, width), parts.dtype),
-            dma(depth), dma(2, depth), dma(2, depth),
-        ],
-        compiler_params=comm_params(number),
-    )(shaped)
-
-
-def dot(left, right):
-    return jnp.dot(left, right, preferred_element_type=FULL)
-
-
-def dot_t(left, right):
-    return lax.dot_general(left, right, (((1,), (1,)), ((), ())), preferred_element_type=FULL)
-
-
-def t_dot(left, right):
-    return lax.dot_general(left, right, (((0,), (0,)), ((), ())), preferred_element_type=FULL)
+    )(*parts, normed_part, tokens, state_cot, scale, gain, out, vectors, normed, grads, gated, gate_grad, up_grad)
+    return results[:matrices], results[matrices:]
 
 
 def body(
@@ -1247,7 +1383,7 @@
     local_experts, _, hidden = w_gate.shape
     experts = local_experts * groups
     chain = LENGTH // row_count
-    if not (parts == 4 and groups % 2 == 0 and experts <= 2 * TOP and chain == 4 and 4 * row_count == LENGTH and WINDOW == 2 * row_count):
+    if not (parts == 4 and groups % 2 == 0 and experts <= min(16, 2 * TOP) and 2 * w_query.shape[1] <= 14 * HD and chain == 4 and 4 * row_count == LENGTH and WINDOW == 2 * row_count):
         return body_routed(
             tokens, documents, routes, norm1_gain, q_gain, k_gain, w_query, w_key, w_value, w_out, norm2_gain, router_w,
             w_gate, w_up, w_down, out_grad,
@@ -1311,18 +1447,6 @@
     all_normed, all_grad = all_normed.reshape(seen, width), all_grad.reshape(seen, width)
     gated, gate_pre_grad, up_pre_grad = (a.reshape(seen, units) for a in (gated, gate_pre_grad, up_pre_grad))
 
-    def expert_grads(left, right):
-        return t_dot(left, right)
-
-    gate_wgrad = expert_grads(all_normed, gate_pre_grad).reshape(width, 2, local_experts, hidden).transpose(1, 2, 0, 3)
-    up_wgrad = expert_grads(all_normed, up_pre_grad).reshape(width, 2, local_experts, hidden).transpose(1, 2, 0, 3)
-    down_wgrad = expert_grads(gated, all_grad).reshape(2, local_experts, hidden, width)
-    swaps = pair_swap([gate_wgrad, up_wgrad, down_wgrad], 8)
-    w_gate_grad, w_up_grad, w_down_grad = (
-        lax.dynamic_index_in_dim(mine, core, 0, keepdims=False) + other
-        for mine, other in zip((gate_wgrad, up_wgrad, down_wgrad), swaps)
-    )
-
     prob_cot = gate_cots[:, :, :local_experts].reshape(depth, 2, 2, local_experts, rows).sum(axis=2)
     plane = jnp.arange(depth, dtype=jnp.int32) ^ (group // 2)
     prob_cot = prob_cot[plane].reshape(experts, rows).T * picked
@@ -1338,8 +1462,6 @@
         state_cot.astype(LOW), queries, kv_all, attended, logs, key_docs, query_docs, w_out, produced, chain, 10
     )
     state_low = state_low.reshape(row_count, width)
-    output = tensor_gather((state + expert_mix).astype(LOW), 9)
-    w_out_grad = t_dot(state_low, attended)
     query_cot = query_cot.reshape(row_count, heads, HD)
     key_cot = kv_cot[:, : heads * HD].reshape(row_count, heads, HD)
     value_low = kv_cot[:, heads * HD :].astype(LOW)
@@ -1363,46 +1485,39 @@
         key_scale * key_gain * key_norm_cot - key_raw * key_scale**3 * inners[1][:, None] / width
     ).astype(LOW)
     normed_part = dot_t(query_raw_cot, w_query) + dot_t(key_raw_cot, w_key) + dot_t(value_low, w_value)
-    normed_one_grad = tensor_scatter(normed_part.astype(LOW), 12)
-    own_scale = quarter(scale_one)
-    norm1_grad = jnp.sum(normed_one_grad * own_inputs * own_scale, axis=0)
-    inner_one = jnp.sum(normed_one_grad * norm1_gain * own_inputs, axis=-1, keepdims=True)
-    input_grad = (
-        state_cot + own_scale * norm1_gain * normed_one_grad - own_inputs * own_scale**3 * inner_one / width
-    )
-    input_grad = tensor_gather(input_grad.astype(LOW), 13).astype(FULL)
-
-    local = jnp.concatenate(
-        [
-            t_dot(normed_one, query_raw_cot),
-            t_dot(normed_one, key_raw_cot),
-            t_dot(normed_one, value_low),
-            w_out_grad,
-        ],
-        axis=1,
-    ).astype(LOW)
-    summed = expert_scatter(local, depth, 14)
-    w_query_grad, w_key_grad, w_value_grad, w_out_grad = jnp.split(summed, 4, axis=1)
-    vectors = jnp.concatenate([router_grad, norm1_grad[None], norm2_grad[None]], axis=0)
-    vectors = lax.psum(lax.psum_scatter(vectors, "expert", scatter_dimension=1, tiled=True), "tensor")
-    gains = lax.psum_scatter(
-        jnp.concatenate([q_gain_local, k_gain_local], axis=0), "expert", scatter_dimension=1, tiled=True
-    )
+    pieces = [
+        t_dot(left, right).astype(LOW).reshape(depth, 2, width // groups, -1)
+        for left, right in (
+            (state_low, attended), (normed_one, value_low), (normed_one, query_raw_cot), (normed_one, key_raw_cot)
+        )
+    ]
+    vectors = jnp.concatenate(
+        [router_grad, jnp.zeros((17 - experts, width), FULL), norm2_grad[None]], axis=0
+    ).reshape(18, groups, width // groups).transpose(1, 0, 2)
+    gains = jnp.concatenate([q_gain_local, k_gain_local], axis=0)
+    gains = jnp.pad(gains, ((0, 14 - 2 * heads), (0, width // groups - HD)))
+    vectors = jnp.concatenate([vectors, jnp.broadcast_to(gains[None], (groups,) + gains.shape)], axis=1)
+    sums, (input_grad, output, vector_sum, gate_own, up_own, down_own, gate_other, up_other, down_other) = run_gradients(
+        pieces, normed_part.astype(LOW).reshape(2, 2, rows, width), quarter(tokens), state_cot, quarter(scale_one),
+        norm1_gain[None], (state + expert_mix).astype(LOW), vectors, all_normed, all_grad, gated, gate_pre_grad, up_pre_grad,
+        local_experts, 14,
+    )
+    own_columns = group * (HD // groups)
     return (
-        output,
-        input_grad,
-        vectors[experts],
-        gains[:heads],
-        gains[heads:],
-        w_query_grad,
-        w_key_grad,
-        w_value_grad,
-        w_out_grad.T,
-        vectors[experts + 1],
-        vectors[:experts].T,
-        w_gate_grad,
-        w_up_grad,
-        w_down_grad,
+        output.reshape(row_count, width),
+        input_grad.reshape(row_count, width).astype(FULL),
+        vector_sum[16],
+        lax.dynamic_slice(vector_sum, (18, own_columns), (heads, HD // groups)),
+        lax.dynamic_slice(vector_sum, (18 + heads, own_columns), (heads, HD // groups)),
+        sums[2],
+        sums[3],
+        sums[1],
+        sums[0].T,
+        vector_sum[17],
+        vector_sum[:experts].T,
+        gate_own + gate_other.astype(FULL),
+        up_own + up_other.astype(FULL),
+        down_own + down_other.astype(FULL),
     )
 
 

time: 945 us -> 787 us (0.83)
  Pallas kernels: 678 us -> 613 us
  matrix products: 74.2 us -> 31.6 us
  local copies, waits for them, and re-layouts: 60 us -> 44.6 us
  other arithmetic: 59.4 us -> 45.4 us
  between operations: 15.1 us -> 1.62 us
  blocking collectives: 48.1 us -> 37 us
    pallas_call x5 -> x1, Pallas kernels: 225 us -> 161 us  [run_gradients(): pl.pallas_call(functools.partial(gradients_kernel, depth, rows, local, hi...]
    dot_general x7 -> x4, matrix products: 53.4 us -> 10.9 us  [t_dot(): lax.dot_general(left, right, (((0,), (0,)), ((), ())), preferred_element_...]
    dot_general x4 -> x0, local copies, waits for them, and re-layouts: 22.1 us -> none  [t_dot(): lax.dot_general(left, right, (((0,), (0,)), ((), ())), preferred_element_...]
    psum x1 -> x0, blocking collectives: 11.1 us -> none  [body(): lax.psum(lax.psum_scatter(vectors, 'expert', scatter_dimension=1, tiled=T...]
  transfers between devices with their start and end apart: 2 -> 0, of which waited for: 0 -> 0; matrix products, arithmetic and copies ran while one was open for 13% -> 0% of each run, Pallas kernels for 24% -> 0%
where the time goes in v4:
time: 787 us; the launch traced here: 774 us
  Pallas kernels  613 us (78%)
  other arithmetic  45.4 us (6%)
  local copies, waits for them, and re-layouts  44.6 us (6%)
  blocking collectives  37 us (5%)
  matrix products  31.6 us (4%)
    pallas_call x1, Pallas kernels, run_experts(): pl.pallas_call(functools.partial(experts_kernel, depth, rows, local, hidd...  207 us
    pallas_call x1, Pallas kernels, run_gradients(): pl.pallas_call(functools.partial(gradients_kernel, depth, rows, local, hi...  161 us
    pallas_call x1, Pallas kernels, run_attention(): pl.pallas_call(functools.partial(attention_kernel, depth, rows, heads, ch...  129 us
    pallas_call x1, Pallas kernels, run_attention_back(): pl.pallas_call(functools.partial(attention_back_kernel, depth, rows, head...  117 us
    all_gather x1, blocking collectives, body(): lax.all_gather(documents, 'expert', tiled=True)  25 us

profile of v4, /device:TPU:10, one launch (start us, length us, event | category | flops | bytes accessed | tf_op | source)
XLA Modules:
  0.0 773.7 jit_solution(526897726370657372)
XLA Ops:
  1.4 2.1 fusion
  5.5 25.0 %all-gather = s32[8,1,512]{2,1,0:T(1,128)S(1)} all-gather(s32[1,1,512]{2,1,0:T(1,128)S(1)} %bitcast.155), channel_id=1, replica_groups=mesh['expert'=8,'tensor'=4] {'expert'}, dimensions={0}, use_global_device_ids=true | all-gather | bytes 18432 | tf_op jit(solution)/shard_map/all_gather | solution.py:1420
  32.6 4.3 convolution_convert_fusion.4
  41.2 2.4 multiply_reduce_fusion.7
  45.2 4.6 multiply_reduce_fusion.8
  49.8 5.7 psum.14
  56.1 2.5 copy.72
  58.6 2.4 multiply_multiply_fusion.1
  61.0 2.5 reshape.290
  64.6 2.5 reshape.291
  67.2 3.4 slice_negate_fusion.2
  74.3 128.8 %shard_map.263 = (bf16[3,512,1024]{2,1,0:T(8,128)(2,1)}, bf16[512,512]{1,0:T(8,128)(2,1)}, f32[4,8,512]{2,1,0:T(8,128)}, f32[128,2048]{1,0:T(8,128)}, bf16[4,512,2048]{2,1,0:T(8,128)(2,1)}) custom-call(bf16[512,512]{1,0:T(8,128)(2,1)} %get-tuple-element.149.query_ref, bf16[512,1024]{1,0:T(8,128)(2,1)} %pad_maximum_fusion.kv_ref, ...), custom_call_target="tpu_custom_call" | custom-call | tf_op jit(solution)/shard_map/pallas_call | solution.py:952
  203.2 2.3 multiply_reduce_fusion.6
  207.7 206.9 %shard_map.264 = (f32[128,2048]{1,0:T(8,128)}, f32[4,4,8,128]{3,2,1,0:T(8,128)}, bf16[4,512,2048]{2,1,0:T(8,128)(2,1)}, bf16[4,512,1024]{2,1,0:T(8,128)(2,1)}, b...) custom-call(bf16[128,2048]{1,0:T(8,128)(2,1)} %copy-done.8, ...), custom_call_target="tpu_custom_call" | custom-call | tf_op jit(solution)/shard_map/pallas_call | solution.py:743
  417.6 2.6 multiply_reduce_fusion.2
  421.0 2.6 fusion.36
  423.6 117.1 %shard_map.265 = (bf16[2,2,128,2048]{3,2,1,0:T(8,128)(2,1)}, f32[512,512]{1,0:T(8,128)}, f32[512,1024]{1,0:T(8,128)}, f32[128,2048]{1,0:T(8,128)}) custom-call(bf16[128,2048]{1,0:T(8,128)(2,1)} %get-tuple-element.136.low_ref, bf16[512,512]{1,0:T(8,128)(2,1)} %get-tuple-element.149.query_ref, bf16[3,512,1024]{2,1,0:T(8,128)(2,1)} %get-tuple-element.47.kv_all, ...), custom_call_target="tpu_custom_call" | custom-call | tf_op jit(solution)/shard_map/pallas_call | solution.py:1069
  540.8 2.6 add_convert_fusion.1.refs_9_
  543.4 2.6 convolution_convert_fusion.3
  546.0 2.6 reshape.298
  548.6 2.3 slice.65
  550.9 2.5 reshape.299
  557.9 2.8 convolution_convert_fusion.2
  565.2 6.4 psum.15
  575.1 2.7 convolution_convert_fusion.1
  577.8 2.7 convolution_convert_fusion
  584.4 2.6 add_convert_fusion
  587.0 160.6 %shard_map.266 = (f32[256,512]{1,0:T(8,128)}, f32[256,512]{1,0:T(8,128)}, f32[256,512]{1,0:T(8,128)}, f32[256,512]{1,0:T(8,128)}, bf16[2,2,128,2048]{3,2,1,0:T(8...) custom-call(bf16[4,2,256,512]{3,2,1,0:T(8,128)(2,1)} %bitcast.116, ...), custom_call_target="tpu_custom_call" | custom-call | tf_op jit(solution)/shard_map/pallas_call | solution.py:1347
  753.7 4.3 bitcast_convert_fusion
  758.0 2.5 convert_add_fusion.2
  762.4 2.5 convert_add_fusion.1
  766.8 2.7 convert_add_fusion
  (154 shorter events, 51.7 us)
Async XLA Ops:
  0.6 40.6 %copy-start = (bf16[2048,512]{1,0:T(8,128)(2,1)S(1)}, bf16[2048,512]{1,0:T(8,128)(2,1)}, u32[]{:S(2)}) copy-start(bf16[2048,512]{1,0:T(8,128)(2,1)} %param.23) | copy-start | bytes 6291460
  0.7 31.9 %copy-start.37 = (f32[2048]{0:T(1024)S(1)}, f32[2048]{0:T(1024)}, u32[]{:S(2)}) copy-start(f32[2048]{0:T(1024)} %param.19) | copy-start | bytes 24580
  0.7 4.2 copy-start.36
  3.5 41.7 %copy-start.41 = (f32[512]{0:T(512)}, f32[512]{0:T(512)S(1)}, u32[]{:S(2)}) copy-start(f32[512]{0:T(512)S(1)} %add_rsqrt_fusion) | copy-start | bytes 6148
  36.9 4.4 copy-start.16
  49.8 8.8 %copy-start.34 = (f32[4,128]{1,0:T(4,128)S(1)}, f32[4,128]{1,0:T(4,128)}, u32[]{:S(2)}) copy-start(f32[4,128]{1,0:T(4,128)} %param.20) | copy-start | bytes 6148
  58.6 4.9 copy-start.33
  203.2 3.4 copy-start.32
  203.2 3.6 copy-start.31
  416.2 4.0 copy-start.43
  417.6 3.4 copy-start.5
  417.6 3.4 copy-start.40
  417.6 3.4 copy-start.44
  540.7 2.6 copy-start.26
  540.7 2.6 copy-start.45
  556.2 1.7 copy-start.9
  556.2 1.7 copy-start.38
  561.5 1.8 copy-start.11
  563.4 8.3 %copy-start.35 = (f32[512]{0:T(512)S(1)}, f32[512]{0:T(512)}, u32[]{:S(2)}) copy-start(f32[512]{0:T(512)} %multiply_multiply_fusion.2) | copy-start | bytes 6148
  571.6 1.7 copy-start.3
  571.6 1.9 copy-start.12
  571.7 2.2 copy-start.25
  573.3 1.7 copy-start.18
  582.2 2.2 copy-start.24
  753.7 4.3 copy-start.15
  753.7 4.3 copy-start.21
  758.0 3.7 copy-start.14
  758.0 4.4 copy-start.20
  762.4 3.7 copy-start.13
  762.4 4.4 copy-start.19
  766.8 2.7 copy-start.22
  769.5 2.2 copy-start.28
  (14 other events, 18.6 us)

commit v5 on v4

--- a/solution.py
+++ b/solution.py
@@ -495,6 +495,10 @@
     def begin(self):
         self.spread(0)
         for step in range(1, len(self.column)):
+            self.lift(step)
+
+    def lift(self, step):
+        if 0 < step < len(self.column):
             self.along[step] = self.copies.start(
                 remote(self.block, self.at(step, self.here, None), self.z_send.at[step], self.z_recv.at[step], self.column[step])
             )
@@ -844,62 +848,188 @@
         key = index * 128 + lax.broadcasted_iota(jnp.int32, (128, length), 0) - (blocks - 1) * length
         query = lax.broadcasted_iota(jnp.int32, (128, length), 1)
         seen = (key_docs[part, :] == query_docs[0:1, :]) & (key <= query) & (query - key < WINDOW)
-        bias[part, :] = jnp.where(seen, 0.0, -1e30)
+        bias[part, :] = jnp.where(seen, 0.0, -1e30).astype(bias.dtype)
+
+
+def exchange(copies, mine, landed, send, recv, mates):
+    return [
+        copies.start(remote(mine, landed.at[number], send.at[number], recv.at[number], device(*mate)))
+        for number, mate in enumerate(mates)
+    ]
+
+
+def mates_of():
+    z, x, y, core = place()
+    return [(z, x, swapped(y, turn // 2), swapped(core, turn % 2)) for turn in range(1, 4)]
+
+
+def as_rows(columns):
+    lanes = lax.broadcasted_iota(jnp.int32, (columns[0].shape[0], 128), 1)
+    wide = jnp.zeros(lanes.shape, FULL)
+    for index, column in enumerate(columns):
+        wide = jnp.where(lanes == index, column, wide)
+    return wide.T[:8]
+
+
+def as_columns(rows_of_eight):
+    length = rows_of_eight.shape[1]
+    return jnp.concatenate([rows_of_eight, jnp.zeros((120, length), FULL)], axis=0).T
 
 
 def attention_kernel(
-    depth, rows, heads, chain,
-    query_ref, kv_ref, key_docs, query_docs, w_out, grad_ref,
-    kv_all, attended, logs, sum_ref, all_grad,
-    scores, bias, partial, from_pair, from_y, t_send, t_recv,
-    z_send, z_recv, p_send, p_recv, h_send, h_recv, local,
+    depth, rows, heads, chain, local,
+    tokens_ref, wq_ref, wk_ref, wv_ref, wo_ref, grad_ref,
+    gain1_ref, q_gain_ref, k_gain_ref, cosine_ref, sine_ref, docs_ref, gain2_ref, router_ref, picked_ref,
+    normed_turned, q_raw, k_raw, queries, kv_all, key_docs, scales, attended, logs, state_ref, normed2_ref, probs_ref, gates_ref,
+    all_grad,
+    tokens, normed_ref, wq, wk, wv, wo, docs_in, squares, squares_in, scores, bias, partial, from_pair, from_y, sum_ref,
+    t_send, t_recv, z_send, z_recv, p_send, p_recv, h_send, h_recv, q_send, q_recv, load,
 ):
     z, x, y, core = place()
     group, part = lax.axis_index("expert"), lax.axis_index("tensor")
     spot = group % chain
-    greet(partners_of(depth))
+    length, width = tokens.shape
+    wide = heads * HD
+    scale = HD ** (-0.5)
+    loads = []
+    for number, (source, target) in enumerate([(tokens_ref, tokens), (wv_ref, wv), (wk_ref, wk), (wq_ref, wq), (wo_ref, wo)]):
+        loads.append(pltpu.make_async_copy(source, target, load.at[number]))
+        loads[-1].start()
+    mates = mates_of()
+    z1, x1 = swapped(z, 1), 1 - x
+    greet(
+        [device(swapped(z, step), x, y, core) for step in range(1, depth)]
+        + [device(z, x1, y, core), device(z1, x1, y, core)]
+        + [device(*mate) for mate in mates]
+    )
     copies = Copies()
-    length = kv_ref.shape[0]
-    scale = HD ** (-0.5)
-
-    def halo_copy(distance, to):
-        return remote(kv_ref, kv_all.at[2 - distance], h_send.at[distance], h_recv.at[distance], (to, part))
-
+    gather = Gather(copies, grad_ref, all_grad, rows, z_send, z_recv, p_send, p_recv)
+    gather.spread(0)
+    gather.lift(1)
+    own = pltpu.make_async_copy(grad_ref, gather.at(0, gather.here, None), load.at[5])
+    own.start()
+    key_part, value_part = pl.ds(0, wide), pl.ds(wide, wide)
+
+    def halo_copy(kind, distance, to):
+        if kind == 2:
+            return remote(docs_ref, docs_in.at[2 - distance], h_send.at[kind, distance], h_recv.at[kind, distance], (to, part))
+        columns = (key_part, value_part)[kind]
+        return remote(
+            kv_all.at[2, :, columns], kv_all.at[2 - distance, :, columns],
+            h_send.at[kind, distance], h_recv.at[kind, distance], (to, part),
+        )
+
+    def halo_start(kind):
+        for distance in (1, 2):
+
+            @pl.when(spot < chain - distance)
+            def _():
+                halo_copy(kind, distance, group + distance).start()
+
+    def halo_arrive(kind, distance):
+        @pl.when(spot >= distance)
+        def _():
+            halo_copy(kind, distance, group - distance).wait_recv()
+
+        @pl.when(spot < distance)
+        def _():
+            if kind == 2:
+                docs_in[2 - distance] = jnp.full_like(docs_ref, -1)
+            else:
+                columns = (key_part, value_part)[kind]
+                kv_all[2 - distance, :, columns] = jnp.zeros((length, wide), LOW)
+
+    halo_start(2)
+    loads[0].wait()
+
+    @pl.loop(0, length // 128)
+    def _(index):
+        part_rows = pl.ds(pl.multiple_of(index * 128, 128), 128)
+        values = tokens[part_rows, :].astype(FULL)
+        factor = lax.rsqrt(jnp.mean(values * values, axis=-1, keepdims=True) + NORM_EPSILON)
+        normed_ref[part_rows, :] = (values * factor * gain1_ref[0:1, :]).astype(LOW)
+
+    def project(weights, store):
+        @pl.loop(0, wide // 256)
+        def _(index):
+            columns = pl.ds(pl.multiple_of(index * 256, 256), 256)
+            store(index, columns, dot(normed_ref[...], weights[:, columns]))
+
+    def keep_value(index, columns, result):
+        kv_all[2, :, pl.ds(pl.multiple_of(wide + index * 256, 256), 256)] = result.astype(LOW)
+
+    def keep_key(index, columns, result):
+        k_raw[:, columns] = result
+
+    def keep_query(index, columns, result):
+        q_raw[:, columns] = result
+
+    loads[2].wait()
+    project(wk, keep_key)
+    loads[3].wait()
+    project(wq, keep_query)
+    squares[...] = as_rows(
+        [jnp.sum(q_raw[...] * q_raw[...], axis=-1, keepdims=True), jnp.sum(k_raw[...] * k_raw[...], axis=-1, keepdims=True)]
+    )
+    sent = exchange(copies, squares, squares_in, q_send, q_recv, mates)
+    loads[1].wait()
+    project(wv, keep_value)
+    halo_start(1)
+
+    @pl.loop(0, width // 256)
+    def _(index):
+        columns = pl.ds(pl.multiple_of(index * 256, 256), 256)
+        normed_turned[columns, :] = normed_ref[:, columns].T
+
+    for copy in sent:
+        copies.arrived(copy)
+    total = squares[...]
+    for number in range(3):
+        total = total + squares_in[number]
+    scales[...] = lax.rsqrt(total * (1.0 / width) + NORM_EPSILON)
+    factors = as_columns(scales[...])
+
+    def turn_heads(raw, gain_ref, factor, store):
+        for head in range(heads):
+            columns = pl.ds(head * HD, HD)
+            normed = raw[:, columns] * factor * gain_ref[0:1, columns]
+            store(head, (normed * cosine_ref[...] + pltpu.roll(normed, HD // 2, 1) * sine_ref[...]).astype(LOW))
+
+    def store_key(head, turned):
+        kv_all[2, :, pl.ds(head * HD, HD)] = turned
+
+    def store_query(head, turned):
+        queries[:, pl.ds(head * HD, HD)] = turned
+
+    turn_heads(k_raw, k_gain_ref, factors[:, 1:2], store_key)
+    halo_start(0)
+    gather.turn(0)
+    gather.spread(1)
+    gather.lift(2)
+    turn_heads(q_raw, q_gain_ref, factors[:, 0:1], store_query)
     for distance in (1, 2):
-
-        @pl.when(spot < chain - distance)
-        def _():
-            halo_copy(distance, group + distance).start()
-
-    gather = Gather(copies, grad_ref, all_grad, rows, z_send, z_recv, p_send, p_recv)
-    gather.begin()
-    own = pltpu.make_async_copy(grad_ref, gather.at(0, gather.here, None), local.at[0])
-    own.start()
-    kv_all[2] = kv_ref[...]
-    mask_bias(bias, key_docs, query_docs, length)
+        halo_arrive(2, distance)
+    for block in range(3):
+        rows_of = docs_in[block] if block < 2 else docs_ref[...]
+        key_docs[pl.ds(block * length, length), :] = rows_of.astype(FULL).T[:, 0:1].astype(jnp.int32)
+    mask_bias(bias, key_docs, docs_ref, length)
 
     def score(block):
         @pl.loop(0, heads)
         def _(head):
             columns = pl.ds(pl.multiple_of(head * HD, HD), HD)
             keys = pl.ds(block * length, length)
-            scores[head, keys, :] = dot_t(kv_all[block, :, columns], query_ref[:, columns]) * scale + bias[keys, :]
+            scores[head, keys, :] = dot_t(kv_all[block, :, columns], queries[:, columns]) * scale + bias[keys, :]
 
     score(2)
-    gather.turn(0)
+    gather.turn(1)
+    gather.spread(2)
+    gather.lift(3)
     for distance in (1, 2):
-
-        @pl.when(spot >= distance)
-        def _():
-            halo_copy(distance, group - distance).wait_recv()
-
-        @pl.when(spot < distance)
-        def _():
-            kv_all[2 - distance] = jnp.zeros_like(kv_ref)
-
+        halo_arrive(0, distance)
         score(2 - distance)
-    if depth > 1:
-        gather.spread(1)
+    for distance in (1, 2):
+        halo_arrive(1, distance)
 
     @pl.loop(0, heads)
     def _(head):
@@ -919,78 +1049,148 @@
         attended[:, columns] = mixed.T.astype(LOW)
         logs[head] = jnp.broadcast_to(highest + jnp.log(total), (8, length))
 
-    if depth > 1:
-        gather.turn(1)
-    if depth > 2:
-        gather.spread(2)
+    gather.turn(2)
+    gather.spread(3)
+    loads[4].wait()
     for index in range(4):
-        partial[index // 2, index % 2] = dot(attended[pl.ds(index * rows, rows), :], w_out[...]).astype(LOW)
+        partial[index // 2, index % 2] = dot(attended[pl.ds(index * rows, rows), :], wo[...]).astype(LOW)
     scatter = TensorScatter(copies, partial, from_pair, from_y, t_send, t_recv)
     scatter.begin()
     scatter.cross()
-    if depth > 2:
-        gather.turn(2)
-    for step in range(3, depth):
-        gather.spread(step)
+    gather.turn(3)
     scatter.result(sum_ref)
-    for step in range(3, depth):
-        gather.turn(step)
+    own_rows = pl.ds(pl.multiple_of(part * rows, rows), rows)
+    state = tokens[own_rows, :].astype(FULL) + sum_ref[...]
+    state_ref[...] = state
+    factor = lax.rsqrt(jnp.mean(state * state, axis=-1, keepdims=True) + NORM_EPSILON)
+    normed2_ref[...] = (state * factor * gain2_ref[0:1, :]).astype(LOW)
+    logits = dot(normed2_ref[...], router_ref[...])
+    experts = gates_ref.shape[0] * local
+    lanes = lax.broadcasted_iota(jnp.int32, logits.shape, 1)
+    logits = jnp.where(lanes < experts, logits, -1e30)
+    weights = jnp.exp(logits - jnp.max(logits, axis=-1, keepdims=True))
+    probs = weights / jnp.sum(weights, axis=-1, keepdims=True)
+    probs_ref[...] = probs
+    gates = (probs * picked_ref[...]).T
+    gates_ref[...] = jnp.zeros_like(gates_ref)
+    for index in range(gates_ref.shape[0]):
+        gates_ref[index, 0:local, :] = gates[index * local : (index + 1) * local]
     own.wait()
-    for distance in (1, 2):
-
-        @pl.when(spot < chain - distance)
-        def _():
-            halo_copy(distance, group + distance).wait_send()
+    for kind in range(3):
+        for distance in (1, 2):
+
+            @pl.when(spot < chain - distance)
+            def _():
+                halo_copy(kind, distance, group + distance).wait_send()
 
     copies.finish()
 
 
-def run_attention(queries, kv, key_docs, query_docs, w_out, grads, depth, chain, number):
-    length, wide = kv.shape
-    heads = wide // (2 * HD)
-    rows, width = grads.shape
+def run_attention(tokens, weights, grads, gains, tables, docs, gain2, router, picked, depth, chain, local, number):
+    length, width = tokens.shape
+    rows = grads.shape[0]
+    wide = weights[0].shape[1]
+    heads = wide // HD
     return pl.pallas_call(
-        functools.partial(attention_kernel, depth, rows, heads, chain),
+        functools.partial(attention_kernel, depth, rows, heads, chain, local),
         out_shape=(
-            jax.ShapeDtypeStruct((3, length, wide), LOW),
-            jax.ShapeDtypeStruct(queries.shape, LOW),
+            jax.ShapeDtypeStruct((width, length), LOW),
+            jax.ShapeDtypeStruct((length, wide), FULL),
+            jax.ShapeDtypeStruct((length, wide), FULL),
+            jax.ShapeDtypeStruct((length, wide), LOW),
+            jax.ShapeDtypeStruct((3, length, 2 * wide), LOW),
+            jax.ShapeDtypeStruct((3 * length, 1), jnp.int32),
+            jax.ShapeDtypeStruct((8, length), FULL),
+            jax.ShapeDtypeStruct((length, wide), LOW),
             jax.ShapeDtypeStruct((heads, 8, length), FULL),
             jax.ShapeDtypeStruct((rows, width), FULL),
+            jax.ShapeDtypeStruct((rows, width), LOW),
+            jax.ShapeDtypeStruct((rows, 128), FULL),
+            jax.ShapeDtypeStruct((2 * depth, 8, rows), FULL),
             jax.ShapeDtypeStruct((depth, 4 * rows, width), LOW),
         ),
-        in_specs=[VMEM] * 5 + [ANY],
-        out_specs=(VMEM, VMEM, VMEM, VMEM, ANY),
-        scratch_shapes=[pltpu.VMEM((heads, 3 * length, length), FULL), pltpu.VMEM((3 * length, length), FULL)]
-        + TensorScatter.scratch(rows, width)
-        + [dma(depth), dma(depth), dma(depth, 6), dma(depth, 6), dma(3), dma(3), dma(1)],
+        in_specs=[ANY] * 6 + [VMEM] * 9,
+        out_specs=(VMEM,) * 13 + (ANY,),
+        scratch_shapes=[
+            pltpu.VMEM(tokens.shape, LOW), pltpu.VMEM(tokens.shape, LOW), pltpu.VMEM((width, wide), LOW), pltpu.VMEM((width, wide), LOW),
+            pltpu.VMEM((width, wide), LOW), pltpu.VMEM((wide, width), LOW), pltpu.VMEM((2, 8, length), jnp.int32),
+            pltpu.VMEM((8, length), FULL), pltpu.VMEM((3, 8, length), FULL),
+            pltpu.VMEM((heads, 3 * length, length), FULL), pltpu.VMEM((3 * length, length), FULL),
+        ]
+        + TensorScatter.scratch(rows, width)[:3]
+        + [
+            pltpu.VMEM((rows, width), FULL), dma(3), dma(3),
+            dma(depth), dma(depth), dma(depth, 6), dma(depth, 6), dma(3, 3), dma(3, 3), dma(3), dma(3), dma(6),
+        ],
         compiler_params=comm_params(number),
-    )(queries, kv, key_docs, query_docs, w_out, grads)
+    )(tokens, *weights, grads, *gains, *tables, docs, gain2, router, picked)
 
 
 def attention_back_kernel(
-    depth, rows, heads, chain,
-    low_ref, query_ref, kv_all, attended, logs, key_docs, query_docs, w_out, produced_ref,
-    lows, query_cot, kv_cot, mix_ref,
-    bias, cots, deltas, turned, sending, landed, work,
-    diagonal, from_x, from_y, from_z, r_send, r_recv, t_send, t_recv, h_send, h_recv, load,
+    depth, rows, heads, chain, local,
+    sum_ref, gate_cots, probs_ref, picked_ref, state_ref, gain2_ref, router_ref, normed2_ref, grad_ref,
+    query_ref, kv_all, attended, logs, key_docs, query_docs, q_raw, k_raw, q_gain_ref, k_gain_ref, cosine_ref, sine_ref, scales,
+    w_out, produced_ref, normed_ref, wq_ref, wk_ref, wv_ref,
+    state_cot_ref, router_grad_ref, norm2_grad_ref, q_grad_ref, k_grad_ref, mix_ref, normed_part, piece0, piece1, piece2, piece3,
+    low, lows, by_expert, bias, cots, deltas, turned, query_cot, kv_cot, sending, landed, work, raw_cots, flipped, wq, wk, wv,
+    inners, inners_in, staging,
+    diagonal, from_x, from_y, from_z, r_send, r_recv, t_send, t_recv, h_send, h_recv, i_send, i_recv, load, saves,
 ):
+    z, x, y, core = place()
     group, part = lax.axis_index("expert"), lax.axis_index("tensor")
     spot = group % chain
-    greet(partners_of(depth))
-    copies = Copies()
-    length = query_ref.shape[0]
+    length, width = query_ref.shape[0], w_out.shape[1]
+    wide = heads * HD
     scale = HD ** (-0.5)
-    wide = heads * HD
-    gather = TensorGather(copies, low_ref, lows, t_send, t_recv)
-    order = [step for step in range(1, depth)] + [0]
+    order = [step for step in range(depth - 1, 0, -1)] + [0]
     loads = {}
     for step in order:
         loads[step] = pltpu.make_async_copy(produced_ref.at[step], work.at[step], load.at[step])
         loads[step].start()
+    others = []
+    for number, (source, target) in enumerate([(wq_ref, wq), (wk_ref, wk), (wv_ref, wv)]):
+        others.append(pltpu.make_async_copy(source, target, load.at[depth + number]))
+        others[-1].start()
+    mates = mates_of()
+    greet(
+        [device(swapped(z, step), x, y, core) for step in range(1, depth)]
+        + [device(z, 1 - x, y, core), device(swapped(z, 1), 1 - x, y, core)]
+        + [device(*mate) for mate in mates]
+    )
+    copies = Copies()
+
+    by_expert[...] = jnp.zeros_like(by_expert)
+    for plane in range(depth):
+        step = swapped(z, plane)
+        for column in range(2):
+            first = (2 * plane + column) * local
+            by_expert[first : first + local, :] = (gate_cots[step, 2 * column] + gate_cots[step, 2 * column + 1])[:local]
+    probs = probs_ref[...]
+    prob_cot = by_expert[...].T * picked_ref[...]
+    logit_cot = probs * (prob_cot - jnp.sum(probs * prob_cot, axis=-1, keepdims=True))
+    normed2_cot = sum_ref[...] + lax.dot_general(
+        logit_cot, router_ref[...].astype(FULL), (((1,), (1,)), ((), ())),
+        precision=HIGHEST_PRECISION, preferred_element_type=FULL,
+    )
+    state = state_ref[...]
+    factor = lax.rsqrt(jnp.mean(state * state, axis=-1, keepdims=True) + NORM_EPSILON)
+    norm2_grad_ref[...] = jnp.broadcast_to(jnp.sum(normed2_cot * state * factor, axis=0, keepdims=True), norm2_grad_ref.shape)
+    inner = jnp.sum(normed2_cot * gain2_ref[0:1, :] * state, axis=-1, keepdims=True)
+    state_cot = (
+        grad_ref[...].astype(FULL)
+        + factor * gain2_ref[0:1, :] * normed2_cot
+        - state * (factor * factor * factor) * inner * (1.0 / width)
+    )
+    state_cot_ref[...] = state_cot
+    low[...] = state_cot.astype(LOW)
+    gather = TensorGather(copies, low, lows, t_send, t_recv)
     scatter = Scatter(copies, work, diagonal, from_x, from_y, from_z, rows, r_send, r_recv)
-    for step in order:
+    for step in order[:2]:
         loads[step].wait()
         scatter.corner(step)
+    router_grad_ref[...] = jnp.dot(
+        logit_cot.T, normed2_ref[...].astype(FULL), precision=HIGHEST_PRECISION, preferred_element_type=FULL
+    )[: router_grad_ref.shape[0]]
     mask_bias(bias, key_docs, query_docs, length)
     gather.cross()
     gather.finish()
@@ -1006,7 +1206,7 @@
         @pl.loop(0, heads)
         def _(head):
             columns = pl.ds(pl.multiple_of(head * HD, HD), HD)
-            others = pl.ds(pl.multiple_of((heads + head) * HD, HD), HD)
+            values = pl.ds(pl.multiple_of((heads + head) * HD, HD), HD)
             query, cot = query_ref[:, columns], cots[:, columns]
             log, delta = logs[head, 0:1, :], deltas[head, 0:1, :]
             tile = 256
@@ -1014,13 +1214,13 @@
             @pl.loop(0, length // tile)
             def _(index):
                 keys = pl.ds(pl.multiple_of(index * tile, tile), tile)
-                key, value = kv_all[block, keys, columns], kv_all[block, keys, others]
-                hidden = bias[pl.ds(pl.multiple_of(block * length + index * tile, tile), tile), :]
+                key, value = kv_all[block, keys, columns], kv_all[block, keys, values]
+                hidden = bias[pl.ds(pl.multiple_of(block * length + index * tile, tile), tile), :].astype(FULL)
                 probs = jnp.exp(dot_t(key, query) * scale + hidden - log)
                 score_cot = (probs * (dot_t(value, cot) - delta)).astype(LOW)
                 turned[head] += t_dot(key, score_cot)
                 target[keys, columns] = (dot(score_cot, query) * scale).astype(target.dtype)
-                target[keys, others] = dot(probs.astype(LOW), cot).astype(target.dtype)
+                target[keys, values] = dot(probs.astype(LOW), cot).astype(target.dtype)
 
     def halo_copy(distance, to):
         return remote(sending.at[2 - distance], landed.at[2 - distance], h_send.at[distance], h_recv.at[distance], (to, part))
@@ -1035,14 +1235,53 @@
     scatter.side(order[0])
     back(0, sending.at[0])
     send(2)
-    for step in order[1:-1]:
-        scatter.side(step)
+    for step in order[2:]:
+        loads[step].wait()
+        scatter.corner(step)
+    scatter.side(order[1])
     back(2, kv_cot)
     for head in range(heads):
         query_cot[:, pl.ds(head * HD, HD)] = turned[head].T * scale
-    scatter.side(order[-1])
-    for step in order[:-1]:
-        scatter.climb(step)
+    scatter.climb(order[0])
+
+    saving = {}
+
+    def weight_piece(number, right, target):
+        piece = target.shape[2]
+        for index in range(2 * depth):
+            slot = index % 2
+            if slot in saving:
+                saving.pop(slot).wait()
+            staging[slot] = dot(flipped[pl.ds(index * piece, piece), :], right).astype(LOW)
+            saving[slot] = pltpu.make_async_copy(staging.at[slot], target.at[index // 2, index % 2], saves.at[slot])
+            saving[slot].start()
+
+    @pl.loop(0, width // 256)
+    def _(index):
+        columns = pl.ds(pl.multiple_of(index * 256, 256), 256)
+        flipped[columns, :] = jnp.concatenate([lows[block // 2, block % 2, :, columns] for block in range(4)], axis=0).T
+
+    weight_piece(0, attended[...], piece0)
+    normed_copy = pltpu.make_async_copy(normed_ref, flipped, load.at[depth + 3])
+    normed_copy.start()
+    for step in order[2:]:
+        scatter.side(step)
+    factors = as_columns(scales[...])
+
+    def turn_back(cot, raw, gain_ref, factor, grad_out):
+        total = jnp.zeros((length, 1), FULL)
+        for head in range(heads):
+            columns = pl.ds(head * HD, HD)
+            mine = cot[:, columns]
+            mine = mine * cosine_ref[...] - pltpu.roll(mine, HD // 2, 1) * sine_ref[...]
+            cot[:, columns] = mine
+            mine = mine * raw[:, columns]
+            grad_out[:, columns] = jnp.broadcast_to(jnp.sum(mine * factor, axis=0, keepdims=True), (8, HD))
+            total = total + jnp.sum(mine * gain_ref[0:1, columns], axis=-1, keepdims=True)
+        return total
+
+    query_inner = turn_back(query_cot, q_raw, q_gain_ref, factors[:, 0:1], q_grad_ref)
+    scatter.climb(order[1])
     for distance in (1, 2):
 
         @pl.when(spot < chain - distance)
@@ -1050,7 +1289,46 @@
             halo_copy(distance, group + distance).wait_recv()
             add_rows(kv_cot, [kv_cot, landed.at[2 - distance]], length)
 
-    scatter.climb(order[-1])
+    key_inner = turn_back(kv_cot, k_raw, k_gain_ref, factors[:, 1:2], k_grad_ref)
+    inners[...] = as_rows([query_inner, key_inner])
+    sent = exchange(copies, inners, inners_in, i_send, i_recv, mates)
+    raw_cots[2] = kv_cot[:, pl.ds(wide, wide)].astype(LOW)
+    normed_copy.wait()
+    weight_piece(1, raw_cots[2], piece1)
+    for copy in sent:
+        copies.arrived(copy)
+    total = inners[...]
+    for number in range(3):
+        total = total + inners_in[number]
+    totals = as_columns(total * (1.0 / width))
+
+    def raw_cot(number, cot, raw, gain_ref):
+        factor = factors[:, number : number + 1]
+        shrink = (factor * factor * factor) * totals[:, number : number + 1]
+        for head in range(heads):
+            columns = pl.ds(head * HD, HD)
+            raw_cots[number, :, columns] = (
+                factor * gain_ref[0:1, columns] * cot[:, columns] - raw[:, columns] * shrink
+            ).astype(LOW)
+
+    raw_cot(0, query_cot, q_raw, q_gain_ref)
+    raw_cot(1, kv_cot, k_raw, k_gain_ref)
+    for copy in others:
+        copy.wait()
+
+    @pl.loop(0, width // 256)
+    def _(index):
+        columns = pl.ds(pl.multiple_of(index * 256, 256), 256)
+        result = (
+            dot_t(raw_cots[0], wq[columns, :]) + dot_t(raw_cots[1], wk[columns, :]) + dot_t(raw_cots[2], wv[columns, :])
+        ).astype(LOW)
+        for block in range(4):
+            normed_part[block // 2, block % 2, :, columns] = result[block * rows : (block + 1) * rows]
+
+    weight_piece(2, raw_cots[0], piece2)
+    weight_piece(3, raw_cots[1], piece3)
+    for step in order[2:]:
+        scatter.climb(step)
     scatter.result(mix_ref)
     for distance in (1, 2):
 
@@ -1058,34 +1336,47 @@
         def _():
             halo_copy(distance, group - distance).wait_send()
 
+    for copy in saving.values():
+        copy.wait()
     copies.finish()
 
 
-def run_attention_back(low, queries, kv_all, attended, logs, key_docs, query_docs, w_out, produced, chain, number):
+def run_attention_back(rows_of, attention, sources, produced, normed, weights, chain, local, experts, number):
     depth = produced.shape[0]
-    rows, width = low.shape
-    length, wide = kv_all.shape[1:]
-    heads = wide // (2 * HD)
+    rows, width = rows_of[0].shape
+    queries, kv_all = attention[0], attention[1]
+    length, wide2 = kv_all.shape[1:]
+    wide = wide2 // 2
+    heads = wide // HD
+    piece = jax.ShapeDtypeStruct((depth, 2, width // (2 * depth), wide), LOW)
     return pl.pallas_call(
-        functools.partial(attention_back_kernel, depth, rows, heads, chain),
+        functools.partial(attention_back_kernel, depth, rows, heads, chain, local),
         out_shape=(
+            jax.ShapeDtypeStruct((rows, width), FULL),
+            jax.ShapeDtypeStruct((experts, width), FULL),
+            jax.ShapeDtypeStruct((8, width), FULL),
+            jax.ShapeDtypeStruct((8, wide), FULL),
+            jax.ShapeDtypeStruct((8, wide), FULL),
+            jax.ShapeDtypeStruct((rows, width), FULL),
             jax.ShapeDtypeStruct((2, 2, rows, width), LOW),
-            jax.ShapeDtypeStruct(queries.shape, FULL),
-            jax.ShapeDtypeStruct((length, wide), FULL),
-            jax.ShapeDtypeStruct((rows, width), FULL),
+            piece, piece, piece, piece,
         ),
-        in_specs=[VMEM] * 8 + [ANY],
-        out_specs=(VMEM,) * 4,
+        in_specs=[VMEM] * 23 + [ANY] * 5,
+        out_specs=(VMEM,) * 7 + (ANY,) * 4,
         scratch_shapes=[
-            pltpu.VMEM((3 * length, length), FULL), pltpu.VMEM((length, wide // 2), LOW),
+            pltpu.VMEM((rows, width), LOW), pltpu.VMEM((2, 2, rows, width), LOW), pltpu.VMEM((128, rows), FULL),
+            pltpu.VMEM((3 * length, length), LOW), pltpu.VMEM((length, wide), LOW),
             pltpu.VMEM((heads, 8, length), FULL), pltpu.VMEM((heads, HD, length), FULL),
-            pltpu.VMEM((2, length, wide), LOW), pltpu.VMEM((2, length, wide), LOW),
-            pltpu.VMEM(produced.shape, LOW),
+            pltpu.VMEM((length, wide), FULL), pltpu.VMEM((length, wide2), FULL),
+            pltpu.VMEM((2, length, wide2), LOW), pltpu.VMEM((2, length, wide2), LOW),
+            pltpu.VMEM(produced.shape, LOW), pltpu.VMEM((3, length, wide), LOW), pltpu.VMEM((width, length), LOW),
+            pltpu.VMEM((width, wide), LOW), pltpu.VMEM((width, wide), LOW), pltpu.VMEM((width, wide), LOW),
+            pltpu.VMEM((8, length), FULL), pltpu.VMEM((3, 8, length), FULL), pltpu.VMEM((2,) + piece.shape[2:], LOW),
         ]
         + Scatter.scratch(depth, rows, width)
-        + [dma(4), dma(3), dma(3), dma(3), dma(depth)],
+        + [dma(4), dma(3), dma(3), dma(3), dma(3), dma(3), dma(depth + 4), dma(2)],
         compiler_params=comm_params(number),
-    )(low, queries, kv_all, attended, logs, key_docs, query_docs, w_out, produced)
+    )(*rows_of, *attention, *sources, produced, normed, *weights)
 
 
 def dot(left, right):
@@ -1398,48 +1689,25 @@
     def quarter(array):
         return lax.dynamic_slice_in_dim(array, part * rows, rows, 0)
 
-    first_row = group * row_count
-    positions = first_row + jnp.arange(row_count, dtype=jnp.int32)
-    cosine, sine = rope_tables(positions % LENGTH)
-    inputs = tokens.astype(FULL)
-    scale_one = lax.rsqrt(jnp.mean(inputs * inputs, axis=-1, keepdims=True) + NORM_EPSILON)
-    normed_one = (inputs * scale_one * norm1_gain).astype(LOW)
-    query_raw = dot(normed_one, w_query)
-    key_raw = dot(normed_one, w_key)
-    values = dot(normed_one, w_value).astype(LOW)
-    squares = lax.psum(
-        jnp.stack([jnp.sum(query_raw * query_raw, axis=-1), jnp.sum(key_raw * key_raw, axis=-1)]), "tensor"
-    )
-    query_scale = lax.rsqrt(squares[0] / width + NORM_EPSILON)[:, None]
-    key_scale = lax.rsqrt(squares[1] / width + NORM_EPSILON)[:, None]
-    query_gain, key_gain = q_gain.reshape(-1), k_gain.reshape(-1)
-    queries = rotate((query_raw * query_scale * query_gain).reshape(row_count, heads, HD), cosine, sine).astype(LOW)
-    key_heads = rotate((key_raw * key_scale * key_gain).reshape(row_count, heads, HD), cosine, sine).astype(LOW)
-    queries = queries.reshape(row_count, -1)
-    own_kv = jnp.concatenate([key_heads.reshape(row_count, -1), values], axis=1)
-    every_doc = jnp.concatenate([jnp.full((2 * row_count,), -1, jnp.int32), lax.all_gather(documents, "expert", tiled=True)])
-    key_docs = lax.dynamic_slice_in_dim(every_doc, first_row, 3 * row_count, 0)
-    spot = group % chain
-    block_of = jnp.arange(3 * row_count, dtype=jnp.int32) // row_count
-    key_docs = jnp.where(spot + block_of >= 2, key_docs, -1)[:, None]
-    query_docs = jnp.broadcast_to(documents[None, :], (8, row_count))
-    kv_all, attended, logs, attention, all_grad = run_attention(
-        queries, own_kv, key_docs, query_docs, w_out, quarter(out_grad), depth, chain, 3
-    )
-
-    own_inputs = quarter(tokens).astype(FULL)
+    def across(vector):
+        return vector.reshape(1, -1)
+
+    positions = group * row_count + jnp.arange(row_count, dtype=jnp.int32)
+    cosine, sine = (table[:, 0, :] for table in rope_tables(positions % LENGTH))
+    sine = jnp.concatenate([-sine[:, : HD // 2], sine[:, HD // 2 :]], axis=1)
+    docs = jnp.broadcast_to(documents[None, :], (8, row_count))
+    picked = jnp.any(quarter(routes)[:, :, None] == jnp.arange(128, dtype=jnp.int32)[None, None, :], axis=1).astype(FULL)
+    router_wide = jnp.pad(router_w, ((0, 0), (0, 128 - experts)))
     own_grad = quarter(out_grad)
-    own_grad_float = own_grad.astype(FULL)
-    state = own_inputs + attention
-    scale_two = lax.rsqrt(jnp.mean(state * state, axis=-1, keepdims=True) + NORM_EPSILON)
-    normed_two = (state * scale_two * norm2_gain).astype(LOW)
-    router_probs = jax.nn.softmax(dot(normed_two, router_w), axis=-1)
-    picked = jnp.any(
-        quarter(routes)[:, :, None] == jnp.arange(experts, dtype=jnp.int32)[None, None, :], axis=1
-    ).astype(FULL)
-
-    gates = (router_probs * picked).T.reshape(groups, local_experts, rows)
-    gates = jnp.concatenate([gates, jnp.zeros((groups, 8 - local_experts, rows), FULL)], axis=1)
+    query_gain, key_gain = across(q_gain), across(k_gain)
+    (
+        normed_one, query_raw, key_raw, queries, kv_all, key_docs, scales, attended, logs, state, normed_two, router_probs, gates,
+        all_grad,
+    ) = run_attention(
+        tokens, (w_query, w_key, w_value, w_out), own_grad, (across(norm1_gain), query_gain, key_gain), (cosine, sine), docs,
+        across(norm2_gain), router_wide, picked, depth, chain, local_experts, 3,
+    )
+
     normed_two_grad, gate_cots, all_normed, gated, gate_pre_grad, up_pre_grad, produced = run_experts(
         normed_two, gates, all_grad, w_gate, w_up, w_down, 5
     )
@@ -1447,58 +1715,24 @@
     all_normed, all_grad = all_normed.reshape(seen, width), all_grad.reshape(seen, width)
     gated, gate_pre_grad, up_pre_grad = (a.reshape(seen, units) for a in (gated, gate_pre_grad, up_pre_grad))
 
-    prob_cot = gate_cots[:, :, :local_experts].reshape(depth, 2, 2, local_experts, rows).sum(axis=2)
-    plane = jnp.arange(depth, dtype=jnp.int32) ^ (group // 2)
-    prob_cot = prob_cot[plane].reshape(experts, rows).T * picked
-    logit_cot = router_probs * (prob_cot - jnp.sum(router_probs * prob_cot, axis=-1, keepdims=True))
-    normed_two_grad = normed_two_grad + jnp.einsum(
-        "te,de->td", logit_cot, router_w.astype(FULL), precision=HIGHEST_PRECISION
-    )
-    router_grad = jnp.einsum("td,te->ed", normed_two.astype(FULL), logit_cot, precision=HIGHEST_PRECISION)
-    norm2_grad = jnp.sum(normed_two_grad * state * scale_two, axis=0)
-    inner_two = jnp.sum(normed_two_grad * norm2_gain * state, axis=-1, keepdims=True)
-    state_cot = own_grad_float + scale_two * norm2_gain * normed_two_grad - state * scale_two**3 * inner_two / width
-    state_low, query_cot, kv_cot, expert_mix = run_attention_back(
-        state_cot.astype(LOW), queries, kv_all, attended, logs, key_docs, query_docs, w_out, produced, chain, 10
-    )
-    state_low = state_low.reshape(row_count, width)
-    query_cot = query_cot.reshape(row_count, heads, HD)
-    key_cot = kv_cot[:, : heads * HD].reshape(row_count, heads, HD)
-    value_low = kv_cot[:, heads * HD :].astype(LOW)
-    query_norm_cot = rotate_back(query_cot, cosine, sine).reshape(row_count, -1)
-    key_norm_cot = rotate_back(key_cot, cosine, sine).reshape(row_count, -1)
-    q_gain_local = jnp.sum(query_norm_cot * query_raw * query_scale, axis=0).reshape(heads, HD)
-    k_gain_local = jnp.sum(key_norm_cot * key_raw * key_scale, axis=0).reshape(heads, HD)
-    inners = lax.psum(
-        jnp.stack(
-            [
-                jnp.sum(query_norm_cot * query_gain * query_raw, axis=-1),
-                jnp.sum(key_norm_cot * key_gain * key_raw, axis=-1),
-            ]
-        ),
-        "tensor",
-    )
-    query_raw_cot = (
-        query_scale * query_gain * query_norm_cot - query_raw * query_scale**3 * inners[0][:, None] / width
-    ).astype(LOW)
-    key_raw_cot = (
-        key_scale * key_gain * key_norm_cot - key_raw * key_scale**3 * inners[1][:, None] / width
-    ).astype(LOW)
-    normed_part = dot_t(query_raw_cot, w_query) + dot_t(key_raw_cot, w_key) + dot_t(value_low, w_value)
-    pieces = [
-        t_dot(left, right).astype(LOW).reshape(depth, 2, width // groups, -1)
-        for left, right in (
-            (state_low, attended), (normed_one, value_low), (normed_one, query_raw_cot), (normed_one, key_raw_cot)
-        )
-    ]
+    (
+        state_cot, router_grad, norm2_grad, q_gain_local, k_gain_local, expert_mix, normed_part, *pieces
+    ) = run_attention_back(
+        (normed_two_grad, gate_cots, router_probs, picked, state, across(norm2_gain), router_wide, normed_two, own_grad),
+        (queries, kv_all, attended, logs, key_docs, docs, query_raw, key_raw, query_gain, key_gain, cosine, sine, scales),
+        (w_out,), produced, normed_one, (w_query, w_key, w_value), chain, local_experts, experts, 10,
+    )
+    own_inputs = quarter(tokens).astype(FULL)
+    own_scale = lax.rsqrt(jnp.mean(own_inputs * own_inputs, axis=-1, keepdims=True) + NORM_EPSILON)
+
     vectors = jnp.concatenate(
-        [router_grad, jnp.zeros((17 - experts, width), FULL), norm2_grad[None]], axis=0
+        [router_grad, jnp.zeros((17 - experts, width), FULL), norm2_grad[:1]], axis=0
     ).reshape(18, groups, width // groups).transpose(1, 0, 2)
-    gains = jnp.concatenate([q_gain_local, k_gain_local], axis=0)
+    gains = jnp.concatenate([q_gain_local[0].reshape(heads, HD), k_gain_local[0].reshape(heads, HD)], axis=0)
     gains = jnp.pad(gains, ((0, 14 - 2 * heads), (0, width // groups - HD)))
     vectors = jnp.concatenate([vectors, jnp.broadcast_to(gains[None], (groups,) + gains.shape)], axis=1)
     sums, (input_grad, output, vector_sum, gate_own, up_own, down_own, gate_other, up_other, down_other) = run_gradients(
-        pieces, normed_part.astype(LOW).reshape(2, 2, rows, width), quarter(tokens), state_cot, quarter(scale_one),
+        pieces, normed_part, quarter(tokens), state_cot, own_scale,
         norm1_gain[None], (state + expert_mix).astype(LOW), vectors, all_normed, all_grad, gated, gate_pre_grad, up_pre_grad,
         local_experts, 14,
     )

time: 787 us -> 661 us (0.84)
  blocking collectives: 37 us -> 0 us
  matrix products: 31.6 us -> 0 us
  local copies, waits for them, and re-layouts: 44.6 us -> 21 us
  other arithmetic: 45.4 us -> 21.8 us
    dot_general x13 -> x0, matrix products: 31.6 us -> none  [the longest x4 11.5 us: dot(): return jnp.dot(left, right, preferred_element_type=FULL)]
    all_gather x1 -> x0, blocking collectives: 25 us -> none  [body(): lax.all_gather(documents, 'expert', tiled=True)]
    psum x2 -> x0, blocking collectives: 12.1 us -> none  [the longest x1 6.39 us: body(): lax.psum(jnp.stack([jnp.sum(query_norm_cot * query_gain * query_raw, axis...]
    pallas_call x1, Pallas kernels: 117 us -> 129 us  [run_attention_back(): pl.pallas_call(functools.partial(attention_back_kernel, depth, rows, head...]
    reshape x4 -> x2, local copies, waits for them, and re-layouts: 10.2 us -> 0.06 us  [body(): vectors = jnp.concatenate([router_grad, jnp.zeros((17 - experts, width),...]
    pallas_call x1, Pallas kernels: 129 us -> 120 us  [run_attention(): pl.pallas_call(functools.partial(attention_kernel, depth, rows, heads, ch...]
where the time goes in v5:
time: 661 us; the launch traced here: 650 us
  Pallas kernels  606 us (92%)
  other arithmetic  21.8 us (3%)
  local copies, waits for them, and re-layouts  21 us (3%)
    pallas_call x1, Pallas kernels, run_experts(): pl.pallas_call(functools.partial(experts_kernel, depth, rows, local, hidd...  203 us
    pallas_call x1, Pallas kernels, run_gradients(): pl.pallas_call(functools.partial(gradients_kernel, depth, rows, local, hi...  154 us
    pallas_call x1, Pallas kernels, run_attention_back(): pl.pallas_call(functools.partial(attention_back_kernel, depth, rows, head...  129 us
    pallas_call x1, Pallas kernels, run_attention(): pl.pallas_call(functools.partial(attention_kernel, depth, rows, heads, ch...  120 us

profile of v5, /device:TPU:10, one launch (start us, length us, event | category | flops | bytes accessed | tf_op | source)
XLA Modules:
  0.0 649.8 jit_solution(14557736410964832039)
XLA Ops:
  0.8 0.8 constant_dynamic-slice_fusion.1
  1.6 1.3 broadcast_in_dim.6.docs_ref.query_docs
  3.3 0.6 convert_element_type.36.picked_ref
  4.0 1.8 fusion.1
  6.0 0.8 pad_maximum_fusion.1.sine_ref
  6.8 0.8 constant_dynamic-slice_fusion.2.grad_ref
  7.6 0.3 copy.39
  7.9 0.9 pad.8.router_ref
  8.8 1.9 multiply_reduce_fusion
  10.8 0.7 copy.42.refs_7_
  11.5 120.0 %shard_map.263 = (bf16[2048,512]{1,0:T(8,128)(2,1)}, f32[512,512]{1,0:T(8,128)}, f32[512,512]{1,0:T(8,128)}, bf16[512,512]{1,0:T(8,128)(2,1)}, bf16[3,512,1024]{...) custom-call(bf16[512,2048]{1,0:T(8,128)(2,1)} %tokens_ref.1, ...), custom_call_target="tpu_custom_call" | custom-call | tf_op jit(solution)/shard_map/pallas_call | solution.py:1094
  131.6 203.5 %shard_map.264 = (f32[128,2048]{1,0:T(8,128)}, f32[4,4,8,128]{3,2,1,0:T(8,128)}, bf16[4,512,2048]{2,1,0:T(8,128)(2,1)}, bf16[4,512,1024]{2,1,0:T(8,128)(2,1)}, b...) custom-call(bf16[128,2048]{1,0:T(8,128)(2,1)} %get-tuple-element.59.x_ref.normed2_ref, ...), custom_call_target="tpu_custom_call" | custom-call | tf_op jit(solution)/shard_map/pallas_call | solution.py:747
  335.0 128.6 %shard_map.265 = (f32[128,2048]{1,0:T(8,128)}, f32[16,2048]{1,0:T(8,128)}, f32[8,2048]{1,0:T(8,128)}, f32[8,512]{1,0:T(8,128)}, f32[8,512]{1,0:T(8,128)}, /*inde...) custom-call(f32[128,2048]{1,0:T(8,128)} %get-tuple-element.62.sum_re, ...), custom_call_target="tpu_custom_call" | custom-call | tf_op jit(solution)/shard_map/pallas_call | solution.py:1352
  463.6 2.2 add_convert_fusion.refs_9_
  465.8 0.7 slice.27
  466.5 0.7 slice.28
  467.2 0.8 slice.26
  468.3 0.7 pad_maximum_fusion.2.refs_10_
  469.1 153.9 %shard_map.266 = (f32[256,512]{1,0:T(8,128)}, f32[256,512]{1,0:T(8,128)}, f32[256,512]{1,0:T(8,128)}, f32[256,512]{1,0:T(8,128)}, bf16[2,2,128,2048]{3,2,1,0:T(8...) custom-call(bf16[4,2,256,512]{3,2,1,0:T(8,128)(2,1)} %get-tuple-elem, ...), custom_call_target="tpu_custom_call" | custom-call | tf_op jit(solution)/shard_map/pallas_call | solution.py:1638
  623.0 1.3 fusion.5
  624.4 1.4 constant_dynamic-slice_fusion.3
  625.8 1.3 slice_bitcast_fusion
  627.1 2.0 copy.43
  629.1 4.3 bitcast_convert_fusion
  633.4 4.6 convert_add_fusion
  638.0 1.0 copy-done.3
  639.0 0.6 copy-done.6
  639.6 4.2 convert_add_fusion.1
  643.8 3.3 copy.51
  647.1 0.8 copy.52
  647.9 0.8 copy.53
  648.7 0.8 copy.54
  (38 shorter events, 1.0 us)
Async XLA Ops:
  0.6 6.2 copy-start
  1.6 6.1 copy-start.12
  335.0 128.6 %copy-start.5 = (f32[128,2048]{1,0:T(8,128)S(1)}, f32[128,2048]{1,0:T(8,128)}, u32[]{:S(2)}) copy-start(f32[128,2048]{1,0:T(8,128)} %get-tuple-element.65.state_ref) | copy-start | bytes 3145732
  463.6 4.5 copy-start.11
  629.1 4.3 copy-start.4
  629.1 8.9 %copy-start.7 = (bf16[2,2048,256]{2,1,0:T(8,128)(2,1)S(1)}, bf16[2,2048,256]{2,1,0:T(8,128)(2,1)}, u32[]{:S(2)}) copy-start(bf16[2,2048,256]{2,1,0:T(8,128)(2,1)} %get-tuple-element.101) | copy-start | bytes 6291460
  633.4 4.6 copy-start.2
  633.4 5.6 copy-start.3
  633.4 6.2 copy-start.6
  643.8 3.3 copy-start.10
  643.8 4.1 copy-start.9
  643.8 5.7 copy-start.1
  647.1 1.6 copy-start.8

commit v6 on v5

--- a/solution.py
+++ b/solution.py
@@ -608,25 +608,6 @@
     ]
     greet([device(*other, core) for _, _, other in others] + [sibling])
     copies = Copies()
-    gather = Gather(copies, x_ref, x_all, rows, z_send, z_recv, p_send, p_recv)
-    gather.begin()
-    plain = []
-
-    def fetch(source, target, sem):
-        copy = pltpu.make_async_copy(source, target, sem)
-        copy.start()
-        return copy
-
-    plain.append(fetch(x_ref, gather.at(0, here, None), local_sem.at[0]))
-    weights = []
-    for index in range(local):
-        first = pl.multiple_of((core * local + index) * hidden, hidden)
-        columns = pl.ds(first, hidden)
-        for number, (source, target) in enumerate(
-            [(gate_ref, wg.at[:, columns]), (up_ref, wu.at[:, columns]), (down_ref, wd.at[columns])]
-        ):
-            weights.append(copies.start(remote(source.at[index], target, w_send.at[number, index], w_recv.at[number, index], sibling)))
-            plain.append(fetch(source.at[index], target, w_load.at[number, index]))
     smalls = []
     for step, turn, other in others:
         oz, ox, oy = other
@@ -638,6 +619,25 @@
                 )
             )
         )
+    gather = Gather(copies, x_ref, x_all, rows, z_send, z_recv, p_send, p_recv)
+    gather.begin()
+    plain = []
+
+    def fetch(source, target, sem):
+        copy = pltpu.make_async_copy(source, target, sem)
+        copy.start()
+        return copy
+
+    plain.append(fetch(x_ref, gather.at(0, here, None), local_sem.at[0]))
+    weights = []
+    for index in range(local):
+        first = pl.multiple_of((core * local + index) * hidden, hidden)
+        columns = pl.ds(first, hidden)
+        for number, (source, target) in enumerate(
+            [(gate_ref, wg.at[:, columns]), (up_ref, wu.at[:, columns]), (down_ref, wd.at[columns])]
+        ):
+            weights.append(copies.start(remote(source.at[index], target, w_send.at[number, index], w_recv.at[number, index], sibling)))
+            plain.append(fetch(source.at[index], target, w_load.at[number, index]))
     plain.append(fetch(gates_ref.at[2 * z + x], gates.at[0, here], local_sem.at[1]))
     grad_copies = [fetch(grad_ref.at[0], grads.at[0], g_load.at[0])]
     scatter = Scatter(copies, work, diagonal, from_x, from_y, from_z, rows, r_send, r_recv)
@@ -678,6 +678,14 @@
 
         for spot in range(4):
             cot_rows[step, spot] = cots[pl.ds(spot * rows, rows), :].T[:8]
+        for other_step, turn, (oz, ox, oy) in others:
+            if other_step == step:
+                copies.start(
+                    remote(
+                        cot_rows.at[step, 2 * ox + oy], cots_ref.at[step, here], s_send.at[1, step, turn], s_recv.at[1, step, turn],
+                        device(oz, ox, oy, core),
+                    )
+                )
         for number, (source, target) in enumerate([(gated, gated_ref), (gate_grad, gate_grad_ref), (up_grad, up_grad_ref)]):
             saving.append(fetch(source, target.at[step], saves.at[number]))
         keeping.append(fetch(x_all.at[step], normed_ref.at[step], saves.at[4 + step]))
@@ -718,13 +726,6 @@
             scatter.climb(step - 2)
         second_half(step)
         scatter.corner(step)
-    for step, turn, (oz, ox, oy) in others:
-        copies.start(
-            remote(
-                cot_rows.at[step, 2 * ox + oy], cots_ref.at[step, here], s_send.at[1, step, turn], s_recv.at[1, step, turn],
-                device(oz, ox, oy, core),
-            )
-        )
     own_cots = fetch(cot_rows.at[0, here], cots_ref.at[0, here], local_sem.at[2])
     if depth > 1:
         scatter.climb(depth - 2)
@@ -883,7 +884,7 @@
     normed_turned, q_raw, k_raw, queries, kv_all, key_docs, scales, attended, logs, state_ref, normed2_ref, probs_ref, gates_ref,
     all_grad,
     tokens, normed_ref, wq, wk, wv, wo, docs_in, squares, squares_in, scores, bias, partial, from_pair, from_y, sum_ref,
-    t_send, t_recv, z_send, z_recv, p_send, p_recv, h_send, h_recv, q_send, q_recv, load,
+    t_send, t_recv, z_send, z_recv, p_send, p_recv, h_send, h_recv, d_send, d_recv, q_send, q_recv, load,
 ):
     z, x, y, core = place()
     group, part = lax.axis_index("expert"), lax.axis_index("tensor")
@@ -903,6 +904,14 @@
         + [device(*mate) for mate in mates]
     )
     copies = Copies()
+    for distance in (1, 2):
+
+        @pl.when(spot < chain - distance)
+        def _():
+            remote(
+                docs_ref, docs_in.at[2 - distance], d_send.at[distance], d_recv.at[distance], (group + distance, part)
+            ).start()
+
     gather = Gather(copies, grad_ref, all_grad, rows, z_send, z_recv, p_send, p_recv)
     gather.spread(0)
     gather.lift(1)
@@ -910,36 +919,51 @@
     own.start()
     key_part, value_part = pl.ds(0, wide), pl.ds(wide, wide)
 
-    def halo_copy(kind, distance, to):
-        if kind == 2:
-            return remote(docs_ref, docs_in.at[2 - distance], h_send.at[kind, distance], h_recv.at[kind, distance], (to, part))
+    high = lax.rem(z, 2)
+    over_x, over_z = device(z, x1, y, core), device(z1, x, y, core)
+
+    def docs_copy(distance, to):
+        return remote(docs_ref, docs_in.at[2 - distance], d_send.at[distance], d_recv.at[distance], (to, part))
+
+    def halo_copy(kind, source, slot, number, to):
         columns = (key_part, value_part)[kind]
         return remote(
-            kv_all.at[2, :, columns], kv_all.at[2 - distance, :, columns],
-            h_send.at[kind, distance], h_recv.at[kind, distance], (to, part),
+            kv_all.at[source, :, columns], kv_all.at[slot, :, columns], h_send.at[kind, number], h_recv.at[kind, number], to
         )
 
+    def x_copy(kind):
+        return halo_copy(kind, 2, 1, 0, over_x)
+
+    def z_copy(kind):
+        return halo_copy(kind, 2, 0, 1, over_z)
+
+    def relay_copy(kind):
+        return halo_copy(kind, 0, 1, 2, over_x)
+
     def halo_start(kind):
-        for distance in (1, 2):
-
-            @pl.when(spot < chain - distance)
-            def _():
-                halo_copy(kind, distance, group + distance).start()
-
-    def halo_arrive(kind, distance):
-        @pl.when(spot >= distance)
-        def _():
-            halo_copy(kind, distance, group - distance).wait_recv()
-
-        @pl.when(spot < distance)
-        def _():
-            if kind == 2:
-                docs_in[2 - distance] = jnp.full_like(docs_ref, -1)
-            else:
-                columns = (key_part, value_part)[kind]
-                kv_all[2 - distance, :, columns] = jnp.zeros((length, wide), LOW)
-
-    halo_start(2)
+        pl.when(x == 0)(lambda: x_copy(kind).start())
+        pl.when(high == 0)(lambda: z_copy(kind).start())
+
+    def halo_relay(kind):
+        pl.when(high == 1)(lambda: z_copy(kind).wait_recv())
+        pl.when(spot == 3)(lambda: relay_copy(kind).start())
+
+    def halo_arrive(kind):
+        columns = (key_part, value_part)[kind]
+        pl.when(x == 1)(lambda: x_copy(kind).wait_recv())
+        pl.when(spot == 2)(lambda: relay_copy(kind).wait_recv())
+
+        def clear(slot):
+            kv_all[slot, :, columns] = jnp.zeros((length, wide), LOW)
+
+        pl.when(spot == 0)(lambda: clear(1))
+        pl.when(high == 0)(lambda: clear(0))
+
+    def halo_sent(kind):
+        pl.when(x == 0)(lambda: x_copy(kind).wait_send())
+        pl.when(high == 0)(lambda: z_copy(kind).wait_send())
+        pl.when(spot == 3)(lambda: relay_copy(kind).wait_send())
+
     loads[0].wait()
 
     @pl.loop(0, length // 128)
@@ -975,6 +999,7 @@
     loads[1].wait()
     project(wv, keep_value)
     halo_start(1)
+    gather.turn(0)
 
     @pl.loop(0, width // 256)
     def _(index):
@@ -1003,12 +1028,19 @@
 
     turn_heads(k_raw, k_gain_ref, factors[:, 1:2], store_key)
     halo_start(0)
-    gather.turn(0)
     gather.spread(1)
     gather.lift(2)
     turn_heads(q_raw, q_gain_ref, factors[:, 0:1], store_query)
     for distance in (1, 2):
-        halo_arrive(2, distance)
+
+        @pl.when(spot >= distance)
+        def _():
+            docs_copy(distance, group - distance).wait_recv()
+
+        @pl.when(spot < distance)
+        def _():
+            docs_in[2 - distance] = jnp.full_like(docs_ref, -1)
+
     for block in range(3):
         rows_of = docs_in[block] if block < 2 else docs_ref[...]
         key_docs[pl.ds(block * length, length), :] = rows_of.astype(FULL).T[:, 0:1].astype(jnp.int32)
@@ -1022,14 +1054,16 @@
             scores[head, keys, :] = dot_t(kv_all[block, :, columns], queries[:, columns]) * scale + bias[keys, :]
 
     score(2)
+    halo_relay(1)
     gather.turn(1)
+    halo_relay(0)
     gather.spread(2)
     gather.lift(3)
-    for distance in (1, 2):
-        halo_arrive(0, distance)
-        score(2 - distance)
-    for distance in (1, 2):
-        halo_arrive(1, distance)
+    halo_arrive(0)
+    score(0)
+    score(1)
+    gather.turn(2)
+    halo_arrive(1)
 
     @pl.loop(0, heads)
     def _(head):
@@ -1049,7 +1083,6 @@
         attended[:, columns] = mixed.T.astype(LOW)
         logs[head] = jnp.broadcast_to(highest + jnp.log(total), (8, length))
 
-    gather.turn(2)
     gather.spread(3)
     loads[4].wait()
     for index in range(4):
@@ -1076,12 +1109,13 @@
     for index in range(gates_ref.shape[0]):
         gates_ref[index, 0:local, :] = gates[index * local : (index + 1) * local]
     own.wait()
-    for kind in range(3):
-        for distance in (1, 2):
-
-            @pl.when(spot < chain - distance)
-            def _():
-                halo_copy(kind, distance, group + distance).wait_send()
+    for kind in range(2):
+        halo_sent(kind)
+    for distance in (1, 2):
+
+        @pl.when(spot < chain - distance)
+        def _():
+            docs_copy(distance, group + distance).wait_send()
 
     copies.finish()
 
@@ -1120,7 +1154,7 @@
         + TensorScatter.scratch(rows, width)[:3]
         + [
             pltpu.VMEM((rows, width), FULL), dma(3), dma(3),
-            dma(depth), dma(depth), dma(depth, 6), dma(depth, 6), dma(3, 3), dma(3, 3), dma(3), dma(3), dma(6),
+            dma(depth), dma(depth), dma(depth, 6), dma(depth, 6), dma(2, 3), dma(2, 3), dma(3), dma(3), dma(3), dma(3), dma(6),
         ],
         compiler_params=comm_params(number),
     )(tokens, *weights, grads, *gains, *tables, docs, gain2, router, picked)
@@ -1154,10 +1188,18 @@
     mates = mates_of()
     greet(
         [device(swapped(z, step), x, y, core) for step in range(1, depth)]
-        + [device(z, 1 - x, y, core), device(swapped(z, 1), 1 - x, y, core)]
+        + [device(z, 1 - x, y, core)]
         + [device(*mate) for mate in mates]
     )
     copies = Copies()
+    scatter = Scatter(copies, work, diagonal, from_x, from_y, from_z, rows, r_send, r_recv)
+
+    def corner(step):
+        loads[step].wait()
+        scatter.corner(step)
+
+    for step in order[:2]:
+        corner(step)
 
     by_expert[...] = jnp.zeros_like(by_expert)
     for plane in range(depth):
@@ -1184,10 +1226,7 @@
     state_cot_ref[...] = state_cot
     low[...] = state_cot.astype(LOW)
     gather = TensorGather(copies, low, lows, t_send, t_recv)
-    scatter = Scatter(copies, work, diagonal, from_x, from_y, from_z, rows, r_send, r_recv)
-    for step in order[:2]:
-        loads[step].wait()
-        scatter.corner(step)
+    scatter.side(order[0])
     router_grad_ref[...] = jnp.dot(
         logit_cot.T, normed2_ref[...].astype(FULL), precision=HIGHEST_PRECISION, preferred_element_type=FULL
     )[: router_grad_ref.shape[0]]
@@ -1222,27 +1261,35 @@
                 target[keys, columns] = (dot(score_cot, query) * scale).astype(target.dtype)
                 target[keys, values] = dot(probs.astype(LOW), cot).astype(target.dtype)
 
-    def halo_copy(distance, to):
-        return remote(sending.at[2 - distance], landed.at[2 - distance], h_send.at[distance], h_recv.at[distance], (to, part))
-
-    def send(distance):
-        @pl.when(spot >= distance)
-        def _():
-            halo_copy(distance, group - distance).start()
+    high = lax.rem(z, 2)
+    over_x, over_z = device(z, 1 - x, y, core), device(swapped(z, 1), x, y, core)
+
+    def x_copy():
+        return remote(sending.at[1], landed.at[1], h_send.at[0], h_recv.at[0], over_x)
+
+    def z_copy():
+        return remote(sending.at[0], landed.at[0], h_send.at[1], h_recv.at[1], over_z)
 
     back(1, sending.at[1])
-    send(1)
-    scatter.side(order[0])
+    pl.when(spot >= 1)(lambda: x_copy().start())
+    corner(1)
+    scatter.side(order[1])
     back(0, sending.at[0])
-    send(2)
-    for step in order[2:]:
-        loads[step].wait()
-        scatter.corner(step)
-    scatter.side(order[1])
+    pl.when(spot == 2)(lambda: z_copy().start())
+    scatter.climb(order[0])
     back(2, kv_cot)
+
+    @pl.when(spot == 3)
+    def _():
+        x_copy().wait_recv()
+        add_rows(sending.at[0], [sending.at[0], landed.at[1]], length)
+        z_copy().start()
+
+    corner(0)
     for head in range(heads):
         query_cot[:, pl.ds(head * HD, HD)] = turned[head].T * scale
-    scatter.climb(order[0])
+    scatter.side(order[2])
+    scatter.climb(order[1])
 
     saving = {}
 
@@ -1264,8 +1311,7 @@
     weight_piece(0, attended[...], piece0)
     normed_copy = pltpu.make_async_copy(normed_ref, flipped, load.at[depth + 3])
     normed_copy.start()
-    for step in order[2:]:
-        scatter.side(step)
+    scatter.side(order[3])
     factors = as_columns(scales[...])
 
     def turn_back(cot, raw, gain_ref, factor, grad_out):
@@ -1281,13 +1327,17 @@
         return total
 
     query_inner = turn_back(query_cot, q_raw, q_gain_ref, factors[:, 0:1], q_grad_ref)
-    scatter.climb(order[1])
-    for distance in (1, 2):
-
-        @pl.when(spot < chain - distance)
-        def _():
-            halo_copy(distance, group + distance).wait_recv()
-            add_rows(kv_cot, [kv_cot, landed.at[2 - distance]], length)
+    scatter.climb(order[2])
+
+    @pl.when(x == 0)
+    def _():
+        x_copy().wait_recv()
+        add_rows(kv_cot, [kv_cot, landed.at[1]], length)
+
+    @pl.when(high == 0)
+    def _():
+        z_copy().wait_recv()
+        add_rows(kv_cot, [kv_cot, landed.at[0]], length)
 
     key_inner = turn_back(kv_cot, k_raw, k_gain_ref, factors[:, 1:2], k_grad_ref)
     inners[...] = as_rows([query_inner, key_inner])
@@ -1327,14 +1377,10 @@
 
     weight_piece(2, raw_cots[0], piece2)
     weight_piece(3, raw_cots[1], piece3)
-    for step in order[2:]:
-        scatter.climb(step)
+    scatter.climb(order[3])
     scatter.result(mix_ref)
-    for distance in (1, 2):
-
-        @pl.when(spot >= distance)
-        def _():
-            halo_copy(distance, group - distance).wait_send()
+    pl.when(spot >= 1)(lambda: x_copy().wait_send())
+    pl.when(spot >= 2)(lambda: z_copy().wait_send())
 
     for copy in saving.values():
         copy.wait()
@@ -1578,16 +1624,6 @@
         experts.climb(1, step)
     grad_gather.cross()
     gate_and_up(3)
-    for copy in vector_copies:
-        copies.arrived(copy)
-    total = vectors[group]
-    for number in range(len(peers)):
-        total = total + vector_in[number]
-    vector_mid[...] = total
-    turn_copies = [
-        copies.start(remote(vector_mid, vector_turn.at[number], u_send.at[number], u_recv.at[number], device(*mate)))
-        for number, mate in enumerate(mates)
-    ]
     for step in experts.order[2:]:
         experts.climb(1, step)
     gated_copy = fetch(gated_ref, acts.at[0], act_load.at[0])
@@ -1604,6 +1640,23 @@
     down(2)
     experts.result(1, sums[1])
     down(3)
+    for index in range(3, matrices):
+        for step in experts.order:
+            experts.climb(index, step)
+    for copy in vector_copies:
+        copies.arrived(copy)
+    total = vectors[group]
+    for number in range(len(peers)):
+        total = total + vector_in[number]
+    vector_mid[...] = total
+    turn_copies = [
+        copies.start(remote(vector_mid, vector_turn.at[number], u_send.at[number], u_recv.at[number], device(*mate)))
+        for number, mate in enumerate(mates)
+    ]
+    for index in range(2, matrices):
+        experts.result(index, sums[index])
+    out_gather.finish()
+    grad_gather.finish()
     for copy in turn_copies:
         copies.arrived(copy)
     total = vector_mid[...]
@@ -1611,13 +1664,6 @@
         total = total + vector_turn[number]
     keep = lax.broadcasted_iota(jnp.int32, total.shape, 0) < 18
     vector_sum[...] = jnp.where(keep, total, vector_mid[...])
-    for index in range(3, matrices):
-        for step in experts.order:
-            experts.climb(index, step)
-    for index in range(2, matrices):
-        experts.result(index, sums[index])
-    out_gather.finish()
-    grad_gather.finish()
     for entries in saving.values():
         for copy, remote_one in entries:
             if not remote_one:

time: 661 us -> 578 us (0.87)
  Pallas kernels: 606 us -> 524 us
    pallas_call x1, Pallas kernels: 154 us -> 119 us  [run_gradients(): pl.pallas_call(functools.partial(gradients_kernel, depth, rows, local, hi...]
    pallas_call x1, Pallas kernels: 203 us -> 173 us  [run_experts(): pl.pallas_call(functools.partial(experts_kernel, depth, rows, local, hidd...]
    pallas_call x1, Pallas kernels: 120 us -> 110 us  [run_attention(): pl.pallas_call(functools.partial(attention_kernel, depth, rows, heads, ch...]
    pallas_call x1, Pallas kernels: 129 us -> 121 us  [run_attention_back(): pl.pallas_call(functools.partial(attention_back_kernel, depth, rows, head...]
where the time goes in v6:
time: 578 us; the launch traced here: 567 us
  Pallas kernels  524 us (91%)
  other arithmetic  21.8 us (4%)
  local copies, waits for them, and re-layouts  21 us (4%)
    pallas_call x1, Pallas kernels, run_experts(): pl.pallas_call(functools.partial(experts_kernel, depth, rows, local, hidd...  173 us
    pallas_call x1, Pallas kernels, run_attention_back(): pl.pallas_call(functools.partial(attention_back_kernel, depth, rows, head...  121 us
    pallas_call x1, Pallas kernels, run_gradients(): pl.pallas_call(functools.partial(gradients_kernel, depth, rows, local, hi...  119 us
    pallas_call x1, Pallas kernels, run_attention(): pl.pallas_call(functools.partial(attention_kernel, depth, rows, heads, ch...  110 us

profile of v6, /device:TPU:10, one launch (start us, length us, event | category | flops | bytes accessed | tf_op | source)
XLA Modules:
  0.0 567.3 jit_solution(13174610864190276681)
XLA Ops:
  0.8 0.8 constant_dynamic-slice_fusion.1
  1.6 1.3 broadcast_in_dim.6.docs_ref.query_docs
  3.3 0.6 convert_element_type.36.picked_ref
  4.0 1.8 fusion.1
  6.0 0.8 pad_maximum_fusion.1.sine_ref
  6.8 0.8 constant_dynamic-slice_fusion.2.grad_ref
  7.6 0.3 copy.39
  7.9 0.9 pad.8.router_ref
  8.8 1.9 multiply_reduce_fusion
  10.8 0.7 copy.42.refs_7_
  11.5 110.4 %shard_map.263 = (bf16[2048,512]{1,0:T(8,128)(2,1)}, f32[512,512]{1,0:T(8,128)}, f32[512,512]{1,0:T(8,128)}, bf16[512,512]{1,0:T(8,128)(2,1)}, bf16[3,512,1024]{...) custom-call(bf16[512,2048]{1,0:T(8,128)(2,1)} %tokens_ref.1, ...), custom_call_target="tpu_custom_call" | custom-call | tf_op jit(solution)/shard_map/pallas_call | solution.py:1128
  121.9 173.4 %shard_map.264 = (f32[128,2048]{1,0:T(8,128)}, f32[4,4,8,128]{3,2,1,0:T(8,128)}, bf16[4,512,2048]{2,1,0:T(8,128)(2,1)}, bf16[4,512,1024]{2,1,0:T(8,128)(2,1)}, b...) custom-call(bf16[128,2048]{1,0:T(8,128)(2,1)} %get-tuple-element.59.x_ref.normed2_ref, ...), custom_call_target="tpu_custom_call" | custom-call | tf_op jit(solution)/shard_map/pallas_call | solution.py:748
  295.3 121.2 %shard_map.265 = (f32[128,2048]{1,0:T(8,128)}, f32[16,2048]{1,0:T(8,128)}, f32[8,2048]{1,0:T(8,128)}, f32[8,512]{1,0:T(8,128)}, f32[8,512]{1,0:T(8,128)}, /*inde...) custom-call(f32[128,2048]{1,0:T(8,128)} %get-tuple-element.62.sum_re, ...), custom_call_target="tpu_custom_call" | custom-call | tf_op jit(solution)/shard_map/pallas_call | solution.py:1398
  416.6 2.2 add_convert_fusion.refs_9_
  418.7 0.7 slice.27
  419.5 0.7 slice.28
  420.2 0.8 slice.26
  421.3 0.7 pad_maximum_fusion.2.refs_10_
  422.0 118.5 %shard_map.266 = (f32[256,512]{1,0:T(8,128)}, f32[256,512]{1,0:T(8,128)}, f32[256,512]{1,0:T(8,128)}, f32[256,512]{1,0:T(8,128)}, bf16[2,2,128,2048]{3,2,1,0:T(8...) custom-call(bf16[4,2,256,512]{3,2,1,0:T(8,128)(2,1)} %get-tuple-elem, ...), custom_call_target="tpu_custom_call" | custom-call | tf_op jit(solution)/shard_map/pallas_call | solution.py:1684
  540.6 1.3 fusion.5
  541.9 1.4 constant_dynamic-slice_fusion.3
  543.3 1.3 slice_bitcast_fusion
  544.7 2.0 copy.43
  546.7 4.3 bitcast_convert_fusion
  551.0 4.6 convert_add_fusion
  555.6 1.0 copy-done.3
  556.6 0.6 copy-done.6
  557.2 4.2 convert_add_fusion.1
  561.4 3.3 copy.51
  564.7 0.8 copy.52
  565.5 0.8 copy.53
  566.3 0.8 copy.54
  (38 shorter events, 1.0 us)
Async XLA Ops:
  0.6 6.2 %copy-start = (bf16[512,2048]{1,0:T(8,128)(2,1)S(1)}, bf16[512,2048]{1,0:T(8,128)(2,1)}, u32[]{:S(2)}) copy-start(bf16[512,2048]{1,0:T(8,128)(2,1)} %param.31) | copy-start | bytes 6291460
  1.6 6.1 %copy-start.12 = (bf16[2048,16]{0,1:T(8,128)(2,1)S(1)}, bf16[2048,16]{0,1:T(8,128)(2,1)}, u32[]{:S(2)}) copy-start(bf16[2048,16]{0,1:T(8,128)(2,1)} %param.27) | copy-start | bytes 196612
  295.3 121.2 %copy-start.5 = (f32[128,2048]{1,0:T(8,128)S(1)}, f32[128,2048]{1,0:T(8,128)}, u32[]{:S(2)}) copy-start(f32[128,2048]{1,0:T(8,128)} %get-tuple-element.65.state_ref) | copy-start | bytes 3145732
  416.6 4.5 copy-start.11
  546.7 4.3 copy-start.4
  546.7 8.9 %copy-start.7 = (bf16[2,2048,256]{2,1,0:T(8,128)(2,1)S(1)}, bf16[2,2048,256]{2,1,0:T(8,128)(2,1)}, u32[]{:S(2)}) copy-start(bf16[2,2048,256]{2,1,0:T(8,128)(2,1)} %get-tuple-element.101) | copy-start | bytes 6291460
  551.0 4.6 copy-start.2
  551.0 5.6 copy-start.3
  551.0 6.2 %copy-start.6 = (bf16[2,2048,256]{2,1,0:T(8,128)(2,1)S(1)}, bf16[2,2048,256]{2,1,0:T(8,128)(2,1)}, u32[]{:S(2)}) copy-start(bf16[2,2048,256]{2,1,0:T(8,128)(2,1)} %get-tuple-element.99) | copy-start | bytes 6291460
  561.4 3.3 copy-start.10
  561.4 4.1 copy-start.9
  561.4 5.7 %copy-start.1 = (bf16[512,2048]{1,0:T(8,128)(2,1)S(1)}, bf16[512,2048]{1,0:T(8,128)(2,1)}, u32[]{:S(2)}) copy-start(bf16[512,2048]{1,0:T(8,128)(2,1)} %param.31) | copy-start | bytes 6291460
  564.7 1.6 copy-start.8

commit v7 on v6

--- a/solution.py
+++ b/solution.py
@@ -392,7 +392,7 @@
 MESH = pl.DeviceIdType.MESH
 ANY = pl.BlockSpec(memory_space=pl.ANY)
 VMEM = pl.BlockSpec(memory_space=pltpu.VMEM)
-VMEM_BYTES = 60 * 1024 * 1024
+VMEM_BYTES = 62 * 1024 * 1024
 LOW = jnp.bfloat16
 FULL = jnp.float32
 
@@ -455,18 +455,19 @@
         self.open.append((copy, set()))
         return copy
 
-    def mark(self, copy, what):
-        for entry, done in self.open:
-            if entry is copy:
-                done.add(what)
+    def once(self, copy, what):
+        done = next(done for entry, done in self.open if entry is copy)
+        new = what not in done
+        done.add(what)
+        return new
 
     def arrived(self, copy):
-        copy.wait_recv()
-        self.mark(copy, "arrived")
+        if self.once(copy, "arrived"):
+            copy.wait_recv()
 
     def sent(self, copy):
-        copy.wait_send()
-        self.mark(copy, "sent")
+        if self.once(copy, "sent"):
+            copy.wait_send()
 
     def finish(self):
         for copy, done in self.open:
@@ -477,59 +478,81 @@
 
 
 class Gather:
-    def __init__(self, copies, block, target, rows, z_send, z_recv, p_send, p_recv):
+    def __init__(self, copies, block, target, rows, z_send, z_recv, p_send, p_recv, c_send, c_recv):
         self.copies, self.block, self.target, self.rows = copies, block, target, rows
         self.z_send, self.z_recv, self.p_send, self.p_recv = z_send, z_recv, p_send, p_recv
+        self.c_send, self.c_recv = c_send, c_recv
         z, x, y, core = place()
         self.over_x, self.over_y = device(z, 1 - x, y, core), device(z, x, 1 - y, core)
         self.here, self.x_place, self.y_place = 2 * x + y, 2 * (1 - x) + y, 2 * x + 1 - y
+        self.far = 2 * (1 - x) + 1 - y
         self.column = [device(swapped(z, step), x, y, core) for step in range(target.shape[0])]
-        self.along, self.planes, self.diagonals = {}, {}, {}
-
-    def at(self, step, spot, part):
-        half = self.rows // 2
-        if part is None:
-            return self.target.at[step, pl.ds(pl.multiple_of(spot * self.rows, self.rows), self.rows)]
-        return self.target.at[step, pl.ds(pl.multiple_of(spot * self.rows + part * half, half), half)]
-
-    def begin(self):
-        self.spread(0)
-        for step in range(1, len(self.column)):
-            self.lift(step)
+        self.along, self.planes, self.diagonals, self.shared = {}, {}, {}, {}
+        edge = rows * 3 // 8
+        self.middle = (edge, rows - 2 * edge)
+        self.halves = {0: ((0, rows // 2), (rows // 2, rows // 2)), 1: ((0, edge), (rows - edge, edge))}
+
+    def at(self, step, spot, span):
+        first, count = span
+        return self.target.at[step, pl.ds(pl.multiple_of(spot * self.rows + first, 16), count)]
 
     def lift(self, step):
-        if 0 < step < len(self.column):
-            self.along[step] = self.copies.start(
-                remote(self.block, self.at(step, self.here, None), self.z_send.at[step], self.z_recv.at[step], self.column[step])
-            )
+        low, whole = step & -step, (0, self.rows)
+        source = self.block if step == low else self.at(step - low, self.here, whole)
+        self.along[step] = self.copies.start(
+            remote(source, self.at(step, self.here, whole), self.z_send.at[step], self.z_recv.at[step], self.column[low])
+        )
 
     def spread(self, step):
         if step:
             self.copies.arrived(self.along[step])
-        half = self.rows // 2
+            bit = 1
+            while bit < step & -step:
+                self.lift(step | bit)
+                bit *= 2
         planes = []
         for number, (to, part) in enumerate([(self.over_x, 0), (self.over_y, 1), (self.over_x, 1), (self.over_y, 0)]):
-            here = self.at(step, self.here, part)
-            source = here if step else self.block.at[pl.ds(part * half, half)]
+            span = self.halves[step % 2][part]
+            here = self.at(step, self.here, span)
+            source = here if step else self.block.at[pl.ds(*span)]
             planes.append(self.copies.start(remote(source, here, self.p_send.at[step, number], self.p_recv.at[step, number], to)))
         self.planes[step] = planes
 
     def turn(self, step):
-        self.copies.arrived(self.planes[step][0])
-        passed = self.at(step, self.x_place, 0)
-        first = self.copies.start(remote(passed, passed, self.p_send.at[step, 4], self.p_recv.at[step, 4], self.over_y))
-        self.copies.arrived(self.planes[step][1])
-        passed = self.at(step, self.y_place, 1)
-        second = self.copies.start(remote(passed, passed, self.p_send.at[step, 5], self.p_recv.at[step, 5], self.over_x))
-        self.diagonals[step] = (first, second)
+        passed = []
+        for part, spot, to in ((0, self.x_place, self.over_y), (1, self.y_place, self.over_x)):
+            self.copies.arrived(self.planes[step][part])
+            here = self.at(step, spot, self.halves[step % 2][part])
+            passed.append(
+                self.copies.start(remote(here, here, self.p_send.at[step, 4 + part], self.p_recv.at[step, 4 + part], to))
+            )
+        self.diagonals[step] = passed
+
+    def share(self, step):
+        self.complete(step)
+        copies = []
+        for number, spot in enumerate((self.x_place, self.y_place, self.far)):
+            copies.append(
+                self.copies.start(
+                    remote(
+                        self.at(step, spot, self.middle), self.at(step + 1, spot, self.middle),
+                        self.c_send.at[step // 2, number], self.c_recv.at[step // 2, number], self.column[1],
+                    )
+                )
+            )
+        self.shared[step + 1] = copies
 
     def complete(self, step):
-        for copy in self.planes[step][2:] + list(self.diagonals[step]):
+        for copy in self.planes[step] + self.diagonals[step] + self.shared.get(step, []):
             self.copies.arrived(copy)
 
+    @staticmethod
+    def scratch(depth):
+        return [dma(depth), dma(depth), dma(depth, 6), dma(depth, 6), dma(depth // 2, 3), dma(depth // 2, 3)]
+
 
 class Scatter:
-    def __init__(self, copies, work, diagonal, from_x, from_y, from_z, rows, send, recv):
+    def __init__(self, copies, work, diagonal, from_x, from_y, from_z, rows, send, recv, middle=None):
         self.copies, self.work, self.rows, self.send, self.recv = copies, work, rows, send, recv
         self.diagonal, self.from_x, self.from_y, self.from_z = diagonal, from_x, from_y, from_z
         z, x, y, core = place()
@@ -537,57 +560,89 @@
         self.here, self.x_place, self.y_place = 2 * x + y, 2 * (1 - x) + y, 2 * x + 1 - y
         self.far = 2 * (1 - x) + 1 - y
         self.column = [device(swapped(z, step), x, y, core) for step in range(work.shape[0])]
-        self.corners, self.sides, self.along = {}, {}, {}
-
-    def at(self, step, spot, part=None):
-        half = self.rows // 2
-        if part is None:
-            return self.work.at[step, pl.ds(pl.multiple_of(spot * self.rows, self.rows), self.rows)]
-        return self.work.at[step, pl.ds(pl.multiple_of(spot * self.rows + part * half, half), half)]
+        self.corners, self.sides, self.along, self.shared, self.middle = {}, {}, {}, {}, middle
+        edge, half = rows * 3 // 8, rows // 2
+        self.center = (edge, rows - 2 * edge)
+        self.halves = {0: ((0, half), (half, half)), 1: ((0, half), (half, half))}
+        self.pieces = {0: ((0, rows),), 1: ((0, rows),)}
+        if middle:
+            self.halves[1] = self.pieces[1] = ((0, edge), (rows - edge, edge))
+
+    def at(self, step, spot, span):
+        first, count = span
+        return self.work.at[step, pl.ds(pl.multiple_of(spot * self.rows + first, 16), count)]
 
     def copy(self, step, number, source, target, to):
         return self.copies.start(remote(source, target, self.send.at[step, number], self.recv.at[step, number], to))
 
+    def share(self, step):
+        landed, send, recv = self.middle
+        self.shared[step - 1] = [
+            self.copies.start(
+                remote(
+                    self.at(step, spot, self.center), landed.at[step // 2, spot],
+                    send.at[step // 2, spot], recv.at[step // 2, spot], self.column[1],
+                )
+            )
+            for spot in range(4)
+        ]
+
     def corner(self, step):
+        for spot, copy in enumerate(self.shared.get(step, [])):
+            self.copies.arrived(copy)
+            mine = self.at(step, spot, self.center)
+            add_rows(mine, [mine, self.middle[0].at[step // 2, spot]], self.center[1])
+        first, second = self.halves[step % 2]
         self.corners[step] = (
-            self.copy(step, 0, self.at(step, self.far, 0), self.diagonal.at[step, 0], self.over_y),
-            self.copy(step, 1, self.at(step, self.far, 1), self.diagonal.at[step, 1], self.over_x),
+            self.copy(step, 0, self.at(step, self.far, first), self.diagonal.at[step, pl.ds(*first)], self.over_y),
+            self.copy(step, 1, self.at(step, self.far, second), self.diagonal.at[step, pl.ds(*second)], self.over_x),
         )
 
     def side(self, step):
+        first, second = self.halves[step % 2]
         via_y, via_x = self.corners[step]
+
+        def to_x(number, span):
+            return self.copy(step, number, self.at(step, self.x_place, span), self.from_x.at[step, pl.ds(*span)], self.over_x)
+
+        def to_y(number, span):
+            return self.copy(step, number, self.at(step, self.y_place, span), self.from_y.at[step, pl.ds(*span)], self.over_y)
+
+        sides = [to_x(2, second), to_y(3, first)]
         self.copies.arrived(via_y)
-        add_rows(self.at(step, self.x_place, 0), [self.at(step, self.x_place, 0), self.diagonal.at[step, 0]], self.rows // 2)
-        to_x = self.copy(step, 2, self.at(step, self.x_place), self.from_x.at[step], self.over_x)
+        mine = self.at(step, self.x_place, first)
+        add_rows(mine, [mine, self.diagonal.at[step, pl.ds(*first)]], first[1])
+        sides.append(to_x(4, first))
         self.copies.arrived(via_x)
-        add_rows(self.at(step, self.y_place, 1), [self.at(step, self.y_place, 1), self.diagonal.at[step, 1]], self.rows // 2)
-        to_y = self.copy(step, 3, self.at(step, self.y_place), self.from_y.at[step], self.over_y)
-        self.sides[step] = (to_x, to_y)
+        mine = self.at(step, self.y_place, second)
+        add_rows(mine, [mine, self.diagonal.at[step, pl.ds(*second)]], second[1])
+        sides.append(to_y(5, second))
+        self.sides[step] = sides
 
     def climb(self, step):
         for copy in self.sides[step]:
             self.copies.arrived(copy)
         if step:
-            here = self.at(step, self.here)
-            add_rows(here, [here, self.from_x.at[step], self.from_y.at[step]], self.rows)
-            self.along[step] = self.copy(step, 4, here, self.from_z.at[step], self.column[step])
-
-    def result(self, target):
-        for copy in self.along.values():
-            self.copies.arrived(copy)
-        terms = [self.at(0, self.here), self.from_x.at[0], self.from_y.at[0]]
-        add_rows(target, terms + [self.from_z.at[step] for step in self.along], self.rows)
+            self.along[step] = []
+            for number, span in enumerate(self.pieces[step % 2]):
+                mine, part = self.at(step, self.here, span), pl.ds(*span)
+                add_rows(mine, [mine, self.from_x.at[step, part], self.from_y.at[step, part]], span[1])
+                self.along[step].append(self.copy(step, 6 + number, mine, self.from_z.at[step, part], self.column[step]))
+
+    def result(self, target, more=()):
+        for copies in self.along.values():
+            for copy in copies:
+                self.copies.arrived(copy)
+        for span in [*self.halves[1], self.center] if self.middle else self.pieces[0]:
+            part = pl.ds(*span)
+            steps = [step for step in self.along if not (self.middle and span is self.center and step % 2)]
+            terms = [self.at(0, self.here, span), self.from_x.at[0, part], self.from_y.at[0, part]]
+            terms += [self.from_z.at[step, part] for step in steps] + [term.at[part] for term in more]
+            add_rows(target.at[part], terms, span[1])
 
     @staticmethod
     def scratch(depth, rows, width):
-        return [
-            pltpu.VMEM((depth, 2, rows // 2, width), LOW),
-            pltpu.VMEM((depth, rows, width), LOW),
-            pltpu.VMEM((depth, rows, width), LOW),
-            pltpu.VMEM((depth, rows, width), LOW),
-            dma(depth, 5),
-            dma(depth, 5),
-        ]
+        return [pltpu.VMEM((depth, rows, width), LOW)] * 4 + [dma(depth, 8), dma(depth, 8)]
 
 
 def experts_kernel(
@@ -596,7 +651,7 @@
     sum_ref, cots_ref, normed_ref, gated_ref, gate_grad_ref, up_grad_ref, produced_ref,
     wg, wu, wd, x_all, grads, work, y_out, gated, gate_grad, up_grad, gates, gate_wide, cots, cot_rows,
     diagonal, from_x, from_y, from_z, r_send, r_recv,
-    z_send, z_recv, p_send, p_recv, s_send, s_recv, w_send, w_recv, w_load, g_load, saves, local_sem,
+    z_send, z_recv, p_send, p_recv, c_send, c_recv, s_send, s_recv, w_send, w_recv, w_load, g_load, saves, local_sem,
 ):
     z, x, y, core = place()
     here, sibling = 2 * x + y, device(z, x, y, 1 - core)
@@ -619,8 +674,10 @@
                 )
             )
         )
-    gather = Gather(copies, x_ref, x_all, rows, z_send, z_recv, p_send, p_recv)
-    gather.begin()
+    gather = Gather(copies, x_ref, x_all, rows, z_send, z_recv, p_send, p_recv, c_send, c_recv)
+    gather.spread(0)
+    gather.lift(1)
+    gather.lift(2)
     plain = []
 
     def fetch(source, target, sem):
@@ -628,7 +685,7 @@
         copy.start()
         return copy
 
-    plain.append(fetch(x_ref, gather.at(0, here, None), local_sem.at[0]))
+    plain.append(fetch(x_ref, gather.at(0, here, (0, rows)), local_sem.at[0]))
     weights = []
     for index in range(local):
         first = pl.multiple_of((core * local + index) * hidden, hidden)
@@ -705,9 +762,8 @@
         producing.append(fetch(y_out, produced_ref.at[step], saves.at[3]))
 
     gather.turn(0)
-    if depth > 1:
-        gather.spread(1)
-    gather.complete(0)
+    gather.spread(1)
+    gather.share(0)
     for copy in plain:
         copy.wait()
     for copy in weights + smalls:
@@ -720,17 +776,22 @@
             gather.turn(step + 1)
         if step + 2 < depth:
             gather.spread(step + 2)
-        if step >= 1:
+        if step == 1:
+            gather.share(2)
+        if step >= 2:
             scatter.side(step - 1)
-        if step >= 2:
+        if step >= 3:
             scatter.climb(step - 2)
         second_half(step)
-        scatter.corner(step)
+        if step:
+            scatter.corner(step)
+    scatter.corner(0)
     own_cots = fetch(cot_rows.at[0, here], cots_ref.at[0, here], local_sem.at[2])
-    if depth > 1:
-        scatter.climb(depth - 2)
     scatter.side(depth - 1)
+    scatter.climb(depth - 2)
+    scatter.side(0)
     scatter.climb(depth - 1)
+    scatter.climb(0)
     scatter.result(sum_ref)
     own_cots.wait()
     for copy in saving + producing + keeping:
@@ -764,7 +825,7 @@
         ]
         + Scatter.scratch(depth, rows, width)
         + [
-            dma(depth), dma(depth), dma(depth, 6), dma(depth, 6), dma(2, depth, 4), dma(2, depth, 4),
+            *Gather.scratch(depth), dma(2, depth, 4), dma(2, depth, 4),
             dma(3, local), dma(3, local), dma(3, local), dma(2), dma(4 + depth), dma(3),
         ],
         compiler_params=comm_params(number),
@@ -883,8 +944,8 @@
     gain1_ref, q_gain_ref, k_gain_ref, cosine_ref, sine_ref, docs_ref, gain2_ref, router_ref, picked_ref,
     normed_turned, q_raw, k_raw, queries, kv_all, key_docs, scales, attended, logs, state_ref, normed2_ref, probs_ref, gates_ref,
     all_grad,
-    tokens, normed_ref, wq, wk, wv, wo, docs_in, squares, squares_in, scores, bias, partial, from_pair, from_y, sum_ref,
-    t_send, t_recv, z_send, z_recv, p_send, p_recv, h_send, h_recv, d_send, d_recv, q_send, q_recv, load,
+    tokens, normed_ref, wq, wk, wv, wo, docs_in, squares, squares_in, scores, totals, bias, partial, from_pair, from_y, sum_ref,
+    t_send, t_recv, z_send, z_recv, p_send, p_recv, c_send, c_recv, h_send, h_recv, d_send, d_recv, q_send, q_recv, load,
 ):
     z, x, y, core = place()
     group, part = lax.axis_index("expert"), lax.axis_index("tensor")
@@ -912,10 +973,10 @@
                 docs_ref, docs_in.at[2 - distance], d_send.at[distance], d_recv.at[distance], (group + distance, part)
             ).start()
 
-    gather = Gather(copies, grad_ref, all_grad, rows, z_send, z_recv, p_send, p_recv)
+    gather = Gather(copies, grad_ref, all_grad, rows, z_send, z_recv, p_send, p_recv, c_send, c_recv)
     gather.spread(0)
     gather.lift(1)
-    own = pltpu.make_async_copy(grad_ref, gather.at(0, gather.here, None), load.at[5])
+    own = pltpu.make_async_copy(grad_ref, gather.at(0, gather.here, (0, rows)), load.at[5])
     own.start()
     key_part, value_part = pl.ds(0, wide), pl.ds(wide, wide)
 
@@ -1052,37 +1113,41 @@
             columns = pl.ds(pl.multiple_of(head * HD, HD), HD)
             keys = pl.ds(block * length, length)
             scores[head, keys, :] = dot_t(kv_all[block, :, columns], queries[:, columns]) * scale + bias[keys, :]
-
     score(2)
     halo_relay(1)
+    halo_relay(0)
+    gather.share(0)
+    gather.spread(2)
+    halo_arrive(0)
     gather.turn(1)
-    halo_relay(0)
-    gather.spread(2)
-    gather.lift(3)
-    halo_arrive(0)
+    score(1)
     score(0)
-    score(1)
-    gather.turn(2)
-    halo_arrive(1)
 
     @pl.loop(0, heads)
     def _(head):
-        columns = pl.ds(pl.multiple_of(head * HD, HD), HD)
         mine = scores.at[head]
         highest = jnp.max(mine[...], axis=0, keepdims=True)
         total = jnp.zeros_like(highest)
-        mixed = jnp.zeros((HD, length), FULL)
         for block in range(3):
             weights = jnp.exp(mine[pl.ds(block * length, length), :] - highest)
             total = total + jnp.sum(weights, axis=0, keepdims=True)
             mine[pl.ds(block * length, length), :] = weights
+        logs[head] = jnp.broadcast_to(highest + jnp.log(total), (8, length))
+        totals[head] = jnp.broadcast_to(1.0 / total, (8, length))
+
+    halo_arrive(1)
+
+    @pl.loop(0, heads)
+    def _(head):
+        columns = pl.ds(pl.multiple_of(head * HD, HD), HD)
+        values = pl.ds(pl.multiple_of((heads + head) * HD, HD), HD)
+        mixed = jnp.zeros((HD, length), FULL)
         for block in range(3):
-            probs = (mine[pl.ds(block * length, length), :] * (1.0 / total)).astype(LOW)
-            values = pl.ds(pl.multiple_of((heads + head) * HD, HD), HD)
+            probs = (scores[head, pl.ds(block * length, length), :] * totals[head, 0:1, :]).astype(LOW)
             mixed = mixed + t_dot(kv_all[block, :, values], probs)
         attended[:, columns] = mixed.T.astype(LOW)
-        logs[head] = jnp.broadcast_to(highest + jnp.log(total), (8, length))
-
+
+    gather.turn(2)
     gather.spread(3)
     loads[4].wait()
     for index in range(4):
@@ -1090,6 +1155,7 @@
     scatter = TensorScatter(copies, partial, from_pair, from_y, t_send, t_recv)
     scatter.begin()
     scatter.cross()
+    gather.share(2)
     gather.turn(3)
     scatter.result(sum_ref)
     own_rows = pl.ds(pl.multiple_of(part * rows, rows), rows)
@@ -1149,12 +1215,13 @@
             pltpu.VMEM(tokens.shape, LOW), pltpu.VMEM(tokens.shape, LOW), pltpu.VMEM((width, wide), LOW), pltpu.VMEM((width, wide), LOW),
             pltpu.VMEM((width, wide), LOW), pltpu.VMEM((wide, width), LOW), pltpu.VMEM((2, 8, length), jnp.int32),
             pltpu.VMEM((8, length), FULL), pltpu.VMEM((3, 8, length), FULL),
-            pltpu.VMEM((heads, 3 * length, length), FULL), pltpu.VMEM((3 * length, length), FULL),
+            pltpu.VMEM((heads, 3 * length, length), FULL), pltpu.VMEM((heads, 8, length), FULL),
+            pltpu.VMEM((3 * length, length), FULL),
         ]
         + TensorScatter.scratch(rows, width)[:3]
         + [
             pltpu.VMEM((rows, width), FULL), dma(3), dma(3),
-            dma(depth), dma(depth), dma(depth, 6), dma(depth, 6), dma(2, 3), dma(2, 3), dma(3), dma(3), dma(3), dma(3), dma(6),
+            *Gather.scratch(depth), dma(2, 3), dma(2, 3), dma(3), dma(3), dma(3), dma(3), dma(6),
         ],
         compiler_params=comm_params(number),
     )(tokens, *weights, grads, *gains, *tables, docs, gain2, router, picked)
@@ -1165,10 +1232,11 @@
     sum_ref, gate_cots, probs_ref, picked_ref, state_ref, gain2_ref, router_ref, normed2_ref, grad_ref,
     query_ref, kv_all, attended, logs, key_docs, query_docs, q_raw, k_raw, q_gain_ref, k_gain_ref, cosine_ref, sine_ref, scales,
     w_out, produced_ref, normed_ref, wq_ref, wk_ref, wv_ref,
-    state_cot_ref, router_grad_ref, norm2_grad_ref, q_grad_ref, k_grad_ref, mix_ref, normed_part, piece0, piece1, piece2, piece3,
+    state_cot_ref, vectors, out_ref, normed_part, piece0, piece1, piece2, piece3,
     low, lows, by_expert, bias, cots, deltas, turned, query_cot, kv_cot, sending, landed, work, raw_cots, flipped, wq, wk, wv,
     inners, inners_in, staging,
-    diagonal, from_x, from_y, from_z, r_send, r_recv, t_send, t_recv, h_send, h_recv, i_send, i_recv, load, saves,
+    diagonal, from_x, from_y, from_z, r_send, r_recv, middle, m_send, m_recv,
+    t_send, t_recv, h_send, h_recv, i_send, i_recv, load, saves,
 ):
     z, x, y, core = place()
     group, part = lax.axis_index("expert"), lax.axis_index("tensor")
@@ -1176,7 +1244,7 @@
     length, width = query_ref.shape[0], w_out.shape[1]
     wide = heads * HD
     scale = HD ** (-0.5)
-    order = [step for step in range(depth - 1, 0, -1)] + [0]
+    order = [step for step in range(depth - 1, 0, -2)] + [step for step in range(depth - 2, -1, -2)]
     loads = {}
     for step in order:
         loads[step] = pltpu.make_async_copy(produced_ref.at[step], work.at[step], load.at[step])
@@ -1192,12 +1260,18 @@
         + [device(*mate) for mate in mates]
     )
     copies = Copies()
-    scatter = Scatter(copies, work, diagonal, from_x, from_y, from_z, rows, r_send, r_recv)
+    scatter = Scatter(
+        copies, work, diagonal, from_x, from_y, from_z, rows, r_send, r_recv, (middle, m_send, m_recv)
+    )
 
     def corner(step):
+        if step % 2 == 0:
+            loads[step].wait()
+        scatter.corner(step)
+
+    for step in order[:2]:
         loads[step].wait()
-        scatter.corner(step)
-
+        scatter.share(step)
     for step in order[:2]:
         corner(step)
 
@@ -1216,7 +1290,11 @@
     )
     state = state_ref[...]
     factor = lax.rsqrt(jnp.mean(state * state, axis=-1, keepdims=True) + NORM_EPSILON)
-    norm2_grad_ref[...] = jnp.broadcast_to(jnp.sum(normed2_cot * state * factor, axis=0, keepdims=True), norm2_grad_ref.shape)
+    groups, _, slice_width = vectors.shape
+    vectors[...] = jnp.zeros_like(vectors)
+    gain_grad = jnp.sum(normed2_cot * state * factor, axis=0, keepdims=True)
+    for index in range(groups):
+        vectors[index, 17:18, :] = gain_grad[:, index * slice_width : (index + 1) * slice_width]
     inner = jnp.sum(normed2_cot * gain2_ref[0:1, :] * state, axis=-1, keepdims=True)
     state_cot = (
         grad_ref[...].astype(FULL)
@@ -1227,9 +1305,11 @@
     low[...] = state_cot.astype(LOW)
     gather = TensorGather(copies, low, lows, t_send, t_recv)
     scatter.side(order[0])
-    router_grad_ref[...] = jnp.dot(
+    router_grad = jnp.dot(
         logit_cot.T, normed2_ref[...].astype(FULL), precision=HIGHEST_PRECISION, preferred_element_type=FULL
-    )[: router_grad_ref.shape[0]]
+    )[:16]
+    for index in range(groups):
+        vectors[index, 0:16, :] = router_grad[:, index * slice_width : (index + 1) * slice_width]
     mask_bias(bias, key_docs, query_docs, length)
     gather.cross()
     gather.finish()
@@ -1241,7 +1321,7 @@
         deltas[head] = jnp.broadcast_to(jnp.sum(product.T, axis=0, keepdims=True), (8, length))
     turned[...] = jnp.zeros_like(turned)
 
-    def back(block, target):
+    def back(block, store, after):
         @pl.loop(0, heads)
         def _(head):
             columns = pl.ds(pl.multiple_of(head * HD, HD), HD)
@@ -1258,34 +1338,44 @@
                 probs = jnp.exp(dot_t(key, query) * scale + hidden - log)
                 score_cot = (probs * (dot_t(value, cot) - delta)).astype(LOW)
                 turned[head] += t_dot(key, score_cot)
-                target[keys, columns] = (dot(score_cot, query) * scale).astype(target.dtype)
-                target[keys, values] = dot(probs.astype(LOW), cot).astype(target.dtype)
+                store(head, keys, dot(score_cot, query) * scale, dot(probs.astype(LOW), cot))
+
+            after(head)
+
+    def store_in(slot):
+        def store(head, keys, key_part, value_part):
+            sending[slot, head, keys, 0:HD] = key_part.astype(LOW)
+            sending[slot, head, keys, HD : 2 * HD] = value_part.astype(LOW)
+
+        return store
+
+    def store_own(head, keys, key_part, value_part):
+        kv_cot[keys, pl.ds(pl.multiple_of(head * HD, HD), HD)] = key_part
+        kv_cot[keys, pl.ds(pl.multiple_of((heads + head) * HD, HD), HD)] = value_part
 
     high = lax.rem(z, 2)
     over_x, over_z = device(z, 1 - x, y, core), device(swapped(z, 1), x, y, core)
 
-    def x_copy():
-        return remote(sending.at[1], landed.at[1], h_send.at[0], h_recv.at[0], over_x)
-
-    def z_copy():
-        return remote(sending.at[0], landed.at[0], h_send.at[1], h_recv.at[1], over_z)
-
-    back(1, sending.at[1])
-    pl.when(spot >= 1)(lambda: x_copy().start())
-    corner(1)
+    def x_copy(head):
+        return remote(sending.at[1, head], landed.at[1, head], h_send.at[0, head], h_recv.at[0, head], over_x)
+
+    def z_copy(head):
+        return remote(sending.at[0, head], landed.at[0, head], h_send.at[1, head], h_recv.at[1, head], over_z)
+
+    def relay(head):
+        @pl.when(spot == 3)
+        def _():
+            x_copy(head).wait_recv()
+            add_rows(sending.at[0, head], [sending.at[0, head], landed.at[1, head]], length, 64)
+            z_copy(head).start()
+
+    back(1, store_in(1), lambda head: pl.when(spot >= 1)(lambda: x_copy(head).start()))
+    corner(order[2])
     scatter.side(order[1])
-    back(0, sending.at[0])
-    pl.when(spot == 2)(lambda: z_copy().start())
+    back(0, store_in(0), lambda head: pl.when(spot == 2)(lambda: z_copy(head).start()))
     scatter.climb(order[0])
-    back(2, kv_cot)
-
-    @pl.when(spot == 3)
-    def _():
-        x_copy().wait_recv()
-        add_rows(sending.at[0], [sending.at[0], landed.at[1]], length)
-        z_copy().start()
-
-    corner(0)
+    back(2, store_own, relay)
+    corner(order[3])
     for head in range(heads):
         query_cot[:, pl.ds(head * HD, HD)] = turned[head].T * scale
     scatter.side(order[2])
@@ -1314,7 +1404,7 @@
     scatter.side(order[3])
     factors = as_columns(scales[...])
 
-    def turn_back(cot, raw, gain_ref, factor, grad_out):
+    def turn_back(cot, raw, gain_ref, factor, first):
         total = jnp.zeros((length, 1), FULL)
         for head in range(heads):
             columns = pl.ds(head * HD, HD)
@@ -1322,24 +1412,27 @@
             mine = mine * cosine_ref[...] - pltpu.roll(mine, HD // 2, 1) * sine_ref[...]
             cot[:, columns] = mine
             mine = mine * raw[:, columns]
-            grad_out[:, columns] = jnp.broadcast_to(jnp.sum(mine * factor, axis=0, keepdims=True), (8, HD))
+            grad = jnp.sum(mine * factor, axis=0, keepdims=True)
+            for index in range(groups):
+                vectors[index, first + head : first + head + 1, 0:HD] = grad
             total = total + jnp.sum(mine * gain_ref[0:1, columns], axis=-1, keepdims=True)
         return total
 
-    query_inner = turn_back(query_cot, q_raw, q_gain_ref, factors[:, 0:1], q_grad_ref)
+    query_inner = turn_back(query_cot, q_raw, q_gain_ref, factors[:, 0:1], 18)
     scatter.climb(order[2])
 
-    @pl.when(x == 0)
-    def _():
-        x_copy().wait_recv()
-        add_rows(kv_cot, [kv_cot, landed.at[1]], length)
-
-    @pl.when(high == 0)
-    def _():
-        z_copy().wait_recv()
-        add_rows(kv_cot, [kv_cot, landed.at[0]], length)
-
-    key_inner = turn_back(kv_cot, k_raw, k_gain_ref, factors[:, 1:2], k_grad_ref)
+    def take(slot, head):
+        (z_copy, x_copy)[slot](head).wait_recv()
+        for part in range(2):
+            mine = kv_cot.at[:, pl.ds((part * heads + head) * HD, HD)]
+            add_rows(mine, [mine, landed.at[slot, head, :, pl.ds(part * HD, HD)]], length, 64)
+
+    for head in range(heads):
+        pl.when(x == 0)(functools.partial(take, 1, head))
+    for head in range(heads):
+        pl.when(high == 0)(functools.partial(take, 0, head))
+
+    key_inner = turn_back(kv_cot, k_raw, k_gain_ref, factors[:, 1:2], 18 + heads)
     inners[...] = as_rows([query_inner, key_inner])
     sent = exchange(copies, inners, inners_in, i_send, i_recv, mates)
     raw_cots[2] = kv_cot[:, pl.ds(wide, wide)].astype(LOW)
@@ -1378,16 +1471,17 @@
     weight_piece(2, raw_cots[0], piece2)
     weight_piece(3, raw_cots[1], piece3)
     scatter.climb(order[3])
-    scatter.result(mix_ref)
-    pl.when(spot >= 1)(lambda: x_copy().wait_send())
-    pl.when(spot >= 2)(lambda: z_copy().wait_send())
+    scatter.result(out_ref, [state_ref])
+    for head in range(heads):
+        pl.when(spot >= 1)(lambda: x_copy(head).wait_send())
+        pl.when(spot >= 2)(lambda: z_copy(head).wait_send())
 
     for copy in saving.values():
         copy.wait()
     copies.finish()
 
 
-def run_attention_back(rows_of, attention, sources, produced, normed, weights, chain, local, experts, number):
+def run_attention_back(rows_of, attention, sources, produced, normed, weights, chain, local, number):
     depth = produced.shape[0]
     rows, width = rows_of[0].shape
     queries, kv_all = attention[0], attention[1]
@@ -1399,28 +1493,26 @@
         functools.partial(attention_back_kernel, depth, rows, heads, chain, local),
         out_shape=(
             jax.ShapeDtypeStruct((rows, width), FULL),
-            jax.ShapeDtypeStruct((experts, width), FULL),
-            jax.ShapeDtypeStruct((8, width), FULL),
-            jax.ShapeDtypeStruct((8, wide), FULL),
-            jax.ShapeDtypeStruct((8, wide), FULL),
-            jax.ShapeDtypeStruct((rows, width), FULL),
+            jax.ShapeDtypeStruct((2 * depth, 32, width // (2 * depth)), FULL),
+            jax.ShapeDtypeStruct((rows, width), LOW),
             jax.ShapeDtypeStruct((2, 2, rows, width), LOW),
             piece, piece, piece, piece,
         ),
         in_specs=[VMEM] * 23 + [ANY] * 5,
-        out_specs=(VMEM,) * 7 + (ANY,) * 4,
+        out_specs=(VMEM,) * 4 + (ANY,) * 4,
         scratch_shapes=[
             pltpu.VMEM((rows, width), LOW), pltpu.VMEM((2, 2, rows, width), LOW), pltpu.VMEM((128, rows), FULL),
             pltpu.VMEM((3 * length, length), LOW), pltpu.VMEM((length, wide), LOW),
             pltpu.VMEM((heads, 8, length), FULL), pltpu.VMEM((heads, HD, length), FULL),
             pltpu.VMEM((length, wide), FULL), pltpu.VMEM((length, wide2), FULL),
-            pltpu.VMEM((2, length, wide2), LOW), pltpu.VMEM((2, length, wide2), LOW),
+            pltpu.VMEM((2, heads, length, 2 * HD), LOW), pltpu.VMEM((2, heads, length, 2 * HD), LOW),
             pltpu.VMEM(produced.shape, LOW), pltpu.VMEM((3, length, wide), LOW), pltpu.VMEM((width, length), LOW),
             pltpu.VMEM((width, wide), LOW), pltpu.VMEM((width, wide), LOW), pltpu.VMEM((width, wide), LOW),
             pltpu.VMEM((8, length), FULL), pltpu.VMEM((3, 8, length), FULL), pltpu.VMEM((2,) + piece.shape[2:], LOW),
         ]
         + Scatter.scratch(depth, rows, width)
-        + [dma(4), dma(3), dma(3), dma(3), dma(3), dma(3), dma(depth + 4), dma(2)],
+        + [pltpu.VMEM((depth // 2, 4, rows // 4, width), LOW), dma(depth // 2, 4), dma(depth // 2, 4)]
+        + [dma(4), dma(3), dma(2, heads), dma(2, heads), dma(3), dma(3), dma(depth + 4), dma(2)],
         compiler_params=comm_params(number),
     )(*rows_of, *attention, *sources, produced, normed, *weights)
 
@@ -1438,48 +1530,100 @@
 
 
 class ExpertScatter:
-    def __init__(self, copies, parts, work, from_x, from_z, load, send, recv):
+    def __init__(self, copies, parts, widths, work, from_x, from_z, load, send, recv):
+        self.widths = widths
         self.copies, self.parts, self.work, self.from_x, self.from_z = copies, parts, work, from_x, from_z
         self.load, self.send, self.recv = load, send, recv
         self.z, self.x, y, core = place()
         self.depth, self.rows = work.shape[1], work.shape[2]
         self.over_x = device(self.z, 1 - self.x, y, core)
         self.column = [device(swapped(self.z, step), self.x, y, core) for step in range(self.depth)]
-        self.order = list(range(self.depth - 1, -1, -1))
+        self.order = sorted(range(self.depth), key=lambda step: (step == 0, step & -step, -step))
+        self.steps = self.order[:-1]
         self.loads, self.sides, self.along = {}, {}, {}
 
     def begin(self, index):
         for step in self.order:
             at = swapped(self.z, step)
+            columns = pl.ds(0, self.widths[index])
             self.sides[index, step] = self.copies.start(
                 remote(
-                    self.parts[index].at[at, 1 - self.x], self.from_x.at[index, step],
+                    self.parts[index].at[at, 1 - self.x, :, columns], self.from_x.at[index, step, :, columns],
                     self.send.at[0, index, step], self.recv.at[0, index, step], self.over_x,
                 )
             )
-            load = pltpu.make_async_copy(self.parts[index].at[at, self.x], self.work.at[index, step], self.load.at[index, step])
+            load = pltpu.make_async_copy(
+                self.parts[index].at[at, self.x, :, columns], self.work.at[index, step, :, columns], self.load.at[index, step]
+            )
             load.start()
             self.loads[index, step] = load
 
     def climb(self, index, step):
         self.loads[index, step].wait()
         self.copies.arrived(self.sides[index, step])
-        mine = self.work.at[index, step]
+        columns = pl.ds(0, self.widths[index])
+        mine = self.work.at[index, step, :, columns]
+        low = step & -step
+        terms = [mine, self.from_x.at[index, step, :, columns]] + self.below(index, step)
+        add_rows(mine, terms, self.rows)
+        self.along[index, step] = self.copies.start(
+            remote(
+                mine, self.from_z.at[index, step, :, columns],
+                self.send.at[1, index, step], self.recv.at[1, index, step], self.column[low],
+            )
+        )
+
+    def below(self, index, step):
+        terms, bit = [], 1
+        while bit < (step & -step if step else self.depth):
+            self.copies.arrived(self.along[index, step | bit])
+            terms.append(self.from_z.at[index, step | bit, :, pl.ds(0, self.widths[index])])
+            bit *= 2
+        return terms
+
+    def result(self, index, target):
+        self.loads[index, 0].wait()
+        self.copies.arrived(self.sides[index, 0])
+        columns = pl.ds(0, self.widths[index])
+        terms = [self.work.at[index, 0, :, columns], self.from_x.at[index, 0, :, columns]] + self.below(index, 0)
+        add_rows(target.at[:, columns], terms, self.rows)
+
+
+class ZScatter:
+    def __init__(self, copies, part, columns, work, from_z, from_x, load, send, recv):
+        self.copies, self.part, self.columns = copies, part, columns
+        self.work, self.from_z, self.from_x, self.load, self.send, self.recv = work, from_z, from_x, load, send, recv
+        self.z, self.x, y, core = place()
+        self.depth, self.rows = work.shape[0], work.shape[2]
+        self.over_x = device(self.z, 1 - self.x, y, core)
+        self.column = [device(swapped(self.z, step), self.x, y, core) for step in range(self.depth)]
+        self.loads, self.along = {}, {}
+
+    def begin(self):
+        for step in range(self.depth):
+            source = self.part.at[swapped(self.z, step), :, :, self.columns]
+            self.loads[step] = pltpu.make_async_copy(source, self.work.at[step], self.load.at[step])
+            self.loads[step].start()
+
+    def climb(self, step):
+        self.loads[step].wait()
+        low = step & -step if step else self.depth
+        bit = 1
+        while bit < low:
+            self.copies.arrived(self.along[step | bit])
+            for column in range(2):
+                mine = self.work.at[step, column]
+                add_rows(mine, [mine, self.from_z.at[step | bit, column]], self.rows, 32)
+            bit *= 2
         if step:
-            add_rows(mine, [mine, self.from_x.at[index, step]], self.rows)
-            self.along[index, step] = self.copies.start(
-                remote(
-                    mine, self.from_z.at[index, step],
-                    self.send.at[1, index, step], self.recv.at[1, index, step], self.column[step],
-                )
-            )
-
-    def result(self, index, target):
-        terms = [self.work.at[index, 0], self.from_x.at[index, 0]]
-        for step in range(1, self.depth):
-            self.copies.arrived(self.along[index, step])
-            terms.append(self.from_z.at[index, step])
-        add_rows(target, terms, self.rows)
+            copy = remote(self.work.at[step], self.from_z.at[step], self.send.at[step], self.recv.at[step], self.column[low])
+        else:
+            copy = remote(self.work.at[0, 1 - self.x], self.from_x, self.send.at[0], self.recv.at[0], self.over_x)
+        self.along[step] = self.copies.start(copy)
+
+    def result(self, target):
+        self.copies.arrived(self.along[0])
+        add_rows(target, [self.work.at[0, self.x], self.from_x], self.rows)
 
 
 def gradients_kernel(
@@ -1487,15 +1631,16 @@
 ):
     parts, refs = refs[:matrices], refs[matrices:]
     (
-        normed_part, tokens_ref, state_cot, scale_ref, gain_ref, out_ref, vector_ref,
+        normed_part, tokens_ref, state_cot, gain_ref, out_ref, vector_ref,
         normed_ref, grad_ref, gated_ref, gate_grad_ref, up_grad_ref,
-    ) = refs[:12]
-    sums, refs = refs[12 : 12 + matrices], refs[12 + matrices :]
+    ) = refs[:11]
+    sums, refs = refs[11 : 11 + matrices], refs[11 + matrices :]
     (
         input_grads, outputs, vector_sum,
-        gate_own, up_own, down_own, gate_other, up_other, down_other,
+        gate_own, up_own, down_own,
         work, from_x, from_z, partial, from_pair, from_y, normed_grad, low, vectors, vector_in, vector_mid, vector_turn,
-        tiles, turned, acts, gated_turned, near, far, near_down, far_down,
+        tiles, turned, acts, gated_turned, near, far, near_down, far_down, other, other_down,
+        f_work, f_from_z, f_from_x, f_load, f_send, f_recv,
         e_load, e_send, e_recv, t_send, t_recv, g_send, g_recv, o_send, o_recv, v_send, v_recv, u_send, u_recv,
         tile_load, act_load, save, pair_send, pair_recv, local_sem,
     ) = refs
@@ -1508,7 +1653,7 @@
     greet(peers + [device(*mate) for mate in mates])
     copies = Copies()
     width = normed_ref.shape[1]
-    tile = 512
+    tile = local * hidden
     count = width // tile
 
     def fetch(source, target, sem):
@@ -1516,9 +1661,14 @@
         copy.start()
         return copy
 
-    experts = ExpertScatter(copies, parts, work, from_x, from_z, e_load, e_send, e_recv)
+    wide = work.shape[3]
+    widths = [wide] * (matrices - 1) + [wide // 2]
+    experts = ExpertScatter(copies, parts, widths, work, from_x, from_z, e_load, e_send, e_recv)
+    eighth = pl.ds(wide // 2, wide // 2)
+    z_first = ZScatter(copies, parts[-1], eighth, f_work, f_from_z, f_from_x, f_load, f_send, f_recv)
     loaded = fetch(normed_part, partial, local_sem.at[0])
     experts.begin(0)
+    z_first.begin()
     loaded.wait()
     scatter = TensorScatter(copies, partial, from_pair, from_y, t_send, t_recv)
     scatter.begin()
@@ -1554,15 +1704,26 @@
                     target[which, slot, expert] = dot(turned[...], acts[which, :, columns]).astype(target.dtype)
 
         saves = []
-        place_of = pl.ds(number * tile, tile)
-        for which, (own, other) in enumerate(((gate_own, gate_other), (up_own, up_other))):
+        for which in range(2):
             away = remote(
-                far.at[which, slot], other.at[:, place_of], pair_send.at[which, number], pair_recv.at[which, number], sibling
+                far.at[which, slot], other.at[which, :, pl.ds(number * tile, tile)],
+                pair_send.at[which, number], pair_recv.at[which, number], sibling,
             )
             copies.start(away)
             saves.append((away, True))
-            saves.append((fetch(near.at[which, slot], own.at[:, place_of], save.at[which, slot]), False))
         saving[slot] = saves
+        if number:
+            settle(number - 1)
+
+    def settle(number):
+        slot, place_of = number % 2, pl.ds(number * tile, tile)
+        for which, own in enumerate((gate_own, up_own)):
+            copies.arrived(saving[slot][which][0])
+            for expert in range(local):
+                mine = near.at[which, slot, expert]
+                add_rows(mine, [mine, other.at[which, expert, place_of]], tile, 64)
+        for which, own in enumerate((gate_own, up_own)):
+            saving[slot].append((fetch(near.at[which, slot], own.at[:, place_of], save.at[which, slot]), False))
 
     def down(number):
         slot = number % 2
@@ -1571,34 +1732,45 @@
             tile_copies.append(fetch_tile(count + number + 1))
         for copy, remote_one in saving.pop(("down", slot), []):
             copies.sent(copy) if remote_one else copy.wait()
-        for owner, target in ((1 - core, far_down), (core, near_down)):
+        for source, target in ((turned, far_down), (gated_turned, near_down)):
 
             @pl.loop(0, local)
             def _(expert):
-                units = pl.ds(pl.multiple_of(first_unit(owner) + expert * hidden, hidden), hidden)
-                target[slot, expert] = dot(gated_turned[units, :], tiles[slot]).astype(target.dtype)
-
-        columns = pl.ds(number * tile, tile)
+                units = pl.ds(pl.multiple_of(expert * hidden, hidden), hidden)
+                target[slot, expert] = dot(source[units, :], tiles[slot]).astype(target.dtype)
+
         away = remote(
-            far_down.at[slot], down_other.at[:, :, columns], pair_send.at[2, number], pair_recv.at[2, number], sibling
+            far_down.at[slot], other_down.at[number], pair_send.at[2, number], pair_recv.at[2, number], sibling
         )
         copies.start(away)
-        saving["down", slot] = [
-            (away, True), (fetch(near_down.at[slot], down_own.at[:, :, columns], save.at[2, slot]), False)
-        ]
+        saving["down", slot] = [(away, True)]
+        settle(count - 1) if number == 0 else settle_down(number - 1)
+
+    def settle_down(number):
+        slot = number % 2
+        copies.arrived(saving["down", slot][0][0])
+        for expert in range(local):
+            mine = near_down.at[slot, expert]
+            add_rows(mine, [mine, other_down.at[number, expert]], hidden, 64)
+        target = down_own.at[:, :, pl.ds(number * tile, tile)]
+        saving["down", slot].append((fetch(near_down.at[slot], target, save.at[2, slot]), False))
 
     for copy in act_copies:
         copy.wait()
+    z_first.climb(3)
+    z_first.climb(1)
     gate_and_up(0)
     scatter.cross()
-    experts.climb(0, experts.order[0])
+    experts.climb(0, experts.steps[0])
     gate_and_up(1)
     out_gather.cross()
-    experts.climb(0, experts.order[1])
+    experts.climb(0, experts.steps[1])
+    z_first.climb(2)
     scatter.result(normed_grad)
 
     inputs = tokens_ref[...].astype(FULL)
-    factor, gain = scale_ref[:, 0:1], gain_ref[0:1, :]
+    factor = lax.rsqrt(jnp.mean(inputs * inputs, axis=-1, keepdims=True) + NORM_EPSILON)
+    gain = gain_ref[0:1, :]
     normed = normed_grad[...]
     inner = jnp.sum(normed * gain * inputs, axis=-1, keepdims=True)
     low[...] = (
@@ -1617,31 +1789,32 @@
             copies.start(remote(vectors.at[to], vector_in.at[number], v_send.at[number], v_recv.at[number], peer))
         )
 
-    for step in experts.order[2:]:
+    for step in experts.steps[2:]:
         experts.climb(0, step)
     gate_and_up(2)
-    for step in experts.order[:2]:
+    for step in experts.steps[:2]:
         experts.climb(1, step)
     grad_gather.cross()
+    z_first.climb(0)
     gate_and_up(3)
-    for step in experts.order[2:]:
+    for step in experts.steps[2:]:
         experts.climb(1, step)
     gated_copy = fetch(gated_ref, acts.at[0], act_load.at[0])
     gated_copy.wait()
-    for index in range(2):
-        half = pl.ds(index * local * hidden, local * hidden)
-        gated_turned[half, :] = acts[0, :, half].T
+    for owner, target in ((1 - core, turned), (core, gated_turned)):
+        target[...] = acts[0, :, pl.ds(pl.multiple_of(first_unit(owner), hidden), local * hidden)].T
     experts.result(0, sums[0])
     down(0)
-    experts.climb(2, experts.order[0])
+    experts.climb(2, experts.steps[0])
     down(1)
-    for step in experts.order[1:]:
+    for step in experts.steps[1:]:
         experts.climb(2, step)
     down(2)
     experts.result(1, sums[1])
     down(3)
+    settle_down(3)
     for index in range(3, matrices):
-        for step in experts.order:
+        for step in experts.steps:
             experts.climb(index, step)
     for copy in vector_copies:
         copies.arrived(copy)
@@ -1655,6 +1828,7 @@
     ]
     for index in range(2, matrices):
         experts.result(index, sums[index])
+    z_first.result(sums[-1].at[:, eighth])
     out_gather.finish()
     grad_gather.finish()
     for copy in turn_copies:
@@ -1671,13 +1845,13 @@
     copies.finish()
 
 
-def run_gradients(parts, normed_part, tokens, state_cot, scale, gain, out, vectors, normed, grads, gated, gate_grad, up_grad, local, number):
+def run_gradients(parts, normed_part, tokens, state_cot, gain, out, vectors, normed, grads, gated, gate_grad, up_grad, local, number):
     matrices = len(parts)
     depth, _, piece, columns = parts[0].shape
     rows, width = tokens.shape
     seen, units = gated.shape
     hidden = units // (2 * local)
-    tile = 512
+    tile = units // 2
     sum_of = jax.ShapeDtypeStruct((piece, columns), FULL)
     spread = jax.ShapeDtypeStruct((2, 2, rows, width), LOW)
     wide, tall = (local, width, hidden), (local, hidden, width)
@@ -1687,10 +1861,9 @@
         + (
             spread, spread, jax.ShapeDtypeStruct(vectors.shape[1:], FULL),
             jax.ShapeDtypeStruct(wide, FULL), jax.ShapeDtypeStruct(wide, FULL), jax.ShapeDtypeStruct(tall, FULL),
-            jax.ShapeDtypeStruct(wide, LOW), jax.ShapeDtypeStruct(wide, LOW), jax.ShapeDtypeStruct(tall, LOW),
         ),
-        in_specs=[ANY] * (matrices + 1) + [VMEM] * 6 + [ANY] * 5,
-        out_specs=(VMEM,) * (matrices + 3) + (ANY,) * 6,
+        in_specs=[ANY] * (matrices + 1) + [VMEM] * 5 + [ANY] * 5,
+        out_specs=(VMEM,) * (matrices + 3) + (ANY,) * 3,
         scratch_shapes=[pltpu.VMEM((matrices, depth, piece, columns), LOW)] * 3
         + TensorScatter.scratch(rows, width)[:3]
         + [
@@ -1698,16 +1871,19 @@
             pltpu.VMEM(vectors.shape, FULL), pltpu.VMEM((2 * depth - 1,) + vectors.shape[1:], FULL),
             pltpu.VMEM(vectors.shape[1:], FULL), pltpu.VMEM((3,) + vectors.shape[1:], FULL),
             pltpu.VMEM((2, seen, tile), LOW), pltpu.VMEM((tile, seen), LOW),
-            pltpu.VMEM((2, seen, units), LOW), pltpu.VMEM((units, seen), LOW),
+            pltpu.VMEM((2, seen, units), LOW), pltpu.VMEM((units // 2, seen), LOW),
             pltpu.VMEM((2, 2, local, tile, hidden), FULL), pltpu.VMEM((2, 2, local, tile, hidden), LOW),
             pltpu.VMEM((2, local, hidden, tile), FULL), pltpu.VMEM((2, local, hidden, tile), LOW),
+            pltpu.VMEM((2, local, width, hidden), LOW), pltpu.VMEM((width // tile, local, hidden, tile), LOW),
+            pltpu.VMEM((depth, 2, piece, columns // 2), LOW), pltpu.VMEM((depth, 2, piece, columns // 2), LOW),
+            pltpu.VMEM((piece, columns // 2), LOW), dma(depth), dma(depth), dma(depth),
             dma(matrices, depth), dma(2, matrices, depth), dma(2, matrices, depth),
             dma(3), dma(3), dma(4), dma(3), dma(4), dma(3),
             dma(2 * depth - 1), dma(2 * depth - 1), dma(3), dma(3),
             dma(2), dma(2), dma(3, 2), dma(3, width // tile), dma(3, width // tile), dma(1),
         ],
         compiler_params=comm_params(number),
-    )(*parts, normed_part, tokens, state_cot, scale, gain, out, vectors, normed, grads, gated, gate_grad, up_grad)
+    )(*parts, normed_part, tokens, state_cot, gain, out, vectors, normed, grads, gated, gate_grad, up_grad)
     return results[:matrices], results[matrices:]
 
 
@@ -1720,7 +1896,7 @@
     local_experts, _, hidden = w_gate.shape
     experts = local_experts * groups
     chain = LENGTH // row_count
-    if not (parts == 4 and groups % 2 == 0 and experts <= min(16, 2 * TOP) and 2 * w_query.shape[1] <= 14 * HD and chain == 4 and 4 * row_count == LENGTH and WINDOW == 2 * row_count):
+    if not (parts == 4 and groups % 2 == 0 and experts <= min(16, 2 * TOP) and 2 * w_query.shape[1] <= 14 * HD and chain == 4 and groups == 8 and 4 * row_count == LENGTH and WINDOW == 2 * row_count):
         return body_routed(
             tokens, documents, routes, norm1_gain, q_gain, k_gain, w_query, w_key, w_value, w_out, norm2_gain, router_w,
             w_gate, w_up, w_down, out_grad,
@@ -1761,25 +1937,13 @@
     all_normed, all_grad = all_normed.reshape(seen, width), all_grad.reshape(seen, width)
     gated, gate_pre_grad, up_pre_grad = (a.reshape(seen, units) for a in (gated, gate_pre_grad, up_pre_grad))
 
-    (
-        state_cot, router_grad, norm2_grad, q_gain_local, k_gain_local, expert_mix, normed_part, *pieces
-    ) = run_attention_back(
+    state_cot, vectors, output_rows, normed_part, *pieces = run_attention_back(
         (normed_two_grad, gate_cots, router_probs, picked, state, across(norm2_gain), router_wide, normed_two, own_grad),
         (queries, kv_all, attended, logs, key_docs, docs, query_raw, key_raw, query_gain, key_gain, cosine, sine, scales),
-        (w_out,), produced, normed_one, (w_query, w_key, w_value), chain, local_experts, experts, 10,
-    )
-    own_inputs = quarter(tokens).astype(FULL)
-    own_scale = lax.rsqrt(jnp.mean(own_inputs * own_inputs, axis=-1, keepdims=True) + NORM_EPSILON)
-
-    vectors = jnp.concatenate(
-        [router_grad, jnp.zeros((17 - experts, width), FULL), norm2_grad[:1]], axis=0
-    ).reshape(18, groups, width // groups).transpose(1, 0, 2)
-    gains = jnp.concatenate([q_gain_local[0].reshape(heads, HD), k_gain_local[0].reshape(heads, HD)], axis=0)
-    gains = jnp.pad(gains, ((0, 14 - 2 * heads), (0, width // groups - HD)))
-    vectors = jnp.concatenate([vectors, jnp.broadcast_to(gains[None], (groups,) + gains.shape)], axis=1)
-    sums, (input_grad, output, vector_sum, gate_own, up_own, down_own, gate_other, up_other, down_other) = run_gradients(
-        pieces, normed_part, quarter(tokens), state_cot, own_scale,
-        norm1_gain[None], (state + expert_mix).astype(LOW), vectors, all_normed, all_grad, gated, gate_pre_grad, up_pre_grad,
+        (w_out,), produced, normed_one, (w_query, w_key, w_value), chain, local_experts, 10,
+    )
+    sums, (input_grad, output, vector_sum, *expert_grads) = run_gradients(
+        pieces, normed_part, quarter(tokens), state_cot, norm1_gain[None], output_rows, vectors, all_normed, all_grad, gated, gate_pre_grad, up_pre_grad,
         local_experts, 14,
     )
     own_columns = group * (HD // groups)
@@ -1795,9 +1959,7 @@
         sums[0].T,
         vector_sum[17],
         vector_sum[:experts].T,
-        gate_own + gate_other.astype(FULL),
-        up_own + up_other.astype(FULL),
-        down_own + down_other.astype(FULL),
+        *expert_grads,
     )
 
 

time: 578 us -> 516 us (0.89)
  the two profiles are of different devices: /device:TPU:10 before, /device:TPU:0 now
where the time goes in v7:
time: 516 us; the launch traced here: 511 us
  Pallas kernels  476 us (92%)
  local copies, waits for them, and re-layouts  25.4 us (5%)
  other arithmetic  8.08 us (2%)
    pallas_call x1, Pallas kernels, run_experts(): pl.pallas_call(functools.partial(experts_kernel, depth, rows, local, hidd...  152 us
    pallas_call x1, Pallas kernels, run_attention_back(): pl.pallas_call(functools.partial(attention_back_kernel, depth, rows, head...  126 us
    pallas_call x1, Pallas kernels, run_attention(): pl.pallas_call(functools.partial(attention_kernel, depth, rows, heads, ch...  99.3 us
    pallas_call x1, Pallas kernels, run_gradients(): pl.pallas_call(functools.partial(gradients_kernel, depth, rows, local, hi...  98.7 us
    unnamed x29, local copies, waits for them, and re-layouts  16.7 us

profile of v7, /device:TPU:0, one launch (start us, length us, event | category | flops | bytes accessed | tf_op | source)
XLA Modules:
  0.0 510.6 jit_solution(14120623924644013763)
XLA Ops:
  0.6 0.0 copy-start
  0.7 0.7 copy-done
  1.4 1.3 broadcast_in_dim.2.docs_ref.query_docs
  2.7 0.1 copy.34
  2.8 0.3 fusion
  3.0 0.6 convert_element_type.19.picked_ref
  3.7 0.1 broadcast_multiply_fusion
  3.8 1.8 fusion.1
  5.6 0.1 slice_negate_fusion
  5.7 0.8 pad_maximum_fusion.1.sine_ref
  6.6 0.3 copy.33
  6.8 0.9 pad.4.router_ref
  7.7 2.3 constant_dynamic-slice_fusion
  10.0 99.3 %shard_map.263 = (bf16[2048,512]{1,0:T(8,128)(2,1)}, f32[512,512]{1,0:T(8,128)}, f32[512,512]{1,0:T(8,128)}, bf16[512,512]{1,0:T(8,128)(2,1)}, bf16[3,512,1024]{...) custom-call(bf16[512,2048]{1,0:T(8,128)(2,1)} %tokens_ref.1, ...), custom_call_target="tpu_custom_call" | custom-call | tf_op jit(solution)/shard_map/pallas_call | solution.py:1194
  109.3 152.4 %shard_map.264 = (f32[128,2048]{1,0:T(8,128)}, f32[4,4,8,128]{3,2,1,0:T(8,128)}, bf16[4,512,2048]{2,1,0:T(8,128)(2,1)}, bf16[4,512,1024]{2,1,0:T(8,128)(2,1)}, b...) custom-call(bf16[128,2048]{1,0:T(8,128)(2,1)} %get-tuple-element.53.x_ref.normed2_ref, ...), custom_call_target="tpu_custom_call" | custom-call | tf_op jit(solution)/shard_map/pallas_call | solution.py:809
  261.7 125.8 %shard_map.265 = (f32[128,2048]{1,0:T(8,128)}, f32[8,32,256]{2,1,0:T(8,128)}, bf16[128,2048]{1,0:T(8,128)(2,1)}, bf16[2,2,128,2048]{3,2,1,0:T(8,128)(2,1)}, bf16...) custom-call(f32[128,2048]{1,0:T(8,128)} %get-tuple-element.56.sum_re, ...), custom_call_target="tpu_custom_call" | custom-call | tf_op jit(solution)/shard_map/pallas_call | solution.py:1492
  387.6 98.7 %shard_map.266 = (f32[256,512]{1,0:T(8,128)}, f32[256,512]{1,0:T(8,128)}, f32[256,512]{1,0:T(8,128)}, f32[256,512]{1,0:T(8,128)}, bf16[2,2,128,2048]{3,2,1,0:T(8...) custom-call(bf16[4,2,256,512]{3,2,1,0:T(8,128)(2,1)} %get-tuple-elem, ...), custom_call_target="tpu_custom_call" | custom-call | tf_op jit(solution)/shard_map/pallas_call | solution.py:1858
  486.2 1.3 fusion.5
  487.6 1.4 constant_dynamic-slice_fusion.3
  489.0 1.3 slice_bitcast_fusion
  490.3 2.0 copy.35
  492.4 4.3 bitcast_convert_fusion
  496.6 1.3 copy.43
  498.0 0.8 copy.44
  498.8 0.8 copy.45
  499.6 0.6 copy-done.6
  500.2 0.8 copy.46
  501.0 2.1 copy.47
  503.1 1.6 copy-done.3
  504.7 2.1 copy.48
  506.8 1.6 copy-done.2
  508.4 2.0 copy.49
  (18 shorter events, 0.1 us)
Async XLA Ops:
  0.6 0.7 copy-start
  0.7 5.9 %copy-start.9 = (bf16[2048,16]{0,1:T(8,128)(2,1)S(1)}, bf16[2048,16]{0,1:T(8,128)(2,1)}, u32[]{:S(2)}) copy-start(bf16[2048,16]{0,1:T(8,128)(2,1)} %param.27) | copy-start | bytes 196612
  492.4 4.3 copy-start.5
  492.4 5.6 %copy-start.8 = (f32[256,512]{1,0:T(8,128)S(1)}, f32[256,512]{1,0:T(8,128)}, u32[]{:S(2)}) copy-start(f32[256,512]{1,0:T(8,128)} %get-tuple-element.149) | copy-start | bytes 1572868
  496.6 2.1 copy-start.7
  496.6 4.3 copy-start.4
  498.0 2.2 copy-start.6
  501.0 3.7 copy-start.3
  504.7 3.7 copy-start.2
  508.4 2.0 copy-start.1

commit v8 on v7

--- a/solution.py
+++ b/solution.py
@@ -619,25 +619,41 @@
         sides.append(to_y(5, second))
         self.sides[step] = sides
 
+    def below(self, step, odd_rows):
+        terms, bit = [], 1
+        while bit < (step & -step if step else len(self.column)):
+            if odd_rows or (step | bit) % 2 == 0:
+                for copy in self.along[step | bit]:
+                    self.copies.arrived(copy)
+                terms.append(self.from_z.at[step | bit])
+            bit *= 2
+        return terms
+
+    def spans(self):
+        return [(span, True) for span in self.pieces[1]] + ([(self.center, False)] if self.middle else [])
+
     def climb(self, step):
         for copy in self.sides[step]:
             self.copies.arrived(copy)
         if step:
+            for span, odd_rows in self.spans():
+                if odd_rows or step % 2 == 0:
+                    mine, part = self.at(step, self.here, span), pl.ds(*span)
+                    terms = [mine, self.from_x.at[step, part], self.from_y.at[step, part]]
+                    terms += [term.at[part] for term in self.below(step, odd_rows)]
+                    add_rows(mine, terms, span[1])
             self.along[step] = []
             for number, span in enumerate(self.pieces[step % 2]):
                 mine, part = self.at(step, self.here, span), pl.ds(*span)
-                add_rows(mine, [mine, self.from_x.at[step, part], self.from_y.at[step, part]], span[1])
-                self.along[step].append(self.copy(step, 6 + number, mine, self.from_z.at[step, part], self.column[step]))
+                self.along[step].append(
+                    self.copy(step, 6 + number, mine, self.from_z.at[step, part], self.column[step & -step])
+                )
 
     def result(self, target, more=()):
-        for copies in self.along.values():
-            for copy in copies:
-                self.copies.arrived(copy)
-        for span in [*self.halves[1], self.center] if self.middle else self.pieces[0]:
+        for span, odd_rows in self.spans():
             part = pl.ds(*span)
-            steps = [step for step in self.along if not (self.middle and span is self.center and step % 2)]
             terms = [self.at(0, self.here, span), self.from_x.at[0, part], self.from_y.at[0, part]]
-            terms += [self.from_z.at[step, part] for step in steps] + [term.at[part] for term in more]
+            terms += [term.at[part] for term in self.below(0, odd_rows)] + [term.at[part] for term in more]
             add_rows(target.at[part], terms, span[1])
 
     @staticmethod
@@ -696,6 +712,7 @@
             weights.append(copies.start(remote(source.at[index], target, w_send.at[number, index], w_recv.at[number, index], sibling)))
             plain.append(fetch(source.at[index], target, w_load.at[number, index]))
     plain.append(fetch(gates_ref.at[2 * z + x], gates.at[0, here], local_sem.at[1]))
+    sequence = (0, 2, 3, 1)
     grad_copies = [fetch(grad_ref.at[0], grads.at[0], g_load.at[0])]
     scatter = Scatter(copies, work, diagonal, from_x, from_y, from_z, rows, r_send, r_recv)
     saving, producing, keeping = [], [], []
@@ -710,10 +727,12 @@
             padded = jnp.concatenate([gates[step, spot], jnp.zeros((120, 128), FULL)], axis=0)
             gate_wide[pl.ds(spot * rows, rows), :] = padded.T
         cots[...] = jnp.zeros_like(cots)
-        grad_copies[step].wait()
-        if step + 1 < depth:
-            grad_copies.append(fetch(grad_ref.at[step + 1], grads.at[(step + 1) % 2], g_load.at[(step + 1) % 2]))
-        grad = grads.at[step % 2]
+        turn = sequence.index(step)
+        grad_copies[turn].wait()
+        if turn + 1 < depth:
+            slot = (turn + 1) % 2
+            grad_copies.append(fetch(grad_ref.at[sequence[turn + 1]], grads.at[slot], g_load.at[slot]))
+        grad = grads.at[turn % 2]
 
         @pl.loop(0, 2 * local)
         def _(unit):
@@ -768,31 +787,36 @@
         copy.wait()
     for copy in weights + smalls:
         copies.arrived(copy)
-    for step in range(depth):
-        if step:
-            gather.complete(step)
-        first_half(step)
-        if step + 1 < depth:
-            gather.turn(step + 1)
-        if step + 2 < depth:
-            gather.spread(step + 2)
-        if step == 1:
-            gather.share(2)
-        if step >= 2:
-            scatter.side(step - 1)
-        if step >= 3:
-            scatter.climb(step - 2)
-        second_half(step)
-        if step:
-            scatter.corner(step)
+    first_half(0)
+    gather.turn(1)
+    gather.spread(2)
+    second_half(0)
+    gather.turn(2)
+    gather.spread(3)
+    gather.share(2)
+    first_half(2)
+    gather.turn(3)
+    second_half(2)
+    scatter.corner(2)
+    gather.complete(3)
+    first_half(3)
+    scatter.side(2)
+    second_half(3)
+    scatter.corner(3)
+    gather.complete(1)
+    first_half(1)
+    scatter.side(3)
+    second_half(1)
+    scatter.corner(1)
     scatter.corner(0)
-    own_cots = fetch(cot_rows.at[0, here], cots_ref.at[0, here], local_sem.at[2])
-    scatter.side(depth - 1)
-    scatter.climb(depth - 2)
+    scatter.climb(3)
+    scatter.side(1)
+    scatter.climb(2)
     scatter.side(0)
-    scatter.climb(depth - 1)
+    scatter.climb(1)
     scatter.climb(0)
     scatter.result(sum_ref)
+    own_cots = fetch(cot_rows.at[0, here], cots_ref.at[0, here], local_sem.at[2])
     own_cots.wait()
     for copy in saving + producing + keeping:
         copy.wait()
@@ -940,11 +964,11 @@
 
 def attention_kernel(
     depth, rows, heads, chain, local,
-    tokens_ref, wq_ref, wk_ref, wv_ref, wo_ref, grad_ref,
-    gain1_ref, q_gain_ref, k_gain_ref, cosine_ref, sine_ref, docs_ref, gain2_ref, router_ref, picked_ref,
-    normed_turned, q_raw, k_raw, queries, kv_all, key_docs, scales, attended, logs, state_ref, normed2_ref, probs_ref, gates_ref,
+    tokens_ref, wq_ref, wk_ref, wv_ref, wo_ref, grads_ref,
+    gain1_ref, q_gain_ref, k_gain_ref, cosine_ref, sine_ref, docs_row, gain2_ref, router_ref, picked_ref,
+    normed_turned, q_raw, k_raw, queries, kv_all, key_docs, scales, attended, logs, state_ref, normed2_ref, probs_ref, gates_ref, own_tokens, own_grads,
     all_grad,
-    tokens, normed_ref, wq, wk, wv, wo, docs_in, squares, squares_in, scores, totals, bias, partial, from_pair, from_y, sum_ref,
+    tokens, normed_ref, wq, wk, wv, wo, docs_ref, logits_ref, docs_in, squares, squares_in, scores, totals, bias, partial, from_pair, from_y, sum_ref,
     t_send, t_recv, z_send, z_recv, p_send, p_recv, c_send, c_recv, h_send, h_recv, d_send, d_recv, q_send, q_recv, load,
 ):
     z, x, y, core = place()
@@ -953,6 +977,11 @@
     length, width = tokens.shape
     wide = heads * HD
     scale = HD ** (-0.5)
+    own_rows = pl.ds(pl.multiple_of(part * rows, rows), rows)
+    grad_ref = grads_ref.at[own_rows]
+    docs_ref[...] = jnp.broadcast_to(docs_row[...], docs_ref.shape)
+    own_copy = pltpu.make_async_copy(grad_ref, own_grads, load.at[6])
+    own_copy.start()
     loads = []
     for number, (source, target) in enumerate([(tokens_ref, tokens), (wv_ref, wv), (wk_ref, wk), (wq_ref, wq), (wo_ref, wo)]):
         loads.append(pltpu.make_async_copy(source, target, load.at[number]))
@@ -1158,15 +1187,15 @@
     gather.share(2)
     gather.turn(3)
     scatter.result(sum_ref)
-    own_rows = pl.ds(pl.multiple_of(part * rows, rows), rows)
-    state = tokens[own_rows, :].astype(FULL) + sum_ref[...]
+    own_tokens[...] = tokens[own_rows, :]
+    state = own_tokens[...].astype(FULL) + sum_ref[...]
     state_ref[...] = state
     factor = lax.rsqrt(jnp.mean(state * state, axis=-1, keepdims=True) + NORM_EPSILON)
     normed2_ref[...] = (state * factor * gain2_ref[0:1, :]).astype(LOW)
-    logits = dot(normed2_ref[...], router_ref[...])
     experts = gates_ref.shape[0] * local
-    lanes = lax.broadcasted_iota(jnp.int32, logits.shape, 1)
-    logits = jnp.where(lanes < experts, logits, -1e30)
+    logits_ref[...] = jnp.full_like(logits_ref, -1e30)
+    logits_ref[:, :experts] = dot_t(normed2_ref[...], router_ref[...])
+    logits = logits_ref[...]
     weights = jnp.exp(logits - jnp.max(logits, axis=-1, keepdims=True))
     probs = weights / jnp.sum(weights, axis=-1, keepdims=True)
     probs_ref[...] = probs
@@ -1175,6 +1204,7 @@
     for index in range(gates_ref.shape[0]):
         gates_ref[index, 0:local, :] = gates[index * local : (index + 1) * local]
     own.wait()
+    own_copy.wait()
     for kind in range(2):
         halo_sent(kind)
     for distance in (1, 2):
@@ -1188,7 +1218,7 @@
 
 def run_attention(tokens, weights, grads, gains, tables, docs, gain2, router, picked, depth, chain, local, number):
     length, width = tokens.shape
-    rows = grads.shape[0]
+    rows = length // 4
     wide = weights[0].shape[1]
     heads = wide // HD
     return pl.pallas_call(
@@ -1207,13 +1237,16 @@
             jax.ShapeDtypeStruct((rows, width), LOW),
             jax.ShapeDtypeStruct((rows, 128), FULL),
             jax.ShapeDtypeStruct((2 * depth, 8, rows), FULL),
+            jax.ShapeDtypeStruct((rows, width), LOW),
+            jax.ShapeDtypeStruct((rows, width), LOW),
             jax.ShapeDtypeStruct((depth, 4 * rows, width), LOW),
         ),
         in_specs=[ANY] * 6 + [VMEM] * 9,
-        out_specs=(VMEM,) * 13 + (ANY,),
+        out_specs=(VMEM,) * 15 + (ANY,),
         scratch_shapes=[
             pltpu.VMEM(tokens.shape, LOW), pltpu.VMEM(tokens.shape, LOW), pltpu.VMEM((width, wide), LOW), pltpu.VMEM((width, wide), LOW),
-            pltpu.VMEM((width, wide), LOW), pltpu.VMEM((wide, width), LOW), pltpu.VMEM((2, 8, length), jnp.int32),
+            pltpu.VMEM((width, wide), LOW), pltpu.VMEM((wide, width), LOW), pltpu.VMEM((8, length), jnp.int32),
+            pltpu.VMEM((rows, 128), FULL), pltpu.VMEM((2, 8, length), jnp.int32),
             pltpu.VMEM((8, length), FULL), pltpu.VMEM((3, 8, length), FULL),
             pltpu.VMEM((heads, 3 * length, length), FULL), pltpu.VMEM((heads, 8, length), FULL),
             pltpu.VMEM((3 * length, length), FULL),
@@ -1221,7 +1254,7 @@
         + TensorScatter.scratch(rows, width)[:3]
         + [
             pltpu.VMEM((rows, width), FULL), dma(3), dma(3),
-            *Gather.scratch(depth), dma(2, 3), dma(2, 3), dma(3), dma(3), dma(3), dma(3), dma(6),
+            *Gather.scratch(depth), dma(2, 3), dma(2, 3), dma(3), dma(3), dma(3), dma(3), dma(7),
         ],
         compiler_params=comm_params(number),
     )(tokens, *weights, grads, *gains, *tables, docs, gain2, router, picked)
@@ -1269,12 +1302,11 @@
             loads[step].wait()
         scatter.corner(step)
 
-    for step in order[:2]:
-        loads[step].wait()
-        scatter.share(step)
-    for step in order[:2]:
-        corner(step)
-
+
+    loads[3].wait()
+    scatter.share(3)
+    loads[1].wait()
+    scatter.share(1)
     by_expert[...] = jnp.zeros_like(by_expert)
     for plane in range(depth):
         step = swapped(z, plane)
@@ -1285,7 +1317,7 @@
     prob_cot = by_expert[...].T * picked_ref[...]
     logit_cot = probs * (prob_cot - jnp.sum(probs * prob_cot, axis=-1, keepdims=True))
     normed2_cot = sum_ref[...] + lax.dot_general(
-        logit_cot, router_ref[...].astype(FULL), (((1,), (1,)), ((), ())),
+        logit_cot[:, : router_ref.shape[0]], router_ref[...].astype(FULL), (((1,), (0,)), ((), ())),
         precision=HIGHEST_PRECISION, preferred_element_type=FULL,
     )
     state = state_ref[...]
@@ -1304,12 +1336,14 @@
     state_cot_ref[...] = state_cot
     low[...] = state_cot.astype(LOW)
     gather = TensorGather(copies, low, lows, t_send, t_recv)
-    scatter.side(order[0])
+    corner(3)
+    corner(1)
     router_grad = jnp.dot(
         logit_cot.T, normed2_ref[...].astype(FULL), precision=HIGHEST_PRECISION, preferred_element_type=FULL
     )[:16]
     for index in range(groups):
         vectors[index, 0:16, :] = router_grad[:, index * slice_width : (index + 1) * slice_width]
+    scatter.side(3)
     mask_bias(bias, key_docs, query_docs, length)
     gather.cross()
     gather.finish()
@@ -1319,6 +1353,7 @@
         columns = pl.ds(head * HD, HD)
         product = cots[:, columns].astype(FULL) * attended[:, columns].astype(FULL)
         deltas[head] = jnp.broadcast_to(jnp.sum(product.T, axis=0, keepdims=True), (8, length))
+    scatter.side(1)
     turned[...] = jnp.zeros_like(turned)
 
     def back(block, store, after):
@@ -1326,18 +1361,17 @@
         def _(head):
             columns = pl.ds(pl.multiple_of(head * HD, HD), HD)
             values = pl.ds(pl.multiple_of((heads + head) * HD, HD), HD)
-            query, cot = query_ref[:, columns], cots[:, columns]
-            log, delta = logs[head, 0:1, :], deltas[head, 0:1, :]
-            tile = 256
-
-            @pl.loop(0, length // tile)
-            def _(index):
-                keys = pl.ds(pl.multiple_of(index * tile, tile), tile)
+            tile = length // 2
+
+            for index, seen in ((0, pl.ds(0, tile if block == 0 else length)), (1, pl.ds(tile, tile) if block == 2 else pl.ds(0, length))):
+                keys = pl.ds(index * tile, tile)
                 key, value = kv_all[block, keys, columns], kv_all[block, keys, values]
-                hidden = bias[pl.ds(pl.multiple_of(block * length + index * tile, tile), tile), :].astype(FULL)
+                query, cot = query_ref[seen, columns], cots[seen, columns]
+                log, delta = logs[head, 0:1, seen], deltas[head, 0:1, seen]
+                hidden = bias[pl.ds(block * length + index * tile, tile), seen].astype(FULL)
                 probs = jnp.exp(dot_t(key, query) * scale + hidden - log)
                 score_cot = (probs * (dot_t(value, cot) - delta)).astype(LOW)
-                turned[head] += t_dot(key, score_cot)
+                turned[head, :, seen] += t_dot(key, score_cot)
                 store(head, keys, dot(score_cot, query) * scale, dot(probs.astype(LOW), cot))
 
             after(head)
@@ -1370,17 +1404,17 @@
             z_copy(head).start()
 
     back(1, store_in(1), lambda head: pl.when(spot >= 1)(lambda: x_copy(head).start()))
-    corner(order[2])
-    scatter.side(order[1])
+    scatter.climb(3)
     back(0, store_in(0), lambda head: pl.when(spot == 2)(lambda: z_copy(head).start()))
-    scatter.climb(order[0])
+    scatter.climb(1)
+    corner(2)
     back(2, store_own, relay)
-    corner(order[3])
+    corner(0)
+    scatter.side(2)
     for head in range(heads):
         query_cot[:, pl.ds(head * HD, HD)] = turned[head].T * scale
-    scatter.side(order[2])
-    scatter.climb(order[1])
-
+
+    scatter.side(0)
     saving = {}
 
     def weight_piece(number, right, target):
@@ -1401,7 +1435,7 @@
     weight_piece(0, attended[...], piece0)
     normed_copy = pltpu.make_async_copy(normed_ref, flipped, load.at[depth + 3])
     normed_copy.start()
-    scatter.side(order[3])
+    scatter.climb(2)
     factors = as_columns(scales[...])
 
     def turn_back(cot, raw, gain_ref, factor, first):
@@ -1419,7 +1453,6 @@
         return total
 
     query_inner = turn_back(query_cot, q_raw, q_gain_ref, factors[:, 0:1], 18)
-    scatter.climb(order[2])
 
     def take(slot, head):
         (z_copy, x_copy)[slot](head).wait_recv()
@@ -1470,7 +1503,7 @@
 
     weight_piece(2, raw_cots[0], piece2)
     weight_piece(3, raw_cots[1], piece3)
-    scatter.climb(order[3])
+    scatter.climb(0)
     scatter.result(out_ref, [state_ref])
     for head in range(heads):
         pl.when(spot >= 1)(lambda: x_copy(head).wait_send())
@@ -1848,7 +1881,7 @@
 def run_gradients(parts, normed_part, tokens, state_cot, gain, out, vectors, normed, grads, gated, gate_grad, up_grad, local, number):
     matrices = len(parts)
     depth, _, piece, columns = parts[0].shape
-    rows, width = tokens.shape
+    rows, width = state_cot.shape
     seen, units = gated.shape
     hidden = units // (2 * local)
     tile = units // 2
@@ -1887,6 +1920,54 @@
     return results[:matrices], results[matrices:]
 
 
+def finish_kernel(
+    experts, heads,
+    in_grad, in_out, in_query, in_key, in_value, in_gate, in_up, in_down, in_w_out, vector_ref,
+    input_grad, output, query, key, value, gate, up, down, w_out, norm1, norm2, router, q_gain, k_gain,
+):
+    input_grad[...] = in_grad[...].astype(FULL)
+    for source, target in (
+        (in_out, output), (in_query, query), (in_key, key), (in_value, value), (in_gate, gate), (in_up, up), (in_down, down),
+    ):
+        target[...] = source[...]
+
+    @pl.when(pl.program_id(0) == 0)
+    def _():
+        w_out[...] = in_w_out[...].T
+        vectors = vector_ref[...]
+        norm1[...], norm2[...] = vectors[16:17], vectors[17:18]
+        router[...] = vectors[:experts]
+        gains = vectors[18 : 18 + 2 * heads, :HD]
+        width = q_gain.shape[1]
+        group = lax.axis_index("expert")
+        total_q, total_k = jnp.zeros(q_gain.shape, FULL), jnp.zeros(k_gain.shape, FULL)
+        for index in range(HD // width):
+            mine = (group == index).astype(FULL)
+            total_q = total_q + gains[:heads, index * width : (index + 1) * width] * mine
+            total_k = total_k + gains[heads:, index * width : (index + 1) * width] * mine
+        q_gain[...], k_gain[...] = total_q, total_k
+
+
+def finish(arrays, w_out, vectors, experts, heads, groups):
+    steps = 4
+    shapes = [jax.ShapeDtypeStruct(a.shape, FULL if i == 0 else a.dtype) for i, a in enumerate(arrays)]
+    blocks = [pl.BlockSpec((a.shape[0] // steps, a.shape[1]), lambda i: (i, 0)) for a in arrays]
+    whole = pl.BlockSpec(memory_space=pltpu.VMEM)
+    piece = vectors.shape[1]
+    small = [
+        jax.ShapeDtypeStruct(shape, FULL)
+        for shape in (w_out.shape[::-1], (1, piece), (1, piece), (experts, piece), (heads, HD // groups), (heads, HD // groups))
+    ]
+    return pl.pallas_call(
+        functools.partial(finish_kernel, experts, heads),
+        grid=(steps,),
+        out_shape=(*shapes, *small),
+        in_specs=blocks + [whole, whole],
+        out_specs=(*blocks, *[whole] * len(small)),
+        compiler_params=pltpu.CompilerParams(vmem_limit_bytes=VMEM_BYTES),
+    )(*arrays, w_out, vectors)
+
+
 def body(
     groups, parts,
     tokens, documents, routes, norm1_gain, q_gain, k_gain, w_query, w_key, w_value, w_out, norm2_gain, router_w,
@@ -1917,17 +1998,14 @@
     positions = group * row_count + jnp.arange(row_count, dtype=jnp.int32)
     cosine, sine = (table[:, 0, :] for table in rope_tables(positions % LENGTH))
     sine = jnp.concatenate([-sine[:, : HD // 2], sine[:, HD // 2 :]], axis=1)
-    docs = jnp.broadcast_to(documents[None, :], (8, row_count))
     picked = jnp.any(quarter(routes)[:, :, None] == jnp.arange(128, dtype=jnp.int32)[None, None, :], axis=1).astype(FULL)
-    router_wide = jnp.pad(router_w, ((0, 0), (0, 128 - experts)))
-    own_grad = quarter(out_grad)
     query_gain, key_gain = across(q_gain), across(k_gain)
     (
         normed_one, query_raw, key_raw, queries, kv_all, key_docs, scales, attended, logs, state, normed_two, router_probs, gates,
-        all_grad,
+        own_tokens, own_grads, all_grad,
     ) = run_attention(
-        tokens, (w_query, w_key, w_value, w_out), own_grad, (across(norm1_gain), query_gain, key_gain), (cosine, sine), docs,
-        across(norm2_gain), router_wide, picked, depth, chain, local_experts, 3,
+        tokens, (w_query, w_key, w_value, w_out), out_grad, (across(norm1_gain), query_gain, key_gain), (cosine, sine), across(documents),
+        across(norm2_gain), router_w.T, picked, depth, chain, local_experts, 3,
     )
 
     normed_two_grad, gate_cots, all_normed, gated, gate_pre_grad, up_pre_grad, produced = run_experts(
@@ -1938,28 +2016,28 @@
     gated, gate_pre_grad, up_pre_grad = (a.reshape(seen, units) for a in (gated, gate_pre_grad, up_pre_grad))
 
     state_cot, vectors, output_rows, normed_part, *pieces = run_attention_back(
-        (normed_two_grad, gate_cots, router_probs, picked, state, across(norm2_gain), router_wide, normed_two, own_grad),
-        (queries, kv_all, attended, logs, key_docs, docs, query_raw, key_raw, query_gain, key_gain, cosine, sine, scales),
+        (normed_two_grad, gate_cots, router_probs, picked, state, across(norm2_gain), router_w.T, normed_two, own_grads),
+        (queries, kv_all, attended, logs, key_docs, across(documents), query_raw, key_raw, query_gain, key_gain, cosine, sine, scales),
         (w_out,), produced, normed_one, (w_query, w_key, w_value), chain, local_experts, 10,
     )
     sums, (input_grad, output, vector_sum, *expert_grads) = run_gradients(
-        pieces, normed_part, quarter(tokens), state_cot, norm1_gain[None], output_rows, vectors, all_normed, all_grad, gated, gate_pre_grad, up_pre_grad,
+        pieces, normed_part, own_tokens, state_cot, norm1_gain[None], output_rows, vectors, all_normed, all_grad, gated, gate_pre_grad, up_pre_grad,
         local_experts, 14,
     )
-    own_columns = group * (HD // groups)
+    (
+        input_grad, output, w_query_grad, w_key_grad, w_value_grad, gate_grad, up_grad, down_grad, w_out_grad,
+        norm1_grad, norm2_grad, router_grad, q_gain_grad, k_gain_grad,
+    ) = finish(
+        (
+            input_grad.reshape(row_count, width), output.reshape(row_count, width), sums[2], sums[3], sums[1],
+            *(a.reshape(-1, a.shape[2]) for a in expert_grads),
+        ),
+        sums[0], vector_sum, experts, heads, groups,
+    )
     return (
-        output.reshape(row_count, width),
-        input_grad.reshape(row_count, width).astype(FULL),
-        vector_sum[16],
-        lax.dynamic_slice(vector_sum, (18, own_columns), (heads, HD // groups)),
-        lax.dynamic_slice(vector_sum, (18 + heads, own_columns), (heads, HD // groups)),
-        sums[2],
-        sums[3],
-        sums[1],
-        sums[0].T,
-        vector_sum[17],
-        vector_sum[:experts].T,
-        *expert_grads,
+        output, input_grad, norm1_grad.reshape(-1), q_gain_grad, k_gain_grad, w_query_grad, w_key_grad, w_value_grad, w_out_grad,
+        norm2_grad.reshape(-1), router_grad.T, gate_grad.reshape(w_gate.shape), up_grad.reshape(w_up.shape),
+        down_grad.reshape(w_down.shape),
     )
 
 

time: 516 us -> 492 us (0.953)
  the two profiles are of different devices: /device:TPU:0 before, /device:TPU:10 now
where the time goes in v8:
time: 492 us; the launch traced here: 483 us
  Pallas kernels  477 us (97%)
    pallas_call x1, Pallas kernels, run_experts(): pl.pallas_call(functools.partial(experts_kernel, depth, rows, local, hidd...  149 us
    pallas_call x1, Pallas kernels, run_attention_back(): pl.pallas_call(functools.partial(attention_back_kernel, depth, rows, head...  113 us
    pallas_call x1, Pallas kernels, run_attention(): pl.pallas_call(functools.partial(attention_kernel, depth, rows, heads, ch...  102 us
    pallas_call x1, Pallas kernels, run_gradients(): pl.pallas_call(functools.partial(gradients_kernel, depth, rows, local, hi...  99.3 us
    pallas_call x1, Pallas kernels, finish(): pl.pallas_call(functools.partial(finish_kernel, experts, heads), grid=(st...  14.1 us

profile of v8, /device:TPU:10, one launch (start us, length us, event | category | flops | bytes accessed | tf_op | source)
XLA Modules:
  0.0 482.9 jit_solution(2640267543150876915)
XLA Ops:
  0.6 0.0 copy-start
  0.7 0.7 copy-done
  1.4 0.1 copy.31
  1.5 0.3 fusion
  1.7 0.6 convert_element_type.11.picked_ref
  2.4 0.1 broadcast_multiply_fusion
  2.5 1.8 fusion.1
  4.3 0.1 slice_negate_fusion
  4.4 0.8 pad_maximum_fusion.1.sine_ref
  5.3 101.9 %shard_map.263 = (bf16[2048,512]{1,0:T(8,128)(2,1)}, f32[512,512]{1,0:T(8,128)}, f32[512,512]{1,0:T(8,128)}, bf16[512,512]{1,0:T(8,128)(2,1)}, bf16[3,512,1024]{...) custom-call(bf16[512,2048]{1,0:T(8,128)(2,1)} %tokens_ref.1, ...), custom_call_target="tpu_custom_call" | custom-call | tf_op jit(solution)/shard_map/pallas_call | solution.py:1224
  107.1 149.5 %shard_map.264 = (f32[128,2048]{1,0:T(8,128)}, f32[4,4,8,128]{3,2,1,0:T(8,128)}, bf16[4,512,2048]{2,1,0:T(8,128)(2,1)}, bf16[4,512,1024]{2,1,0:T(8,128)(2,1)}, b...) custom-call(bf16[128,2048]{1,0:T(8,128)(2,1)} %get-tuple-element.69.x_ref.normed2_ref, ...), custom_call_target="tpu_custom_call" | custom-call | tf_op jit(solution)/shard_map/pallas_call | solution.py:833
  256.6 112.6 %shard_map.265 = (f32[128,2048]{1,0:T(8,128)}, f32[8,32,256]{2,1,0:T(8,128)}, bf16[128,2048]{1,0:T(8,128)(2,1)}, bf16[2,2,128,2048]{3,2,1,0:T(8,128)(2,1)}, bf16...) custom-call(f32[128,2048]{1,0:T(8,128)} %get-tuple-element.72.sum_re, ...), custom_call_target="tpu_custom_call" | custom-call | tf_op jit(solution)/shard_map/pallas_call | solution.py:1525
  369.2 99.3 %shard_map.266 = (f32[256,512]{1,0:T(8,128)}, f32[256,512]{1,0:T(8,128)}, f32[256,512]{1,0:T(8,128)}, f32[256,512]{1,0:T(8,128)}, bf16[2,2,128,2048]{3,2,1,0:T(8...) custom-call(bf16[4,2,256,512]{3,2,1,0:T(8,128)(2,1)} %get-tuple-elem, ...), custom_call_target="tpu_custom_call" | custom-call | tf_op jit(solution)/shard_map/pallas_call | solution.py:1891
  468.6 0.0 copy-start.1
  468.6 14.1 %shard_map.267 = (f32[512,2048]{1,0:T(8,128)}, bf16[512,2048]{1,0:T(8,128)(2,1)}, f32[256,512]{1,0:T(8,128)}, f32[256,512]{1,0:T(8,128)}, f32[256,512]{1,0:T(8,1...) custom-call(bf16[512,2048]{1,0:T(8,128)(2,1)} %bitcast.30, ...), custom_call_target="tpu_custom_call" | custom-call | tf_op jit(solution)/shard_map/pallas_call | solution.py:1961
  482.7 0.0 copy-done.1
  (3 shorter events, 0.0 us)
Async XLA Ops:
  0.6 0.7 copy-start
  468.6 14.1 %copy-start.1 = (s32[512,8]{0,1:T(8,128)S(1)}, s32[512,8]{0,1:T(8,128)}, u32[]{:S(2)}) copy-start(s32[512,8]{0,1:T(8,128)} %param.18) | copy-start | bytes 49156

commit v9 on v8

--- a/solution.py
+++ b/solution.py
@@ -966,10 +966,10 @@
     depth, rows, heads, chain, local,
     tokens_ref, wq_ref, wk_ref, wv_ref, wo_ref, grads_ref,
     gain1_ref, q_gain_ref, k_gain_ref, cosine_ref, sine_ref, docs_row, gain2_ref, router_ref, picked_ref,
-    normed_turned, q_raw, k_raw, queries, kv_all, key_docs, scales, attended, logs, state_ref, normed2_ref, probs_ref, gates_ref, own_tokens, own_grads,
+    normed_out, q_out, k_out, queries_out, kv_out, key_docs, scales, attended, logs, state_ref, normed2_ref, probs_ref, gates_ref, own_tokens, own_grads,
     all_grad,
-    tokens, normed_ref, wq, wk, wv, wo, docs_ref, logits_ref, docs_in, squares, squares_in, scores, totals, bias, partial, from_pair, from_y, sum_ref,
-    t_send, t_recv, z_send, z_recv, p_send, p_recv, c_send, c_recv, h_send, h_recv, d_send, d_recv, q_send, q_recv, load,
+    normed_turned, q_raw, k_raw, queries, kv_all, tokens, normed_ref, wq, wk, wv, wo, docs_ref, logits_ref, docs_in, squares, squares_in, scores, totals, bias, partial, from_pair, from_y, sum_ref,
+    t_send, t_recv, z_send, z_recv, p_send, p_recv, c_send, c_recv, h_send, h_recv, d_send, d_recv, q_send, q_recv, load, save,
 ):
     z, x, y, core = place()
     group, part = lax.axis_index("expert"), lax.axis_index("tensor")
@@ -1086,6 +1086,14 @@
         [jnp.sum(q_raw[...] * q_raw[...], axis=-1, keepdims=True), jnp.sum(k_raw[...] * k_raw[...], axis=-1, keepdims=True)]
     )
     sent = exchange(copies, squares, squares_in, q_send, q_recv, mates)
+    saving = []
+
+    def leave(source, target):
+        saving.append(pltpu.make_async_copy(source, target, save.at[len(saving)]))
+        saving[-1].start()
+
+    leave(q_raw, q_out)
+    leave(k_raw, k_out)
     loads[1].wait()
     project(wv, keep_value)
     halo_start(1)
@@ -1095,6 +1103,8 @@
     def _(index):
         columns = pl.ds(pl.multiple_of(index * 256, 256), 256)
         normed_turned[columns, :] = normed_ref[:, columns].T
+
+    leave(normed_turned, normed_out)
 
     for copy in sent:
         copies.arrived(copy)
@@ -1121,6 +1131,7 @@
     gather.spread(1)
     gather.lift(2)
     turn_heads(q_raw, q_gain_ref, factors[:, 0:1], store_query)
+    leave(queries, queries_out)
     for distance in (1, 2):
 
         @pl.when(spot >= distance)
@@ -1178,6 +1189,7 @@
 
     gather.turn(2)
     gather.spread(3)
+    leave(kv_all, kv_out)
     loads[4].wait()
     for index in range(4):
         partial[index // 2, index % 2] = dot(attended[pl.ds(index * rows, rows), :], wo[...]).astype(LOW)
@@ -1205,6 +1217,8 @@
         gates_ref[index, 0:local, :] = gates[index * local : (index + 1) * local]
     own.wait()
     own_copy.wait()
+    for copy in saving:
+        copy.wait()
     for kind in range(2):
         halo_sent(kind)
     for distance in (1, 2):
@@ -1242,8 +1256,10 @@
             jax.ShapeDtypeStruct((depth, 4 * rows, width), LOW),
         ),
         in_specs=[ANY] * 6 + [VMEM] * 9,
-        out_specs=(VMEM,) * 15 + (ANY,),
+        out_specs=(ANY,) * 5 + (VMEM,) * 10 + (ANY,),
         scratch_shapes=[
+            pltpu.VMEM((width, length), LOW), pltpu.VMEM((length, wide), FULL), pltpu.VMEM((length, wide), FULL),
+            pltpu.VMEM((length, wide), LOW), pltpu.VMEM((3, length, 2 * wide), LOW),
             pltpu.VMEM(tokens.shape, LOW), pltpu.VMEM(tokens.shape, LOW), pltpu.VMEM((width, wide), LOW), pltpu.VMEM((width, wide), LOW),
             pltpu.VMEM((width, wide), LOW), pltpu.VMEM((wide, width), LOW), pltpu.VMEM((8, length), jnp.int32),
             pltpu.VMEM((rows, 128), FULL), pltpu.VMEM((2, 8, length), jnp.int32),
@@ -1254,7 +1270,7 @@
         + TensorScatter.scratch(rows, width)[:3]
         + [
             pltpu.VMEM((rows, width), FULL), dma(3), dma(3),
-            *Gather.scratch(depth), dma(2, 3), dma(2, 3), dma(3), dma(3), dma(3), dma(3), dma(7),
+            *Gather.scratch(depth), dma(2, 3), dma(2, 3), dma(3), dma(3), dma(3), dma(3), dma(7), dma(5),
         ],
         compiler_params=comm_params(number),
     )(tokens, *weights, grads, *gains, *tables, docs, gain2, router, picked)
@@ -1263,13 +1279,13 @@
 def attention_back_kernel(
     depth, rows, heads, chain, local,
     sum_ref, gate_cots, probs_ref, picked_ref, state_ref, gain2_ref, router_ref, normed2_ref, grad_ref,
-    query_ref, kv_all, attended, logs, key_docs, query_docs, q_raw, k_raw, q_gain_ref, k_gain_ref, cosine_ref, sine_ref, scales,
-    w_out, produced_ref, normed_ref, wq_ref, wk_ref, wv_ref,
+    query_ref, kv_ref, attended, logs, docs_ref, query_docs, q_ref, k_ref, q_gain_ref, k_gain_ref, cosine_ref, sine_ref, scales,
+    w_out_ref, produced_ref, normed_ref, wq_ref, wk_ref, wv_ref,
     state_cot_ref, vectors, out_ref, normed_part, piece0, piece1, piece2, piece3,
-    low, lows, by_expert, bias, cots, deltas, turned, query_cot, kv_cot, sending, landed, work, raw_cots, flipped, wq, wk, wv,
+    kv_all, key_docs, q_raw, k_raw, w_out, low, lows, by_expert, bias, cots, deltas, turned, query_cot, kv_cot, sending, landed, work, raw_cots, flipped, wq, wk, wv,
     inners, inners_in, staging,
     diagonal, from_x, from_y, from_z, r_send, r_recv, middle, m_send, m_recv,
-    t_send, t_recv, h_send, h_recv, i_send, i_recv, load, saves,
+    t_send, t_recv, h_send, h_recv, i_send, i_recv, load, saves, early_load,
 ):
     z, x, y, core = place()
     group, part = lax.axis_index("expert"), lax.axis_index("tensor")
@@ -1286,6 +1302,12 @@
     for number, (source, target) in enumerate([(wq_ref, wq), (wk_ref, wk), (wv_ref, wv)]):
         others.append(pltpu.make_async_copy(source, target, load.at[depth + number]))
         others[-1].start()
+    early = []
+    for number, (source, target) in enumerate(
+        [(docs_ref, key_docs), (w_out_ref, w_out), (kv_ref, kv_all), (q_ref, q_raw), (k_ref, k_raw)]
+    ):
+        early.append(pltpu.make_async_copy(source, target, early_load.at[number]))
+        early[-1].start()
     mates = mates_of()
     greet(
         [device(swapped(z, step), x, y, core) for step in range(1, depth)]
@@ -1307,6 +1329,7 @@
     scatter.share(3)
     loads[1].wait()
     scatter.share(1)
+    corner(3)
     by_expert[...] = jnp.zeros_like(by_expert)
     for plane in range(depth):
         step = swapped(z, plane)
@@ -1336,16 +1359,19 @@
     state_cot_ref[...] = state_cot
     low[...] = state_cot.astype(LOW)
     gather = TensorGather(copies, low, lows, t_send, t_recv)
-    corner(3)
-    corner(1)
+    scatter.side(3)
+    corner(2)
     router_grad = jnp.dot(
         logit_cot.T, normed2_ref[...].astype(FULL), precision=HIGHEST_PRECISION, preferred_element_type=FULL
     )[:16]
     for index in range(groups):
         vectors[index, 0:16, :] = router_grad[:, index * slice_width : (index + 1) * slice_width]
-    scatter.side(3)
+    early[0].wait()
     mask_bias(bias, key_docs, query_docs, length)
+    for copy in early[1:]:
+        copy.wait()
     gather.cross()
+    scatter.side(2)
     gather.finish()
     for index in range(4):
         cots[pl.ds(index * rows, rows), :] = dot_t(lows[index // 2, index % 2], w_out[...]).astype(LOW)
@@ -1353,7 +1379,6 @@
         columns = pl.ds(head * HD, HD)
         product = cots[:, columns].astype(FULL) * attended[:, columns].astype(FULL)
         deltas[head] = jnp.broadcast_to(jnp.sum(product.T, axis=0, keepdims=True), (8, length))
-    scatter.side(1)
     turned[...] = jnp.zeros_like(turned)
 
     def back(block, store, after):
@@ -1406,15 +1431,14 @@
     back(1, store_in(1), lambda head: pl.when(spot >= 1)(lambda: x_copy(head).start()))
     scatter.climb(3)
     back(0, store_in(0), lambda head: pl.when(spot == 2)(lambda: z_copy(head).start()))
-    scatter.climb(1)
-    corner(2)
     back(2, store_own, relay)
+    scatter.climb(2)
+    corner(1)
     corner(0)
-    scatter.side(2)
     for head in range(heads):
         query_cot[:, pl.ds(head * HD, HD)] = turned[head].T * scale
 
-    scatter.side(0)
+    scatter.side(1)
     saving = {}
 
     def weight_piece(number, right, target):
@@ -1435,7 +1459,7 @@
     weight_piece(0, attended[...], piece0)
     normed_copy = pltpu.make_async_copy(normed_ref, flipped, load.at[depth + 3])
     normed_copy.start()
-    scatter.climb(2)
+    scatter.side(0)
     factors = as_columns(scales[...])
 
     def turn_back(cot, raw, gain_ref, factor, first):
@@ -1454,6 +1478,7 @@
 
     query_inner = turn_back(query_cot, q_raw, q_gain_ref, factors[:, 0:1], 18)
 
+    scatter.climb(1)
     def take(slot, head):
         (z_copy, x_copy)[slot](head).wait_recv()
         for part in range(2):
@@ -1531,9 +1556,11 @@
             jax.ShapeDtypeStruct((2, 2, rows, width), LOW),
             piece, piece, piece, piece,
         ),
-        in_specs=[VMEM] * 23 + [ANY] * 5,
+        in_specs=[VMEM] * 10 + [ANY] + [VMEM] * 2 + [ANY] + [VMEM] + [ANY] * 2 + [VMEM] * 5 + [ANY] * 6,
         out_specs=(VMEM,) * 4 + (ANY,) * 4,
         scratch_shapes=[
+            pltpu.VMEM(kv_all.shape, LOW), pltpu.VMEM((3 * length, 1), jnp.int32), pltpu.VMEM((length, wide), FULL),
+            pltpu.VMEM((length, wide), FULL), pltpu.VMEM((wide, width), LOW),
             pltpu.VMEM((rows, width), LOW), pltpu.VMEM((2, 2, rows, width), LOW), pltpu.VMEM((128, rows), FULL),
             pltpu.VMEM((3 * length, length), LOW), pltpu.VMEM((length, wide), LOW),
             pltpu.VMEM((heads, 8, length), FULL), pltpu.VMEM((heads, HD, length), FULL),
@@ -1545,7 +1572,7 @@
         ]
         + Scatter.scratch(depth, rows, width)
         + [pltpu.VMEM((depth // 2, 4, rows // 4, width), LOW), dma(depth // 2, 4), dma(depth // 2, 4)]
-        + [dma(4), dma(3), dma(2, heads), dma(2, heads), dma(3), dma(3), dma(depth + 4), dma(2)],
+        + [dma(4), dma(3), dma(2, heads), dma(2, heads), dma(3), dma(3), dma(depth + 4), dma(2), dma(5)],
         compiler_params=comm_params(number),
     )(*rows_of, *attention, *sources, produced, normed, *weights)
 
@@ -1669,13 +1696,13 @@
     ) = refs[:11]
     sums, refs = refs[11 : 11 + matrices], refs[11 + matrices :]
     (
-        input_grads, outputs, vector_sum,
+        input_out, output_out, vector_sum,
         gate_own, up_own, down_own,
-        work, from_x, from_z, partial, from_pair, from_y, normed_grad, low, vectors, vector_in, vector_mid, vector_turn,
+        input_grads, outputs, work, from_x, from_z, partial, from_pair, from_y, normed_grad, low, vectors, vector_in, vector_mid, vector_turn,
         tiles, turned, acts, gated_turned, near, far, near_down, far_down, other, other_down,
         f_work, f_from_z, f_from_x, f_load, f_send, f_recv,
         e_load, e_send, e_recv, t_send, t_recv, g_send, g_recv, o_send, o_recv, v_send, v_recv, u_send, u_recv,
-        tile_load, act_load, save, pair_send, pair_recv, local_sem,
+        tile_load, act_load, save, pair_send, pair_recv, local_sem, leave_sem,
     ) = refs
     z, x, y, core = place()
     group = 2 * z + x
@@ -1706,8 +1733,7 @@
     scatter = TensorScatter(copies, partial, from_pair, from_y, t_send, t_recv)
     scatter.begin()
     out_gather = TensorGather(copies, out_ref, outputs, o_send, o_recv)
-    for index in range(1, matrices):
-        experts.begin(index)
+    experts.begin(1)
     act_copies = [fetch(gate_grad_ref, acts.at[0], act_load.at[0]), fetch(up_grad_ref, acts.at[1], act_load.at[1])]
 
     def fetch_tile(number):
@@ -1821,6 +1847,8 @@
         vector_copies.append(
             copies.start(remote(vectors.at[to], vector_in.at[number], v_send.at[number], v_recv.at[number], peer))
         )
+    for index in range(2, matrices):
+        experts.begin(index)
 
     for step in experts.steps[2:]:
         experts.climb(0, step)
@@ -1837,18 +1865,17 @@
     for owner, target in ((1 - core, turned), (core, gated_turned)):
         target[...] = acts[0, :, pl.ds(pl.multiple_of(first_unit(owner), hidden), local * hidden)].T
     experts.result(0, sums[0])
+    out_gather.finish()
+    leaving = [fetch(outputs, output_out, leave_sem.at[0])]
     down(0)
+    grad_gather.finish()
+    leaving.append(fetch(input_grads, input_out, leave_sem.at[1]))
     experts.climb(2, experts.steps[0])
     down(1)
     for step in experts.steps[1:]:
         experts.climb(2, step)
     down(2)
     experts.result(1, sums[1])
-    down(3)
-    settle_down(3)
-    for index in range(3, matrices):
-        for step in experts.steps:
-            experts.climb(index, step)
     for copy in vector_copies:
         copies.arrived(copy)
     total = vectors[group]
@@ -1859,11 +1886,8 @@
         copies.start(remote(vector_mid, vector_turn.at[number], u_send.at[number], u_recv.at[number], device(*mate)))
         for number, mate in enumerate(mates)
     ]
-    for index in range(2, matrices):
-        experts.result(index, sums[index])
-    z_first.result(sums[-1].at[:, eighth])
-    out_gather.finish()
-    grad_gather.finish()
+    down(3)
+    settle_down(3)
     for copy in turn_copies:
         copies.arrived(copy)
     total = vector_mid[...]
@@ -1871,6 +1895,14 @@
         total = total + vector_turn[number]
     keep = lax.broadcasted_iota(jnp.int32, total.shape, 0) < 18
     vector_sum[...] = jnp.where(keep, total, vector_mid[...])
+    for index in range(3, matrices):
+        for step in experts.steps:
+            experts.climb(index, step)
+    for index in range(2, matrices):
+        experts.result(index, sums[index])
+    z_first.result(sums[-1].at[:, eighth])
+    for copy in leaving:
+        copy.wait()
     for entries in saving.values():
         for copy, remote_one in entries:
             if not remote_one:
@@ -1896,8 +1928,9 @@
             jax.ShapeDtypeStruct(wide, FULL), jax.ShapeDtypeStruct(wide, FULL), jax.ShapeDtypeStruct(tall, FULL),
         ),
         in_specs=[ANY] * (matrices + 1) + [VMEM] * 5 + [ANY] * 5,
-        out_specs=(VMEM,) * (matrices + 3) + (ANY,) * 3,
-        scratch_shapes=[pltpu.VMEM((matrices, depth, piece, columns), LOW)] * 3
+        out_specs=(VMEM,) * matrices + (ANY, ANY, VMEM) + (ANY,) * 3,
+        scratch_shapes=[pltpu.VMEM((2, 2, rows, width), LOW)] * 2
+        + [pltpu.VMEM((matrices, depth, piece, columns), LOW)] * 3
         + TensorScatter.scratch(rows, width)[:3]
         + [
             pltpu.VMEM((rows, width), FULL), pltpu.VMEM((rows, width), LOW),
@@ -1913,7 +1946,7 @@
             dma(matrices, depth), dma(2, matrices, depth), dma(2, matrices, depth),
             dma(3), dma(3), dma(4), dma(3), dma(4), dma(3),
             dma(2 * depth - 1), dma(2 * depth - 1), dma(3), dma(3),
-            dma(2), dma(2), dma(3, 2), dma(3, width // tile), dma(3, width // tile), dma(1),
+            dma(2), dma(2), dma(3, 2), dma(3, width // tile), dma(3, width // tile), dma(1), dma(2),
         ],
         compiler_params=comm_params(number),
     )(*parts, normed_part, tokens, state_cot, gain, out, vectors, normed, grads, gated, gate_grad, up_grad)

time: 492 us -> 486 us (0.988)
  Pallas kernels: 477 us -> 471 us
where the time goes in v9:
time: 486 us; the launch traced here: 477 us
  Pallas kernels  471 us (97%)
    pallas_call x1, Pallas kernels, run_experts(): pl.pallas_call(functools.partial(experts_kernel, depth, rows, local, hidd...  150 us
    pallas_call x1, Pallas kernels, run_attention_back(): pl.pallas_call(functools.partial(attention_back_kernel, depth, rows, head...  109 us
    pallas_call x1, Pallas kernels, run_attention(): pl.pallas_call(functools.partial(attention_kernel, depth, rows, heads, ch...  99.5 us
    pallas_call x1, Pallas kernels, run_gradients(): pl.pallas_call(functools.partial(gradients_kernel, depth, rows, local, hi...  98.9 us
    pallas_call x1, Pallas kernels, finish(): pl.pallas_call(functools.partial(finish_kernel, experts, heads), grid=(st...  14.1 us

profile of v9, /device:TPU:10, one launch (start us, length us, event | category | flops | bytes accessed | tf_op | source)
XLA Modules:
  0.0 477.0 jit_solution(4878125125147119136)
XLA Ops:
  0.6 0.0 copy-start
  0.7 0.7 copy-done
  1.4 0.1 copy.31
  1.5 0.3 fusion
  1.7 0.6 convert_element_type.11.picked_ref
  2.4 0.1 broadcast_multiply_fusion
  2.5 1.8 fusion.1
  4.3 0.1 slice_negate_fusion
  4.4 0.8 pad_maximum_fusion.1.sine_ref
  5.3 99.5 %shard_map.263 = (bf16[2048,512]{1,0:T(8,128)(2,1)}, f32[512,512]{1,0:T(8,128)}, f32[512,512]{1,0:T(8,128)}, bf16[512,512]{1,0:T(8,128)(2,1)}, bf16[3,512,1024]{...) custom-call(bf16[512,2048]{1,0:T(8,128)(2,1)} %tokens_ref.1, ...), custom_call_target="tpu_custom_call" | custom-call | tf_op jit(solution)/shard_map/pallas_call | solution.py:1238
  104.8 149.6 %shard_map.264 = (f32[128,2048]{1,0:T(8,128)}, f32[4,4,8,128]{3,2,1,0:T(8,128)}, bf16[4,512,2048]{2,1,0:T(8,128)(2,1)}, bf16[4,512,1024]{2,1,0:T(8,128)(2,1)}, b...) custom-call(bf16[128,2048]{1,0:T(8,128)(2,1)} %get-tuple-element.69.x_ref.normed2_ref, ...), custom_call_target="tpu_custom_call" | custom-call | tf_op jit(solution)/shard_map/pallas_call | solution.py:833
  254.4 109.3 %shard_map.265 = (f32[128,2048]{1,0:T(8,128)}, f32[8,32,256]{2,1,0:T(8,128)}, bf16[128,2048]{1,0:T(8,128)(2,1)}, bf16[2,2,128,2048]{3,2,1,0:T(8,128)(2,1)}, bf16...) custom-call(f32[128,2048]{1,0:T(8,128)} %get-tuple-element.72.sum_re, ...), custom_call_target="tpu_custom_call" | custom-call | tf_op jit(solution)/shard_map/pallas_call | solution.py:1550
  363.7 98.9 %shard_map.266 = (f32[256,512]{1,0:T(8,128)}, f32[256,512]{1,0:T(8,128)}, f32[256,512]{1,0:T(8,128)}, f32[256,512]{1,0:T(8,128)}, bf16[2,2,128,2048]{3,2,1,0:T(8...) custom-call(bf16[4,2,256,512]{3,2,1,0:T(8,128)(2,1)} %get-tuple-elem, ...), custom_call_target="tpu_custom_call" | custom-call | tf_op jit(solution)/shard_map/pallas_call | solution.py:1923
  462.6 0.0 copy-start.1
  462.6 14.1 %shard_map.267 = (f32[512,2048]{1,0:T(8,128)}, bf16[512,2048]{1,0:T(8,128)(2,1)}, f32[256,512]{1,0:T(8,128)}, f32[256,512]{1,0:T(8,128)}, f32[256,512]{1,0:T(8,1...) custom-call(bf16[512,2048]{1,0:T(8,128)(2,1)} %bitcast.30, ...), custom_call_target="tpu_custom_call" | custom-call | tf_op jit(solution)/shard_map/pallas_call | solution.py:1994
  476.7 0.0 copy-done.1
  (3 shorter events, 0.0 us)
Async XLA Ops:
  0.6 0.7 copy-start
  462.6 14.1 %copy-start.1 = (s32[512,8]{0,1:T(8,128)S(1)}, s32[512,8]{0,1:T(8,128)}, u32[]{:S(2)}) copy-start(s32[512,8]{0,1:T(8,128)} %param.18) | copy-start | bytes 49156

commit v10 on v9

--- a/solution.py
+++ b/solution.py
@@ -1,5 +1,6 @@
 import functools
 
+import numpy as np
 import jax
 import jax.numpy as jnp
 from jax import lax
@@ -390,6 +391,15 @@
 
 
 MESH = pl.DeviceIdType.MESH
+
+
+def whole_tables():
+    angles = np.arange(LENGTH)[:, None] * 10000.0 ** (-np.arange(HD // 2) * 2.0 / HD)[None, :]
+    cosine, sine = np.cos(angles), np.sin(angles)
+    cosine, sine = np.concatenate([cosine, cosine], axis=1), np.concatenate([-sine, sine], axis=1)
+    return cosine.astype(np.float32), sine.astype(np.float32)
+
+
 ANY = pl.BlockSpec(memory_space=pl.ANY)
 VMEM = pl.BlockSpec(memory_space=pltpu.VMEM)
 VMEM_BYTES = 62 * 1024 * 1024
@@ -478,7 +488,7 @@
 
 
 class Gather:
-    def __init__(self, copies, block, target, rows, z_send, z_recv, p_send, p_recv, c_send, c_recv):
+    def __init__(self, copies, block, target, rows, cut, z_send, z_recv, p_send, p_recv, c_send, c_recv):
         self.copies, self.block, self.target, self.rows = copies, block, target, rows
         self.z_send, self.z_recv, self.p_send, self.p_recv = z_send, z_recv, p_send, p_recv
         self.c_send, self.c_recv = c_send, c_recv
@@ -490,7 +500,7 @@
         self.along, self.planes, self.diagonals, self.shared = {}, {}, {}, {}
         edge = rows * 3 // 8
         self.middle = (edge, rows - 2 * edge)
-        self.halves = {0: ((0, rows // 2), (rows // 2, rows // 2)), 1: ((0, edge), (rows - edge, edge))}
+        self.halves = {0: ((0, cut), (cut, rows - cut)), 1: ((0, edge), (rows - edge, edge))}
 
     def at(self, step, spot, span):
         first, count = span
@@ -690,7 +700,7 @@
                 )
             )
         )
-    gather = Gather(copies, x_ref, x_all, rows, z_send, z_recv, p_send, p_recv, c_send, c_recv)
+    gather = Gather(copies, x_ref, x_all, rows, rows // 2, z_send, z_recv, p_send, p_recv, c_send, c_recv)
     gather.spread(0)
     gather.lift(1)
     gather.lift(2)
@@ -965,8 +975,8 @@
 def attention_kernel(
     depth, rows, heads, chain, local,
     tokens_ref, wq_ref, wk_ref, wv_ref, wo_ref, grads_ref,
-    gain1_ref, q_gain_ref, k_gain_ref, cosine_ref, sine_ref, docs_row, gain2_ref, router_ref, picked_ref,
-    normed_out, q_out, k_out, queries_out, kv_out, key_docs, scales, attended, logs, state_ref, normed2_ref, probs_ref, gates_ref, own_tokens, own_grads,
+    gain1_ref, q_gain_ref, k_gain_ref, cosines_ref, sines_ref, docs_row, gain2_ref, router_ref, picked_ref,
+    normed_out, q_out, k_out, queries_out, kv_out, key_docs, scales, attended, logs, state_ref, normed2_ref, probs_ref, gates_ref, own_tokens, own_grads, cosine_ref, sine_ref,
     all_grad,
     normed_turned, q_raw, k_raw, queries, kv_all, tokens, normed_ref, wq, wk, wv, wo, docs_ref, logits_ref, docs_in, squares, squares_in, scores, totals, bias, partial, from_pair, from_y, sum_ref,
     t_send, t_recv, z_send, z_recv, p_send, p_recv, c_send, c_recv, h_send, h_recv, d_send, d_recv, q_send, q_recv, load, save,
@@ -982,6 +992,11 @@
     docs_ref[...] = jnp.broadcast_to(docs_row[...], docs_ref.shape)
     own_copy = pltpu.make_async_copy(grad_ref, own_grads, load.at[6])
     own_copy.start()
+    positions = pl.ds(pl.multiple_of(lax.rem(lax.axis_index("expert"), chain) * tokens.shape[0], 8), tokens.shape[0])
+    tables = []
+    for number, (source, target) in enumerate([(cosines_ref, cosine_ref), (sines_ref, sine_ref)]):
+        tables.append(pltpu.make_async_copy(source.at[positions], target, load.at[7 + number]))
+        tables[-1].start()
     loads = []
     for number, (source, target) in enumerate([(tokens_ref, tokens), (wv_ref, wv), (wk_ref, wk), (wq_ref, wq), (wo_ref, wo)]):
         loads.append(pltpu.make_async_copy(source, target, load.at[number]))
@@ -1002,7 +1017,7 @@
                 docs_ref, docs_in.at[2 - distance], d_send.at[distance], d_recv.at[distance], (group + distance, part)
             ).start()
 
-    gather = Gather(copies, grad_ref, all_grad, rows, z_send, z_recv, p_send, p_recv, c_send, c_recv)
+    gather = Gather(copies, grad_ref, all_grad, rows, rows * 3 // 8, z_send, z_recv, p_send, p_recv, c_send, c_recv)
     gather.spread(0)
     gather.lift(1)
     own = pltpu.make_async_copy(grad_ref, gather.at(0, gather.here, (0, rows)), load.at[5])
@@ -1126,6 +1141,8 @@
     def store_query(head, turned):
         queries[:, pl.ds(head * HD, HD)] = turned
 
+    for copy in tables:
+        copy.wait()
     turn_heads(k_raw, k_gain_ref, factors[:, 1:2], store_key)
     halo_start(0)
     gather.spread(1)
@@ -1253,10 +1270,12 @@
             jax.ShapeDtypeStruct((2 * depth, 8, rows), FULL),
             jax.ShapeDtypeStruct((rows, width), LOW),
             jax.ShapeDtypeStruct((rows, width), LOW),
+            jax.ShapeDtypeStruct((length, HD), FULL),
+            jax.ShapeDtypeStruct((length, HD), FULL),
             jax.ShapeDtypeStruct((depth, 4 * rows, width), LOW),
         ),
-        in_specs=[ANY] * 6 + [VMEM] * 9,
-        out_specs=(ANY,) * 5 + (VMEM,) * 10 + (ANY,),
+        in_specs=[ANY] * 6 + [VMEM] * 3 + [ANY] * 2 + [VMEM] * 4,
+        out_specs=(ANY,) * 5 + (VMEM,) * 12 + (ANY,),
         scratch_shapes=[
             pltpu.VMEM((width, length), LOW), pltpu.VMEM((length, wide), FULL), pltpu.VMEM((length, wide), FULL),
             pltpu.VMEM((length, wide), LOW), pltpu.VMEM((3, length, 2 * wide), LOW),
@@ -1270,7 +1289,7 @@
         + TensorScatter.scratch(rows, width)[:3]
         + [
             pltpu.VMEM((rows, width), FULL), dma(3), dma(3),
-            *Gather.scratch(depth), dma(2, 3), dma(2, 3), dma(3), dma(3), dma(3), dma(3), dma(7), dma(5),
+            *Gather.scratch(depth), dma(2, 3), dma(2, 3), dma(3), dma(3), dma(3), dma(3), dma(9), dma(5),
         ],
         compiler_params=comm_params(number),
     )(tokens, *weights, grads, *gains, *tables, docs, gain2, router, picked)
@@ -1371,7 +1390,6 @@
     for copy in early[1:]:
         copy.wait()
     gather.cross()
-    scatter.side(2)
     gather.finish()
     for index in range(4):
         cots[pl.ds(index * rows, rows), :] = dot_t(lows[index // 2, index % 2], w_out[...]).astype(LOW)
@@ -1379,6 +1397,7 @@
         columns = pl.ds(head * HD, HD)
         product = cots[:, columns].astype(FULL) * attended[:, columns].astype(FULL)
         deltas[head] = jnp.broadcast_to(jnp.sum(product.T, axis=0, keepdims=True), (8, length))
+    scatter.side(2)
     turned[...] = jnp.zeros_like(turned)
 
     def back(block, store, after):
@@ -2028,16 +2047,13 @@
     def across(vector):
         return vector.reshape(1, -1)
 
-    positions = group * row_count + jnp.arange(row_count, dtype=jnp.int32)
-    cosine, sine = (table[:, 0, :] for table in rope_tables(positions % LENGTH))
-    sine = jnp.concatenate([-sine[:, : HD // 2], sine[:, HD // 2 :]], axis=1)
     picked = jnp.any(quarter(routes)[:, :, None] == jnp.arange(128, dtype=jnp.int32)[None, None, :], axis=1).astype(FULL)
     query_gain, key_gain = across(q_gain), across(k_gain)
     (
         normed_one, query_raw, key_raw, queries, kv_all, key_docs, scales, attended, logs, state, normed_two, router_probs, gates,
-        own_tokens, own_grads, all_grad,
+        own_tokens, own_grads, cosine, sine, all_grad,
     ) = run_attention(
-        tokens, (w_query, w_key, w_value, w_out), out_grad, (across(norm1_gain), query_gain, key_gain), (cosine, sine), across(documents),
+        tokens, (w_query, w_key, w_value, w_out), out_grad, (across(norm1_gain), query_gain, key_gain), [jnp.asarray(table) for table in whole_tables()], across(documents),
         across(norm2_gain), router_w.T, picked, depth, chain, local_experts, 3,
     )
 

time: 486 us -> 479 us (0.986)
  no operation moved by 1% of the time
where the time goes in v10:
time: 479 us; the launch traced here: 471 us
  Pallas kernels  468 us (98%)
    pallas_call x1, Pallas kernels, run_experts(): pl.pallas_call(functools.partial(experts_kernel, depth, rows, local, hidd...  149 us
    pallas_call x1, Pallas kernels, run_attention_back(): pl.pallas_call(functools.partial(attention_back_kernel, depth, rows, head...  109 us
    pallas_call x1, Pallas kernels, run_attention(): pl.pallas_call(functools.partial(attention_kernel, depth, rows, heads, ch...  99.5 us
    pallas_call x1, Pallas kernels, run_gradients(): pl.pallas_call(functools.partial(gradients_kernel, depth, rows, local, hi...  96.7 us
    pallas_call x1, Pallas kernels, finish(): pl.pallas_call(functools.partial(finish_kernel, experts, heads), grid=(st...  14.1 us

profile of v10, /device:TPU:10, one launch (start us, length us, event | category | flops | bytes accessed | tf_op | source)
XLA Modules:
  0.0 470.8 jit_solution(10349321239431904600)
XLA Ops:
  0.6 0.0 copy-start
  0.7 0.7 copy-done
  1.4 0.1 copy.33
  1.5 0.3 fusion
  1.7 0.6 convert_element_type.3.picked_ref
  2.4 99.5 %shard_map.281 = (bf16[2048,512]{1,0:T(8,128)(2,1)}, f32[512,512]{1,0:T(8,128)}, f32[512,512]{1,0:T(8,128)}, bf16[512,512]{1,0:T(8,128)(2,1)}, bf16[3,512,1024]{...) custom-call(bf16[512,2048]{1,0:T(8,128)(2,1)} %tokens_ref.1, ...), custom_call_target="tpu_custom_call" | custom-call | tf_op jit(solution)/shard_map/pallas_call | solution.py:1255
  101.9 149.1 %shard_map.282 = (f32[128,2048]{1,0:T(8,128)}, f32[4,4,8,128]{3,2,1,0:T(8,128)}, bf16[4,512,2048]{2,1,0:T(8,128)(2,1)}, bf16[4,512,1024]{2,1,0:T(8,128)(2,1)}, b...) custom-call(bf16[128,2048]{1,0:T(8,128)(2,1)} %get-tuple-element.71.x_ref.normed2_ref, ...), custom_call_target="tpu_custom_call" | custom-call | tf_op jit(solution)/shard_map/pallas_call | solution.py:843
  251.0 108.6 %shard_map.283 = (f32[128,2048]{1,0:T(8,128)}, f32[8,32,256]{2,1,0:T(8,128)}, bf16[128,2048]{1,0:T(8,128)(2,1)}, bf16[2,2,128,2048]{3,2,1,0:T(8,128)(2,1)}, bf16...) custom-call(f32[128,2048]{1,0:T(8,128)} %get-tuple-element.74.sum_re, ...), custom_call_target="tpu_custom_call" | custom-call | tf_op jit(solution)/shard_map/pallas_call | solution.py:1569
  359.6 96.7 %shard_map.284 = (f32[256,512]{1,0:T(8,128)}, f32[256,512]{1,0:T(8,128)}, f32[256,512]{1,0:T(8,128)}, f32[256,512]{1,0:T(8,128)}, bf16[2,2,128,2048]{3,2,1,0:T(8...) custom-call(bf16[4,2,256,512]{3,2,1,0:T(8,128)(2,1)} %get-tuple-elem, ...), custom_call_target="tpu_custom_call" | custom-call | tf_op jit(solution)/shard_map/pallas_call | solution.py:1942
  456.4 0.0 copy-start.1
  456.4 14.1 %shard_map.285 = (f32[512,2048]{1,0:T(8,128)}, bf16[512,2048]{1,0:T(8,128)(2,1)}, f32[256,512]{1,0:T(8,128)}, f32[256,512]{1,0:T(8,128)}, f32[256,512]{1,0:T(8,1...) custom-call(bf16[512,2048]{1,0:T(8,128)(2,1)} %bitcast.30, ...), custom_call_target="tpu_custom_call" | custom-call | tf_op jit(solution)/shard_map/pallas_call | solution.py:2013
  470.5 0.0 copy-done.1
  (1 shorter events, 0.0 us)
Async XLA Ops:
  0.6 0.7 copy-start
  456.4 14.1 %copy-start.1 = (s32[512,8]{0,1:T(8,128)S(1)}, s32[512,8]{0,1:T(8,128)}, u32[]{:S(2)}) copy-start(s32[512,8]{0,1:T(8,128)} %param.20) | copy-start | bytes 49156
